TPU v7x, 128 devices: a whole 4x4x4 slice. The times are simulated.
128 devices in a mesh: dp: 2 (over core), vocab: 16 (over y, z), mp: 4 (over x).
Axes of the slice: x: 4, y: 4, z: 4, core: 2. Of those that a mesh axis runs over, the one named last changes fastest.
Arguments:
- grad_parts: bfloat16 [2, 16384, 16384], P('dp', 'vocab', 'mp'), may hold values from -150 to 150
- old_basis: float32 [64, 16384], P(None, 'mp'), may hold values from -0.046875 to 0.046875
- first_moment: float32 [64, 16384], P(None, 'mp'), may hold values from -3 to 3
- second_moment: float32 [64, 16384], P(None, 'mp'), may hold values from 0.5 to 4
Outputs:
- update: bfloat16 [16384, 16384], P('vocab', 'mp')
- new_basis: float32 [64, 16384], P(None, 'mp')
- new_first: float32 [64, 16384], P(None, 'mp')
- new_second: float32 [64, 16384], P(None, 'mp')
All inputs are finite; a program needn't handle non-finite values.
Results may differ from a plain program's by a relative error of at most 0.035.
Values may be sent and summed in bfloat16 or wider, within the bound.
No kernel may reach another device: no remote copies, remote signals or barrier semaphores. Data moves between devices by JAX's collectives and lax.ppermute only.
A program may use at most 128 MiB of HBM per device.

v0:
```python
import math

import jax
import jax.numpy as jnp
from jax import lax
from jax.sharding import PartitionSpec as P

ITERS = 2


def factor_solve(gram, block):
    factor = jnp.linalg.cholesky(gram)
    return jax.scipy.linalg.solve_triangular(factor, block, lower=True)


def gram_of(block):
    return jnp.dot(block, block.T, precision=lax.Precision.HIGHEST)


def rows_times(basis_half, slab):
    return lax.dot_general(
        basis_half, slab, (((1,), (1,)), ((), ())), preferred_element_type=jnp.float32
    )


def local(grad_parts, old_basis, first_moment, second_moment):
    partial_value = grad_parts[0]
    owned = lax.psum_scatter(partial_value, "dp", scatter_dimension=0, tiled=True).astype(
        jnp.float32
    )
    owned_high = owned.astype(jnp.bfloat16)
    owned_low = (owned - owned_high.astype(jnp.float32)).astype(jnp.bfloat16)
    basis = old_basis
    for step in range(ITERS):
        basis_half = basis.astype(jnp.bfloat16)
        local_rows = rows_times(basis_half, owned_high) + rows_times(basis_half, owned_low)
        rows = lax.psum(local_rows.astype(jnp.bfloat16), "mp").astype(jnp.float32)
        row_gram = lax.psum(gram_of(rows), ("dp", "vocab"))
        left_half = factor_solve(row_gram, rows).astype(jnp.bfloat16)
        local_cols = jnp.dot(left_half, owned_high, preferred_element_type=jnp.float32) + jnp.dot(
            left_half, owned_low, preferred_element_type=jnp.float32
        )
        columns = lax.psum(local_cols.astype(jnp.bfloat16), ("dp", "vocab")).astype(jnp.float32)
        column_gram = lax.psum(gram_of(columns), "mp")
        basis = factor_solve(column_gram, columns)
    new_first = 0.9 * first_moment + 0.1 * columns
    new_second = 0.999 * second_moment + 0.001 * columns * columns
    corr_one = 1.0 - 0.9**10
    corr_two = 1.0 - 0.999**10
    direction = new_first / corr_one / (jnp.sqrt(new_second / corr_two) + 1e-08)
    direction_half = direction.astype(jnp.bfloat16)
    vocab_total = partial_value.shape[0] * lax.axis_size("vocab")
    update = lax.dot_general(
        left_half, direction_half, (((0,), (0,)), ((), ())), preferred_element_type=jnp.float32
    )
    update = (update * math.sqrt(vocab_total)).astype(jnp.bfloat16)
    update = lax.all_gather(update, "dp", axis=0, tiled=True)
    return (update, basis, new_first, new_second)


def solution(mesh):
    placed = (P("dp", "vocab", "mp"), P(None, "mp"), P(None, "mp"), P(None, "mp"))
    return jax.shard_map(
        local,
        mesh=mesh,
        in_specs=placed,
        out_specs=(P("vocab", "mp"), P(None, "mp"), P(None, "mp"), P(None, "mp")),
        check_vma=False,
    )
```

profile of v0, /device:TPU:1, one launch (start us, length us, event | category | flops | bytes accessed | tf_op | source)
XLA Modules:
  0.0 702.6 jit_solution(2374228502697008098)
XLA Ops:
  7.9 25.6 %reduce-scatter.2.cloned.1.call-done = bf16[512,4096]{1,0:T(8,128)(2,1)} async-done(((bf16[1024,4096]{1,0:T(8,128)(2,1)}), bf16[512,4096]{1,0:T(8,128)(2,1)}) %reduce-scatter.2.cloned.1.call-update) | async-done | bytes 4194320 | tf_op jit(solution)/shard_map/reduce_scatter | solution.py:28
  33.6 3.7 fusion.6
  37.3 2.0 fusion.7
  39.4 39.9 %all-reduce.5.cloned.1.call-done = bf16[64,512]{1,0:T(8,128)(2,1)} async-done(((bf16[64,512]{1,0:T(8,128)(2,1)}), bf16[64,512]{1,0:T(8,128)(2,1)}) %all-reduce.5.cloned.1.call-update) | async-done | bytes 65552 | tf_op jit(solution)/shard_map/psum | solution.py:37
  80.4 131.2 %psum.57 = f32[64,64]{0,1:T(8,128)S(1)} all-reduce(f32[64,64]{0,1:T(8,128)S(1)} %fusion.38), channel_id=1, replica_groups=mesh['dp'=2,'vocab'=16,'mp'=4] {'dp','vocab'}, use_global_device_ids=true, to_apply=%region_2.0 | all-reduce | flops 4096 | bytes 32768 | tf_op jit(solution)/shard_map/psum | solution.py:38
  211.6 5.8 cholesky.74
  218.8 4.9 custom-call.10
  223.8 1.3 convolution_convert_fusion.2
  225.1 3.0 fusion.39
  228.1 1.8 fusion
  230.0 98.7 %all-reduce.7.cloned.1.call-done = bf16[64,4096]{1,0:T(8,128)(2,1)} async-done(((bf16[64,4096]{1,0:T(8,128)(2,1)}), bf16[64,4096]{1,0:T(8,128)(2,1)}) %all-reduce.7.cloned.1.call-update) | async-done | bytes 524304 | tf_op jit(solution)/shard_map/psum | solution.py:43
  328.7 1.5 fusion.40
  330.2 13.2 %psum.59 = f32[64,64]{0,1:T(8,128)S(1)} all-reduce(f32[64,64]{0,1:T(8,128)S(1)} %fusion.40), channel_id=1, replica_groups=mesh['dp'=2,'vocab'=16,'mp'=4] {'mp'}, use_global_device_ids=true, to_apply=%region_6.9 | all-reduce | flops 4096 | bytes 32768 | tf_op jit(solution)/shard_map/psum | solution.py:44
  343.6 5.8 cholesky.85
  350.8 4.9 custom-call.11
  355.7 2.2 convolution_convert_fusion
  357.9 3.6 fusion.2
  361.5 2.0 fusion.8
  363.6 40.2 %all-reduce.9.cloned.1.call-done = bf16[64,512]{1,0:T(8,128)(2,1)} async-done(((bf16[64,512]{1,0:T(8,128)(2,1)}), bf16[64,512]{1,0:T(8,128)(2,1)}) %all-reduce.9.cloned.1.call-update) | async-done | bytes 65552 | tf_op jit(solution)/shard_map/psum | solution.py:37
  404.9 131.4 %psum.61 = f32[64,64]{0,1:T(8,128)S(1)} all-reduce(f32[64,64]{0,1:T(8,128)S(1)} %fusion.41), channel_id=1, replica_groups=mesh['dp'=2,'vocab'=16,'mp'=4] {'dp','vocab'}, use_global_device_ids=true, to_apply=%region_8.0 | all-reduce | flops 4096 | bytes 32768 | tf_op jit(solution)/shard_map/psum | solution.py:38
  536.4 5.8 cholesky.96
  543.6 4.9 custom-call.12
  549.8 3.0 fusion.42
  552.8 1.8 fusion.1
  554.8 98.7 %all-reduce.11.cloned.1.call-done = bf16[64,4096]{1,0:T(8,128)(2,1)} async-done(((bf16[64,4096]{1,0:T(8,128)(2,1)}), bf16[64,4096]{1,0:T(8,128)(2,1)}) %all-reduce.11.cloned.1.call-update) | async-done | bytes 524304 | tf_op jit(solution)/shard_map/psum | solution.py:43
  653.5 1.3 fusion.9
  655.8 3.3 multiply_convert_fusion
  660.5 13.2 %psum.63 = f32[64,64]{0,1:T(8,128)S(1)} all-reduce(f32[64,64]{0,1:T(8,128)S(1)} %fusion.43), channel_id=1, replica_groups=mesh['dp'=2,'vocab'=16,'mp'=4] {'mp'}, use_global_device_ids=true, to_apply=%region_10.14 | all-reduce | flops 4096 | bytes 32768 | tf_op jit(solution)/shard_map/psum | solution.py:44
  673.8 5.8 cholesky.107
  681.0 4.9 custom-call.13
  685.9 2.0 fusion.4
  687.9 7.9 %copy.25 = bf16[1024,4096]{1,0:T(8,128)(2,1)} copy(bf16[1024,4096]{1,0:T(8,128)(2,1)} %all-gather.2.cloned.1.call-done) | data formatting | bytes 16777216
  (57 shorter events, 12.4 us)
Async XLA Ops:
  7.2 26.4 %reduce-scatter.2.cloned.1.call-start = ((), (), s32[]{:S(2)}) async-start(), calls=%async_computation.1 | async-start | bytes 12582912 | tf_op jit(solution)/shard_map/reduce_scatter | solution.py:28
  7.2 26.4 %copy-start.5 = (f32[64,4096]{1,0:T(8,128)S(1)}, f32[64,4096]{1,0:T(8,128)}, u32[]{:S(2)}) copy-start(f32[64,4096]{1,0:T(8,128)} %param.10) | copy-start | bytes 3145732
  7.9 71.4 %all-reduce.5.cloned.1.call-start = ((), (), s32[]{:S(2)}) async-start(), calls=%async_computation.2 | async-start | bytes 131072 | tf_op jit(solution)/shard_map/psum | solution.py:37
  33.6 3.7 copy-start
  39.4 289.4 %all-reduce.7.cloned.1.call-start = ((), (), s32[]{:S(2)}) async-start(), calls=%async_computation.3 | async-start | bytes 1048576 | tf_op jit(solution)/shard_map/psum | solution.py:43
  223.7 4.4 copy-start.1
  230.0 173.9 %all-reduce.9.cloned.1.call-start = ((), (), s32[]{:S(2)}) async-start(), calls=%async_computation.4 | async-start | bytes 131072 | tf_op jit(solution)/shard_map/psum | solution.py:37
  355.7 5.9 copy-start.2
  363.6 289.9 %all-reduce.11.cloned.1.call-start = ((), (), s32[]{:S(2)}) async-start(), calls=%async_computation.5 | async-start | bytes 1048576 | tf_op jit(solution)/shard_map/psum | solution.py:43
  548.4 4.4 copy-start.3
  552.8 100.7 %copy-start.6 = (f32[64,4096]{1,0:T(8,128)S(1)}, f32[64,4096]{1,0:T(8,128)}, u32[]{:S(2)}) copy-start(f32[64,4096]{1,0:T(8,128)} %param.11) | copy-start | bytes 3145732
  552.8 100.7 %copy-start.7 = (f32[64,4096]{1,0:T(8,128)S(1)}, f32[64,4096]{1,0:T(8,128)}, u32[]{:S(2)}) copy-start(f32[64,4096]{1,0:T(8,128)} %param.12) | copy-start | bytes 3145732
  554.7 133.2 %all-gather.2.cloned.1.call-start = ((), (), s32[]{:S(2)}) async-start(), calls=%async_computation.6 | async-start | bytes 12582912 | tf_op jit(solution)/shard_map/all_gather | solution.py:57
  654.8 1.0 copy-start.9
  654.8 4.3 copy-start.8
  659.1 1.0 copy-start.4
Sparse Core Ops, SparseCore 0:
  10.4 23.1 reduce-scatter.1
  39.5 39.7 all-reduce.4
  230.1 98.6 all-reduce.6
  363.7 40.0 all-reduce.8
  554.8 98.6 all-reduce.10
  659.3 22.9 all-gather.1
where the time goes:
time: 707 us; the launch traced here: 703 us
  waiting for transfers between devices  304 us (43%)
  blocking collectives  289 us (41%)
  other arithmetic  49.6 us (7%)
  matrix products  35.2 us (5%)
  between operations  14.4 us (2%)
  local copies, waits for them, and re-layouts  10.2 us (1%)
    psum x2, blocking collectives, local(): row_gram = lax.psum(gram_of(rows), ('dp', 'vocab'))  263 us
    psum x2, waiting for transfers between devices, local(): lax.psum(local_cols.astype(jnp.bfloat16), ('dp', 'vocab'))  197 us
    psum x2, waiting for transfers between devices, local(): rows = lax.psum(local_rows.astype(jnp.bfloat16), 'mp').astype(jnp.float32)  80.1 us
    psum x2, blocking collectives, local(): column_gram = lax.psum(gram_of(columns), 'mp')  26.5 us
    another operation x12, other arithmetic, factor_solve(): factor = jnp.linalg.cholesky(gram)  26.1 us
    reduce_scatter x1, waiting for transfers between devices, local(): lax.psum_scatter(partial_value, 'dp', scatter_dimension=0, tiled=True)  25.6 us
    another operation x8, other arithmetic, factor_solve(): return jax.scipy.linalg.solve_triangular(factor, block, lower=True)  22.2 us
  transfers between devices with their start and end apart: 6, of which 5 were waited for; matrix products, arithmetic and copies ran while one was open for 2% of the time, Pallas kernels for 0%

commit v1 on v0

v1 whole, which is shorter than its diff:
```python
import functools
import math

import jax
import jax.numpy as jnp
from jax import lax
from jax.experimental import pallas as pl
from jax.experimental.pallas import tpu as pltpu
from jax.sharding import PartitionSpec as P

F32 = jnp.float32
BF16 = jnp.bfloat16
LANE = 128
EXTRA = 16
TILE = 512
WIDE = 256
VMEM_LIMIT = 28 * 1024 * 1024

VMEM = pl.BlockSpec(memory_space=pltpu.VMEM)
SMEM = pl.BlockSpec(memory_space=pltpu.SMEM)


def thirds(value):
    high = value.astype(BF16).astype(F32)
    rest = value - high
    mid = rest.astype(BF16).astype(F32)
    return high, mid, rest - mid


def stacked(value):
    return jnp.concatenate(thirds(value), axis=0).astype(BF16)


def dot(a, b, ca, cb):
    return lax.dot_general(a, b, (((ca,), (cb,)), ((), ())), preferred_element_type=F32)


def inverse_factor(gram):
    rank = gram.shape[0]
    lanes = lax.broadcasted_iota(jnp.int32, (8, rank), 1)
    subs = lax.broadcasted_iota(jnp.int32, (8, LANE), 0)
    blocks = rank // 8
    both = []
    for b in range(blocks):
        eye = jnp.where(lanes == subs[:, :rank] + 8 * b, 1.0, 0.0).astype(F32)
        both.append(jnp.concatenate([gram[8 * b : 8 * b + 8, :], eye], axis=1))
    scale = []
    for b in range(blocks):
        diag = jnp.ones((8, LANE), F32)
        cols = {
            (j, i): jnp.broadcast_to(both[i][:, 8 * b + j : 8 * b + j + 1], (8, LANE))
            for j in range(8)
            for i in range(b, blocks)
        }
        for j in range(8):
            pivot = cols[j, b][j : j + 1, :]
            inverse = 1.0 / pivot
            diag = jnp.where(subs == j, pivot, diag)
            row = both[b][j : j + 1, :] * inverse
            heads = {m: cols[m, b][j : j + 1, :] * inverse for m in range(j + 1, 8)}
            for i in range(b, blocks):
                f = cols[j, i]
                if i == b:
                    f = jnp.where(subs > j, f, 0.0)
                both[i] = both[i] - f * row
                for m in range(j + 1, 8):
                    cols[m, i] = cols[m, i] - f * heads[m]
        scale.append(lax.rsqrt(diag))
    return jnp.concatenate(
        [both[b][:, rank:] * scale[b][:, :rank] for b in range(blocks)], axis=0
    )


def applied(factor3, block):
    rank = factor3.shape[0] // 3
    r = dot(factor3, block, 1, 0)
    return r[:rank] + r[rank : 2 * rank] + r[2 * rank :]


def gathered_gram(chunks_ref, rank):
    n = chunks_ref.shape[0]
    each = rank // n
    parts = []
    for c in range(n):
        e = chunks_ref[c, rank : rank + EXTRA, :].astype(F32)
        parts.append(e[:each] + e[each : 2 * each] + e[2 * each : 3 * each])
    return jnp.concatenate(parts, axis=0)[:, :rank]


def extra_rows(piece):
    pad = jnp.zeros((EXTRA - 3 * piece.shape[0], piece.shape[1]), F32)
    return jnp.concatenate([*thirds(piece), pad], axis=0).astype(BF16)


def split_products(me, left, slab_ref, theirs_ref, mine_ref):
    half = slab_ref.shape[0] // 2
    for base, out in (((1 - me) * half, theirs_ref), (me * half, mine_ref)):
        for t in range(0, half, WIDE):
            rows = pl.ds(pl.multiple_of(base + t, WIDE), WIDE)
            out[:, t : t + WIDE] = dot(left, slab_ref[rows, :], 1, 1).astype(out.dtype)


def first_rows_kernel(me_ref, basis_ref, slab_ref, theirs_ref, mine_ref):
    split_products(me_ref[0], basis_ref[...].astype(BF16), slab_ref, theirs_ref, mine_ref)


def next_rows_kernel(me_ref, chunks_ref, slab_ref, theirs_ref, mine_ref, pack_ref, half_ref):
    me = me_ref[0]
    rank = half_ref.shape[0]
    factor3 = stacked(inverse_factor(gathered_gram(chunks_ref, rank)))
    per = TILE // LANE
    total = jnp.zeros((3 * rank, 3 * rank), F32)
    for j in range(chunks_ref.shape[0] // per):
        block = jnp.concatenate([chunks_ref[j * per + q, :rank, :] for q in range(per)], axis=1)
        columns = applied(factor3, block)
        half_ref[:, j * TILE : (j + 1) * TILE] = columns.astype(BF16)
        three = stacked(columns)
        total = total + dot(three, three, 1, 1)
    gram = folded(total, rank)
    own = jnp.where(me == 0, gram[: rank // 2], gram[rank // 2 :])
    quarter = rank // 4
    own = jnp.concatenate([own[:quarter], own[quarter:]], axis=1)
    pad = jnp.zeros((EXTRA, pack_ref.shape[1] - 3 * LANE), F32)
    pack_ref[...] = jnp.concatenate([*thirds(own), pad], axis=1).astype(BF16)
    split_products(me, half_ref[...], slab_ref, theirs_ref, mine_ref)


def folded(total, rank):
    wide = total[:rank] + total[rank : 2 * rank] + total[2 * rank :]
    return wide[:, :rank] + wide[:, rank : 2 * rank] + wide[:, 2 * rank :]


def packed_half(ref, rank):
    e = ref[rank:, :].astype(F32)
    g = e[:, :LANE] + e[:, LANE : 2 * LANE] + e[:, 2 * LANE : 3 * LANE]
    return jnp.concatenate([g[:, :rank], g[:, rank:]], axis=0)


def columns_kernel(orthogonal, me_ref, mine_ref, other_ref, slab_ref, chunks_ref, rows_ref, gram_ref):
    me = me_ref[0]
    rank = rows_ref.shape[0]
    half = mine_ref.shape[1]
    mine, other = mine_ref[:rank, :], other_ref[:rank, :]
    if orthogonal:
        a, b = packed_half(mine_ref, rank), packed_half(other_ref, rank)
        first = me == 0
        gram = jnp.concatenate([jnp.where(first, a, b), jnp.where(first, b, a)], axis=0)
        factor3 = stacked(inverse_factor(gram))
        mine = applied(factor3, mine).astype(BF16)
        other = applied(factor3, other).astype(BF16)
    rows_ref[:, pl.ds(pl.multiple_of(me * half, half), half)] = mine
    rows_ref[:, pl.ds(pl.multiple_of((1 - me) * half, half), half)] = other
    gram_ref[...] = jnp.zeros_like(gram_ref)
    gram_ref[:, :rank] = dot(mine, mine, 1, 1)
    n = chunks_ref.shape[0]
    each = rank // n
    rows = rows_ref[...]
    per = TILE // LANE
    for j in range(n // per):
        product = dot(rows, slab_ref[:, j * TILE : (j + 1) * TILE], 1, 0).astype(BF16)
        for q in range(per):
            c = j * per + q
            chunks_ref[c, :rank, :] = product[:, q * LANE : (q + 1) * LANE]
            chunks_ref[c, rank:, :] = extra_rows(gram_ref[c * each : (c + 1) * each, :])


def sum_chunks_kernel(parts_ref, out_ref):
    n = parts_ref.shape[0]
    rank = parts_ref.shape[1] - EXTRA
    each = rank // n
    total = parts_ref[0].astype(F32)
    for c in range(1, n):
        total = total + parts_ref[c].astype(F32)
    e = total[rank:]
    gram = e[:each] + e[each : 2 * each] + e[2 * each : 3 * each]
    piece = jnp.concatenate([total[:rank].astype(BF16), extra_rows(gram)], axis=0)
    for c in range(n):
        out_ref[c] = piece


def sum_packed_kernel(a_ref, b_ref, c_ref, d_ref, out_ref):
    total = (a_ref[...].astype(F32) + b_ref[...].astype(F32)) + (
        c_ref[...].astype(F32) + d_ref[...].astype(F32)
    )
    rank = out_ref.shape[0] - EXTRA
    out_ref[:rank, :] = total[:rank].astype(BF16)
    e = total[rank:]
    g = e[:, :LANE] + e[:, LANE : 2 * LANE] + e[:, 2 * LANE : 3 * LANE]
    pad = jnp.zeros((EXTRA, out_ref.shape[1] - 3 * LANE), F32)
    out_ref[rank:, :] = jnp.concatenate([*thirds(g), pad], axis=1).astype(BF16)


def moments_kernel(
    chunks_ref, rows_ref, first_ref, second_ref,
    columns_ref, gram_ref, new_first_ref, new_second_ref, direction_ref, left_ref,
):
    rank = rows_ref.shape[0]
    factor3 = stacked(inverse_factor(gathered_gram(chunks_ref, rank)))
    left_ref[...] = applied(factor3, rows_ref[...]).astype(BF16)
    corr_one = 1.0 - 0.9**10
    corr_two = 1.0 - 0.999**10
    per = TILE // LANE
    total = jnp.zeros((3 * rank, 3 * rank), F32)
    for j in range(chunks_ref.shape[0] // per):
        at = slice(j * TILE, (j + 1) * TILE)
        block = jnp.concatenate([chunks_ref[j * per + q, :rank, :] for q in range(per)], axis=1)
        columns = applied(factor3, block)
        columns_ref[:, at] = columns
        three = stacked(columns)
        total = total + dot(three, three, 1, 1)
        new_first = 0.9 * first_ref[:, at] + 0.1 * columns
        new_second = 0.999 * second_ref[:, at] + 0.001 * columns * columns
        new_first_ref[:, at] = new_first
        new_second_ref[:, at] = new_second
        direction = new_first / corr_one / (jnp.sqrt(new_second / corr_two) + 1e-08)
        direction_ref[:, at] = direction.astype(BF16)
    gram_ref[...] = folded(total, rank)


def update_kernel(scale, left_ref, direction_ref, update_ref):
    left = left_ref[...]
    for t in range(0, direction_ref.shape[1], TILE):
        product = dot(left, direction_ref[:, t : t + TILE], 0, 0)
        update_ref[:, t : t + TILE] = (product * scale).astype(BF16)


def basis_kernel(a_ref, b_ref, c_ref, d_ref, columns_ref, basis_ref):
    factor = inverse_factor((a_ref[...] + b_ref[...]) + (c_ref[...] + d_ref[...]))
    factor3 = stacked(factor)
    for t in range(0, columns_ref.shape[1], TILE):
        high, mid, low = thirds(columns_ref[:, t : t + TILE])
        basis_ref[:, t : t + TILE] = (
            applied(factor3, high.astype(BF16))
            + applied(factor3, mid.astype(BF16))
            + applied(factor3, low.astype(BF16))
        )


def call(kernel, outs, operands, scratch=(), flops=0, moved=0):
    return pl.pallas_call(
        kernel,
        out_shape=[jax.ShapeDtypeStruct(s, t) for s, t in outs],
        in_specs=[SMEM if x.dtype == jnp.int32 else VMEM for x in operands],
        out_specs=[VMEM] * len(outs),
        scratch_shapes=[pltpu.VMEM(s, t) for s, t in scratch],
        compiler_params=pltpu.CompilerParams(vmem_limit_bytes=VMEM_LIMIT),
        cost_estimate=pl.CostEstimate(flops=flops, bytes_accessed=moved, transcendentals=0),
    )(*operands)


def swapped(x):
    return lax.ppermute(x, "dp", [(0, 1), (1, 0)])


def others(x):
    n = lax.axis_size("mp")
    return [lax.ppermute(x, "mp", [(i, (i + k) % n) for i in range(n)]) for k in (1, 3, 2)]


def sum_over_owners(chunks):
    axes = ("dp", "vocab")
    parts = lax.all_to_all(chunks, axes, 0, 0)
    copies = call(sum_chunks_kernel, [(parts.shape, BF16)], [parts])[0]
    return lax.all_to_all(copies, axes, 0, 0)


def local(grad_parts, old_basis, first_moment, second_moment):
    slab = grad_parts[0]
    vocab, width = slab.shape
    rank = old_basis.shape[0]
    half = vocab // 2
    owners = lax.axis_size("dp") * lax.axis_size("vocab")
    me = lax.axis_index("dp").astype(jnp.int32).reshape(1)
    halves = [((rank, half), BF16), ((rank, half), F32)]
    chunks_out = [((owners, rank + EXTRA, LANE), BF16), ((rank, vocab), BF16)]
    gram_scratch = [((rank, LANE), F32)]

    theirs, mine = call(first_rows_kernel, halves, [me, old_basis, slab])
    mine = (mine + swapped(theirs).astype(F32)).astype(BF16)
    total = mine.astype(F32)
    for x in others(mine):
        total = total + x.astype(F32)
    mine = total.astype(BF16)
    chunks, _ = call(
        functools.partial(columns_kernel, False),
        chunks_out,
        [me, mine, swapped(mine), slab],
        gram_scratch,
    )
    chunks = sum_over_owners(chunks)

    theirs, mine, pack = call(
        next_rows_kernel,
        halves + [((EXTRA, half), BF16)],
        [me, chunks, slab],
        [((rank, width), BF16)],
    )
    mine = (mine + swapped(theirs).astype(F32)).astype(BF16)
    mine = jnp.concatenate([mine, pack], axis=0)
    mine = call(sum_packed_kernel, [(mine.shape, BF16)], [mine, *others(mine)])[0]
    chunks, rows = call(
        functools.partial(columns_kernel, True),
        chunks_out,
        [me, mine, swapped(mine), slab],
        gram_scratch,
    )
    chunks = sum_over_owners(chunks)

    wide = ((rank, width), F32)
    columns, gram, new_first, new_second, direction, left = call(
        moments_kernel,
        [wide, ((rank, rank), F32), wide, wide, ((rank, width), BF16), ((rank, vocab), BF16)],
        [chunks, rows, first_moment, second_moment],
    )
    gram_others = others(gram)
    scale = math.sqrt(vocab * lax.axis_size("vocab"))
    update = pl.pallas_call(
        functools.partial(update_kernel, scale),
        out_shape=jax.ShapeDtypeStruct((vocab, width), BF16),
        grid=(vocab // WIDE,),
        in_specs=[
            pl.BlockSpec((rank, WIDE), lambda i: (0, i)),
            pl.BlockSpec((rank, width), lambda i: (0, 0)),
        ],
        out_specs=pl.BlockSpec((WIDE, width), lambda i: (i, 0)),
        compiler_params=pltpu.CompilerParams(vmem_limit_bytes=VMEM_LIMIT),
        cost_estimate=pl.CostEstimate(
            flops=2 * rank * vocab * width, bytes_accessed=2 * vocab * width, transcendentals=0
        ),
    )(left, direction)
    basis = call(basis_kernel, [wide], [gram, *gram_others, columns])[0]
    return (update, basis, new_first, new_second)


def solution(mesh):
    placed = (P("dp", "vocab", "mp"), P(None, "mp"), P(None, "mp"), P(None, "mp"))
    return jax.shard_map(
        local,
        mesh=mesh,
        in_specs=placed,
        out_specs=(P("vocab", "mp"), P(None, "mp"), P(None, "mp"), P(None, "mp")),
        check_vma=False,
    )
```

time: 707 us -> 129 us (0.18)
  waiting for transfers between devices: 304 us -> 12.1 us
  blocking collectives: 289 us -> 69.7 us
  other arithmetic: 49.6 us -> 0.07 us
  matrix products: 35.2 us -> 0 us
  Pallas kernels: 0 us -> 26.6 us
  starting transfers between devices: 0.24 us -> 14.6 us
  between operations: 14.4 us -> 0.72 us
    psum x4 -> x0, blocking collectives: 289 us -> none  [the longest x2 263 us: local(): row_gram = lax.psum(gram_of(rows), ('dp', 'vocab'))]
    psum x4 -> x0, waiting for transfers between devices: 278 us -> none  [the longest x2 197 us: local(): lax.psum(local_cols.astype(jnp.bfloat16), ('dp', 'vocab'))]
    all_to_all x0 -> x4, blocking collectives: none -> 69.7 us  [the longest x2 36.6 us: sum_over_owners(): parts = lax.all_to_all(chunks, axes, 0, 0)]
    another operation x20 -> x0, other arithmetic: 48.3 us -> none  [the longest x12 26.1 us: factor_solve(): factor = jnp.linalg.cholesky(gram)]
    dot_general x13 -> x0, matrix products: 28.3 us -> none  [the longest x4 11.4 us: rows_times(): lax.dot_general(basis_half, slab, (((1,), (1,)), ((), ())), preferred_ele...]
    pallas_call x0 -> x10, Pallas kernels: none -> 26.6 us  [the longest x9 21.8 us: call(): pl.pallas_call(kernel, out_shape=[jax.ShapeDtypeStruct(s, t) for s, t in...]
    reduce_scatter x1 -> x0, waiting for transfers between devices: 25.6 us -> none  [local(): lax.psum_scatter(partial_value, 'dp', scatter_dimension=0, tiled=True)]
    ppermute x0 -> x13, starting transfers between devices: none -> 14.6 us  [the longest x9 7.8 us: others(): lax.ppermute(x, 'mp', [(i, (i + k) % n) for i in range(n)])]
  transfers between devices with their start and end apart: 6 -> 13, of which waited for: 5 -> 9; matrix products, arithmetic and copies ran while one was open for 2% -> 0% of each run, Pallas kernels for 0% -> 4%
where the time goes in v1:
time: 129 us
  blocking collectives  69.7 us (54%)
  Pallas kernels  26.6 us (21%)
  starting transfers between devices  14.6 us (11%)
  waiting for transfers between devices  12.1 us (9%)
  local copies, waits for them, and re-layouts  4.62 us (4%)
    all_to_all x2, blocking collectives, sum_over_owners(): parts = lax.all_to_all(chunks, axes, 0, 0)  36.6 us
    all_to_all x2, blocking collectives, sum_over_owners(): return lax.all_to_all(copies, axes, 0, 0)  33.1 us
    pallas_call x9, Pallas kernels, call(): pl.pallas_call(kernel, out_shape=[jax.ShapeDtypeStruct(s, t) for s, t in...  21.8 us
    ppermute x9, waiting for transfers between devices, others(): lax.ppermute(x, 'mp', [(i, (i + k) % n) for i in range(n)])  8.51 us
    ppermute x9, starting transfers between devices, others(): lax.ppermute(x, 'mp', [(i, (i + k) % n) for i in range(n)])  7.8 us
    ppermute x4, starting transfers between devices, swapped(): return lax.ppermute(x, 'dp', [(0, 1), (1, 0)])  6.83 us
    pallas_call x1, Pallas kernels, local(): pl.pallas_call(functools.partial(update_kernel, scale), out_shape=jax.Sha...  4.87 us
    unnamed x10, local copies, waits for them, and re-layouts  4.62 us
  transfers between devices with their start and end apart: 13, of which 9 were waited for; matrix products, arithmetic and copies ran while one was open for 0% of the time, Pallas kernels for 4%

profile of v1, /device:TPU:1, one launch (start us, length us, event | category | flops | bytes accessed | tf_op | source)
XLA Modules:
  0.0 128.5 jit_solution(5639416647699090328)
XLA Ops:
  0.6 3.4 %copy-done = bf16[1,1024,4096]{2,1,0:T(8,128)(2,1)S(1)} copy-done((bf16[1,1024,4096]{2,1,0:T(8,128)(2,1)S(1)}, bf16[1,1024,4096]{2,1,0:T(8,128)(2,1)}, u32[]{:S(2)}) %copy-start) | copy-done | bytes 8388632
  4.0 1.2 copy-done.2
  5.2 2.7 %shard_map.75 = (bf16[64,512]{1,0:T(8,128)(2,1)S(1)}, f32[64,512]{1,0:T(8,128)S(1)}) custom-call(s32[1]{0:T(128)} %bitcast.me_ref, f32[64,4096]{1,0:T(8,128)S(1)} %copy-done.2, bf16[1024,4096]{1,0:T(8,128)(2,1)S(1)} %bitcast.2), custom_call_target="tpu_custom_call" | custom-call | tf_op jit(solution)/shard_map/pallas_call | solution.py:240
  7.9 1.5 %collective-permute-start = (bf16[64,512]{1,0:T(8,128)(2,1)S(1)}, bf16[64,512]{1,0:T(8,128)(2,1)S(1)}, u32[]{:S(2)}, u32[]{:S(2)}) collective-permute-start(bf16[64,512]{1,0:T(8,128)(2,1)S(1)} %get-tuple-element.19), channel_id=1, source_target_pairs={{0,64},{64,0},{1,65},{65,1},{2,66},{66,2},{3,67},{67,3},{4,68},{68... | collective-permute-start | bytes 196616 | tf_op jit(solution)/shard_map/ppermute | solution.py:252
  9.4 0.9 collective-permute-done
  10.3 2.9 %collective-permute-start.3 = (bf16[64,512]{1,0:T(8,128)(2,1)S(1)}, bf16[64,512]{1,0:T(8,128)(2,1)S(1)}, u32[]{:S(2)}, u32[]{:S(2)}) collective-permute-start(bf16[64,512]{1,0:T(8,128)(2,1)S(1)} %add_convert_fusion.2), channel_id=1, source_target_pairs={{0,2},{1,3},{2,0},{3,1},{4,6},{5,7},{6,4},{7,5},{8,10},{9,11},{10,... | collective-permute-start | bytes 196616 | tf_op jit(solution)/shard_map/ppermute | solution.py:257
  13.2 0.9 collective-permute-start.2
  14.1 0.6 collective-permute-start.1
  14.7 0.3 collective-permute-done.3
  15.0 1.7 %collective-permute-done.2 = bf16[64,512]{1,0:T(8,128)(2,1)S(1)} collective-permute-done((bf16[64,512]{1,0:T(8,128)(2,1)S(1)}, bf16[64,512]{1,0:T(8,128)(2,1)S(1)}, u32[]{:S(2)}, u32[]{:S(2)}) %collective-permute-start.2) | collective-permute-done | bytes 65568 | tf_op jit(solution)/shard_map/ppermute | solution.py:257
  16.7 1.7 %collective-permute-done.1 = bf16[64,512]{1,0:T(8,128)(2,1)S(1)} collective-permute-done((bf16[64,512]{1,0:T(8,128)(2,1)S(1)}, bf16[64,512]{1,0:T(8,128)(2,1)S(1)}, u32[]{:S(2)}, u32[]{:S(2)}) %collective-permute-start.1) | collective-permute-done | bytes 65568 | tf_op jit(solution)/shard_map/ppermute | solution.py:257
  18.5 2.1 %collective-permute-start.4 = (bf16[64,512]{1,0:T(8,128)(2,1)S(1)}, bf16[64,512]{1,0:T(8,128)(2,1)S(1)}, u32[]{:S(2)}, u32[]{:S(2)}) collective-permute-start(bf16[64,512]{1,0:T(8,128)(2,1)S(1)} %add_convert_fusion.1.mine_ref), channel_id=1, source_target_pairs={{0,64},{64,0},{1,65},{65,1},{2,66},{66,2},{3,67},{67,3},{4,68},{68... | collective-permute-start | bytes 196616 | tf_op jit(solution)/shard_map/ppermute | solution.py:252
  20.6 0.9 collective-permute-done.4.other_ref
  21.5 2.1 %shard_map.76 = (bf16[32,80,128]{2,1,0:T(8,128)(2,1)S(1)}, bf16[64,1024]{1,0:T(8,128)(2,1)}) custom-call(s32[1]{0:T(128)} %bitcast.me_ref, bf16[64,512]{1,0:T(8,128)(2,1)S(1)} %add_convert_fusion.1.mine_ref, bf16[64,512]{1,0:T(8,128)(2,1)S(1)} %collective-permute-done.4.other_ref, bf16[1024,4096]{1,0:T(8,128)(2,1)S(1)} %bitcast.3), custom_call_target="tpu_custom_call" | custom-call | tf_op jit(solution)/shard_map/pallas_call | solution.py:240
  23.6 20.7 %all_to_all.20.parts_ref = bf16[32,80,128]{2,1,0:T(8,128)(2,1)S(1)} all-to-all(bf16[32,80,128]{2,1,0:T(8,128)(2,1)S(1)} %get-tuple-element.20), channel_id=1, replica_groups=mesh['dp'=2,'vocab'=16,'mp'=4] {'dp','vocab'}, dimensions={0} | all-to-all | bytes 1310720 | tf_op jit(solution)/shard_map/all_to_all | solution.py:262
  44.5 16.6 %all_to_all.21.chunks_ref = bf16[32,80,128]{2,1,0:T(8,128)(2,1)S(1)} all-to-all(bf16[32,80,128]{2,1,0:T(8,128)(2,1)S(1)} %shard_map.77), channel_id=1, replica_groups=mesh['dp'=2,'vocab'=16,'mp'=4] {'dp','vocab'}, dimensions={0} | all-to-all | bytes 1310720 | tf_op jit(solution)/shard_map/all_to_all | solution.py:264
  61.1 5.0 %shard_map.78 = (bf16[64,512]{1,0:T(8,128)(2,1)S(1)}, f32[64,512]{1,0:T(8,128)S(1)}, bf16[16,512]{1,0:T(8,128)(2,1)S(1)}) custom-call(s32[1]{0:T(128)} %bitcast.me_ref, bf16[32,80,128]{2,1,0:T(8,128)(2,1)S(1)} %all_to_all.21.chunks_ref, bf16[1024,4096]{1,0:T(8,128)(2,1)S(1)} %bitcast.4), custom_call_target="tpu_custom_call" | custom-call | tf_op jit(solution)/shard_map/pallas_call | solution.py:240
  66.1 1.1 collective-permute-start.5
  67.3 0.9 collective-permute-done.5
  68.2 0.2 collective-permute-start.8
  68.5 1.6 %collective-permute-start.7 = (bf16[80,512]{1,0:T(8,128)(2,1)S(1)}, bf16[80,512]{1,0:T(8,128)(2,1)S(1)}, u32[]{:S(2)}, u32[]{:S(2)}) collective-permute-start(bf16[80,512]{1,0:T(8,128)(2,1)S(1)} %pad_maximum_fusion.a_ref), channel_id=1, source_target_pairs={{0,3},{1,0},{2,1},{3,2},{4,7},{5,4},{6,5},{7,6},{8,11},{9,8},{10,9... | collective-permute-start | bytes 245768 | tf_op jit(solution)/shard_map/ppermute | solution.py:257
  70.1 3.4 %collective-permute-done.8.d_ref = bf16[80,512]{1,0:T(8,128)(2,1)S(1)} collective-permute-done((bf16[80,512]{1,0:T(8,128)(2,1)S(1)}, bf16[80,512]{1,0:T(8,128)(2,1)S(1)}, u32[]{:S(2)}, u32[]{:S(2)}) %collective-permute-start.8) | collective-permute-done | bytes 81952 | tf_op jit(solution)/shard_map/ppermute | solution.py:257
  73.5 1.4 %collective-permute-done.6.b_ref = bf16[80,512]{1,0:T(8,128)(2,1)S(1)} collective-permute-done((bf16[80,512]{1,0:T(8,128)(2,1)S(1)}, bf16[80,512]{1,0:T(8,128)(2,1)S(1)}, u32[]{:S(2)}, u32[]{:S(2)}) %collective-permute-start.6) | collective-permute-done | bytes 81952 | tf_op jit(solution)/shard_map/ppermute | solution.py:257
  74.9 2.0 %collective-permute-start.9 = (bf16[80,512]{1,0:T(8,128)(2,1)S(1)}, bf16[80,512]{1,0:T(8,128)(2,1)S(1)}, u32[]{:S(2)}, u32[]{:S(2)}) collective-permute-start(bf16[80,512]{1,0:T(8,128)(2,1)S(1)} %shard_map.79.mine_ref), channel_id=1, source_target_pairs={{0,64},{64,0},{1,65},{65,1},{2,66},{66,2},{3,67},{67,3},{4,68},{68... | collective-permute-start | bytes 245768 | tf_op jit(solution)/shard_map/ppermute | solution.py:252
  76.9 0.9 collective-permute-done.9.other_ref
  77.9 3.5 %shard_map.80 = (bf16[32,80,128]{2,1,0:T(8,128)(2,1)S(1)}, bf16[64,1024]{1,0:T(8,128)(2,1)S(1)}) custom-call(s32[1]{0:T(128)} %bitcast.me_ref, bf16[80,512]{1,0:T(8,128)(2,1)S(1)} %shard_map.79.mine_ref, bf16[80,512]{1,0:T(8,128)(2,1)S(1)} %collective-permute-done.9.other_ref, bf16[1024,4096]{1,0:T(8,128)(2,1)S(1)} %bitcast.5), custom_call_target="tpu_custom_call" | custom-call | tf_op jit(solution)/shard_map/pallas_call | solution.py:240
  81.4 15.9 %all_to_all.22.parts_ref = bf16[32,80,128]{2,1,0:T(8,128)(2,1)S(1)} all-to-all(bf16[32,80,128]{2,1,0:T(8,128)(2,1)S(1)} %get-tuple-element.24), channel_id=1, replica_groups=mesh['dp'=2,'vocab'=16,'mp'=4] {'dp','vocab'}, dimensions={0} | all-to-all | bytes 1310720 | tf_op jit(solution)/shard_map/all_to_all | solution.py:262
  97.3 16.6 %all_to_all.23.chunks_ref = bf16[32,80,128]{2,1,0:T(8,128)(2,1)S(1)} all-to-all(bf16[32,80,128]{2,1,0:T(8,128)(2,1)S(1)} %shard_map.81), channel_id=1, replica_groups=mesh['dp'=2,'vocab'=16,'mp'=4] {'dp','vocab'}, dimensions={0} | all-to-all | bytes 1310720 | tf_op jit(solution)/shard_map/all_to_all | solution.py:264
  113.9 4.2 %shard_map.82 = (f32[64,4096]{1,0:T(8,128)S(1)}, f32[64,64]{1,0:T(8,128)S(1)}, f32[64,4096]{1,0:T(8,128)}, f32[64,4096]{1,0:T(8,128)}, bf16[64,4096]{1,0:T(8,128)(2,1)S(1)}, /*index=5*/bf16[64,1024]{1,0:T(8,128)(2,1)S(1)}) custom-call(bf16[32,80,128]{2,1,0:T(8,128)(2,1)S(1)} %all_to_all.23.chunks_ref, bf16[64,1024]{1,0:T(8,128)(2,1)S(1)} %get-tuple-element.25.rows_ref, ...), custom_call_target="tpu_custom_call" | custom-call | tf_op jit(solution)/shard_map/pallas_call | solution.py:240
  118.1 1.6 %collective-permute-start.11 = (f32[64,64]{1,0:T(8,128)S(1)}, f32[64,64]{1,0:T(8,128)S(1)}, u32[]{:S(2)}, u32[]{:S(2)}) collective-permute-start(f32[64,64]{1,0:T(8,128)S(1)} %get-tuple-element.28.a_ref), channel_id=1, source_target_pairs={{0,3},{1,0},{2,1},{3,2},{4,7},{5,4},{6,5},{7,6},{8,11},{9,8},{10,9... | collective-permute-start | bytes 49160 | tf_op jit(solution)/shard_map/ppermute | solution.py:257
  119.7 4.9 %shard_map.83 = bf16[1024,4096]{1,0:T(8,128)(2,1)} custom-call(bf16[64,1024]{1,0:T(8,128)(2,1)S(1)} %get-tuple-element.26.left_ref, bf16[64,4096]{1,0:T(8,128)(2,1)S(1)} %get-tuple-element.27.direction_ref), custom_call_target="tpu_custom_call" | custom-call | flops 536870912 | bytes 8388608 | tf_op jit(solution)/shard_map/pallas_call | solution.py:317
  124.5 4.0 %shard_map.84 = f32[64,4096]{1,0:T(8,128)} custom-call(f32[64,64]{1,0:T(8,128)S(1)} %get-tuple-element.28.a_ref, f32[64,64]{1,0:T(8,128)S(1)} %collective-permute-done.10.b_ref, f32[64,64]{1,0:T(8,128)S(1)} %collective-permute-done.11.c_ref, f32[64,64]{1,0:T(8,128)S(1)} %collective-permute-done.12.d_ref, f32[64,4096]{1,0:T(8,128)S(1)} %get-tuple-element.29.columns_ref), custom_call_target="tpu_custom_call" | custom-call | tf_op jit(solution)/shard_map/pallas_call | solution.py:240
  (22 shorter events, 0.4 us)
Async XLA Ops:
  0.6 3.4 %copy-start = (bf16[1,1024,4096]{2,1,0:T(8,128)(2,1)S(1)}, bf16[1,1024,4096]{2,1,0:T(8,128)(2,1)}, u32[]{:S(2)}) copy-start(bf16[1,1024,4096]{2,1,0:T(8,128)(2,1)} %param.4) | copy-start | bytes 25165828
  4.0 1.2 copy-start.2
  5.2 16.3 %copy-start.1 = (bf16[1,1024,4096]{2,1,0:T(8,128)(2,1)S(1)}, bf16[1,1024,4096]{2,1,0:T(8,128)(2,1)}, u32[]{:S(2)}) copy-start(bf16[1,1024,4096]{2,1,0:T(8,128)(2,1)} %param.4) | copy-start | bytes 25165828
  7.9 2.4 %collective-permute-start = (bf16[64,512]{1,0:T(8,128)(2,1)S(1)}, bf16[64,512]{1,0:T(8,128)(2,1)S(1)}, u32[]{:S(2)}, u32[]{:S(2)}) collective-permute-start(bf16[64,512]{1,0:T(8,128)(2,1)S(1)} %get-tuple-element.19), channel_id=1, source_target_pairs={{0,64},{64,0},{1,65},{65,1},{2,66},{66,2},{3,67},{67,3},{4,68},{68... | collective-permute-start | bytes 196616 | tf_op jit(solution)/shard_map/ppermute | solution.py:252
  10.3 4.7 %collective-permute-start.3 = (bf16[64,512]{1,0:T(8,128)(2,1)S(1)}, bf16[64,512]{1,0:T(8,128)(2,1)S(1)}, u32[]{:S(2)}, u32[]{:S(2)}) collective-permute-start(bf16[64,512]{1,0:T(8,128)(2,1)S(1)} %add_convert_fusion.2), channel_id=1, source_target_pairs={{0,2},{1,3},{2,0},{3,1},{4,6},{5,7},{6,4},{7,5},{8,10},{9,11},{10,... | collective-permute-start | bytes 196616 | tf_op jit(solution)/shard_map/ppermute | solution.py:257
  13.2 3.5 %collective-permute-start.2 = (bf16[64,512]{1,0:T(8,128)(2,1)S(1)}, bf16[64,512]{1,0:T(8,128)(2,1)S(1)}, u32[]{:S(2)}, u32[]{:S(2)}) collective-permute-start(bf16[64,512]{1,0:T(8,128)(2,1)S(1)} %add_convert_fusion.2), channel_id=1, source_target_pairs={{0,3},{1,0},{2,1},{3,2},{4,7},{5,4},{6,5},{7,6},{8,11},{9,8},{10,9... | collective-permute-start | bytes 196616 | tf_op jit(solution)/shard_map/ppermute | solution.py:257
  14.1 4.3 %collective-permute-start.1 = (bf16[64,512]{1,0:T(8,128)(2,1)S(1)}, bf16[64,512]{1,0:T(8,128)(2,1)S(1)}, u32[]{:S(2)}, u32[]{:S(2)}) collective-permute-start(bf16[64,512]{1,0:T(8,128)(2,1)S(1)} %add_convert_fusion.2), channel_id=1, source_target_pairs={{0,1},{1,2},{2,3},{3,0},{4,5},{5,6},{6,7},{7,4},{8,9},{9,10},{10,1... | collective-permute-start | bytes 196616 | tf_op jit(solution)/shard_map/ppermute | solution.py:257
  18.5 3.0 %collective-permute-start.4 = (bf16[64,512]{1,0:T(8,128)(2,1)S(1)}, bf16[64,512]{1,0:T(8,128)(2,1)S(1)}, u32[]{:S(2)}, u32[]{:S(2)}) collective-permute-start(bf16[64,512]{1,0:T(8,128)(2,1)S(1)} %add_convert_fusion.1.mine_ref), channel_id=1, source_target_pairs={{0,64},{64,0},{1,65},{65,1},{2,66},{66,2},{3,67},{67,3},{4,68},{68... | collective-permute-start | bytes 196616 | tf_op jit(solution)/shard_map/ppermute | solution.py:252
  66.1 47.8 %copy-start.3 = (f32[64,4096]{1,0:T(8,128)S(1)}, f32[64,4096]{1,0:T(8,128)}, u32[]{:S(2)}) copy-start(f32[64,4096]{1,0:T(8,128)} %first_ref.1) | copy-start | bytes 3145732
  66.1 47.8 %copy-start.4 = (f32[64,4096]{1,0:T(8,128)S(1)}, f32[64,4096]{1,0:T(8,128)}, u32[]{:S(2)}) copy-start(f32[64,4096]{1,0:T(8,128)} %second_ref.1) | copy-start | bytes 3145732
  66.1 2.1 %collective-permute-start.5 = (bf16[64,512]{1,0:T(8,128)(2,1)S(1)}, bf16[64,512]{1,0:T(8,128)(2,1)S(1)}, u32[]{:S(2)}, u32[]{:S(2)}) collective-permute-start(bf16[64,512]{1,0:T(8,128)(2,1)S(1)} %get-tuple-element.22), channel_id=1, source_target_pairs={{0,64},{64,0},{1,65},{65,1},{2,66},{66,2},{3,67},{67,3},{4,68},{68... | collective-permute-start | bytes 196616 | tf_op jit(solution)/shard_map/ppermute | solution.py:252
  68.2 5.3 %collective-permute-start.8 = (bf16[80,512]{1,0:T(8,128)(2,1)S(1)}, bf16[80,512]{1,0:T(8,128)(2,1)S(1)}, u32[]{:S(2)}, u32[]{:S(2)}) collective-permute-start(bf16[80,512]{1,0:T(8,128)(2,1)S(1)} %pad_maximum_fusion.a_ref), channel_id=1, source_target_pairs={{0,2},{1,3},{2,0},{3,1},{4,6},{5,7},{6,4},{7,5},{8,10},{9,11},{10,... | collective-permute-start | bytes 245768 | tf_op jit(solution)/shard_map/ppermute | solution.py:257
  68.5 5.0 %collective-permute-start.7 = (bf16[80,512]{1,0:T(8,128)(2,1)S(1)}, bf16[80,512]{1,0:T(8,128)(2,1)S(1)}, u32[]{:S(2)}, u32[]{:S(2)}) collective-permute-start(bf16[80,512]{1,0:T(8,128)(2,1)S(1)} %pad_maximum_fusion.a_ref), channel_id=1, source_target_pairs={{0,3},{1,0},{2,1},{3,2},{4,7},{5,4},{6,5},{7,6},{8,11},{9,8},{10,9... | collective-permute-start | bytes 245768 | tf_op jit(solution)/shard_map/ppermute | solution.py:257
  70.1 4.8 %collective-permute-start.6 = (bf16[80,512]{1,0:T(8,128)(2,1)S(1)}, bf16[80,512]{1,0:T(8,128)(2,1)S(1)}, u32[]{:S(2)}, u32[]{:S(2)}) collective-permute-start(bf16[80,512]{1,0:T(8,128)(2,1)S(1)} %pad_maximum_fusion.a_ref), channel_id=1, source_target_pairs={{0,1},{1,2},{2,3},{3,0},{4,5},{5,6},{6,7},{7,4},{8,9},{9,10},{10,1... | collective-permute-start | bytes 245768 | tf_op jit(solution)/shard_map/ppermute | solution.py:257
  74.9 3.0 %collective-permute-start.9 = (bf16[80,512]{1,0:T(8,128)(2,1)S(1)}, bf16[80,512]{1,0:T(8,128)(2,1)S(1)}, u32[]{:S(2)}, u32[]{:S(2)}) collective-permute-start(bf16[80,512]{1,0:T(8,128)(2,1)S(1)} %shard_map.79.mine_ref), channel_id=1, source_target_pairs={{0,64},{64,0},{1,65},{65,1},{2,66},{66,2},{3,67},{67,3},{4,68},{68... | collective-permute-start | bytes 245768 | tf_op jit(solution)/shard_map/ppermute | solution.py:252
  118.1 6.4 %collective-permute-start.12 = (f32[64,64]{1,0:T(8,128)S(1)}, f32[64,64]{1,0:T(8,128)S(1)}, u32[]{:S(2)}, u32[]{:S(2)}) collective-permute-start(f32[64,64]{1,0:T(8,128)S(1)} %get-tuple-element.28.a_ref), channel_id=1, source_target_pairs={{0,2},{1,3},{2,0},{3,1},{4,6},{5,7},{6,4},{7,5},{8,10},{9,11},{10,... | collective-permute-start | bytes 49160 | tf_op jit(solution)/shard_map/ppermute | solution.py:257
  118.1 6.4 %collective-permute-start.11 = (f32[64,64]{1,0:T(8,128)S(1)}, f32[64,64]{1,0:T(8,128)S(1)}, u32[]{:S(2)}, u32[]{:S(2)}) collective-permute-start(f32[64,64]{1,0:T(8,128)S(1)} %get-tuple-element.28.a_ref), channel_id=1, source_target_pairs={{0,3},{1,0},{2,1},{3,2},{4,7},{5,4},{6,5},{7,6},{8,11},{9,8},{10,9... | collective-permute-start | bytes 49160 | tf_op jit(solution)/shard_map/ppermute | solution.py:257
  119.7 4.9 %collective-permute-start.10 = (f32[64,64]{1,0:T(8,128)S(1)}, f32[64,64]{1,0:T(8,128)S(1)}, u32[]{:S(2)}, u32[]{:S(2)}) collective-permute-start(f32[64,64]{1,0:T(8,128)S(1)} %get-tuple-element.28.a_ref), channel_id=1, source_target_pairs={{0,1},{1,2},{2,3},{3,0},{4,5},{5,6},{6,7},{7,4},{8,9},{9,10},{10,1... | collective-permute-start | bytes 49160 | tf_op jit(solution)/shard_map/ppermute | solution.py:257

commit v2 on v1

v2 whole, which is shorter than its diff:
```python
import functools
import math

import jax
import jax.numpy as jnp
from jax import lax
from jax.experimental import pallas as pl
from jax.experimental.pallas import tpu as pltpu
from jax.sharding import PartitionSpec as P

F32 = jnp.float32
BF16 = jnp.bfloat16
LANE = 128
EXTRA = 16
TILE = 512
WIDE = 256
VMEM_LIMIT = 28 * 1024 * 1024

VMEM = pl.BlockSpec(memory_space=pltpu.VMEM)
SMEM = pl.BlockSpec(memory_space=pltpu.SMEM)


def thirds(value):
    high = value.astype(BF16).astype(F32)
    rest = value - high
    mid = rest.astype(BF16).astype(F32)
    return high, mid, rest - mid


def stacked(value, axis=0):
    return jnp.concatenate(thirds(value), axis=axis).astype(BF16)


def dot(a, b, ca, cb):
    return lax.dot_general(a, b, (((ca,), (cb,)), ((), ())), preferred_element_type=F32)


def inverse_factor(gram):
    rank = gram.shape[0]
    lanes = lax.broadcasted_iota(jnp.int32, (8, rank), 1)
    subs = lax.broadcasted_iota(jnp.int32, (8, LANE), 0)
    blocks = rank // 8
    both = []
    for b in range(blocks):
        eye = jnp.where(lanes == subs[:, :rank] + 8 * b, 1.0, 0.0).astype(F32)
        both.append(jnp.concatenate([gram[8 * b : 8 * b + 8, :], eye], axis=1))
    scale = []
    for b in range(blocks):
        diag = jnp.ones((8, LANE), F32)
        cols = {
            (j, i): jnp.broadcast_to(both[i][:, 8 * b + j : 8 * b + j + 1], (8, LANE))
            for j in range(8)
            for i in range(b, blocks)
        }
        for j in range(8):
            pivot = cols[j, b][j : j + 1, :]
            inverse = 1.0 / pivot
            diag = jnp.where(subs == j, pivot, diag)
            row = both[b][j : j + 1, :] * inverse
            heads = {m: cols[m, b][j : j + 1, :] * inverse for m in range(j + 1, 8)}
            for i in range(b, blocks):
                f = cols[j, i]
                if i == b:
                    f = jnp.where(subs > j, f, 0.0)
                both[i] = both[i] - f * row
                for m in range(j + 1, 8):
                    cols[m, i] = cols[m, i] - f * heads[m]
        scale.append(lax.rsqrt(diag))
    return jnp.concatenate(
        [both[b][:, rank:] * scale[b][:, :rank] for b in range(blocks)], axis=0
    )


def applied(factor3, block):
    return dot(factor3, jnp.concatenate([block] * 3, axis=0), 1, 0)


def folded(total, rank):
    wide = total[:rank] + total[rank : 2 * rank] + total[2 * rank :]
    return wide[:, :rank] + wide[:, rank : 2 * rank] + wide[:, 2 * rank :]


def in_order(me, own, other):
    first = me == 0
    return jnp.concatenate([jnp.where(first, own, other), jnp.where(first, other, own)], axis=0)


def span(base, size):
    return pl.ds(pl.multiple_of(base, size), size)


def extra_rows(piece):
    pad = jnp.zeros((EXTRA - 3 * piece.shape[0], piece.shape[1]), F32)
    return jnp.concatenate([*thirds(piece), pad], axis=0).astype(BF16)


def from_extra(e, each):
    return e[:each] + e[each : 2 * each] + e[2 * each : 3 * each]


def gathered_gram(me, own_ref, other_ref, rank):
    n = own_ref.shape[0]
    each = rank // (2 * n)
    halves = [
        jnp.concatenate(
            [from_extra(ref[c, rank : rank + EXTRA, :].astype(F32), each) for c in range(n)], axis=0
        )
        for ref in (own_ref, other_ref)
    ]
    return in_order(me, *halves)[:, :rank]


def gathered_blocks(me, own_ref, other_ref, rank):
    n = own_ref.shape[0]
    per = TILE // LANE
    for core, ref in ((me, own_ref), (1 - me, other_ref)):
        for j in range(n // per):
            block = jnp.concatenate([ref[j * per + q, :rank, :] for q in range(per)], axis=1)
            yield span(core * (n * LANE) + j * TILE, TILE), block


def packed_gram(own):
    quarter = own.shape[0] // 2
    return stacked(jnp.concatenate([own[:quarter], own[quarter:]], axis=1), 1)


def from_packed(e):
    return e[:, :LANE] + e[:, LANE : 2 * LANE] + e[:, 2 * LANE : 3 * LANE]


def packed_half(ref, rank):
    g = from_packed(ref[rank:, :].astype(F32))
    return jnp.concatenate([g[:, :rank], g[:, rank:]], axis=0)


def split_rows(me, half):
    for t in range(0, 2 * half, WIDE):
        core = 1 - me if t < half else me
        yield t < half, t % half, span(core * half + t % half, WIDE)


def first_rows_kernel(
    me_ref, basis_hbm, slab_hbm, theirs_ref, mine_ref, slab_ref, basis_ref, sems
):
    half = slab_ref.shape[0] // 2
    order = list(split_rows(me_ref[0], half))
    basis_copy = pltpu.make_async_copy(basis_hbm, basis_ref, sems.at[len(order)])
    basis_copy.start()
    copies = [
        pltpu.make_async_copy(slab_hbm.at[rows, :], slab_ref.at[rows, :], sems.at[i])
        for i, (_, _, rows) in enumerate(order)
    ]
    for copy in copies:
        copy.start()
    basis_copy.wait()
    left = basis_ref[...].astype(BF16)
    for copy, (foreign, t, rows) in zip(copies, order):
        copy.wait()
        out = theirs_ref if foreign else mine_ref
        out[:, t : t + WIDE] = dot(left, slab_ref[rows, :], 1, 1).astype(out.dtype)


def next_rows_kernel(
    me_ref, own_ref, other_ref, slab_ref, theirs_ref, mine_ref, pack_ref, half_ref
):
    me = me_ref[0]
    rank = half_ref.shape[0]
    factor3 = stacked(inverse_factor(gathered_gram(me, own_ref, other_ref, rank)), 1)
    total = jnp.zeros((3 * rank, 3 * rank), F32)
    for at, block in gathered_blocks(me, own_ref, other_ref, rank):
        columns = applied(factor3, block)
        half_ref[:, at] = columns.astype(BF16)
        three = stacked(columns)
        total = total + dot(three, three, 1, 1)
    gram = folded(total, rank)
    own = jnp.where(me == 0, gram[: rank // 2], gram[rank // 2 :])
    pack_ref[...] = jnp.zeros_like(pack_ref)
    pack_ref[:, : 3 * LANE] = packed_gram(own)
    left = half_ref[...]
    for foreign, t, rows in split_rows(me, slab_ref.shape[0] // 2):
        out = theirs_ref if foreign else mine_ref
        out[:, t : t + WIDE] = dot(left, slab_ref[rows, :], 1, 1).astype(out.dtype)


def columns_kernel(
    orthogonal, me_ref, mine_ref, other_ref, slab_ref,
    theirs_ref, owned_ref, extra_ref, rows_ref, gram_ref,
):
    me = me_ref[0]
    rank = rows_ref.shape[0]
    half = mine_ref.shape[1]
    mine, other = mine_ref[:rank, :], other_ref[:rank, :]
    if orthogonal:
        gram = in_order(me, packed_half(mine_ref, rank), packed_half(other_ref, rank))
        factor3 = stacked(inverse_factor(gram), 1)
        mine = applied(factor3, mine).astype(BF16)
        other = applied(factor3, other).astype(BF16)
    rows_ref[:, span(me * half, half)] = mine
    rows_ref[:, span((1 - me) * half, half)] = other
    rows = rows_ref[...]
    gram = dot(rows, rows, 1, 1)
    gram_ref[...] = jnp.zeros_like(gram_ref)
    gram_ref[:, :rank] = jnp.where(me == 0, gram[: rank // 2], gram[rank // 2 :])
    n = owned_ref.shape[0]
    each = rank // (2 * n)
    for c in range(n):
        extra_ref[c] = extra_rows(gram_ref[c * each : (c + 1) * each, :])
    per = TILE // LANE
    for core, out in ((1 - me, theirs_ref), (me, owned_ref)):
        for j in range(n // per):
            at = span(core * (n * LANE) + j * TILE, TILE)
            product = dot(rows, slab_ref[:, at], 1, 0).astype(out.dtype)
            for q in range(per):
                out[j * per + q] = product[:, q * LANE : (q + 1) * LANE]


def join_chunks_kernel(owned_ref, got_ref, extra_ref, out_ref):
    rank = owned_ref.shape[1]
    for c in range(out_ref.shape[0]):
        out_ref[c, :rank, :] = (owned_ref[c] + got_ref[c].astype(F32)).astype(BF16)
        out_ref[c, rank:, :] = extra_ref[c]


def sum_chunks_kernel(parts_ref, out_ref):
    n = parts_ref.shape[0]
    rank = parts_ref.shape[1] - EXTRA
    each = rank // (2 * n)
    total = parts_ref[0].astype(F32)
    for c in range(1, n):
        total = total + parts_ref[c].astype(F32)
    extra = extra_rows(from_extra(total[rank:], each))
    piece = jnp.concatenate([total[:rank].astype(BF16), extra], axis=0)
    for c in range(n):
        out_ref[c] = piece


def join_rows_kernel(mine_ref, got_ref, pack_ref, out_ref):
    rank = mine_ref.shape[0]
    out_ref[:rank, :] = (mine_ref[...] + got_ref[...].astype(F32)).astype(BF16)
    out_ref[rank:, :] = pack_ref[...]


def sum_packed_kernel(a_ref, b_ref, c_ref, d_ref, out_ref):
    total = (a_ref[...].astype(F32) + b_ref[...].astype(F32)) + (
        c_ref[...].astype(F32) + d_ref[...].astype(F32)
    )
    rank = out_ref.shape[0] - EXTRA
    out_ref[:rank, :] = total[:rank].astype(BF16)
    out_ref[rank:, :] = jnp.zeros((EXTRA, out_ref.shape[1]), BF16)
    out_ref[rank:, : 3 * LANE] = stacked(from_packed(total[rank:]), 1)


def moments_kernel(
    scale, me_ref, own_ref, other_ref, rows_ref, first_ref, second_ref,
    columns_ref, gram_ref, new_first_ref, new_second_ref, direction_ref, left_ref,
):
    me = me_ref[0]
    rank = rows_ref.shape[0]
    factor3 = stacked(inverse_factor(gathered_gram(me, own_ref, other_ref, rank)), 1)
    left = applied(factor3, rows_ref[...]).astype(BF16)
    left_ref[...] = (left.astype(F32) * scale).astype(BF16)
    corr_one = 1.0 - 0.9**10
    corr_two = 1.0 - 0.999**10
    total = jnp.zeros((3 * rank, 3 * rank), F32)
    for at, block in gathered_blocks(me, own_ref, other_ref, rank):
        columns = applied(factor3, block)
        columns_ref[:, at] = columns
        three = stacked(columns)
        total = total + dot(three, three, 1, 1)
        new_first = 0.9 * first_ref[:, at] + 0.1 * columns
        new_second = 0.999 * second_ref[:, at] + 0.001 * columns * columns
        new_first_ref[:, at] = new_first
        new_second_ref[:, at] = new_second
        direction = new_first / corr_one / (jnp.sqrt(new_second / corr_two) + 1e-08)
        direction_ref[:, at] = direction.astype(BF16)
    gram_ref[...] = folded(total, rank)


def update_kernel(left_ref, direction_ref, update_ref):
    left = left_ref[...]
    for t in range(0, direction_ref.shape[1], TILE):
        product = dot(left, direction_ref[:, t : t + TILE], 0, 0)
        update_ref[:, t : t + TILE] = product.astype(BF16)


def basis_kernel(a_ref, b_ref, c_ref, d_ref, columns_ref, basis_ref):
    factor = inverse_factor((a_ref[...] + b_ref[...]) + (c_ref[...] + d_ref[...]))
    high, mid, low = thirds(factor)
    wide = jnp.concatenate([low, mid, high, mid, high, high], axis=1).astype(BF16)
    for t in range(0, columns_ref.shape[1], TILE):
        high, mid, low = (x.astype(BF16) for x in thirds(columns_ref[:, t : t + TILE]))
        tall = jnp.concatenate([high, mid, low, high, mid, high], axis=0)
        basis_ref[:, t : t + TILE] = dot(wide, tall, 1, 0)


def call(kernel, outs, operands, scratch=(), hbm=()):
    def spec(i, x):
        if x.dtype == jnp.int32:
            return SMEM
        return pl.BlockSpec(memory_space=pltpu.HBM) if i in hbm else VMEM

    return pl.pallas_call(
        kernel,
        out_shape=[jax.ShapeDtypeStruct(s, t) for s, t in outs],
        in_specs=[spec(i, x) for i, x in enumerate(operands)],
        out_specs=[VMEM] * len(outs),
        scratch_shapes=[pltpu.VMEM(*s) if isinstance(s, tuple) else s for s in scratch],
        compiler_params=pltpu.CompilerParams(vmem_limit_bytes=VMEM_LIMIT),
    )(*operands)


def swapped(x):
    return lax.ppermute(x, "dp", [(0, 1), (1, 0)])


def others(x):
    n = lax.axis_size("mp")
    return [lax.ppermute(x, "mp", [(i, (i + k) % n) for i in range(n)]) for k in (1, 3, 2)]


def sum_over_owners(theirs, owned, extra):
    n, rank, lane = owned.shape
    whole = [((n, rank + EXTRA, lane), BF16)]
    chunks = call(join_chunks_kernel, whole, [owned, swapped(theirs), extra])[0]
    parts = lax.all_to_all(chunks, "vocab", 0, 0)
    copies = call(sum_chunks_kernel, whole, [parts])[0]
    own = lax.all_to_all(copies, "vocab", 0, 0)
    return own, swapped(own)


def local(grad_parts, old_basis, first_moment, second_moment):
    slab = grad_parts[0]
    vocab, width = slab.shape
    rank = old_basis.shape[0]
    half = vocab // 2
    owners = lax.axis_size("vocab")
    me = lax.axis_index("dp").astype(jnp.int32).reshape(1)
    halves = [((rank, half), BF16), ((rank, half), F32)]
    chunk = (owners, rank, LANE)
    chunks_out = [(chunk, BF16), (chunk, F32), ((owners, EXTRA, LANE), BF16), ((rank, vocab), BF16)]
    gram_scratch = [((rank // 2, LANE), F32)]

    theirs, mine, slab = call(
        first_rows_kernel,
        halves + [(slab.shape, BF16)],
        [me, *(pltpu.with_memory_space_constraint(x, pltpu.HBM) for x in (old_basis, slab))],
        [((rank, width), F32), pltpu.SemaphoreType.DMA((vocab // WIDE + 1,))],
        hbm=(1, 2),
    )
    mine = (mine + swapped(theirs).astype(F32)).astype(BF16)
    total = mine.astype(F32)
    for x in others(mine):
        total = total + x.astype(F32)
    mine = total.astype(BF16)
    theirs, owned, extra, _ = call(
        functools.partial(columns_kernel, False),
        chunks_out,
        [me, mine, swapped(mine), slab],
        gram_scratch,
    )
    own, other = sum_over_owners(theirs, owned, extra)

    theirs, mine, pack = call(
        next_rows_kernel,
        halves + [((EXTRA, half), BF16)],
        [me, own, other, slab],
        [((rank, width), BF16)],
    )
    packed = [((rank + EXTRA, half), BF16)]
    mine = call(join_rows_kernel, packed, [mine, swapped(theirs), pack])[0]
    mine = call(sum_packed_kernel, packed, [mine, *others(mine)])[0]
    theirs, owned, extra, rows = call(
        functools.partial(columns_kernel, True),
        chunks_out,
        [me, mine, swapped(mine), slab],
        gram_scratch,
    )
    own, other = sum_over_owners(theirs, owned, extra)

    wide = ((rank, width), F32)
    scale = math.sqrt(vocab * owners)
    assert scale == 2.0 ** round(math.log2(scale))
    columns, gram, new_first, new_second, direction, left = call(
        functools.partial(moments_kernel, scale),
        [wide, ((rank, rank), F32), wide, wide, ((rank, width), BF16), ((rank, vocab), BF16)],
        [me, own, other, rows, first_moment, second_moment],
    )
    gram_others = others(gram)
    update = pl.pallas_call(
        update_kernel,
        out_shape=jax.ShapeDtypeStruct((vocab, width), BF16),
        grid=(vocab // WIDE,),
        in_specs=[
            pl.BlockSpec((rank, WIDE), lambda i: (0, i)),
            pl.BlockSpec((rank, width), lambda i: (0, 0)),
        ],
        out_specs=pl.BlockSpec((WIDE, width), lambda i: (i, 0)),
        compiler_params=pltpu.CompilerParams(vmem_limit_bytes=VMEM_LIMIT),
        cost_estimate=pl.CostEstimate(
            flops=2 * rank * vocab * width, bytes_accessed=2 * vocab * width, transcendentals=0
        ),
    )(left, direction)
    basis = call(basis_kernel, [wide], [gram, *gram_others, columns])[0]
    return (update, basis, new_first, new_second)


def solution(mesh):
    placed = (P("dp", "vocab", "mp"), P(None, "mp"), P(None, "mp"), P(None, "mp"))
    return jax.shard_map(
        local,
        mesh=mesh,
        in_specs=placed,
        out_specs=(P("vocab", "mp"), P(None, "mp"), P(None, "mp"), P(None, "mp")),
        check_vma=False,
    )
```

time: 129 us -> 118 us (0.915)
  blocking collectives: 69.7 us -> 49.7 us
  starting transfers between devices: 14.6 us -> 20.6 us
  waiting for transfers between devices: 12.1 us -> 17 us
  local copies, waits for them, and re-layouts: 4.62 us -> 0.01 us
  Pallas kernels: 26.6 us -> 30 us
    all_to_all x4, blocking collectives: 69.7 us -> 49.7 us  [the longest x2 26.7 us: sum_over_owners(): parts = lax.all_to_all(chunks, 'vocab', 0, 0)]
    ppermute x4 -> x8, starting transfers between devices: 6.83 us -> 12.8 us  [swapped(): return lax.ppermute(x, 'dp', [(0, 1), (1, 0)])]
    ppermute x4 -> x8, waiting for transfers between devices: 3.63 us -> 8.51 us  [swapped(): return lax.ppermute(x, 'dp', [(0, 1), (1, 0)])]
    unnamed x10 -> x4, local copies, waits for them, and re-layouts: 4.62 us -> 0.01 us
    pallas_call x9 -> x12, Pallas kernels: 21.8 us -> 25.1 us  [call(): pl.pallas_call(kernel, out_shape=[jax.ShapeDtypeStruct(s, t) for s, t in...]
  transfers between devices with their start and end apart: 13 -> 17, of which waited for: 9 -> 13; matrix products, arithmetic and copies ran while one was open for 0% -> 0% of each run, Pallas kernels for 4% -> 4%
where the time goes in v2:
time: 118 us
  blocking collectives  49.7 us (42%)
  Pallas kernels  30 us (25%)
  starting transfers between devices  20.6 us (17%)
  waiting for transfers between devices  17 us (14%)
    all_to_all x2, blocking collectives, sum_over_owners(): parts = lax.all_to_all(chunks, 'vocab', 0, 0)  26.7 us
    pallas_call x12, Pallas kernels, call(): pl.pallas_call(kernel, out_shape=[jax.ShapeDtypeStruct(s, t) for s, t in...  25.1 us
    all_to_all x2, blocking collectives, sum_over_owners(): own = lax.all_to_all(copies, 'vocab', 0, 0)  23 us
    ppermute x8, starting transfers between devices, swapped(): return lax.ppermute(x, 'dp', [(0, 1), (1, 0)])  12.8 us
    ppermute x9, waiting for transfers between devices, others(): lax.ppermute(x, 'mp', [(i, (i + k) % n) for i in range(n)])  8.51 us
    ppermute x8, waiting for transfers between devices, swapped(): return lax.ppermute(x, 'dp', [(0, 1), (1, 0)])  8.51 us
    ppermute x9, starting transfers between devices, others(): lax.ppermute(x, 'mp', [(i, (i + k) % n) for i in range(n)])  7.8 us
    pallas_call x1, Pallas kernels, local(): pl.pallas_call(update_kernel, out_shape=jax.ShapeDtypeStruct((vocab, widt...  4.87 us
  transfers between devices with their start and end apart: 17, of which 13 were waited for; matrix products, arithmetic and copies ran while one was open for 0% of the time, Pallas kernels for 4%

profile of v2, /device:TPU:1, one launch (start us, length us, event | category | flops | bytes accessed | tf_op | source)
XLA Modules:
  0.0 118.1 jit_solution(3415607847907198563)
XLA Ops:
  0.6 6.8 %shard_map.75 = (bf16[64,512]{1,0:T(8,128)(2,1)S(1)}, f32[64,512]{1,0:T(8,128)S(1)}, bf16[1024,4096]{1,0:T(8,128)(2,1)S(1)}) custom-call(s32[1]{0:T(128)} %bitcast.me_ref, f32[64,4096]{1,0:T(8,128)} %basis_hbm.1, bf16[1024,4096]{1,0:T(8,128)(2,1)} %bitcast.2), custom_call_target="tpu_custom_call" | custom-call | tf_op jit(solution)/shard_map/pallas_call | solution.py:302
  7.5 1.5 %collective-permute-start = (bf16[64,512]{1,0:T(8,128)(2,1)S(1)}, bf16[64,512]{1,0:T(8,128)(2,1)S(1)}, u32[]{:S(2)}, u32[]{:S(2)}) collective-permute-start(bf16[64,512]{1,0:T(8,128)(2,1)S(1)} %get-tuple-element.24), channel_id=1, source_target_pairs={{0,64},{64,0},{1,65},{65,1},{2,66},{66,2},{3,67},{67,3},{4,68},{68... | collective-permute-start | bytes 196616 | tf_op jit(solution)/shard_map/ppermute | solution.py:313
  9.0 0.9 collective-permute-done
  9.9 2.9 %collective-permute-start.3 = (bf16[64,512]{1,0:T(8,128)(2,1)S(1)}, bf16[64,512]{1,0:T(8,128)(2,1)S(1)}, u32[]{:S(2)}, u32[]{:S(2)}) collective-permute-start(bf16[64,512]{1,0:T(8,128)(2,1)S(1)} %add_convert_fusion.1), channel_id=1, source_target_pairs={{0,2},{1,3},{2,0},{3,1},{4,6},{5,7},{6,4},{7,5},{8,10},{9,11},{10,... | collective-permute-start | bytes 196616 | tf_op jit(solution)/shard_map/ppermute | solution.py:318
  12.8 0.9 collective-permute-start.2
  14.6 1.7 %collective-permute-done.2 = bf16[64,512]{1,0:T(8,128)(2,1)S(1)} collective-permute-done((bf16[64,512]{1,0:T(8,128)(2,1)S(1)}, bf16[64,512]{1,0:T(8,128)(2,1)S(1)}, u32[]{:S(2)}, u32[]{:S(2)}) %collective-permute-start.2) | collective-permute-done | bytes 65568 | tf_op jit(solution)/shard_map/ppermute | solution.py:318
  16.3 1.7 %collective-permute-done.1 = bf16[64,512]{1,0:T(8,128)(2,1)S(1)} collective-permute-done((bf16[64,512]{1,0:T(8,128)(2,1)S(1)}, bf16[64,512]{1,0:T(8,128)(2,1)S(1)}, u32[]{:S(2)}, u32[]{:S(2)}) %collective-permute-start.1) | collective-permute-done | bytes 65568 | tf_op jit(solution)/shard_map/ppermute | solution.py:318
  18.0 2.1 %collective-permute-start.4 = (bf16[64,512]{1,0:T(8,128)(2,1)S(1)}, bf16[64,512]{1,0:T(8,128)(2,1)S(1)}, u32[]{:S(2)}, u32[]{:S(2)}) collective-permute-start(bf16[64,512]{1,0:T(8,128)(2,1)S(1)} %add_convert_fusion.mine_ref), channel_id=1, source_target_pairs={{0,64},{64,0},{1,65},{65,1},{2,66},{66,2},{3,67},{67,3},{4,68},{68... | collective-permute-start | bytes 196616 | tf_op jit(solution)/shard_map/ppermute | solution.py:313
  20.2 0.9 collective-permute-done.4.other_ref
  21.1 2.0 %shard_map.76 = (bf16[16,64,128]{2,1,0:T(8,128)(2,1)S(1)}, f32[16,64,128]{2,1,0:T(8,128)S(1)}, bf16[16,16,128]{2,1,0:T(8,128)(2,1)S(1)}, bf16[64,1024]{1,0:T(8,128)(2,1)}) custom-call(s32[1]{0:T(128)} %bitcast.me_ref, bf16[64,512]{1,0:T(8,128)(2,1)S(1)} %add_convert_fusion.mine_ref, bf16[64,512]{1,0:T(8,128)(2,1)S(1)} %collective-permute-done.4.other_ref, ...), custom_call_target="tpu_custom_call" | custom-call | tf_op jit(solution)/shard_map/pallas_call | solution.py:302
  23.5 1.2 %collective-permute-done.5.got_ref = bf16[16,64,128]{2,1,0:T(8,128)(2,1)S(1)} collective-permute-done((bf16[16,64,128]{2,1,0:T(8,128)(2,1)S(1)}, bf16[16,64,128]{2,1,0:T(8,128)(2,1)S(1)}, u32[]{:S(2)}, u32[]{:S(2)}) %collective-permute-start.5) | collective-permute-done | bytes 262176 | tf_op jit(solution)/shard_map/ppermute | solution.py:313
  24.7 15.5 %all_to_all.20.parts_ref = bf16[16,80,128]{2,1,0:T(8,128)(2,1)S(1)} all-to-all(bf16[16,80,128]{2,1,0:T(8,128)(2,1)S(1)} %shard_map.77), channel_id=1, replica_groups=mesh['dp'=2,'vocab'=16,'mp'=4] {'vocab'}, dimensions={0} | all-to-all | bytes 655360 | tf_op jit(solution)/shard_map/all_to_all | solution.py:325
  40.3 11.5 %all_to_all.21.own_ref = bf16[16,80,128]{2,1,0:T(8,128)(2,1)S(1)} all-to-all(bf16[16,80,128]{2,1,0:T(8,128)(2,1)S(1)} %shard_map.78), channel_id=1, replica_groups=mesh['dp'=2,'vocab'=16,'mp'=4] {'vocab'}, dimensions={0} | all-to-all | bytes 655360 | tf_op jit(solution)/shard_map/all_to_all | solution.py:327
  51.8 2.9 %collective-permute-start.6 = (bf16[16,80,128]{2,1,0:T(8,128)(2,1)S(1)}, bf16[16,80,128]{2,1,0:T(8,128)(2,1)S(1)}, u32[]{:S(2)}, u32[]{:S(2)}) collective-permute-start(bf16[16,80,128]{2,1,0:T(8,128)(2,1)S(1)} %all_to_all.21.own_ref), channel_id=1, source_target_pairs={{0,64},{64,0},{1,65},{65,1},{2,66},{66,2},{3,67},{67,3},{4,68},{68... | collective-permute-start | bytes 983048 | tf_op jit(solution)/shard_map/ppermute | solution.py:313
  54.8 1.3 %collective-permute-done.6.other_ref = bf16[16,80,128]{2,1,0:T(8,128)(2,1)S(1)} collective-permute-done((bf16[16,80,128]{2,1,0:T(8,128)(2,1)S(1)}, bf16[16,80,128]{2,1,0:T(8,128)(2,1)S(1)}, u32[]{:S(2)}, u32[]{:S(2)}) %collective-permute-start.6) | collective-permute-done | bytes 327712 | tf_op jit(solution)/shard_map/ppermute | solution.py:313
  56.0 4.7 %shard_map.79 = (bf16[64,512]{1,0:T(8,128)(2,1)S(1)}, f32[64,512]{1,0:T(8,128)S(1)}, bf16[16,512]{1,0:T(8,128)(2,1)S(1)}) custom-call(s32[1]{0:T(128)} %bitcast.me_ref, bf16[16,80,128]{2,1,0:T(8,128)(2,1)S(1)} %all_to_all.21.own_ref, bf16[16,80,128]{2,1,0:T(8,128)(2,1)S(1)} %collective-permute-done.6.other_ref, bf16[1024,4096]{1,0:T(8,128)(2,1)S(1)} %get-tuple-element.25.slab_ref), custom_call_target="tpu_custom_call" | custom-call | tf_op jit(solution)/shard_map/pallas_call | solution.py:302
  61.2 0.9 collective-permute-done.7.got_ref
  62.4 1.6 %collective-permute-start.9 = (bf16[80,512]{1,0:T(8,128)(2,1)S(1)}, bf16[80,512]{1,0:T(8,128)(2,1)S(1)}, u32[]{:S(2)}, u32[]{:S(2)}) collective-permute-start(bf16[80,512]{1,0:T(8,128)(2,1)S(1)} %shard_map.80.a_ref), channel_id=1, source_target_pairs={{0,3},{1,0},{2,1},{3,2},{4,7},{5,4},{6,5},{7,6},{8,11},{9,8},{10,9... | collective-permute-start | bytes 245768 | tf_op jit(solution)/shard_map/ppermute | solution.py:318
  64.0 3.4 %collective-permute-done.10.d_ref = bf16[80,512]{1,0:T(8,128)(2,1)S(1)} collective-permute-done((bf16[80,512]{1,0:T(8,128)(2,1)S(1)}, bf16[80,512]{1,0:T(8,128)(2,1)S(1)}, u32[]{:S(2)}, u32[]{:S(2)}) %collective-permute-start.10) | collective-permute-done | bytes 81952 | tf_op jit(solution)/shard_map/ppermute | solution.py:318
  67.4 1.4 %collective-permute-done.8.b_ref = bf16[80,512]{1,0:T(8,128)(2,1)S(1)} collective-permute-done((bf16[80,512]{1,0:T(8,128)(2,1)S(1)}, bf16[80,512]{1,0:T(8,128)(2,1)S(1)}, u32[]{:S(2)}, u32[]{:S(2)}) %collective-permute-start.8) | collective-permute-done | bytes 81952 | tf_op jit(solution)/shard_map/ppermute | solution.py:318
  68.8 2.0 %collective-permute-start.11 = (bf16[80,512]{1,0:T(8,128)(2,1)S(1)}, bf16[80,512]{1,0:T(8,128)(2,1)S(1)}, u32[]{:S(2)}, u32[]{:S(2)}) collective-permute-start(bf16[80,512]{1,0:T(8,128)(2,1)S(1)} %shard_map.81.mine_ref), channel_id=1, source_target_pairs={{0,64},{64,0},{1,65},{65,1},{2,66},{66,2},{3,67},{67,3},{4,68},{68... | collective-permute-start | bytes 245768 | tf_op jit(solution)/shard_map/ppermute | solution.py:313
  70.9 0.9 collective-permute-done.11.other_ref
  71.8 3.4 %shard_map.82 = (bf16[16,64,128]{2,1,0:T(8,128)(2,1)S(1)}, f32[16,64,128]{2,1,0:T(8,128)S(1)}, bf16[16,16,128]{2,1,0:T(8,128)(2,1)S(1)}, bf16[64,1024]{1,0:T(8,128)(2,1)S(1)}) custom-call(s32[1]{0:T(128)} %bitcast.me_ref, bf16[80,512]{1,0:T(8,128)(2,1)S(1)} %shard_map.81.mine_ref, bf16[80,512]{1,0:T(8,128)(2,1)S(1)} %collective-permute-done.11.other_ref, ...), custom_call_target="tpu_custom_call" | custom-call | tf_op jit(solution)/shard_map/pallas_call | solution.py:302
  75.7 1.2 %collective-permute-done.12.got_ref = bf16[16,64,128]{2,1,0:T(8,128)(2,1)S(1)} collective-permute-done((bf16[16,64,128]{2,1,0:T(8,128)(2,1)S(1)}, bf16[16,64,128]{2,1,0:T(8,128)(2,1)S(1)}, u32[]{:S(2)}, u32[]{:S(2)}) %collective-permute-start.12) | collective-permute-done | bytes 262176 | tf_op jit(solution)/shard_map/ppermute | solution.py:313
  76.9 11.2 %all_to_all.22.parts_ref = bf16[16,80,128]{2,1,0:T(8,128)(2,1)S(1)} all-to-all(bf16[16,80,128]{2,1,0:T(8,128)(2,1)S(1)} %shard_map.83), channel_id=1, replica_groups=mesh['dp'=2,'vocab'=16,'mp'=4] {'vocab'}, dimensions={0} | all-to-all | bytes 655360 | tf_op jit(solution)/shard_map/all_to_all | solution.py:325
  88.1 11.5 %all_to_all.23.own_ref = bf16[16,80,128]{2,1,0:T(8,128)(2,1)S(1)} all-to-all(bf16[16,80,128]{2,1,0:T(8,128)(2,1)S(1)} %shard_map.84), channel_id=1, replica_groups=mesh['dp'=2,'vocab'=16,'mp'=4] {'vocab'}, dimensions={0} | all-to-all | bytes 655360 | tf_op jit(solution)/shard_map/all_to_all | solution.py:327
  99.6 2.9 %collective-permute-start.13 = (bf16[16,80,128]{2,1,0:T(8,128)(2,1)S(1)}, bf16[16,80,128]{2,1,0:T(8,128)(2,1)S(1)}, u32[]{:S(2)}, u32[]{:S(2)}) collective-permute-start(bf16[16,80,128]{2,1,0:T(8,128)(2,1)S(1)} %all_to_all.23.own_ref), channel_id=1, source_target_pairs={{0,64},{64,0},{1,65},{65,1},{2,66},{66,2},{3,67},{67,3},{4,68},{68... | collective-permute-start | bytes 983048 | tf_op jit(solution)/shard_map/ppermute | solution.py:313
  102.6 1.3 %collective-permute-done.13.other_ref = bf16[16,80,128]{2,1,0:T(8,128)(2,1)S(1)} collective-permute-done((bf16[16,80,128]{2,1,0:T(8,128)(2,1)S(1)}, bf16[16,80,128]{2,1,0:T(8,128)(2,1)S(1)}, u32[]{:S(2)}, u32[]{:S(2)}) %collective-permute-start.13) | collective-permute-done | bytes 327712 | tf_op jit(solution)/shard_map/ppermute | solution.py:313
  103.8 4.5 %shard_map.85 = (f32[64,4096]{1,0:T(8,128)S(1)}, f32[64,64]{1,0:T(8,128)S(1)}, f32[64,4096]{1,0:T(8,128)}, f32[64,4096]{1,0:T(8,128)}, bf16[64,4096]{1,0:T(8,128)(2,1)S(1)}, /*index=5*/bf16[64,1024]{1,0:T(8,128)(2,1)S(1)}) custom-call(s32[1]{0:T(128)} %bitcast.me_ref, bf16[16,80,128]{2,1,0:T(8,128)(2,1)S(1)} %all_to_all.23.own_ref, ...), custom_call_target="tpu_custom_call" | custom-call | tf_op jit(solution)/shard_map/pallas_call | solution.py:302
  108.3 1.6 %collective-permute-start.15 = (f32[64,64]{1,0:T(8,128)S(1)}, f32[64,64]{1,0:T(8,128)S(1)}, u32[]{:S(2)}, u32[]{:S(2)}) collective-permute-start(f32[64,64]{1,0:T(8,128)S(1)} %get-tuple-element.38.a_ref), channel_id=1, source_target_pairs={{0,3},{1,0},{2,1},{3,2},{4,7},{5,4},{6,5},{7,6},{8,11},{9,8},{10,9... | collective-permute-start | bytes 49160 | tf_op jit(solution)/shard_map/ppermute | solution.py:318
  109.9 4.9 %shard_map.86 = bf16[1024,4096]{1,0:T(8,128)(2,1)} custom-call(bf16[64,1024]{1,0:T(8,128)(2,1)S(1)} %get-tuple-element.36.left_ref, bf16[64,4096]{1,0:T(8,128)(2,1)S(1)} %get-tuple-element.37.direction_ref), custom_call_target="tpu_custom_call" | custom-call | flops 536870912 | bytes 8388608 | tf_op jit(solution)/shard_map/pallas_call | solution.py:389
  114.8 3.3 %shard_map.87 = f32[64,4096]{1,0:T(8,128)} custom-call(f32[64,64]{1,0:T(8,128)S(1)} %get-tuple-element.38.a_ref, f32[64,64]{1,0:T(8,128)S(1)} %collective-permute-done.14.b_ref, f32[64,64]{1,0:T(8,128)S(1)} %collective-permute-done.15.c_ref, f32[64,64]{1,0:T(8,128)S(1)} %collective-permute-done.16.d_ref, f32[64,4096]{1,0:T(8,128)S(1)} %get-tuple-element.39.columns_ref), custom_call_target="tpu_custom_call" | custom-call | tf_op jit(solution)/shard_map/pallas_call | solution.py:302
  (25 shorter events, 2.8 us)
Async XLA Ops:
  7.5 2.4 %collective-permute-start = (bf16[64,512]{1,0:T(8,128)(2,1)S(1)}, bf16[64,512]{1,0:T(8,128)(2,1)S(1)}, u32[]{:S(2)}, u32[]{:S(2)}) collective-permute-start(bf16[64,512]{1,0:T(8,128)(2,1)S(1)} %get-tuple-element.24), channel_id=1, source_target_pairs={{0,64},{64,0},{1,65},{65,1},{2,66},{66,2},{3,67},{67,3},{4,68},{68... | collective-permute-start | bytes 196616 | tf_op jit(solution)/shard_map/ppermute | solution.py:313
  9.9 4.7 %collective-permute-start.3 = (bf16[64,512]{1,0:T(8,128)(2,1)S(1)}, bf16[64,512]{1,0:T(8,128)(2,1)S(1)}, u32[]{:S(2)}, u32[]{:S(2)}) collective-permute-start(bf16[64,512]{1,0:T(8,128)(2,1)S(1)} %add_convert_fusion.1), channel_id=1, source_target_pairs={{0,2},{1,3},{2,0},{3,1},{4,6},{5,7},{6,4},{7,5},{8,10},{9,11},{10,... | collective-permute-start | bytes 196616 | tf_op jit(solution)/shard_map/ppermute | solution.py:318
  12.8 3.5 %collective-permute-start.2 = (bf16[64,512]{1,0:T(8,128)(2,1)S(1)}, bf16[64,512]{1,0:T(8,128)(2,1)S(1)}, u32[]{:S(2)}, u32[]{:S(2)}) collective-permute-start(bf16[64,512]{1,0:T(8,128)(2,1)S(1)} %add_convert_fusion.1), channel_id=1, source_target_pairs={{0,3},{1,0},{2,1},{3,2},{4,7},{5,4},{6,5},{7,6},{8,11},{9,8},{10,9... | collective-permute-start | bytes 196616 | tf_op jit(solution)/shard_map/ppermute | solution.py:318
  13.6 4.3 %collective-permute-start.1 = (bf16[64,512]{1,0:T(8,128)(2,1)S(1)}, bf16[64,512]{1,0:T(8,128)(2,1)S(1)}, u32[]{:S(2)}, u32[]{:S(2)}) collective-permute-start(bf16[64,512]{1,0:T(8,128)(2,1)S(1)} %add_convert_fusion.1), channel_id=1, source_target_pairs={{0,1},{1,2},{2,3},{3,0},{4,5},{5,6},{6,7},{7,4},{8,9},{9,10},{10,1... | collective-permute-start | bytes 196616 | tf_op jit(solution)/shard_map/ppermute | solution.py:318
  18.0 3.0 %collective-permute-start.4 = (bf16[64,512]{1,0:T(8,128)(2,1)S(1)}, bf16[64,512]{1,0:T(8,128)(2,1)S(1)}, u32[]{:S(2)}, u32[]{:S(2)}) collective-permute-start(bf16[64,512]{1,0:T(8,128)(2,1)S(1)} %add_convert_fusion.mine_ref), channel_id=1, source_target_pairs={{0,64},{64,0},{1,65},{65,1},{2,66},{66,2},{3,67},{67,3},{4,68},{68... | collective-permute-start | bytes 196616 | tf_op jit(solution)/shard_map/ppermute | solution.py:313
  23.1 1.5 %collective-permute-start.5 = (bf16[16,64,128]{2,1,0:T(8,128)(2,1)S(1)}, bf16[16,64,128]{2,1,0:T(8,128)(2,1)S(1)}, u32[]{:S(2)}, u32[]{:S(2)}) collective-permute-start(bf16[16,64,128]{2,1,0:T(8,128)(2,1)S(1)} %get-tuple-element.27), channel_id=1, source_target_pairs={{0,64},{64,0},{1,65},{65,1},{2,66},{66,2},{3,67},{67,3},{4,68},{68... | collective-permute-start | bytes 786440 | tf_op jit(solution)/shard_map/ppermute | solution.py:313
  51.8 4.2 %collective-permute-start.6 = (bf16[16,80,128]{2,1,0:T(8,128)(2,1)S(1)}, bf16[16,80,128]{2,1,0:T(8,128)(2,1)S(1)}, u32[]{:S(2)}, u32[]{:S(2)}) collective-permute-start(bf16[16,80,128]{2,1,0:T(8,128)(2,1)S(1)} %all_to_all.21.own_ref), channel_id=1, source_target_pairs={{0,64},{64,0},{1,65},{65,1},{2,66},{66,2},{3,67},{67,3},{4,68},{68... | collective-permute-start | bytes 983048 | tf_op jit(solution)/shard_map/ppermute | solution.py:313
  60.7 43.1 %copy-start = (f32[64,4096]{1,0:T(8,128)S(1)}, f32[64,4096]{1,0:T(8,128)}, u32[]{:S(2)}) copy-start(f32[64,4096]{1,0:T(8,128)} %first_ref.1) | copy-start | bytes 3145732
  60.8 43.1 %copy-start.1 = (f32[64,4096]{1,0:T(8,128)S(1)}, f32[64,4096]{1,0:T(8,128)}, u32[]{:S(2)}) copy-start(f32[64,4096]{1,0:T(8,128)} %second_ref.1) | copy-start | bytes 3145732
  60.8 1.4 %collective-permute-start.7 = (bf16[64,512]{1,0:T(8,128)(2,1)S(1)}, bf16[64,512]{1,0:T(8,128)(2,1)S(1)}, u32[]{:S(2)}, u32[]{:S(2)}) collective-permute-start(bf16[64,512]{1,0:T(8,128)(2,1)S(1)} %get-tuple-element.30), channel_id=1, source_target_pairs={{0,64},{64,0},{1,65},{65,1},{2,66},{66,2},{3,67},{67,3},{4,68},{68... | collective-permute-start | bytes 196616 | tf_op jit(solution)/shard_map/ppermute | solution.py:313
  62.1 5.3 %collective-permute-start.10 = (bf16[80,512]{1,0:T(8,128)(2,1)S(1)}, bf16[80,512]{1,0:T(8,128)(2,1)S(1)}, u32[]{:S(2)}, u32[]{:S(2)}) collective-permute-start(bf16[80,512]{1,0:T(8,128)(2,1)S(1)} %shard_map.80.a_ref), channel_id=1, source_target_pairs={{0,2},{1,3},{2,0},{3,1},{4,6},{5,7},{6,4},{7,5},{8,10},{9,11},{10,... | collective-permute-start | bytes 245768 | tf_op jit(solution)/shard_map/ppermute | solution.py:318
  62.4 5.0 %collective-permute-start.9 = (bf16[80,512]{1,0:T(8,128)(2,1)S(1)}, bf16[80,512]{1,0:T(8,128)(2,1)S(1)}, u32[]{:S(2)}, u32[]{:S(2)}) collective-permute-start(bf16[80,512]{1,0:T(8,128)(2,1)S(1)} %shard_map.80.a_ref), channel_id=1, source_target_pairs={{0,3},{1,0},{2,1},{3,2},{4,7},{5,4},{6,5},{7,6},{8,11},{9,8},{10,9... | collective-permute-start | bytes 245768 | tf_op jit(solution)/shard_map/ppermute | solution.py:318
  64.0 4.8 %collective-permute-start.8 = (bf16[80,512]{1,0:T(8,128)(2,1)S(1)}, bf16[80,512]{1,0:T(8,128)(2,1)S(1)}, u32[]{:S(2)}, u32[]{:S(2)}) collective-permute-start(bf16[80,512]{1,0:T(8,128)(2,1)S(1)} %shard_map.80.a_ref), channel_id=1, source_target_pairs={{0,1},{1,2},{2,3},{3,0},{4,5},{5,6},{6,7},{7,4},{8,9},{9,10},{10,1... | collective-permute-start | bytes 245768 | tf_op jit(solution)/shard_map/ppermute | solution.py:318
  68.8 3.0 %collective-permute-start.11 = (bf16[80,512]{1,0:T(8,128)(2,1)S(1)}, bf16[80,512]{1,0:T(8,128)(2,1)S(1)}, u32[]{:S(2)}, u32[]{:S(2)}) collective-permute-start(bf16[80,512]{1,0:T(8,128)(2,1)S(1)} %shard_map.81.mine_ref), channel_id=1, source_target_pairs={{0,64},{64,0},{1,65},{65,1},{2,66},{66,2},{3,67},{67,3},{4,68},{68... | collective-permute-start | bytes 245768 | tf_op jit(solution)/shard_map/ppermute | solution.py:313
  75.2 1.6 %collective-permute-start.12 = (bf16[16,64,128]{2,1,0:T(8,128)(2,1)S(1)}, bf16[16,64,128]{2,1,0:T(8,128)(2,1)S(1)}, u32[]{:S(2)}, u32[]{:S(2)}) collective-permute-start(bf16[16,64,128]{2,1,0:T(8,128)(2,1)S(1)} %get-tuple-element.33), channel_id=1, source_target_pairs={{0,64},{64,0},{1,65},{65,1},{2,66},{66,2},{3,67},{67,3},{4,68},{68... | collective-permute-start | bytes 786440 | tf_op jit(solution)/shard_map/ppermute | solution.py:313
  99.6 4.2 %collective-permute-start.13 = (bf16[16,80,128]{2,1,0:T(8,128)(2,1)S(1)}, bf16[16,80,128]{2,1,0:T(8,128)(2,1)S(1)}, u32[]{:S(2)}, u32[]{:S(2)}) collective-permute-start(bf16[16,80,128]{2,1,0:T(8,128)(2,1)S(1)} %all_to_all.23.own_ref), channel_id=1, source_target_pairs={{0,64},{64,0},{1,65},{65,1},{2,66},{66,2},{3,67},{67,3},{4,68},{68... | collective-permute-start | bytes 983048 | tf_op jit(solution)/shard_map/ppermute | solution.py:313
  108.3 6.4 %collective-permute-start.16 = (f32[64,64]{1,0:T(8,128)S(1)}, f32[64,64]{1,0:T(8,128)S(1)}, u32[]{:S(2)}, u32[]{:S(2)}) collective-permute-start(f32[64,64]{1,0:T(8,128)S(1)} %get-tuple-element.38.a_ref), channel_id=1, source_target_pairs={{0,2},{1,3},{2,0},{3,1},{4,6},{5,7},{6,4},{7,5},{8,10},{9,11},{10,... | collective-permute-start | bytes 49160 | tf_op jit(solution)/shard_map/ppermute | solution.py:318
  108.3 6.4 %collective-permute-start.15 = (f32[64,64]{1,0:T(8,128)S(1)}, f32[64,64]{1,0:T(8,128)S(1)}, u32[]{:S(2)}, u32[]{:S(2)}) collective-permute-start(f32[64,64]{1,0:T(8,128)S(1)} %get-tuple-element.38.a_ref), channel_id=1, source_target_pairs={{0,3},{1,0},{2,1},{3,2},{4,7},{5,4},{6,5},{7,6},{8,11},{9,8},{10,9... | collective-permute-start | bytes 49160 | tf_op jit(solution)/shard_map/ppermute | solution.py:318
  109.9 4.9 %collective-permute-start.14 = (f32[64,64]{1,0:T(8,128)S(1)}, f32[64,64]{1,0:T(8,128)S(1)}, u32[]{:S(2)}, u32[]{:S(2)}) collective-permute-start(f32[64,64]{1,0:T(8,128)S(1)} %get-tuple-element.38.a_ref), channel_id=1, source_target_pairs={{0,1},{1,2},{2,3},{3,0},{4,5},{5,6},{6,7},{7,4},{8,9},{9,10},{10,1... | collective-permute-start | bytes 49160 | tf_op jit(solution)/shard_map/ppermute | solution.py:318

commit v3 on v2

v3 whole, which is shorter than its diff:
```python
import functools
import math

import jax
import jax.numpy as jnp
from jax import lax
from jax.experimental import pallas as pl
from jax.experimental.pallas import tpu as pltpu
from jax.sharding import PartitionSpec as P

F32 = jnp.float32
BF16 = jnp.bfloat16
LANE = 128
EXTRA = 16
TILE = 512
WIDE = 256
VMEM_LIMIT = 28 * 1024 * 1024

VMEM = pl.BlockSpec(memory_space=pltpu.VMEM)
SMEM = pl.BlockSpec(memory_space=pltpu.SMEM)


def thirds(value):
    high = value.astype(BF16).astype(F32)
    rest = value - high
    mid = rest.astype(BF16).astype(F32)
    return high, mid, rest - mid


def stacked(value, axis=0):
    return jnp.concatenate(thirds(value), axis=axis).astype(BF16)


def dot(a, b, ca, cb):
    return lax.dot_general(a, b, (((ca,), (cb,)), ((), ())), preferred_element_type=F32)


def inverse_factor(gram):
    rank = gram.shape[0]
    lanes = lax.broadcasted_iota(jnp.int32, (8, rank), 1)
    subs = lax.broadcasted_iota(jnp.int32, (8, LANE), 0)
    blocks = rank // 8
    both = []
    for b in range(blocks):
        eye = jnp.where(lanes == subs[:, :rank] + 8 * b, 1.0, 0.0).astype(F32)
        both.append(jnp.concatenate([gram[8 * b : 8 * b + 8, :], eye], axis=1))
    scale = []
    for b in range(blocks):
        diag = jnp.ones((8, LANE), F32)
        cols = {
            (j, i): jnp.broadcast_to(both[i][:, 8 * b + j : 8 * b + j + 1], (8, LANE))
            for j in range(8)
            for i in range(b, blocks)
        }
        for j in range(8):
            pivot = cols[j, b][j : j + 1, :]
            inverse = 1.0 / pivot
            diag = jnp.where(subs == j, pivot, diag)
            row = both[b][j : j + 1, :] * inverse
            heads = {m: cols[m, b][j : j + 1, :] * inverse for m in range(j + 1, 8)}
            for i in range(b, blocks):
                f = cols[j, i]
                if i == b:
                    f = jnp.where(subs > j, f, 0.0)
                both[i] = both[i] - f * row
                for m in range(j + 1, 8):
                    cols[m, i] = cols[m, i] - f * heads[m]
        scale.append(lax.rsqrt(diag))
    return jnp.concatenate(
        [both[b][:, rank:] * scale[b][:, :rank] for b in range(blocks)], axis=0
    )


def applied(factor3, block):
    return dot(factor3, jnp.concatenate([block] * 3, axis=0), 1, 0)


def folded(total, rank):
    wide = total[:rank] + total[rank : 2 * rank] + total[2 * rank :]
    return wide[:, :rank] + wide[:, rank : 2 * rank] + wide[:, 2 * rank :]


def span(base, size):
    return pl.ds(pl.multiple_of(base, size), size)


def extra_rows(piece):
    pad = jnp.zeros((EXTRA - 3 * piece.shape[0], piece.shape[1]), F32)
    return jnp.concatenate([*thirds(piece), pad], axis=0).astype(BF16)


def from_extra(e, each):
    return e[:each] + e[each : 2 * each] + e[2 * each : 3 * each]


def gathered_gram(chunks_ref, rank):
    n = chunks_ref.shape[0]
    pieces = [
        from_extra(chunks_ref[c, rank : rank + EXTRA, :].astype(F32), rank // n) for c in range(n)
    ]
    return jnp.concatenate(pieces, axis=0)[:, :rank]


def blocks_of(chunks_ref, rank):
    per = TILE // LANE
    for j in range(chunks_ref.shape[0] // per):
        block = jnp.concatenate([chunks_ref[j * per + q, :rank, :] for q in range(per)], axis=1)
        yield slice(j * TILE, (j + 1) * TILE), block


def gram_of(columns_ref, at):
    three = stacked(columns_ref[:, at])
    return dot(three, three, 1, 1)


def first_rows(half, left, slab_hbm, out_ref, slab_ref, sems):
    rows = slab_ref.shape[0]
    copies = [
        pltpu.make_async_copy(
            slab_hbm.at[span(half * rows + t, LANE), :], slab_ref.at[t : t + LANE, :], sems.at[t // LANE]
        )
        for t in range(0, rows, LANE)
    ]
    copies[0].start()
    copies[1].start()
    left = left()
    for i, copy in enumerate(copies):
        copy.wait()
        if i + 2 < len(copies):
            copies[i + 2].start()
        at = slice(i * LANE, (i + 1) * LANE)
        out_ref[:, at] = dot(left, slab_ref[at, :], 1, 1).astype(out_ref.dtype)


def first_theirs_kernel(
    me_ref, basis_hbm, slab_hbm, theirs_ref, slab_ref, left_ref, basis_ref, sems, basis_sem
):
    copy = pltpu.make_async_copy(basis_hbm, basis_ref, basis_sem.at[0])
    copy.start()

    def left():
        copy.wait()
        left_ref[...] = basis_ref[...].astype(BF16)
        return left_ref[...]

    first_rows(1 - me_ref[0], left, slab_hbm, theirs_ref, slab_ref, sems)


def first_mine_kernel(me_ref, left_ref, slab_hbm, mine_ref, slab_ref, sems):
    first_rows(me_ref[0], lambda: left_ref[...], slab_hbm, mine_ref, slab_ref, sems)


def columns_mine_kernel(orthogonal, *refs):
    if orthogonal:
        mine_ref, gram_in_ref, slab_ref, acc_ref, gram_ref, factor_ref, rows_ref = refs
        factor3 = stacked(inverse_factor(gram_in_ref[...]), 1)
        factor_ref[...] = factor3
        mine = applied(factor3, mine_ref[...]).astype(BF16)
        rows_ref[...] = mine
    else:
        mine_ref, slab_ref, acc_ref, gram_ref = refs
        mine = mine_ref[...]
    gram_ref[...] = dot(mine, mine, 1, 1)
    for t in range(0, acc_ref.shape[1], TILE):
        acc_ref[:, t : t + TILE] = dot(mine, slab_ref[:, t : t + TILE], 1, 0)


def add_half(core, rows, acc_ref, slab_ref, out_ref):
    n = out_ref.shape[0]
    per = TILE // LANE
    for j in range(n // per):
        at = span(core * (n * LANE) + j * TILE, TILE)
        product = (acc_ref[:, at] + dot(rows, slab_ref[:, at], 1, 0)).astype(out_ref.dtype)
        for q in range(per):
            out_ref[j * per + q] = product[:, q * LANE : (q + 1) * LANE]


def columns_theirs_kernel(orthogonal, *refs):
    if orthogonal:
        me_ref, other_ref, acc_ref, slab_ref, factor_ref, theirs_ref, rows_ref = refs
        other = applied(factor_ref[...], other_ref[...]).astype(BF16)
        rows_ref[...] = other
    else:
        me_ref, other_ref, acc_ref, slab_ref, theirs_ref = refs
        other = other_ref[...]
    add_half(1 - me_ref[0], other, acc_ref, slab_ref, theirs_ref)


def columns_owned_kernel(
    me_ref, other_ref, acc_ref, slab_ref, gram_mine_ref, owned_ref, extra_ref, gram_ref
):
    other = other_ref[...]
    rank = other.shape[0]
    gram_ref[...] = jnp.zeros_like(gram_ref)
    gram_ref[:, :rank] = gram_mine_ref[...] + dot(other, other, 1, 1)
    each = rank // extra_ref.shape[0]
    for c in range(extra_ref.shape[0]):
        extra_ref[c] = extra_rows(gram_ref[c * each : (c + 1) * each, :])
    add_half(me_ref[0], other, acc_ref, slab_ref, owned_ref)


def join_chunks_kernel(owned_ref, got_ref, extra_ref, out_ref):
    rank = owned_ref.shape[1]
    for c in range(out_ref.shape[0]):
        out_ref[c, :rank, :] = (owned_ref[c] + got_ref[c].astype(F32)).astype(BF16)
        out_ref[c, rank:, :] = extra_ref[c]


def sum_chunks_kernel(parts_ref, out_ref):
    n = parts_ref.shape[0]
    rank = parts_ref.shape[1] - EXTRA
    total = parts_ref[0].astype(F32)
    for c in range(1, n):
        total = total + parts_ref[c].astype(F32)
    extra = extra_rows(from_extra(total[rank:], rank // n))
    piece = jnp.concatenate([total[:rank].astype(BF16), extra], axis=0)
    for c in range(n):
        out_ref[c] = piece


def add_rows(columns, core, acc_ref, slab_ref, out_ref):
    at = span(core * columns.shape[1], columns.shape[1])
    for t in range(0, out_ref.shape[1], WIDE):
        product = dot(columns, slab_ref[t : t + WIDE, at], 1, 1)
        if acc_ref is not None:
            product = acc_ref[:, t : t + WIDE] + product
        out_ref[:, t : t + WIDE] = product.astype(out_ref.dtype)


def rows_own_kernel(
    me_ref, own_ref, theirs_slab_ref, mine_slab_ref,
    factor_ref, theirs_ref, mine_ref, gram_ref, columns_ref, half_ref,
):
    rank = gram_ref.shape[0]
    factor3 = stacked(inverse_factor(gathered_gram(own_ref, rank)), 1)
    factor_ref[...] = factor3
    total = jnp.zeros((3 * rank, 3 * rank), F32)
    for at, block in blocks_of(own_ref, rank):
        columns = applied(factor3, block)
        columns_ref[:, at] = columns
        half_ref[:, at] = columns.astype(BF16)
        total = total + gram_of(columns_ref, at)
    gram_ref[...] = folded(total, rank)
    half = half_ref[...]
    add_rows(half, me_ref[0], None, theirs_slab_ref, theirs_ref)
    add_rows(half, me_ref[0], None, mine_slab_ref, mine_ref)


def rows_theirs_kernel(
    me_ref, other_ref, factor_ref, acc_ref, slab_ref, theirs_ref, columns_ref, half_ref
):
    factor3 = factor_ref[...]
    for at, block in blocks_of(other_ref, factor3.shape[0]):
        columns = applied(factor3, block)
        columns_ref[:, at] = columns
        half_ref[:, at] = columns.astype(BF16)
    add_rows(half_ref[...], 1 - me_ref[0], acc_ref, slab_ref, theirs_ref)


def rows_mine_kernel(
    me_ref, half_ref, columns_ref, gram_own_ref, acc_ref, slab_ref, mine_ref, pack_ref
):
    rank, width = columns_ref.shape
    total = jnp.zeros((3 * rank, 3 * rank), F32)
    for t in range(0, width, TILE):
        total = total + gram_of(columns_ref, slice(t, t + TILE))
    gram = gram_own_ref[...] + folded(total, rank)
    gram = jnp.concatenate([gram[: rank // 2], gram[rank // 2 :]], axis=1)
    pack_ref[...] = jnp.zeros_like(pack_ref)
    pack_ref[:, : 3 * LANE] = stacked(gram, 1)
    add_rows(half_ref[...], 1 - me_ref[0], acc_ref, slab_ref, mine_ref)


def join_rows_kernel(mine_ref, got_ref, pack_ref, out_ref):
    rank = mine_ref.shape[0]
    out_ref[:rank, :] = (mine_ref[...] + got_ref[...].astype(F32)).astype(BF16)
    out_ref[rank:, :] = pack_ref[...]


def sum_packed_kernel(a_ref, b_ref, c_ref, d_ref, rows_ref, gram_ref):
    total = (a_ref[...].astype(F32) + b_ref[...].astype(F32)) + (
        c_ref[...].astype(F32) + d_ref[...].astype(F32)
    )
    rank = rows_ref.shape[0]
    rows_ref[...] = total[:rank].astype(BF16)
    e = total[rank:]
    g = e[:, :LANE] + e[:, LANE : 2 * LANE] + e[:, 2 * LANE : 3 * LANE]
    gram_ref[...] = jnp.concatenate([g[:, :rank], g[:, rank:]], axis=0)


def final_own_kernel(
    scale, me_ref, own_ref, rows_mine_ref, rows_other_ref,
    factor_ref, columns_ref, gram_ref, left_ref,
):
    me = me_ref[0]
    rank, half = rows_mine_ref.shape
    factor3 = stacked(inverse_factor(gathered_gram(own_ref, rank)), 1)
    factor_ref[...] = factor3
    for core, ref in ((me, rows_mine_ref), (1 - me, rows_other_ref)):
        left = applied(factor3, ref[...]).astype(BF16)
        left_ref[:, span(core * half, half)] = (left.astype(F32) * scale).astype(BF16)
    total = jnp.zeros((3 * rank, 3 * rank), F32)
    for at, block in blocks_of(own_ref, rank):
        columns_ref[:, at] = applied(factor3, block)
        total = total + gram_of(columns_ref, at)
    gram_ref[...] = folded(total, rank)


def moments_kernel(
    me_ref, other_ref, factor_ref, own_columns_ref, gram_own_ref, first_ref, second_ref,
    columns_ref, gram_ref, new_first_ref, new_second_ref, direction_ref,
):
    me = me_ref[0]
    factor3 = factor_ref[...]
    rank, width = own_columns_ref.shape
    corr_one = 1.0 - 0.9**10
    corr_two = 1.0 - 0.999**10

    def moments(at, columns):
        columns_ref[:, at] = columns
        new_first = 0.9 * first_ref[:, at] + 0.1 * columns
        new_second = 0.999 * second_ref[:, at] + 0.001 * columns * columns
        new_first_ref[:, at] = new_first
        new_second_ref[:, at] = new_second
        direction = new_first / corr_one / (jnp.sqrt(new_second / corr_two) + 1e-08)
        direction_ref[:, at] = direction.astype(BF16)

    total = jnp.zeros((3 * rank, 3 * rank), F32)
    for part, block in blocks_of(other_ref, rank):
        at = span((1 - me) * width + part.start, TILE)
        moments(at, applied(factor3, block))
        total = total + gram_of(columns_ref, at)
        at = span(me * width + part.start, TILE)
        moments(at, own_columns_ref[:, part])
    gram_ref[...] = gram_own_ref[...] + folded(total, rank)


def update_kernel(left_ref, direction_ref, update_ref):
    left = left_ref[...]
    for t in range(0, direction_ref.shape[1], TILE):
        product = dot(left, direction_ref[:, t : t + TILE], 0, 0)
        update_ref[:, t : t + TILE] = product.astype(BF16)


def basis_kernel(a_ref, b_ref, c_ref, d_ref, columns_ref, basis_ref):
    factor = inverse_factor((a_ref[...] + b_ref[...]) + (c_ref[...] + d_ref[...]))
    high, mid, low = thirds(factor)
    wide = jnp.concatenate([low, mid, high, mid, high, high], axis=1).astype(BF16)
    for t in range(0, columns_ref.shape[1], TILE):
        high, mid, low = (x.astype(BF16) for x in thirds(columns_ref[:, t : t + TILE]))
        tall = jnp.concatenate([high, mid, low, high, mid, high], axis=0)
        basis_ref[:, t : t + TILE] = dot(wide, tall, 1, 0)


def call(kernel, outs, operands, scratch=(), hbm=()):
    def spec(i, x):
        if x.dtype == jnp.int32:
            return SMEM
        return pl.BlockSpec(memory_space=pl.ANY) if i in hbm else VMEM

    moved = sum(x.size * x.dtype.itemsize for x in operands)
    return pl.pallas_call(
        kernel,
        out_shape=[jax.ShapeDtypeStruct(s, t) for s, t in outs],
        in_specs=[spec(i, x) for i, x in enumerate(operands)],
        out_specs=[VMEM] * len(outs),
        scratch_shapes=[pltpu.VMEM(*s) if isinstance(s, tuple) else s for s in scratch],
        compiler_params=pltpu.CompilerParams(vmem_limit_bytes=VMEM_LIMIT),
        cost_estimate=pl.CostEstimate(flops=64 * moved, bytes_accessed=moved, transcendentals=0),
    )(*operands)


def swapped(x):
    return lax.ppermute(x, "dp", [(0, 1), (1, 0)])


def others(x):
    n = lax.axis_size("mp")
    return [lax.ppermute(x, "mp", [(i, (i + k) % n) for i in range(n)]) for k in (1, 3, 2)]


def columns_of(me, mine, slabs, owners, gram=None):
    theirs_slab, mine_slab = slabs
    rank, half = mine.shape
    width = mine_slab.shape[1]
    orthogonal = gram is not None
    square = ((rank, rank), F32)
    acc = ((rank, width), F32)
    halves = ((rank, half), BF16)
    chunk = (owners, rank, LANE)
    whole = [((owners, rank + EXTRA, LANE), BF16)]

    other = swapped(mine)
    if orthogonal:
        outs = [acc, square, ((rank, 3 * rank), BF16), halves]
        operands = [mine, gram, mine_slab]
    else:
        outs = [acc, square]
        operands = [mine, mine_slab]
    acc, gram_mine, *rest = call(functools.partial(columns_mine_kernel, orthogonal), outs, operands)
    if orthogonal:
        factor, mine = rest
        theirs, other = call(
            functools.partial(columns_theirs_kernel, True),
            [(chunk, BF16), halves],
            [me, other, acc, theirs_slab, factor],
        )
    else:
        theirs = call(
            functools.partial(columns_theirs_kernel, False),
            [(chunk, BF16)],
            [me, other, acc, theirs_slab],
        )[0]
    got = swapped(theirs)
    owned, extra = call(
        columns_owned_kernel,
        [(chunk, F32), ((owners, EXTRA, LANE), BF16)],
        [me, other, acc, theirs_slab, gram_mine],
        [((rank, LANE), F32)],
    )
    chunks = call(join_chunks_kernel, whole, [owned, got, extra])[0]
    parts = lax.all_to_all(chunks, "vocab", 0, 0)
    copies = call(sum_chunks_kernel, whole, [parts])[0]
    own = lax.all_to_all(copies, "vocab", 0, 0)
    return own, swapped(own), mine, other


def local(grad_parts, old_basis, first_moment, second_moment):
    slab = grad_parts[0]
    vocab, width = slab.shape
    rank = old_basis.shape[0]
    half = vocab // 2
    owners = lax.axis_size("vocab")
    me = lax.axis_index("dp").astype(jnp.int32).reshape(1)
    theirs_out, mine_out = ((rank, half), BF16), ((rank, half), F32)
    wide = ((rank, width), F32)
    narrow = ((rank, width // 2), F32)
    square = ((rank, rank), F32)
    factor_out = ((rank, 3 * rank), BF16)
    half_slab = ((half, width), BF16)
    sems = pltpu.SemaphoreType.DMA((half // LANE,))

    slab, basis = (pltpu.with_memory_space_constraint(x, pltpu.HBM) for x in (slab, old_basis))
    theirs, theirs_slab, left = call(
        first_theirs_kernel,
        [theirs_out, half_slab, ((rank, width), BF16)],
        [me, basis, slab],
        [((rank, width), F32), sems, pltpu.SemaphoreType.DMA((1,))],
        hbm=(1, 2),
    )
    got = swapped(theirs)
    mine, mine_slab = call(
        first_mine_kernel, [mine_out, half_slab], [me, left, slab], [sems], hbm=(2,)
    )
    slabs = (theirs_slab, mine_slab)
    mine = (mine + got.astype(F32)).astype(BF16)
    total = mine.astype(F32)
    for x in others(mine):
        total = total + x.astype(F32)
    own, other, _, _ = columns_of(me, total.astype(BF16), slabs, owners)

    factor, theirs_acc, mine_acc, gram = call(
        rows_own_kernel,
        [factor_out, mine_out, mine_out, square],
        [me, own, theirs_slab, mine_slab],
        [narrow, ((rank, width // 2), BF16)],
    )
    theirs, columns, columns_half = call(
        rows_theirs_kernel,
        [theirs_out, narrow, ((rank, width // 2), BF16)],
        [me, other, factor, theirs_acc, theirs_slab],
    )
    got = swapped(theirs)
    mine, pack = call(
        rows_mine_kernel,
        [mine_out, ((rank // 2, half), BF16)],
        [me, columns_half, columns, gram, mine_acc, mine_slab],
    )
    mine = call(join_rows_kernel, [((rank + rank // 2, half), BF16)], [mine, got, pack])[0]
    mine, gram = call(sum_packed_kernel, [theirs_out, square], [mine, *others(mine)])
    own, other, rows_mine, rows_other = columns_of(me, mine, slabs, owners, gram)

    scale = math.sqrt(vocab * owners)
    assert scale == 2.0 ** round(math.log2(scale))
    factor, columns, gram, left = call(
        functools.partial(final_own_kernel, scale),
        [factor_out, narrow, square, ((rank, vocab), BF16)],
        [me, own, rows_mine, rows_other],
    )
    columns, gram, new_first, new_second, direction = call(
        moments_kernel,
        [wide, square, wide, wide, ((rank, width), BF16)],
        [me, other, factor, columns, gram, first_moment, second_moment],
    )
    gram_others = others(gram)
    update = pl.pallas_call(
        update_kernel,
        out_shape=jax.ShapeDtypeStruct((vocab, width), BF16),
        grid=(vocab // WIDE,),
        in_specs=[
            pl.BlockSpec((rank, WIDE), lambda i: (0, i)),
            pl.BlockSpec((rank, width), lambda i: (0, 0)),
        ],
        out_specs=pl.BlockSpec((WIDE, width), lambda i: (i, 0)),
        compiler_params=pltpu.CompilerParams(vmem_limit_bytes=VMEM_LIMIT),
        cost_estimate=pl.CostEstimate(
            flops=2 * rank * vocab * width, bytes_accessed=2 * vocab * width, transcendentals=0
        ),
    )(left, direction)
    basis = call(basis_kernel, [wide], [gram, *gram_others, columns])[0]
    return (update, basis, new_first, new_second)


def solution(mesh):
    placed = (P("dp", "vocab", "mp"), P(None, "mp"), P(None, "mp"), P(None, "mp"))
    return jax.shard_map(
        local,
        mesh=mesh,
        in_specs=placed,
        out_specs=(P("vocab", "mp"), P(None, "mp"), P(None, "mp"), P(None, "mp")),
        check_vma=False,
    )
```

time: 118 us -> 115 us (0.975)
  waiting for transfers between devices: 17 us -> 11.5 us
  Pallas kernels: 30 us -> 33 us
  starting transfers between devices: 20.6 us -> 19.1 us
    ppermute x8, waiting for transfers between devices: 8.51 us -> 1.94 us  [swapped(): return lax.ppermute(x, 'dp', [(0, 1), (1, 0)])]
    pallas_call x12 -> x20, Pallas kernels: 25.1 us -> 28.1 us  [call(): pl.pallas_call(kernel, out_shape=[jax.ShapeDtypeStruct(s, t) for s, t in...]
    ppermute x8, starting transfers between devices: 12.8 us -> 10.7 us  [swapped(): return lax.ppermute(x, 'dp', [(0, 1), (1, 0)])]
  transfers between devices with their start and end apart: 17 -> 17, of which waited for: 13 -> 8; matrix products, arithmetic and copies ran while one was open for 0% -> 0% of each run, Pallas kernels for 4% -> 18%
where the time goes in v3:
time: 115 us; the launch traced here: 114 us
  blocking collectives  50 us (43%)
  Pallas kernels  33 us (29%)
  starting transfers between devices  19.1 us (17%)
  waiting for transfers between devices  11.5 us (10%)
    pallas_call x20, Pallas kernels, call(): pl.pallas_call(kernel, out_shape=[jax.ShapeDtypeStruct(s, t) for s, t in...  28.1 us
    all_to_all x2, blocking collectives, columns_of(): parts = lax.all_to_all(chunks, 'vocab', 0, 0)  26.9 us
    all_to_all x2, blocking collectives, columns_of(): own = lax.all_to_all(copies, 'vocab', 0, 0)  23.1 us
    ppermute x8, starting transfers between devices, swapped(): return lax.ppermute(x, 'dp', [(0, 1), (1, 0)])  10.7 us
    ppermute x9, waiting for transfers between devices, others(): lax.ppermute(x, 'mp', [(i, (i + k) % n) for i in range(n)])  9.55 us
    ppermute x9, starting transfers between devices, others(): lax.ppermute(x, 'mp', [(i, (i + k) % n) for i in range(n)])  8.35 us
    pallas_call x1, Pallas kernels, local(): pl.pallas_call(update_kernel, out_shape=jax.ShapeDtypeStruct((vocab, widt...  4.86 us
  transfers between devices with their start and end apart: 17, of which 8 were waited for; matrix products, arithmetic and copies ran while one was open for 0% of the time, Pallas kernels for 18%

profile of v3, /device:TPU:1, one launch (start us, length us, event | category | flops | bytes accessed | tf_op | source)
XLA Modules:
  0.0 114.4 jit_solution(13772495454850247035)
XLA Ops:
  0.6 4.4 %shard_map.75 = (bf16[64,512]{1,0:T(8,128)(2,1)S(1)}, bf16[512,4096]{1,0:T(8,128)(2,1)S(1)}, bf16[64,4096]{1,0:T(8,128)(2,1)S(1)}) custom-call(s32[1]{0:T(128)} %bitcast.me_ref.refs_0_, f32[64,4096]{1,0:T(8,128)} %basis_hbm.1, bf16[1024,4096]{1,0:T(8,128)(2,1)} %bitcast.2), custom_call_target="tpu_custom_call" | custom-call | flops 603980032 | bytes 9437188 | tf_op jit(solution)/shard_map/pallas_call | solution.py:362
  5.0 1.5 %collective-permute-start = (bf16[64,512]{1,0:T(8,128)(2,1)S(1)}, bf16[64,512]{1,0:T(8,128)(2,1)S(1)}, u32[]{:S(2)}, u32[]{:S(2)}) collective-permute-start(bf16[64,512]{1,0:T(8,128)(2,1)S(1)} %get-tuple-element.43), channel_id=1, source_target_pairs={{0,64},{64,0},{1,65},{65,1},{2,66},{66,2},{3,67},{67,3},{4,68},{68... | collective-permute-start | bytes 196616 | tf_op jit(solution)/shard_map/ppermute | solution.py:374
  6.5 4.0 %shard_map.76 = (f32[64,512]{1,0:T(8,128)S(1)}, bf16[512,4096]{1,0:T(8,128)(2,1)S(1)}) custom-call(s32[1]{0:T(128)} %bitcast.me_ref.refs_0_, bf16[64,4096]{1,0:T(8,128)(2,1)S(1)} %get-tuple-element.41.left_ref, bf16[1024,4096]{1,0:T(8,128)(2,1)} %bitcast.3), custom_call_target="tpu_custom_call" | custom-call | flops 570425600 | bytes 8912900 | tf_op jit(solution)/shard_map/pallas_call | solution.py:362
  10.5 2.9 %collective-permute-start.3 = (bf16[64,512]{1,0:T(8,128)(2,1)S(1)}, bf16[64,512]{1,0:T(8,128)(2,1)S(1)}, u32[]{:S(2)}, u32[]{:S(2)}) collective-permute-start(bf16[64,512]{1,0:T(8,128)(2,1)S(1)} %add_convert_fusion.1), channel_id=1, source_target_pairs={{0,2},{1,3},{2,0},{3,1},{4,6},{5,7},{6,4},{7,5},{8,10},{9,11},{10,... | collective-permute-start | bytes 196616 | tf_op jit(solution)/shard_map/ppermute | solution.py:379
  13.4 0.9 collective-permute-start.2
  14.3 0.6 collective-permute-start.1
  14.9 0.9 collective-permute-done.3
  15.8 1.5 %collective-permute-done.2 = bf16[64,512]{1,0:T(8,128)(2,1)S(1)} collective-permute-done((bf16[64,512]{1,0:T(8,128)(2,1)S(1)}, bf16[64,512]{1,0:T(8,128)(2,1)S(1)}, u32[]{:S(2)}, u32[]{:S(2)}) %collective-permute-start.2) | collective-permute-done | bytes 65568 | tf_op jit(solution)/shard_map/ppermute | solution.py:379
  17.3 1.3 %collective-permute-done.1 = bf16[64,512]{1,0:T(8,128)(2,1)S(1)} collective-permute-done((bf16[64,512]{1,0:T(8,128)(2,1)S(1)}, bf16[64,512]{1,0:T(8,128)(2,1)S(1)}, u32[]{:S(2)}, u32[]{:S(2)}) %collective-permute-start.1) | collective-permute-done | bytes 65568 | tf_op jit(solution)/shard_map/ppermute | solution.py:379
  18.6 1.8 %collective-permute-start.4 = (bf16[64,512]{1,0:T(8,128)(2,1)S(1)}, bf16[64,512]{1,0:T(8,128)(2,1)S(1)}, u32[]{:S(2)}, u32[]{:S(2)}) collective-permute-start(bf16[64,512]{1,0:T(8,128)(2,1)S(1)} %add_convert_fusion.refs_0_), channel_id=1, source_target_pairs={{0,64},{64,0},{1,65},{65,1},{2,66},{66,2},{3,67},{67,3},{4,68},{68... | collective-permute-start | bytes 196616 | tf_op jit(solution)/shard_map/ppermute | solution.py:374
  20.5 0.9 shard_map.77
  22.8 0.7 collective-permute-done.5.got_ref
  23.5 15.5 %all_to_all.20.parts_ref = bf16[16,80,128]{2,1,0:T(8,128)(2,1)S(1)} all-to-all(bf16[16,80,128]{2,1,0:T(8,128)(2,1)S(1)} %shard_map.80), channel_id=1, replica_groups=mesh['dp'=2,'vocab'=16,'mp'=4] {'vocab'}, dimensions={0} | all-to-all | bytes 655360 | tf_op jit(solution)/shard_map/all_to_all | solution.py:422
  39.1 11.5 %all_to_all.21.own_ref = bf16[16,80,128]{2,1,0:T(8,128)(2,1)S(1)} all-to-all(bf16[16,80,128]{2,1,0:T(8,128)(2,1)S(1)} %shard_map.81), channel_id=1, replica_groups=mesh['dp'=2,'vocab'=16,'mp'=4] {'vocab'}, dimensions={0} | all-to-all | bytes 655360 | tf_op jit(solution)/shard_map/all_to_all | solution.py:424
  50.6 2.9 %collective-permute-start.6 = (bf16[16,80,128]{2,1,0:T(8,128)(2,1)S(1)}, bf16[16,80,128]{2,1,0:T(8,128)(2,1)S(1)}, u32[]{:S(2)}, u32[]{:S(2)}) collective-permute-start(bf16[16,80,128]{2,1,0:T(8,128)(2,1)S(1)} %all_to_all.21.own_ref), channel_id=1, source_target_pairs={{0,64},{64,0},{1,65},{65,1},{2,66},{66,2},{3,67},{67,3},{4,68},{68... | collective-permute-start | bytes 983048 | tf_op jit(solution)/shard_map/ppermute | solution.py:374
  53.6 3.4 %shard_map.82 = (bf16[64,192]{1,0:T(8,128)(2,1)S(1)}, f32[64,512]{1,0:T(8,128)S(1)}, f32[64,512]{1,0:T(8,128)S(1)}, f32[64,64]{1,0:T(8,128)S(1)}) custom-call(s32[1]{0:T(128)} %bitcast.me_ref.refs_0_, bf16[16,80,128]{2,1,0:T(8,128)(2,1)S(1)} %all_to_all.21.own_ref, bf16[512,4096]{1,0:T(8,128)(2,1)S(1)} %get-tuple-element.46.slab_ref.refs_3_.theirs_slab_ref, ...), custom_call_target="tpu_custom_call" | custom-call | flops 557842688 | bytes 8716292 | tf_op jit(solution)/shard_map/pallas_call | solution.py:362
  56.9 0.9 shard_map.83
  57.9 0.9 shard_map.84
  59.8 1.3 %collective-permute-start.9 = (bf16[96,512]{1,0:T(8,128)(2,1)S(1)}, bf16[96,512]{1,0:T(8,128)(2,1)S(1)}, u32[]{:S(2)}, u32[]{:S(2)}) collective-permute-start(bf16[96,512]{1,0:T(8,128)(2,1)S(1)} %shard_map.85.a_ref), channel_id=1, source_target_pairs={{0,3},{1,0},{2,1},{3,2},{4,7},{5,4},{6,5},{7,6},{8,11},{9,8},{10,9... | collective-permute-start | bytes 294920 | tf_op jit(solution)/shard_map/ppermute | solution.py:379
  61.2 3.7 %collective-permute-done.10.d_ref = bf16[96,512]{1,0:T(8,128)(2,1)S(1)} collective-permute-done((bf16[96,512]{1,0:T(8,128)(2,1)S(1)}, bf16[96,512]{1,0:T(8,128)(2,1)S(1)}, u32[]{:S(2)}, u32[]{:S(2)}) %collective-permute-start.10) | collective-permute-done | bytes 98336 | tf_op jit(solution)/shard_map/ppermute | solution.py:379
  65.0 2.1 %collective-permute-done.8.b_ref = bf16[96,512]{1,0:T(8,128)(2,1)S(1)} collective-permute-done((bf16[96,512]{1,0:T(8,128)(2,1)S(1)}, bf16[96,512]{1,0:T(8,128)(2,1)S(1)}, u32[]{:S(2)}, u32[]{:S(2)}) %collective-permute-start.8) | collective-permute-done | bytes 98336 | tf_op jit(solution)/shard_map/ppermute | solution.py:379
  67.2 1.2 %collective-permute-start.11 = (bf16[64,512]{1,0:T(8,128)(2,1)S(1)}, bf16[64,512]{1,0:T(8,128)(2,1)S(1)}, u32[]{:S(2)}, u32[]{:S(2)}) collective-permute-start(bf16[64,512]{1,0:T(8,128)(2,1)S(1)} %get-tuple-element.59.refs_0_), channel_id=1, source_target_pairs={{0,64},{64,0},{1,65},{65,1},{2,66},{66,2},{3,67},{67,3},{4,68},{68... | collective-permute-start | bytes 196616 | tf_op jit(solution)/shard_map/ppermute | solution.py:374
  68.4 2.6 %shard_map.87 = (f32[64,4096]{1,0:T(8,128)S(1)}, f32[64,64]{1,0:T(8,128)S(1)}, bf16[64,192]{1,0:T(8,128)(2,1)S(1)}, bf16[64,512]{1,0:T(8,128)(2,1)S(1)}) custom-call(bf16[64,512]{1,0:T(8,128)(2,1)S(1)} %get-tuple-element.59.refs_0_, f32[64,64]{1,0:T(8,128)S(1)} %get-tuple-element.60.refs_1_, ...), custom_call_target="tpu_custom_call" | custom-call | flops 273678336 | bytes 4276224 | tf_op jit(solution)/shard_map/pallas_call | solution.py:362
  72.3 1.0 collective-permute-done.12.got_ref
  73.4 11.4 %all_to_all.22.parts_ref = bf16[16,80,128]{2,1,0:T(8,128)(2,1)S(1)} all-to-all(bf16[16,80,128]{2,1,0:T(8,128)(2,1)S(1)} %shard_map.90), channel_id=1, replica_groups=mesh['dp'=2,'vocab'=16,'mp'=4] {'vocab'}, dimensions={0} | all-to-all | bytes 655360 | tf_op jit(solution)/shard_map/all_to_all | solution.py:422
  84.8 11.6 %all_to_all.23.own_ref = bf16[16,80,128]{2,1,0:T(8,128)(2,1)S(1)} all-to-all(bf16[16,80,128]{2,1,0:T(8,128)(2,1)S(1)} %shard_map.91), channel_id=1, replica_groups=mesh['dp'=2,'vocab'=16,'mp'=4] {'vocab'}, dimensions={0} | all-to-all | bytes 655360 | tf_op jit(solution)/shard_map/all_to_all | solution.py:424
  96.4 2.6 %collective-permute-start.13 = (bf16[16,80,128]{2,1,0:T(8,128)(2,1)S(1)}, bf16[16,80,128]{2,1,0:T(8,128)(2,1)S(1)}, u32[]{:S(2)}, u32[]{:S(2)}) collective-permute-start(bf16[16,80,128]{2,1,0:T(8,128)(2,1)S(1)} %all_to_all.23.own_ref), channel_id=1, source_target_pairs={{0,64},{64,0},{1,65},{65,1},{2,66},{66,2},{3,67},{67,3},{4,68},{68... | collective-permute-start | bytes 983048 | tf_op jit(solution)/shard_map/ppermute | solution.py:374
  99.0 2.6 %shard_map.92 = (bf16[64,192]{1,0:T(8,128)(2,1)S(1)}, f32[64,2048]{1,0:T(8,128)S(1)}, f32[64,64]{1,0:T(8,128)S(1)}, bf16[64,1024]{1,0:T(8,128)(2,1)S(1)}) custom-call(s32[1]{0:T(128)} %bitcast.me_ref.refs_0_, bf16[16,80,128]{2,1,0:T(8,128)(2,1)S(1)} %all_to_all.23.own_ref, bf16[64,512]{1,0:T(8,128)(2,1)S(1)} %get-tuple-element.68.rows_mine_ref, ...), custom_call_target="tpu_custom_call" | custom-call | flops 29360384 | bytes 458756 | tf_op jit(solution)/shard_map/pallas_call | solution.py:362
  101.7 2.7 %shard_map.93 = (f32[64,4096]{1,0:T(8,128)S(1)}, f32[64,64]{1,0:T(8,128)S(1)}, f32[64,4096]{1,0:T(8,128)}, f32[64,4096]{1,0:T(8,128)}, bf16[64,4096]{1,0:T(8,128)(2,1)S(1)}) custom-call(s32[1]{0:T(128)} %bitcast.me_ref.refs_0_, bf16[16,80,128]{2,1,0:T(8,128)(2,1)S(1)} %collective-permute-done.13.other_ref, bf16[64,192]{1,0:T(8,128)(2,1)S(1)} %get-tuple-element.70.factor_ref, ...), custom_call_target="tpu_custom_call" | custom-call | flops 191365376 | bytes 2990084 | tf_op jit(solution)/shard_map/pallas_call | solution.py:362
  104.8 1.3 %collective-permute-start.15 = (f32[64,64]{1,0:T(8,128)S(1)}, f32[64,64]{1,0:T(8,128)S(1)}, u32[]{:S(2)}, u32[]{:S(2)}) collective-permute-start(f32[64,64]{1,0:T(8,128)S(1)} %get-tuple-element.74.a_ref), channel_id=1, source_target_pairs={{0,3},{1,0},{2,1},{3,2},{4,7},{5,4},{6,5},{7,6},{8,11},{9,8},{10,9... | collective-permute-start | bytes 49160 | tf_op jit(solution)/shard_map/ppermute | solution.py:379
  106.3 4.9 %shard_map.94 = bf16[1024,4096]{1,0:T(8,128)(2,1)} custom-call(bf16[64,1024]{1,0:T(8,128)(2,1)S(1)} %get-tuple-element.69.left_ref, bf16[64,4096]{1,0:T(8,128)(2,1)S(1)} %get-tuple-element.73.direction_ref), custom_call_target="tpu_custom_call" | custom-call | flops 536870912 | bytes 8388608 | tf_op jit(solution)/shard_map/pallas_call | solution.py:496
  111.2 3.3 %shard_map.95 = f32[64,4096]{1,0:T(8,128)} custom-call(f32[64,64]{1,0:T(8,128)S(1)} %get-tuple-element.74.a_ref, f32[64,64]{1,0:T(8,128)S(1)} %collective-permute-done.14.b_ref, f32[64,64]{1,0:T(8,128)S(1)} %collective-permute-done.15.c_ref, f32[64,64]{1,0:T(8,128)S(1)} %collective-permute-done.16.d_ref, f32[64,4096]{1,0:T(8,128)S(1)} %get-tuple-element.75.columns_ref), custom_call_target="tpu_custom_call" | custom-call | flops 71303168 | bytes 1114112 | tf_op jit(solution)/shard_map/pallas_call | solution.py:362
  (33 shorter events, 4.9 us)
Async XLA Ops:
  5.0 5.5 %collective-permute-start = (bf16[64,512]{1,0:T(8,128)(2,1)S(1)}, bf16[64,512]{1,0:T(8,128)(2,1)S(1)}, u32[]{:S(2)}, u32[]{:S(2)}) collective-permute-start(bf16[64,512]{1,0:T(8,128)(2,1)S(1)} %get-tuple-element.43), channel_id=1, source_target_pairs={{0,64},{64,0},{1,65},{65,1},{2,66},{66,2},{3,67},{67,3},{4,68},{68... | collective-permute-start | bytes 196616 | tf_op jit(solution)/shard_map/ppermute | solution.py:374
  10.5 5.3 %collective-permute-start.3 = (bf16[64,512]{1,0:T(8,128)(2,1)S(1)}, bf16[64,512]{1,0:T(8,128)(2,1)S(1)}, u32[]{:S(2)}, u32[]{:S(2)}) collective-permute-start(bf16[64,512]{1,0:T(8,128)(2,1)S(1)} %add_convert_fusion.1), channel_id=1, source_target_pairs={{0,2},{1,3},{2,0},{3,1},{4,6},{5,7},{6,4},{7,5},{8,10},{9,11},{10,... | collective-permute-start | bytes 196616 | tf_op jit(solution)/shard_map/ppermute | solution.py:379
  13.4 3.9 %collective-permute-start.2 = (bf16[64,512]{1,0:T(8,128)(2,1)S(1)}, bf16[64,512]{1,0:T(8,128)(2,1)S(1)}, u32[]{:S(2)}, u32[]{:S(2)}) collective-permute-start(bf16[64,512]{1,0:T(8,128)(2,1)S(1)} %add_convert_fusion.1), channel_id=1, source_target_pairs={{0,3},{1,0},{2,1},{3,2},{4,7},{5,4},{6,5},{7,6},{8,11},{9,8},{10,9... | collective-permute-start | bytes 196616 | tf_op jit(solution)/shard_map/ppermute | solution.py:379
  14.3 4.3 %collective-permute-start.1 = (bf16[64,512]{1,0:T(8,128)(2,1)S(1)}, bf16[64,512]{1,0:T(8,128)(2,1)S(1)}, u32[]{:S(2)}, u32[]{:S(2)}) collective-permute-start(bf16[64,512]{1,0:T(8,128)(2,1)S(1)} %add_convert_fusion.1), channel_id=1, source_target_pairs={{0,1},{1,2},{2,3},{3,0},{4,5},{5,6},{6,7},{7,4},{8,9},{9,10},{10,1... | collective-permute-start | bytes 196616 | tf_op jit(solution)/shard_map/ppermute | solution.py:379
  18.6 2.7 %collective-permute-start.4 = (bf16[64,512]{1,0:T(8,128)(2,1)S(1)}, bf16[64,512]{1,0:T(8,128)(2,1)S(1)}, u32[]{:S(2)}, u32[]{:S(2)}) collective-permute-start(bf16[64,512]{1,0:T(8,128)(2,1)S(1)} %add_convert_fusion.refs_0_), channel_id=1, source_target_pairs={{0,64},{64,0},{1,65},{65,1},{2,66},{66,2},{3,67},{67,3},{4,68},{68... | collective-permute-start | bytes 196616 | tf_op jit(solution)/shard_map/ppermute | solution.py:374
  21.9 1.6 %collective-permute-start.5 = (bf16[16,64,128]{2,1,0:T(8,128)(2,1)S(1)}, bf16[16,64,128]{2,1,0:T(8,128)(2,1)S(1)}, u32[]{:S(2)}, u32[]{:S(2)}) collective-permute-start(bf16[16,64,128]{2,1,0:T(8,128)(2,1)S(1)} %shard_map.79), channel_id=1, source_target_pairs={{0,64},{64,0},{1,65},{65,1},{2,66},{66,2},{3,67},{67,3},{4,68},{68... | collective-permute-start | bytes 786440 | tf_op jit(solution)/shard_map/ppermute | solution.py:374
  50.6 6.3 %collective-permute-start.6 = (bf16[16,80,128]{2,1,0:T(8,128)(2,1)S(1)}, bf16[16,80,128]{2,1,0:T(8,128)(2,1)S(1)}, u32[]{:S(2)}, u32[]{:S(2)}) collective-permute-start(bf16[16,80,128]{2,1,0:T(8,128)(2,1)S(1)} %all_to_all.21.own_ref), channel_id=1, source_target_pairs={{0,64},{64,0},{1,65},{65,1},{2,66},{66,2},{3,67},{67,3},{4,68},{68... | collective-permute-start | bytes 983048 | tf_op jit(solution)/shard_map/ppermute | solution.py:374
  57.9 1.3 %collective-permute-start.7 = (bf16[64,512]{1,0:T(8,128)(2,1)S(1)}, bf16[64,512]{1,0:T(8,128)(2,1)S(1)}, u32[]{:S(2)}, u32[]{:S(2)}) collective-permute-start(bf16[64,512]{1,0:T(8,128)(2,1)S(1)} %get-tuple-element.57), channel_id=1, source_target_pairs={{0,64},{64,0},{1,65},{65,1},{2,66},{66,2},{3,67},{67,3},{4,68},{68... | collective-permute-start | bytes 196616 | tf_op jit(solution)/shard_map/ppermute | solution.py:374
  59.2 5.8 %collective-permute-start.10 = (bf16[96,512]{1,0:T(8,128)(2,1)S(1)}, bf16[96,512]{1,0:T(8,128)(2,1)S(1)}, u32[]{:S(2)}, u32[]{:S(2)}) collective-permute-start(bf16[96,512]{1,0:T(8,128)(2,1)S(1)} %shard_map.85.a_ref), channel_id=1, source_target_pairs={{0,2},{1,3},{2,0},{3,1},{4,6},{5,7},{6,4},{7,5},{8,10},{9,11},{10,... | collective-permute-start | bytes 294920 | tf_op jit(solution)/shard_map/ppermute | solution.py:379
  59.8 5.2 %collective-permute-start.9 = (bf16[96,512]{1,0:T(8,128)(2,1)S(1)}, bf16[96,512]{1,0:T(8,128)(2,1)S(1)}, u32[]{:S(2)}, u32[]{:S(2)}) collective-permute-start(bf16[96,512]{1,0:T(8,128)(2,1)S(1)} %shard_map.85.a_ref), channel_id=1, source_target_pairs={{0,3},{1,0},{2,1},{3,2},{4,7},{5,4},{6,5},{7,6},{8,11},{9,8},{10,9... | collective-permute-start | bytes 294920 | tf_op jit(solution)/shard_map/ppermute | solution.py:379
  61.1 6.0 %collective-permute-start.8 = (bf16[96,512]{1,0:T(8,128)(2,1)S(1)}, bf16[96,512]{1,0:T(8,128)(2,1)S(1)}, u32[]{:S(2)}, u32[]{:S(2)}) collective-permute-start(bf16[96,512]{1,0:T(8,128)(2,1)S(1)} %shard_map.85.a_ref), channel_id=1, source_target_pairs={{0,1},{1,2},{2,3},{3,0},{4,5},{5,6},{6,7},{7,4},{8,9},{9,10},{10,1... | collective-permute-start | bytes 294920 | tf_op jit(solution)/shard_map/ppermute | solution.py:379
  67.2 3.9 %collective-permute-start.11 = (bf16[64,512]{1,0:T(8,128)(2,1)S(1)}, bf16[64,512]{1,0:T(8,128)(2,1)S(1)}, u32[]{:S(2)}, u32[]{:S(2)}) collective-permute-start(bf16[64,512]{1,0:T(8,128)(2,1)S(1)} %get-tuple-element.59.refs_0_), channel_id=1, source_target_pairs={{0,64},{64,0},{1,65},{65,1},{2,66},{66,2},{3,67},{67,3},{4,68},{68... | collective-permute-start | bytes 196616 | tf_op jit(solution)/shard_map/ppermute | solution.py:374
  68.4 33.2 %copy-start = (f32[64,4096]{1,0:T(8,128)S(1)}, f32[64,4096]{1,0:T(8,128)}, u32[]{:S(2)}) copy-start(f32[64,4096]{1,0:T(8,128)} %first_ref.1) | copy-start | bytes 3145732
  68.4 33.2 %copy-start.1 = (f32[64,4096]{1,0:T(8,128)S(1)}, f32[64,4096]{1,0:T(8,128)}, u32[]{:S(2)}) copy-start(f32[64,4096]{1,0:T(8,128)} %second_ref.1) | copy-start | bytes 3145732
  71.7 1.6 %collective-permute-start.12 = (bf16[16,64,128]{2,1,0:T(8,128)(2,1)S(1)}, bf16[16,64,128]{2,1,0:T(8,128)(2,1)S(1)}, u32[]{:S(2)}, u32[]{:S(2)}) collective-permute-start(bf16[16,64,128]{2,1,0:T(8,128)(2,1)S(1)} %get-tuple-element.66), channel_id=1, source_target_pairs={{0,64},{64,0},{1,65},{65,1},{2,66},{66,2},{3,67},{67,3},{4,68},{68... | collective-permute-start | bytes 786440 | tf_op jit(solution)/shard_map/ppermute | solution.py:374
  96.4 5.2 %collective-permute-start.13 = (bf16[16,80,128]{2,1,0:T(8,128)(2,1)S(1)}, bf16[16,80,128]{2,1,0:T(8,128)(2,1)S(1)}, u32[]{:S(2)}, u32[]{:S(2)}) collective-permute-start(bf16[16,80,128]{2,1,0:T(8,128)(2,1)S(1)} %all_to_all.23.own_ref), channel_id=1, source_target_pairs={{0,64},{64,0},{1,65},{65,1},{2,66},{66,2},{3,67},{67,3},{4,68},{68... | collective-permute-start | bytes 983048 | tf_op jit(solution)/shard_map/ppermute | solution.py:374
  104.3 6.8 %collective-permute-start.16 = (f32[64,64]{1,0:T(8,128)S(1)}, f32[64,64]{1,0:T(8,128)S(1)}, u32[]{:S(2)}, u32[]{:S(2)}) collective-permute-start(f32[64,64]{1,0:T(8,128)S(1)} %get-tuple-element.74.a_ref), channel_id=1, source_target_pairs={{0,2},{1,3},{2,0},{3,1},{4,6},{5,7},{6,4},{7,5},{8,10},{9,11},{10,... | collective-permute-start | bytes 49160 | tf_op jit(solution)/shard_map/ppermute | solution.py:379
  104.8 6.3 %collective-permute-start.15 = (f32[64,64]{1,0:T(8,128)S(1)}, f32[64,64]{1,0:T(8,128)S(1)}, u32[]{:S(2)}, u32[]{:S(2)}) collective-permute-start(f32[64,64]{1,0:T(8,128)S(1)} %get-tuple-element.74.a_ref), channel_id=1, source_target_pairs={{0,3},{1,0},{2,1},{3,2},{4,7},{5,4},{6,5},{7,6},{8,11},{9,8},{10,9... | collective-permute-start | bytes 49160 | tf_op jit(solution)/shard_map/ppermute | solution.py:379
  106.1 5.0 %collective-permute-start.14 = (f32[64,64]{1,0:T(8,128)S(1)}, f32[64,64]{1,0:T(8,128)S(1)}, u32[]{:S(2)}, u32[]{:S(2)}) collective-permute-start(f32[64,64]{1,0:T(8,128)S(1)} %get-tuple-element.74.a_ref), channel_id=1, source_target_pairs={{0,1},{1,2},{2,3},{3,0},{4,5},{5,6},{6,7},{7,4},{8,9},{9,10},{10,1... | collective-permute-start | bytes 49160 | tf_op jit(solution)/shard_map/ppermute | solution.py:379

commit v4 on v3

--- a/solution.py
+++ b/solution.py
@@ -113,41 +113,46 @@
     return dot(three, three, 1, 1)
 
 
-def first_rows(half, left, slab_hbm, out_ref, slab_ref, sems):
-    rows = slab_ref.shape[0]
-    copies = [
-        pltpu.make_async_copy(
-            slab_hbm.at[span(half * rows + t, LANE), :], slab_ref.at[t : t + LANE, :], sems.at[t // LANE]
+def first_theirs_kernel(
+    me_ref, basis_hbm, slab_hbm, theirs_ref, left_ref, theirs_slab_ref, mine_slab_ref, basis_ref, sems
+):
+    me = me_ref[0]
+    half = theirs_slab_ref.shape[0]
+    basis_copy = pltpu.make_async_copy(basis_hbm, basis_ref, sems.at[0])
+    theirs_copies, mine_copies = (
+        [
+            pltpu.make_async_copy(
+                slab_hbm.at[span(core * half + t, WIDE), :],
+                ref.at[t : t + WIDE, :],
+                sems.at[first + t // WIDE],
+            )
+            for t in range(0, half, WIDE)
+        ]
+        for core, ref, first in (
+            (1 - me, theirs_slab_ref, 1),
+            (me, mine_slab_ref, 1 + half // WIDE),
         )
-        for t in range(0, rows, LANE)
-    ]
-    copies[0].start()
-    copies[1].start()
-    left = left()
-    for i, copy in enumerate(copies):
+    )
+    for copy in (basis_copy, *theirs_copies):
+        copy.start()
+    basis_copy.wait()
+    for copy in mine_copies:
+        copy.start()
+    left = basis_ref[...].astype(BF16)
+    left_ref[...] = left
+    for copy in theirs_copies:
         copy.wait()
-        if i + 2 < len(copies):
-            copies[i + 2].start()
-        at = slice(i * LANE, (i + 1) * LANE)
-        out_ref[:, at] = dot(left, slab_ref[at, :], 1, 1).astype(out_ref.dtype)
-
-
-def first_theirs_kernel(
-    me_ref, basis_hbm, slab_hbm, theirs_ref, slab_ref, left_ref, basis_ref, sems, basis_sem
-):
-    copy = pltpu.make_async_copy(basis_hbm, basis_ref, basis_sem.at[0])
-    copy.start()
-
-    def left():
+    for t in range(0, half, WIDE):
+        at = slice(t, t + WIDE)
+        theirs_ref[:, at] = dot(left, theirs_slab_ref[at, :], 1, 1).astype(BF16)
+    for copy in mine_copies:
         copy.wait()
-        left_ref[...] = basis_ref[...].astype(BF16)
-        return left_ref[...]
-
-    first_rows(1 - me_ref[0], left, slab_hbm, theirs_ref, slab_ref, sems)
-
-
-def first_mine_kernel(me_ref, left_ref, slab_hbm, mine_ref, slab_ref, sems):
-    first_rows(me_ref[0], lambda: left_ref[...], slab_hbm, mine_ref, slab_ref, sems)
+
+
+def first_mine_kernel(left_ref, slab_ref, mine_ref):
+    left = left_ref[...]
+    for t in range(0, mine_ref.shape[1], WIDE):
+        mine_ref[:, t : t + WIDE] = dot(left, slab_ref[t : t + WIDE, :], 1, 1)
 
 
 def columns_mine_kernel(orthogonal, *refs):
@@ -335,24 +340,48 @@
     gram_ref[...] = gram_own_ref[...] + folded(total, rank)
 
 
-def update_kernel(left_ref, direction_ref, update_ref):
-    left = left_ref[...]
-    for t in range(0, direction_ref.shape[1], TILE):
-        product = dot(left, direction_ref[:, t : t + TILE], 0, 0)
-        update_ref[:, t : t + TILE] = product.astype(BF16)
-
-
-def basis_kernel(a_ref, b_ref, c_ref, d_ref, columns_ref, basis_ref):
+def update_kernel(
+    left_ref, direction_ref, first_ref, second_ref, update_hbm, first_hbm, second_hbm, buffer_ref, sems
+):
+    copies = [
+        pltpu.make_async_copy(first_ref, first_hbm, sems.at[0]),
+        pltpu.make_async_copy(second_ref, second_hbm, sems.at[1]),
+    ]
+    for copy in copies:
+        copy.start()
+    left = left_ref[...].T
+    for i in range(left.shape[0] // TILE):
+        rows = slice(i * TILE, (i + 1) * TILE)
+        for t in range(0, direction_ref.shape[1], TILE):
+            product = dot(left[rows, :], direction_ref[:, t : t + TILE], 1, 0)
+            buffer_ref[rows, t : t + TILE] = product.astype(BF16)
+        copy = pltpu.make_async_copy(buffer_ref.at[rows, :], update_hbm.at[rows, :], sems.at[2 + i])
+        copy.start()
+        copies.append(copy)
+    for copy in copies:
+        copy.wait()
+
+
+def basis_kernel(a_ref, b_ref, c_ref, d_ref, columns_ref, basis_hbm, basis_ref, sems):
     factor = inverse_factor((a_ref[...] + b_ref[...]) + (c_ref[...] + d_ref[...]))
     high, mid, low = thirds(factor)
     wide = jnp.concatenate([low, mid, high, mid, high, high], axis=1).astype(BF16)
-    for t in range(0, columns_ref.shape[1], TILE):
-        high, mid, low = (x.astype(BF16) for x in thirds(columns_ref[:, t : t + TILE]))
-        tall = jnp.concatenate([high, mid, low, high, mid, high], axis=0)
-        basis_ref[:, t : t + TILE] = dot(wide, tall, 1, 0)
-
-
-def call(kernel, outs, operands, scratch=(), hbm=()):
+    copies = []
+    width = columns_ref.shape[1]
+    for part in range(2):
+        for t in range(part * width // 2, (part + 1) * width // 2, TILE):
+            high, mid, low = (x.astype(BF16) for x in thirds(columns_ref[:, t : t + TILE]))
+            tall = jnp.concatenate([high, mid, low, high, mid, high], axis=0)
+            basis_ref[:, t : t + TILE] = dot(wide, tall, 1, 0)
+        at = slice(part * width // 2, (part + 1) * width // 2)
+        copy = pltpu.make_async_copy(basis_ref.at[:, at], basis_hbm.at[:, at], sems.at[part])
+        copy.start()
+        copies.append(copy)
+    for copy in copies:
+        copy.wait()
+
+
+def call(kernel, outs, operands, scratch=(), hbm=(), hbm_out=False):
     def spec(i, x):
         if x.dtype == jnp.int32:
             return SMEM
@@ -363,7 +392,7 @@
         kernel,
         out_shape=[jax.ShapeDtypeStruct(s, t) for s, t in outs],
         in_specs=[spec(i, x) for i, x in enumerate(operands)],
-        out_specs=[VMEM] * len(outs),
+        out_specs=[pl.BlockSpec(memory_space=pl.ANY) if hbm_out else VMEM] * len(outs),
         scratch_shapes=[pltpu.VMEM(*s) if isinstance(s, tuple) else s for s in scratch],
         compiler_params=pltpu.CompilerParams(vmem_limit_bytes=VMEM_LIMIT),
         cost_estimate=pl.CostEstimate(flops=64 * moved, bytes_accessed=moved, transcendentals=0),
@@ -438,20 +467,17 @@
     square = ((rank, rank), F32)
     factor_out = ((rank, 3 * rank), BF16)
     half_slab = ((half, width), BF16)
-    sems = pltpu.SemaphoreType.DMA((half // LANE,))
 
     slab, basis = (pltpu.with_memory_space_constraint(x, pltpu.HBM) for x in (slab, old_basis))
-    theirs, theirs_slab, left = call(
+    theirs, left, theirs_slab, mine_slab = call(
         first_theirs_kernel,
-        [theirs_out, half_slab, ((rank, width), BF16)],
+        [theirs_out, ((rank, width), BF16), half_slab, half_slab],
         [me, basis, slab],
-        [((rank, width), F32), sems, pltpu.SemaphoreType.DMA((1,))],
+        [((rank, width), F32), pltpu.SemaphoreType.DMA((1 + vocab // WIDE,))],
         hbm=(1, 2),
     )
     got = swapped(theirs)
-    mine, mine_slab = call(
-        first_mine_kernel, [mine_out, half_slab], [me, left, slab], [sems], hbm=(2,)
-    )
+    mine = call(first_mine_kernel, [mine_out], [left, mine_slab])[0]
     slabs = (theirs_slab, mine_slab)
     mine = (mine + got.astype(F32)).astype(BF16)
     total = mine.astype(F32)
@@ -493,21 +519,20 @@
         [me, other, factor, columns, gram, first_moment, second_moment],
     )
     gram_others = others(gram)
-    update = pl.pallas_call(
+    update, new_first, new_second = call(
         update_kernel,
-        out_shape=jax.ShapeDtypeStruct((vocab, width), BF16),
-        grid=(vocab // WIDE,),
-        in_specs=[
-            pl.BlockSpec((rank, WIDE), lambda i: (0, i)),
-            pl.BlockSpec((rank, width), lambda i: (0, 0)),
-        ],
-        out_specs=pl.BlockSpec((WIDE, width), lambda i: (i, 0)),
-        compiler_params=pltpu.CompilerParams(vmem_limit_bytes=VMEM_LIMIT),
-        cost_estimate=pl.CostEstimate(
-            flops=2 * rank * vocab * width, bytes_accessed=2 * vocab * width, transcendentals=0
-        ),
-    )(left, direction)
-    basis = call(basis_kernel, [wide], [gram, *gram_others, columns])[0]
+        [((vocab, width), BF16), wide, wide],
+        [left, direction, new_first, new_second],
+        [((vocab, width), BF16), pltpu.SemaphoreType.DMA((2 + vocab // TILE,))],
+        hbm_out=True,
+    )
+    basis = call(
+        basis_kernel,
+        [wide],
+        [gram, *gram_others, columns],
+        [((rank, width), F32), pltpu.SemaphoreType.DMA((2,))],
+        hbm_out=True,
+    )[0]
     return (update, basis, new_first, new_second)
 
 

time: 115 us -> 111 us (0.965)
  Pallas kernels: 33 us -> 28.8 us
    pallas_call x1 -> x0, Pallas kernels: 4.86 us -> none  [local(): pl.pallas_call(update_kernel, out_shape=jax.ShapeDtypeStruct((vocab, widt...]
    pallas_call x20 -> x21, Pallas kernels: 28.1 us -> 28.8 us  [call(): pl.pallas_call(kernel, out_shape=[jax.ShapeDtypeStruct(s, t) for s, t in...]
  transfers between devices with their start and end apart: 17 -> 17, of which waited for: 8 -> 8; matrix products, arithmetic and copies ran while one was open for 0% -> 0% of each run, Pallas kernels for 18% -> 16%
where the time goes in v4:
time: 111 us
  blocking collectives  50 us (45%)
  Pallas kernels  28.8 us (26%)
  starting transfers between devices  19.2 us (17%)
  waiting for transfers between devices  11.5 us (10%)
    pallas_call x21, Pallas kernels, call(): pl.pallas_call(kernel, out_shape=[jax.ShapeDtypeStruct(s, t) for s, t in...  28.8 us
    all_to_all x2, blocking collectives, columns_of(): parts = lax.all_to_all(chunks, 'vocab', 0, 0)  26.9 us
    all_to_all x2, blocking collectives, columns_of(): own = lax.all_to_all(copies, 'vocab', 0, 0)  23.1 us
    ppermute x8, starting transfers between devices, swapped(): return lax.ppermute(x, 'dp', [(0, 1), (1, 0)])  10.7 us
    ppermute x9, waiting for transfers between devices, others(): lax.ppermute(x, 'mp', [(i, (i + k) % n) for i in range(n)])  9.54 us
    ppermute x9, starting transfers between devices, others(): lax.ppermute(x, 'mp', [(i, (i + k) % n) for i in range(n)])  8.45 us
  transfers between devices with their start and end apart: 17, of which 8 were waited for; matrix products, arithmetic and copies ran while one was open for 0% of the time, Pallas kernels for 16%

profile of v4, /device:TPU:1, one launch (start us, length us, event | category | flops | bytes accessed | tf_op | source)
XLA Modules:
  0.0 110.5 jit_solution(234142917268043633)
XLA Ops:
  0.6 4.0 %shard_map.75 = (bf16[64,512]{1,0:T(8,128)(2,1)S(1)}, bf16[64,4096]{1,0:T(8,128)(2,1)S(1)}, bf16[512,4096]{1,0:T(8,128)(2,1)S(1)}, bf16[512,4096]{1,0:T(8,128)(2,1)S(1)}) custom-call(s32[1]{0:T(128)} %bitcast.me_ref.refs_0_, f32[64,4096]{1,0:T(8,128)} %basis_hbm.1, bf16[1024,4096]{1,0:T(8,128)(2,1)} %bitcast.2), custom_call_target="tpu_custom_call" | custom-call | flops 603980032 | bytes 9437188 | tf_op jit(solution)/shard_map/pallas_call | solution.py:391
  4.7 1.5 %collective-permute-start = (bf16[64,512]{1,0:T(8,128)(2,1)S(1)}, bf16[64,512]{1,0:T(8,128)(2,1)S(1)}, u32[]{:S(2)}, u32[]{:S(2)}) collective-permute-start(bf16[64,512]{1,0:T(8,128)(2,1)S(1)} %get-tuple-element.45), channel_id=1, source_target_pairs={{0,64},{64,0},{1,65},{65,1},{2,66},{66,2},{3,67},{67,3},{4,68},{68... | collective-permute-start | bytes 196616 | tf_op jit(solution)/shard_map/ppermute | solution.py:403
  6.2 1.4 %shard_map.76 = f32[64,512]{1,0:T(8,128)S(1)} custom-call(bf16[64,4096]{1,0:T(8,128)(2,1)S(1)} %get-tuple-element.43.left_ref, bf16[512,4096]{1,0:T(8,128)(2,1)S(1)} %get-tuple-element.44.slab_ref.refs_1_.mine_slab_ref.refs_2_), custom_call_target="tpu_custom_call" | custom-call | flops 301989888 | bytes 4718592 | tf_op jit(solution)/shard_map/pallas_call | solution.py:391
  7.6 2.9 %collective-permute-start.3 = (bf16[64,512]{1,0:T(8,128)(2,1)S(1)}, bf16[64,512]{1,0:T(8,128)(2,1)S(1)}, u32[]{:S(2)}, u32[]{:S(2)}) collective-permute-start(bf16[64,512]{1,0:T(8,128)(2,1)S(1)} %add_convert_fusion.1), channel_id=1, source_target_pairs={{0,2},{1,3},{2,0},{3,1},{4,6},{5,7},{6,4},{7,5},{8,10},{9,11},{10,... | collective-permute-start | bytes 196616 | tf_op jit(solution)/shard_map/ppermute | solution.py:408
  10.5 0.9 collective-permute-start.2
  11.4 0.6 collective-permute-start.1
  12.0 0.9 collective-permute-done.3
  12.9 1.5 %collective-permute-done.2 = bf16[64,512]{1,0:T(8,128)(2,1)S(1)} collective-permute-done((bf16[64,512]{1,0:T(8,128)(2,1)S(1)}, bf16[64,512]{1,0:T(8,128)(2,1)S(1)}, u32[]{:S(2)}, u32[]{:S(2)}) %collective-permute-start.2) | collective-permute-done | bytes 65568 | tf_op jit(solution)/shard_map/ppermute | solution.py:408
  14.4 1.3 %collective-permute-done.1 = bf16[64,512]{1,0:T(8,128)(2,1)S(1)} collective-permute-done((bf16[64,512]{1,0:T(8,128)(2,1)S(1)}, bf16[64,512]{1,0:T(8,128)(2,1)S(1)}, u32[]{:S(2)}, u32[]{:S(2)}) %collective-permute-start.1) | collective-permute-done | bytes 65568 | tf_op jit(solution)/shard_map/ppermute | solution.py:408
  15.7 1.8 %collective-permute-start.4 = (bf16[64,512]{1,0:T(8,128)(2,1)S(1)}, bf16[64,512]{1,0:T(8,128)(2,1)S(1)}, u32[]{:S(2)}, u32[]{:S(2)}) collective-permute-start(bf16[64,512]{1,0:T(8,128)(2,1)S(1)} %add_convert_fusion.refs_0_), channel_id=1, source_target_pairs={{0,64},{64,0},{1,65},{65,1},{2,66},{66,2},{3,67},{67,3},{4,68},{68... | collective-permute-start | bytes 196616 | tf_op jit(solution)/shard_map/ppermute | solution.py:403
  17.5 0.9 shard_map.77
  19.9 0.7 collective-permute-done.5.got_ref
  20.6 15.5 %all_to_all.20.parts_ref = bf16[16,80,128]{2,1,0:T(8,128)(2,1)S(1)} all-to-all(bf16[16,80,128]{2,1,0:T(8,128)(2,1)S(1)} %shard_map.80), channel_id=1, replica_groups=mesh['dp'=2,'vocab'=16,'mp'=4] {'vocab'}, dimensions={0} | all-to-all | bytes 655360 | tf_op jit(solution)/shard_map/all_to_all | solution.py:451
  36.2 11.5 %all_to_all.21.own_ref = bf16[16,80,128]{2,1,0:T(8,128)(2,1)S(1)} all-to-all(bf16[16,80,128]{2,1,0:T(8,128)(2,1)S(1)} %shard_map.81), channel_id=1, replica_groups=mesh['dp'=2,'vocab'=16,'mp'=4] {'vocab'}, dimensions={0} | all-to-all | bytes 655360 | tf_op jit(solution)/shard_map/all_to_all | solution.py:453
  47.7 2.9 %collective-permute-start.6 = (bf16[16,80,128]{2,1,0:T(8,128)(2,1)S(1)}, bf16[16,80,128]{2,1,0:T(8,128)(2,1)S(1)}, u32[]{:S(2)}, u32[]{:S(2)}) collective-permute-start(bf16[16,80,128]{2,1,0:T(8,128)(2,1)S(1)} %all_to_all.21.own_ref), channel_id=1, source_target_pairs={{0,64},{64,0},{1,65},{65,1},{2,66},{66,2},{3,67},{67,3},{4,68},{68... | collective-permute-start | bytes 983048 | tf_op jit(solution)/shard_map/ppermute | solution.py:403
  50.7 3.4 %shard_map.82 = (bf16[64,192]{1,0:T(8,128)(2,1)S(1)}, f32[64,512]{1,0:T(8,128)S(1)}, f32[64,512]{1,0:T(8,128)S(1)}, f32[64,64]{1,0:T(8,128)S(1)}) custom-call(s32[1]{0:T(128)} %bitcast.me_ref.refs_0_, bf16[16,80,128]{2,1,0:T(8,128)(2,1)S(1)} %all_to_all.21.own_ref, bf16[512,4096]{1,0:T(8,128)(2,1)S(1)} %get-tuple-element.47.slab_ref.refs_3_.theirs_slab_ref, ...), custom_call_target="tpu_custom_call" | custom-call | flops 557842688 | bytes 8716292 | tf_op jit(solution)/shard_map/pallas_call | solution.py:391
  54.0 0.9 shard_map.83
  55.0 0.9 shard_map.84
  56.9 1.3 %collective-permute-start.9 = (bf16[96,512]{1,0:T(8,128)(2,1)S(1)}, bf16[96,512]{1,0:T(8,128)(2,1)S(1)}, u32[]{:S(2)}, u32[]{:S(2)}) collective-permute-start(bf16[96,512]{1,0:T(8,128)(2,1)S(1)} %shard_map.85.a_ref), channel_id=1, source_target_pairs={{0,3},{1,0},{2,1},{3,2},{4,7},{5,4},{6,5},{7,6},{8,11},{9,8},{10,9... | collective-permute-start | bytes 294920 | tf_op jit(solution)/shard_map/ppermute | solution.py:408
  58.3 3.7 %collective-permute-done.10.d_ref = bf16[96,512]{1,0:T(8,128)(2,1)S(1)} collective-permute-done((bf16[96,512]{1,0:T(8,128)(2,1)S(1)}, bf16[96,512]{1,0:T(8,128)(2,1)S(1)}, u32[]{:S(2)}, u32[]{:S(2)}) %collective-permute-start.10) | collective-permute-done | bytes 98336 | tf_op jit(solution)/shard_map/ppermute | solution.py:408
  62.1 2.1 %collective-permute-done.8.b_ref = bf16[96,512]{1,0:T(8,128)(2,1)S(1)} collective-permute-done((bf16[96,512]{1,0:T(8,128)(2,1)S(1)}, bf16[96,512]{1,0:T(8,128)(2,1)S(1)}, u32[]{:S(2)}, u32[]{:S(2)}) %collective-permute-start.8) | collective-permute-done | bytes 98336 | tf_op jit(solution)/shard_map/ppermute | solution.py:408
  64.3 1.2 %collective-permute-start.11 = (bf16[64,512]{1,0:T(8,128)(2,1)S(1)}, bf16[64,512]{1,0:T(8,128)(2,1)S(1)}, u32[]{:S(2)}, u32[]{:S(2)}) collective-permute-start(bf16[64,512]{1,0:T(8,128)(2,1)S(1)} %get-tuple-element.60.refs_0_), channel_id=1, source_target_pairs={{0,64},{64,0},{1,65},{65,1},{2,66},{66,2},{3,67},{67,3},{4,68},{68... | collective-permute-start | bytes 196616 | tf_op jit(solution)/shard_map/ppermute | solution.py:403
  65.5 2.7 %shard_map.87 = (f32[64,4096]{1,0:T(8,128)S(1)}, f32[64,64]{1,0:T(8,128)S(1)}, bf16[64,192]{1,0:T(8,128)(2,1)S(1)}, bf16[64,512]{1,0:T(8,128)(2,1)S(1)}) custom-call(bf16[64,512]{1,0:T(8,128)(2,1)S(1)} %get-tuple-element.60.refs_0_, f32[64,64]{1,0:T(8,128)S(1)} %get-tuple-element.61.refs_1_, ...), custom_call_target="tpu_custom_call" | custom-call | flops 273678336 | bytes 4276224 | tf_op jit(solution)/shard_map/pallas_call | solution.py:391
  69.4 1.0 collective-permute-done.12.got_ref
  70.5 11.4 %all_to_all.22.parts_ref = bf16[16,80,128]{2,1,0:T(8,128)(2,1)S(1)} all-to-all(bf16[16,80,128]{2,1,0:T(8,128)(2,1)S(1)} %shard_map.90), channel_id=1, replica_groups=mesh['dp'=2,'vocab'=16,'mp'=4] {'vocab'}, dimensions={0} | all-to-all | bytes 655360 | tf_op jit(solution)/shard_map/all_to_all | solution.py:451
  81.9 11.6 %all_to_all.23.own_ref = bf16[16,80,128]{2,1,0:T(8,128)(2,1)S(1)} all-to-all(bf16[16,80,128]{2,1,0:T(8,128)(2,1)S(1)} %shard_map.91), channel_id=1, replica_groups=mesh['dp'=2,'vocab'=16,'mp'=4] {'vocab'}, dimensions={0} | all-to-all | bytes 655360 | tf_op jit(solution)/shard_map/all_to_all | solution.py:453
  93.5 2.6 %collective-permute-start.13 = (bf16[16,80,128]{2,1,0:T(8,128)(2,1)S(1)}, bf16[16,80,128]{2,1,0:T(8,128)(2,1)S(1)}, u32[]{:S(2)}, u32[]{:S(2)}) collective-permute-start(bf16[16,80,128]{2,1,0:T(8,128)(2,1)S(1)} %all_to_all.23.own_ref), channel_id=1, source_target_pairs={{0,64},{64,0},{1,65},{65,1},{2,66},{66,2},{3,67},{67,3},{4,68},{68... | collective-permute-start | bytes 983048 | tf_op jit(solution)/shard_map/ppermute | solution.py:403
  96.1 2.6 %shard_map.92 = (bf16[64,192]{1,0:T(8,128)(2,1)S(1)}, f32[64,2048]{1,0:T(8,128)S(1)}, f32[64,64]{1,0:T(8,128)S(1)}, bf16[64,1024]{1,0:T(8,128)(2,1)S(1)}) custom-call(s32[1]{0:T(128)} %bitcast.me_ref.refs_0_, bf16[16,80,128]{2,1,0:T(8,128)(2,1)S(1)} %all_to_all.23.own_ref, bf16[64,512]{1,0:T(8,128)(2,1)S(1)} %get-tuple-element.69.rows_mine_ref, ...), custom_call_target="tpu_custom_call" | custom-call | flops 29360384 | bytes 458756 | tf_op jit(solution)/shard_map/pallas_call | solution.py:391
  98.8 1.7 %shard_map.93 = (f32[64,4096]{1,0:T(8,128)S(1)}, f32[64,64]{1,0:T(8,128)S(1)}, f32[64,4096]{1,0:T(8,128)S(1)}, f32[64,4096]{1,0:T(8,128)S(1)}, bf16[64,4096]{1,0:T(8,128)(2,1)S(1)}) custom-call(s32[1]{0:T(128)} %bitcast.me_ref.refs_0_, bf16[16,80,128]{2,1,0:T(8,128)(2,1)S(1)} %collective-permute-done.13.other_ref, ...), custom_call_target="tpu_custom_call" | custom-call | flops 191365376 | bytes 2990084 | tf_op jit(solution)/shard_map/pallas_call | solution.py:391
  101.1 1.3 %collective-permute-start.15 = (f32[64,64]{1,0:T(8,128)S(1)}, f32[64,64]{1,0:T(8,128)S(1)}, u32[]{:S(2)}, u32[]{:S(2)}) collective-permute-start(f32[64,64]{1,0:T(8,128)S(1)} %get-tuple-element.78.a_ref), channel_id=1, source_target_pairs={{0,3},{1,0},{2,1},{3,2},{4,7},{5,4},{6,5},{7,6},{8,11},{9,8},{10,9... | collective-permute-start | bytes 49160 | tf_op jit(solution)/shard_map/ppermute | solution.py:408
  102.5 4.7 %shard_map.94 = (bf16[1024,4096]{1,0:T(8,128)(2,1)}, f32[64,4096]{1,0:T(8,128)}, f32[64,4096]{1,0:T(8,128)}) custom-call(bf16[64,1024]{1,0:T(8,128)(2,1)S(1)} %get-tuple-element.70.left_ref, bf16[64,4096]{1,0:T(8,128)(2,1)S(1)} %get-tuple-element.74.direction_ref, f32[64,4096]{1,0:T(8,128)S(1)} %get-tuple-element.75.first_ref, ...), custom_call_target="tpu_custom_call" | custom-call | flops 176160768 | bytes 2752512 | tf_op jit(solution)/shard_map/pallas_call | solution.py:391
  107.3 3.1 %shard_map.95 = f32[64,4096]{1,0:T(8,128)} custom-call(f32[64,64]{1,0:T(8,128)S(1)} %get-tuple-element.78.a_ref, f32[64,64]{1,0:T(8,128)S(1)} %collective-permute-done.14.b_ref, f32[64,64]{1,0:T(8,128)S(1)} %collective-permute-done.15.c_ref, f32[64,64]{1,0:T(8,128)S(1)} %collective-permute-done.16.d_ref, f32[64,4096]{1,0:T(8,128)S(1)} %get-tuple-element.79.columns_ref), custom_call_target="tpu_custom_call" | custom-call | flops 71303168 | bytes 1114112 | tf_op jit(solution)/shard_map/pallas_call | solution.py:391
  (33 shorter events, 5.0 us)
Async XLA Ops:
  4.7 2.9 %collective-permute-start = (bf16[64,512]{1,0:T(8,128)(2,1)S(1)}, bf16[64,512]{1,0:T(8,128)(2,1)S(1)}, u32[]{:S(2)}, u32[]{:S(2)}) collective-permute-start(bf16[64,512]{1,0:T(8,128)(2,1)S(1)} %get-tuple-element.45), channel_id=1, source_target_pairs={{0,64},{64,0},{1,65},{65,1},{2,66},{66,2},{3,67},{67,3},{4,68},{68... | collective-permute-start | bytes 196616 | tf_op jit(solution)/shard_map/ppermute | solution.py:403
  7.6 5.3 %collective-permute-start.3 = (bf16[64,512]{1,0:T(8,128)(2,1)S(1)}, bf16[64,512]{1,0:T(8,128)(2,1)S(1)}, u32[]{:S(2)}, u32[]{:S(2)}) collective-permute-start(bf16[64,512]{1,0:T(8,128)(2,1)S(1)} %add_convert_fusion.1), channel_id=1, source_target_pairs={{0,2},{1,3},{2,0},{3,1},{4,6},{5,7},{6,4},{7,5},{8,10},{9,11},{10,... | collective-permute-start | bytes 196616 | tf_op jit(solution)/shard_map/ppermute | solution.py:408
  10.5 3.9 %collective-permute-start.2 = (bf16[64,512]{1,0:T(8,128)(2,1)S(1)}, bf16[64,512]{1,0:T(8,128)(2,1)S(1)}, u32[]{:S(2)}, u32[]{:S(2)}) collective-permute-start(bf16[64,512]{1,0:T(8,128)(2,1)S(1)} %add_convert_fusion.1), channel_id=1, source_target_pairs={{0,3},{1,0},{2,1},{3,2},{4,7},{5,4},{6,5},{7,6},{8,11},{9,8},{10,9... | collective-permute-start | bytes 196616 | tf_op jit(solution)/shard_map/ppermute | solution.py:408
  11.4 4.3 %collective-permute-start.1 = (bf16[64,512]{1,0:T(8,128)(2,1)S(1)}, bf16[64,512]{1,0:T(8,128)(2,1)S(1)}, u32[]{:S(2)}, u32[]{:S(2)}) collective-permute-start(bf16[64,512]{1,0:T(8,128)(2,1)S(1)} %add_convert_fusion.1), channel_id=1, source_target_pairs={{0,1},{1,2},{2,3},{3,0},{4,5},{5,6},{6,7},{7,4},{8,9},{9,10},{10,1... | collective-permute-start | bytes 196616 | tf_op jit(solution)/shard_map/ppermute | solution.py:408
  15.7 2.7 %collective-permute-start.4 = (bf16[64,512]{1,0:T(8,128)(2,1)S(1)}, bf16[64,512]{1,0:T(8,128)(2,1)S(1)}, u32[]{:S(2)}, u32[]{:S(2)}) collective-permute-start(bf16[64,512]{1,0:T(8,128)(2,1)S(1)} %add_convert_fusion.refs_0_), channel_id=1, source_target_pairs={{0,64},{64,0},{1,65},{65,1},{2,66},{66,2},{3,67},{67,3},{4,68},{68... | collective-permute-start | bytes 196616 | tf_op jit(solution)/shard_map/ppermute | solution.py:403
  19.0 1.6 %collective-permute-start.5 = (bf16[16,64,128]{2,1,0:T(8,128)(2,1)S(1)}, bf16[16,64,128]{2,1,0:T(8,128)(2,1)S(1)}, u32[]{:S(2)}, u32[]{:S(2)}) collective-permute-start(bf16[16,64,128]{2,1,0:T(8,128)(2,1)S(1)} %shard_map.79), channel_id=1, source_target_pairs={{0,64},{64,0},{1,65},{65,1},{2,66},{66,2},{3,67},{67,3},{4,68},{68... | collective-permute-start | bytes 786440 | tf_op jit(solution)/shard_map/ppermute | solution.py:403
  47.7 6.3 %collective-permute-start.6 = (bf16[16,80,128]{2,1,0:T(8,128)(2,1)S(1)}, bf16[16,80,128]{2,1,0:T(8,128)(2,1)S(1)}, u32[]{:S(2)}, u32[]{:S(2)}) collective-permute-start(bf16[16,80,128]{2,1,0:T(8,128)(2,1)S(1)} %all_to_all.21.own_ref), channel_id=1, source_target_pairs={{0,64},{64,0},{1,65},{65,1},{2,66},{66,2},{3,67},{67,3},{4,68},{68... | collective-permute-start | bytes 983048 | tf_op jit(solution)/shard_map/ppermute | solution.py:403
  54.9 1.3 %collective-permute-start.7 = (bf16[64,512]{1,0:T(8,128)(2,1)S(1)}, bf16[64,512]{1,0:T(8,128)(2,1)S(1)}, u32[]{:S(2)}, u32[]{:S(2)}) collective-permute-start(bf16[64,512]{1,0:T(8,128)(2,1)S(1)} %get-tuple-element.58), channel_id=1, source_target_pairs={{0,64},{64,0},{1,65},{65,1},{2,66},{66,2},{3,67},{67,3},{4,68},{68... | collective-permute-start | bytes 196616 | tf_op jit(solution)/shard_map/ppermute | solution.py:403
  56.3 5.8 %collective-permute-start.10 = (bf16[96,512]{1,0:T(8,128)(2,1)S(1)}, bf16[96,512]{1,0:T(8,128)(2,1)S(1)}, u32[]{:S(2)}, u32[]{:S(2)}) collective-permute-start(bf16[96,512]{1,0:T(8,128)(2,1)S(1)} %shard_map.85.a_ref), channel_id=1, source_target_pairs={{0,2},{1,3},{2,0},{3,1},{4,6},{5,7},{6,4},{7,5},{8,10},{9,11},{10,... | collective-permute-start | bytes 294920 | tf_op jit(solution)/shard_map/ppermute | solution.py:408
  56.9 5.2 %collective-permute-start.9 = (bf16[96,512]{1,0:T(8,128)(2,1)S(1)}, bf16[96,512]{1,0:T(8,128)(2,1)S(1)}, u32[]{:S(2)}, u32[]{:S(2)}) collective-permute-start(bf16[96,512]{1,0:T(8,128)(2,1)S(1)} %shard_map.85.a_ref), channel_id=1, source_target_pairs={{0,3},{1,0},{2,1},{3,2},{4,7},{5,4},{6,5},{7,6},{8,11},{9,8},{10,9... | collective-permute-start | bytes 294920 | tf_op jit(solution)/shard_map/ppermute | solution.py:408
  58.2 6.0 %collective-permute-start.8 = (bf16[96,512]{1,0:T(8,128)(2,1)S(1)}, bf16[96,512]{1,0:T(8,128)(2,1)S(1)}, u32[]{:S(2)}, u32[]{:S(2)}) collective-permute-start(bf16[96,512]{1,0:T(8,128)(2,1)S(1)} %shard_map.85.a_ref), channel_id=1, source_target_pairs={{0,1},{1,2},{2,3},{3,0},{4,5},{5,6},{6,7},{7,4},{8,9},{9,10},{10,1... | collective-permute-start | bytes 294920 | tf_op jit(solution)/shard_map/ppermute | solution.py:408
  64.3 3.9 %collective-permute-start.11 = (bf16[64,512]{1,0:T(8,128)(2,1)S(1)}, bf16[64,512]{1,0:T(8,128)(2,1)S(1)}, u32[]{:S(2)}, u32[]{:S(2)}) collective-permute-start(bf16[64,512]{1,0:T(8,128)(2,1)S(1)} %get-tuple-element.60.refs_0_), channel_id=1, source_target_pairs={{0,64},{64,0},{1,65},{65,1},{2,66},{66,2},{3,67},{67,3},{4,68},{68... | collective-permute-start | bytes 196616 | tf_op jit(solution)/shard_map/ppermute | solution.py:403
  65.5 33.2 %copy-start = (f32[64,4096]{1,0:T(8,128)S(1)}, f32[64,4096]{1,0:T(8,128)}, u32[]{:S(2)}) copy-start(f32[64,4096]{1,0:T(8,128)} %first_ref.1) | copy-start | bytes 3145732
  65.5 33.2 %copy-start.1 = (f32[64,4096]{1,0:T(8,128)S(1)}, f32[64,4096]{1,0:T(8,128)}, u32[]{:S(2)}) copy-start(f32[64,4096]{1,0:T(8,128)} %second_ref.1) | copy-start | bytes 3145732
  68.8 1.6 %collective-permute-start.12 = (bf16[16,64,128]{2,1,0:T(8,128)(2,1)S(1)}, bf16[16,64,128]{2,1,0:T(8,128)(2,1)S(1)}, u32[]{:S(2)}, u32[]{:S(2)}) collective-permute-start(bf16[16,64,128]{2,1,0:T(8,128)(2,1)S(1)} %get-tuple-element.67), channel_id=1, source_target_pairs={{0,64},{64,0},{1,65},{65,1},{2,66},{66,2},{3,67},{67,3},{4,68},{68... | collective-permute-start | bytes 786440 | tf_op jit(solution)/shard_map/ppermute | solution.py:403
  93.5 5.2 %collective-permute-start.13 = (bf16[16,80,128]{2,1,0:T(8,128)(2,1)S(1)}, bf16[16,80,128]{2,1,0:T(8,128)(2,1)S(1)}, u32[]{:S(2)}, u32[]{:S(2)}) collective-permute-start(bf16[16,80,128]{2,1,0:T(8,128)(2,1)S(1)} %all_to_all.23.own_ref), channel_id=1, source_target_pairs={{0,64},{64,0},{1,65},{65,1},{2,66},{66,2},{3,67},{67,3},{4,68},{68... | collective-permute-start | bytes 983048 | tf_op jit(solution)/shard_map/ppermute | solution.py:403
  100.5 6.8 %collective-permute-start.16 = (f32[64,64]{1,0:T(8,128)S(1)}, f32[64,64]{1,0:T(8,128)S(1)}, u32[]{:S(2)}, u32[]{:S(2)}) collective-permute-start(f32[64,64]{1,0:T(8,128)S(1)} %get-tuple-element.78.a_ref), channel_id=1, source_target_pairs={{0,2},{1,3},{2,0},{3,1},{4,6},{5,7},{6,4},{7,5},{8,10},{9,11},{10,... | collective-permute-start | bytes 49160 | tf_op jit(solution)/shard_map/ppermute | solution.py:408
  101.1 6.2 %collective-permute-start.15 = (f32[64,64]{1,0:T(8,128)S(1)}, f32[64,64]{1,0:T(8,128)S(1)}, u32[]{:S(2)}, u32[]{:S(2)}) collective-permute-start(f32[64,64]{1,0:T(8,128)S(1)} %get-tuple-element.78.a_ref), channel_id=1, source_target_pairs={{0,3},{1,0},{2,1},{3,2},{4,7},{5,4},{6,5},{7,6},{8,11},{9,8},{10,9... | collective-permute-start | bytes 49160 | tf_op jit(solution)/shard_map/ppermute | solution.py:408
  102.4 4.9 %collective-permute-start.14 = (f32[64,64]{1,0:T(8,128)S(1)}, f32[64,64]{1,0:T(8,128)S(1)}, u32[]{:S(2)}, u32[]{:S(2)}) collective-permute-start(f32[64,64]{1,0:T(8,128)S(1)} %get-tuple-element.78.a_ref), channel_id=1, source_target_pairs={{0,1},{1,2},{2,3},{3,0},{4,5},{5,6},{6,7},{7,4},{8,9},{9,10},{10,1... | collective-permute-start | bytes 49160 | tf_op jit(solution)/shard_map/ppermute | solution.py:408

commit v5 on v4

--- a/solution.py
+++ b/solution.py
@@ -75,6 +75,15 @@
     return dot(factor3, jnp.concatenate([block] * 3, axis=0), 1, 0)
 
 
+def applied_wide(factor3, three):
+    rank = factor3.shape[0]
+    high, mid, low = (factor3[:, i * rank : (i + 1) * rank] for i in range(3))
+    first, second, third = (three[i * rank : (i + 1) * rank] for i in range(3))
+    wide = jnp.concatenate([low, mid, high, mid, high, high], axis=1)
+    tall = jnp.concatenate([first, second, third, first, second, first], axis=0)
+    return dot(wide, tall, 1, 0)
+
+
 def folded(total, rank):
     wide = total[:rank] + total[rank : 2 * rank] + total[2 * rank :]
     return wide[:, :rank] + wide[:, rank : 2 * rank] + wide[:, 2 * rank :]
@@ -106,11 +115,6 @@
     for j in range(chunks_ref.shape[0] // per):
         block = jnp.concatenate([chunks_ref[j * per + q, :rank, :] for q in range(per)], axis=1)
         yield slice(j * TILE, (j + 1) * TILE), block
-
-
-def gram_of(columns_ref, at):
-    three = stacked(columns_ref[:, at])
-    return dot(three, three, 1, 1)
 
 
 def first_theirs_kernel(
@@ -223,57 +227,59 @@
         out_ref[c] = piece
 
 
-def add_rows(columns, core, acc_ref, slab_ref, out_ref):
-    at = span(core * columns.shape[1], columns.shape[1])
+def rows_of(half, core, slab_ref, t):
+    return dot(half, slab_ref[t : t + WIDE, span(core * half.shape[1], half.shape[1])], 1, 1)
+
+
+def whole_half(chunks_ref, rank):
+    return jnp.concatenate([chunks_ref[c, :rank, :] for c in range(chunks_ref.shape[0])], axis=1)
+
+
+def rows_own_kernel(
+    me_ref, own_ref, theirs_slab_ref, mine_slab_ref, factor_ref, theirs_ref, mine_ref, gram_ref
+):
+    me = me_ref[0]
+    rank = gram_ref.shape[0]
+    half = whole_half(own_ref, rank)
+    factor3 = stacked(inverse_factor(gathered_gram(own_ref, rank)), 1)
+    for slab_ref, out_ref in ((theirs_slab_ref, theirs_ref), (mine_slab_ref, mine_ref)):
+        for t in range(0, out_ref.shape[1], WIDE):
+            out_ref[:, t : t + WIDE] = rows_of(half, me, slab_ref, t)
+    factor_ref[...] = factor3
+    gram_ref[...] = columns_gram(factor3, own_ref)
+
+
+def columns_gram(factor3, chunks_ref):
+    rank = factor3.shape[0]
+    total = jnp.zeros((3 * rank, 3 * rank), F32)
+    for _, block in blocks_of(chunks_ref, rank):
+        three = stacked(applied(factor3, block))
+        total = total + dot(three, three, 1, 1)
+    return folded(total, rank)
+
+
+def add_rows(me_ref, other_ref, factor3, acc_ref, slab_ref, out_ref):
+    half = whole_half(other_ref, factor3.shape[0])
     for t in range(0, out_ref.shape[1], WIDE):
-        product = dot(columns, slab_ref[t : t + WIDE, at], 1, 1)
-        if acc_ref is not None:
-            product = acc_ref[:, t : t + WIDE] + product
-        out_ref[:, t : t + WIDE] = product.astype(out_ref.dtype)
-
-
-def rows_own_kernel(
-    me_ref, own_ref, theirs_slab_ref, mine_slab_ref,
-    factor_ref, theirs_ref, mine_ref, gram_ref, columns_ref, half_ref,
-):
-    rank = gram_ref.shape[0]
-    factor3 = stacked(inverse_factor(gathered_gram(own_ref, rank)), 1)
-    factor_ref[...] = factor3
-    total = jnp.zeros((3 * rank, 3 * rank), F32)
-    for at, block in blocks_of(own_ref, rank):
-        columns = applied(factor3, block)
-        columns_ref[:, at] = columns
-        half_ref[:, at] = columns.astype(BF16)
-        total = total + gram_of(columns_ref, at)
-    gram_ref[...] = folded(total, rank)
-    half = half_ref[...]
-    add_rows(half, me_ref[0], None, theirs_slab_ref, theirs_ref)
-    add_rows(half, me_ref[0], None, mine_slab_ref, mine_ref)
-
-
-def rows_theirs_kernel(
-    me_ref, other_ref, factor_ref, acc_ref, slab_ref, theirs_ref, columns_ref, half_ref
+        at = slice(t, t + WIDE)
+        product = acc_ref[:, at] + rows_of(half, 1 - me_ref[0], slab_ref, t)
+        out_ref[:, at] = applied_wide(factor3, stacked(product)).astype(out_ref.dtype)
+
+
+def rows_theirs_kernel(me_ref, other_ref, factor_ref, acc_ref, slab_ref, theirs_ref):
+    add_rows(me_ref, other_ref, factor_ref[...], acc_ref, slab_ref, theirs_ref)
+
+
+def rows_mine_kernel(
+    me_ref, other_ref, factor_ref, acc_ref, slab_ref, gram_own_ref, mine_ref, pack_ref
 ):
     factor3 = factor_ref[...]
-    for at, block in blocks_of(other_ref, factor3.shape[0]):
-        columns = applied(factor3, block)
-        columns_ref[:, at] = columns
-        half_ref[:, at] = columns.astype(BF16)
-    add_rows(half_ref[...], 1 - me_ref[0], acc_ref, slab_ref, theirs_ref)
-
-
-def rows_mine_kernel(
-    me_ref, half_ref, columns_ref, gram_own_ref, acc_ref, slab_ref, mine_ref, pack_ref
-):
-    rank, width = columns_ref.shape
-    total = jnp.zeros((3 * rank, 3 * rank), F32)
-    for t in range(0, width, TILE):
-        total = total + gram_of(columns_ref, slice(t, t + TILE))
-    gram = gram_own_ref[...] + folded(total, rank)
+    rank = factor3.shape[0]
+    add_rows(me_ref, other_ref, factor3, acc_ref, slab_ref, mine_ref)
+    gram = gram_own_ref[...] + columns_gram(factor3, other_ref)
     gram = jnp.concatenate([gram[: rank // 2], gram[rank // 2 :]], axis=1)
     pack_ref[...] = jnp.zeros_like(pack_ref)
     pack_ref[:, : 3 * LANE] = stacked(gram, 1)
-    add_rows(half_ref[...], 1 - me_ref[0], acc_ref, slab_ref, mine_ref)
 
 
 def join_rows_kernel(mine_ref, got_ref, pack_ref, out_ref):
@@ -304,76 +310,65 @@
     for core, ref in ((me, rows_mine_ref), (1 - me, rows_other_ref)):
         left = applied(factor3, ref[...]).astype(BF16)
         left_ref[:, span(core * half, half)] = (left.astype(F32) * scale).astype(BF16)
+    gram_ref[...] = keep_columns(factor3, own_ref, columns_ref)
+
+
+def keep_columns(factor3, chunks_ref, columns_ref):
+    rank = factor3.shape[0]
     total = jnp.zeros((3 * rank, 3 * rank), F32)
-    for at, block in blocks_of(own_ref, rank):
-        columns_ref[:, at] = applied(factor3, block)
-        total = total + gram_of(columns_ref, at)
-    gram_ref[...] = folded(total, rank)
-
-
-def moments_kernel(
-    me_ref, other_ref, factor_ref, own_columns_ref, gram_own_ref, first_ref, second_ref,
-    columns_ref, gram_ref, new_first_ref, new_second_ref, direction_ref,
+    for at, block in blocks_of(chunks_ref, rank):
+        columns = applied(factor3, block)
+        columns_ref[:, at] = columns
+        three = stacked(columns)
+        total = total + dot(three, three, 1, 1)
+    return folded(total, rank)
+
+
+def final_other_kernel(other_ref, factor_ref, gram_own_ref, columns_ref, gram_ref):
+    gram_ref[...] = gram_own_ref[...] + keep_columns(factor_ref[...], other_ref, columns_ref)
+
+
+def update_kernel(
+    me_ref, own_ref, other_ref, left_ref, first_ref, second_ref,
+    update_hbm, first_hbm, second_hbm, three_ref,
+    update_ref, new_first_ref, new_second_ref, sems,
 ):
     me = me_ref[0]
-    factor3 = factor_ref[...]
-    rank, width = own_columns_ref.shape
     corr_one = 1.0 - 0.9**10
     corr_two = 1.0 - 0.999**10
-
-    def moments(at, columns):
-        columns_ref[:, at] = columns
-        new_first = 0.9 * first_ref[:, at] + 0.1 * columns
-        new_second = 0.999 * second_ref[:, at] + 0.001 * columns * columns
-        new_first_ref[:, at] = new_first
-        new_second_ref[:, at] = new_second
-        direction = new_first / corr_one / (jnp.sqrt(new_second / corr_two) + 1e-08)
-        direction_ref[:, at] = direction.astype(BF16)
-
-    total = jnp.zeros((3 * rank, 3 * rank), F32)
-    for part, block in blocks_of(other_ref, rank):
-        at = span((1 - me) * width + part.start, TILE)
-        moments(at, applied(factor3, block))
-        total = total + gram_of(columns_ref, at)
-        at = span(me * width + part.start, TILE)
-        moments(at, own_columns_ref[:, part])
-    gram_ref[...] = gram_own_ref[...] + folded(total, rank)
-
-
-def update_kernel(
-    left_ref, direction_ref, first_ref, second_ref, update_hbm, first_hbm, second_hbm, buffer_ref, sems
-):
-    copies = [
-        pltpu.make_async_copy(first_ref, first_hbm, sems.at[0]),
-        pltpu.make_async_copy(second_ref, second_hbm, sems.at[1]),
-    ]
-    for copy in copies:
-        copy.start()
+    width = own_ref.shape[1]
     left = left_ref[...].T
-    for i in range(left.shape[0] // TILE):
-        rows = slice(i * TILE, (i + 1) * TILE)
-        for t in range(0, direction_ref.shape[1], TILE):
-            product = dot(left[rows, :], direction_ref[:, t : t + TILE], 1, 0)
-            buffer_ref[rows, t : t + TILE] = product.astype(BF16)
-        copy = pltpu.make_async_copy(buffer_ref.at[rows, :], update_hbm.at[rows, :], sems.at[2 + i])
-        copy.start()
-        copies.append(copy)
+    copies = []
+    for i, (core, columns_ref) in enumerate(((me, own_ref), (1 - me, other_ref))):
+        for t in range(0, width, TILE):
+            at = span(core * width + t, TILE)
+            columns = columns_ref[:, t : t + TILE]
+            three_ref[:, at] = stacked(columns)
+            new_first = 0.9 * first_ref[:, at] + 0.1 * columns
+            new_second = 0.999 * second_ref[:, at] + 0.001 * columns * columns
+            new_first_ref[:, at] = new_first
+            new_second_ref[:, at] = new_second
+            direction = new_first / corr_one / (jnp.sqrt(new_second / corr_two) + 1e-08)
+            update_ref[:, at] = dot(left, direction.astype(BF16), 1, 0).astype(BF16)
+        at = span(core * width, width)
+        for j, (ref, hbm) in enumerate(
+            ((update_ref, update_hbm), (new_first_ref, first_hbm), (new_second_ref, second_hbm))
+        ):
+            copy = pltpu.make_async_copy(ref.at[:, at], hbm.at[:, at], sems.at[3 * i + j])
+            copy.start()
+            copies.append(copy)
     for copy in copies:
         copy.wait()
 
 
-def basis_kernel(a_ref, b_ref, c_ref, d_ref, columns_ref, basis_hbm, basis_ref, sems):
-    factor = inverse_factor((a_ref[...] + b_ref[...]) + (c_ref[...] + d_ref[...]))
-    high, mid, low = thirds(factor)
-    wide = jnp.concatenate([low, mid, high, mid, high, high], axis=1).astype(BF16)
+def basis_kernel(a_ref, b_ref, c_ref, d_ref, three_ref, basis_hbm, basis_ref, sems):
+    factor3 = stacked(inverse_factor((a_ref[...] + b_ref[...]) + (c_ref[...] + d_ref[...])), 1)
     copies = []
-    width = columns_ref.shape[1]
+    half = three_ref.shape[1] // 2
     for part in range(2):
-        for t in range(part * width // 2, (part + 1) * width // 2, TILE):
-            high, mid, low = (x.astype(BF16) for x in thirds(columns_ref[:, t : t + TILE]))
-            tall = jnp.concatenate([high, mid, low, high, mid, high], axis=0)
-            basis_ref[:, t : t + TILE] = dot(wide, tall, 1, 0)
-        at = slice(part * width // 2, (part + 1) * width // 2)
+        for t in range(part * half, (part + 1) * half, TILE):
+            basis_ref[:, t : t + TILE] = applied_wide(factor3, three_ref[:, t : t + TILE])
+        at = slice(part * half, (part + 1) * half)
         copy = pltpu.make_async_copy(basis_ref.at[:, at], basis_hbm.at[:, at], sems.at[part])
         copy.start()
         copies.append(copy)
@@ -381,7 +376,7 @@
         copy.wait()
 
 
-def call(kernel, outs, operands, scratch=(), hbm=(), hbm_out=False):
+def call(kernel, outs, operands, scratch=(), hbm=(), hbm_out=()):
     def spec(i, x):
         if x.dtype == jnp.int32:
             return SMEM
@@ -392,7 +387,9 @@
         kernel,
         out_shape=[jax.ShapeDtypeStruct(s, t) for s, t in outs],
         in_specs=[spec(i, x) for i, x in enumerate(operands)],
-        out_specs=[pl.BlockSpec(memory_space=pl.ANY) if hbm_out else VMEM] * len(outs),
+        out_specs=[
+            pl.BlockSpec(memory_space=pl.ANY) if i in hbm_out else VMEM for i in range(len(outs))
+        ],
         scratch_shapes=[pltpu.VMEM(*s) if isinstance(s, tuple) else s for s in scratch],
         compiler_params=pltpu.CompilerParams(vmem_limit_bytes=VMEM_LIMIT),
         cost_estimate=pl.CostEstimate(flops=64 * moved, bytes_accessed=moved, transcendentals=0),
@@ -489,18 +486,13 @@
         rows_own_kernel,
         [factor_out, mine_out, mine_out, square],
         [me, own, theirs_slab, mine_slab],
-        [narrow, ((rank, width // 2), BF16)],
-    )
-    theirs, columns, columns_half = call(
-        rows_theirs_kernel,
-        [theirs_out, narrow, ((rank, width // 2), BF16)],
-        [me, other, factor, theirs_acc, theirs_slab],
-    )
+    )
+    theirs = call(rows_theirs_kernel, [theirs_out], [me, other, factor, theirs_acc, theirs_slab])[0]
     got = swapped(theirs)
     mine, pack = call(
         rows_mine_kernel,
         [mine_out, ((rank // 2, half), BF16)],
-        [me, columns_half, columns, gram, mine_acc, mine_slab],
+        [me, other, factor, mine_acc, mine_slab, gram],
     )
     mine = call(join_rows_kernel, [((rank + rank // 2, half), BF16)], [mine, got, pack])[0]
     mine, gram = call(sum_packed_kernel, [theirs_out, square], [mine, *others(mine)])
@@ -508,30 +500,27 @@
 
     scale = math.sqrt(vocab * owners)
     assert scale == 2.0 ** round(math.log2(scale))
-    factor, columns, gram, left = call(
+    factor, columns_own, gram, left = call(
         functools.partial(final_own_kernel, scale),
         [factor_out, narrow, square, ((rank, vocab), BF16)],
         [me, own, rows_mine, rows_other],
     )
-    columns, gram, new_first, new_second, direction = call(
-        moments_kernel,
-        [wide, square, wide, wide, ((rank, width), BF16)],
-        [me, other, factor, columns, gram, first_moment, second_moment],
-    )
+    columns_other, gram = call(final_other_kernel, [narrow, square], [other, factor, gram])
     gram_others = others(gram)
-    update, new_first, new_second = call(
+    update_out = ((vocab, width), BF16)
+    update, new_first, new_second, three = call(
         update_kernel,
-        [((vocab, width), BF16), wide, wide],
-        [left, direction, new_first, new_second],
-        [((vocab, width), BF16), pltpu.SemaphoreType.DMA((2 + vocab // TILE,))],
-        hbm_out=True,
+        [update_out, wide, wide, ((3 * rank, width), BF16)],
+        [me, columns_own, columns_other, left, first_moment, second_moment],
+        [update_out, wide, wide, pltpu.SemaphoreType.DMA((6,))],
+        hbm_out=(0, 1, 2),
     )
     basis = call(
         basis_kernel,
         [wide],
-        [gram, *gram_others, columns],
-        [((rank, width), F32), pltpu.SemaphoreType.DMA((2,))],
-        hbm_out=True,
+        [gram, *gram_others, three],
+        [wide, pltpu.SemaphoreType.DMA((2,))],
+        hbm_out=(0,),
     )[0]
     return (update, basis, new_first, new_second)
 

time: 111 us -> 112 us (level)
  starting transfers between devices: 19.2 us -> 22.9 us
  waiting for transfers between devices: 11.5 us -> 8.27 us
    ppermute x9, starting transfers between devices: 8.45 us -> 12.1 us  [others(): lax.ppermute(x, 'mp', [(i, (i + k) % n) for i in range(n)])]
    ppermute x9, waiting for transfers between devices: 9.54 us -> 6.61 us  [others(): lax.ppermute(x, 'mp', [(i, (i + k) % n) for i in range(n)])]
  transfers between devices with their start and end apart: 17 -> 17, of which waited for: 8 -> 6; matrix products, arithmetic and copies ran while one was open for 0% -> 0% of each run, Pallas kernels for 16% -> 17%
where the time goes in v5:
time: 112 us
  blocking collectives  50.1 us (45%)
  Pallas kernels  29.8 us (27%)
  starting transfers between devices  22.9 us (20%)
  waiting for transfers between devices  8.27 us (7%)
    pallas_call x21, Pallas kernels, call(): pl.pallas_call(kernel, out_shape=[jax.ShapeDtypeStruct(s, t) for s, t in...  29.8 us
    all_to_all x2, blocking collectives, columns_of(): parts = lax.all_to_all(chunks, 'vocab', 0, 0)  27 us
    all_to_all x2, blocking collectives, columns_of(): own = lax.all_to_all(copies, 'vocab', 0, 0)  23.1 us
    ppermute x9, starting transfers between devices, others(): lax.ppermute(x, 'mp', [(i, (i + k) % n) for i in range(n)])  12.1 us
    ppermute x8, starting transfers between devices, swapped(): return lax.ppermute(x, 'dp', [(0, 1), (1, 0)])  10.7 us
    ppermute x9, waiting for transfers between devices, others(): lax.ppermute(x, 'mp', [(i, (i + k) % n) for i in range(n)])  6.61 us
  transfers between devices with their start and end apart: 17, of which 6 were waited for; matrix products, arithmetic and copies ran while one was open for 0% of the time, Pallas kernels for 17%

profile of v5, /device:TPU:1, one launch (start us, length us, event | category | flops | bytes accessed | tf_op | source)
XLA Modules:
  0.0 112.1 jit_solution(10935901198167829898)
XLA Ops:
  0.6 4.0 %shard_map.75 = (bf16[64,512]{1,0:T(8,128)(2,1)S(1)}, bf16[64,4096]{1,0:T(8,128)(2,1)S(1)}, bf16[512,4096]{1,0:T(8,128)(2,1)S(1)}, bf16[512,4096]{1,0:T(8,128)(2,1)S(1)}) custom-call(s32[1]{0:T(128)} %bitcast.me_ref.refs_0_, f32[64,4096]{1,0:T(8,128)} %basis_hbm.1, bf16[1024,4096]{1,0:T(8,128)(2,1)} %bitcast.2), custom_call_target="tpu_custom_call" | custom-call | flops 603980032 | bytes 9437188 | tf_op jit(solution)/shard_map/pallas_call | solution.py:386
  4.7 1.5 %collective-permute-start = (bf16[64,512]{1,0:T(8,128)(2,1)S(1)}, bf16[64,512]{1,0:T(8,128)(2,1)S(1)}, u32[]{:S(2)}, u32[]{:S(2)}) collective-permute-start(bf16[64,512]{1,0:T(8,128)(2,1)S(1)} %get-tuple-element.40), channel_id=1, source_target_pairs={{0,64},{64,0},{1,65},{65,1},{2,66},{66,2},{3,67},{67,3},{4,68},{68... | collective-permute-start | bytes 196616 | tf_op jit(solution)/shard_map/ppermute | solution.py:400
  6.2 1.4 %shard_map.76 = f32[64,512]{1,0:T(8,128)S(1)} custom-call(bf16[64,4096]{1,0:T(8,128)(2,1)S(1)} %get-tuple-element.38.left_ref, bf16[512,4096]{1,0:T(8,128)(2,1)S(1)} %get-tuple-element.39.slab_ref.refs_1_.mine_slab_ref.refs_2_), custom_call_target="tpu_custom_call" | custom-call | flops 301989888 | bytes 4718592 | tf_op jit(solution)/shard_map/pallas_call | solution.py:386
  7.6 1.4 %collective-permute-start.1 = (bf16[64,512]{1,0:T(8,128)(2,1)S(1)}, bf16[64,512]{1,0:T(8,128)(2,1)S(1)}, u32[]{:S(2)}, u32[]{:S(2)}) collective-permute-start(bf16[64,512]{1,0:T(8,128)(2,1)S(1)} %add_convert_fusion.1), channel_id=1, source_target_pairs={{0,1},{1,2},{2,3},{3,0},{4,5},{5,6},{6,7},{7,4},{8,9},{9,10},{10,1... | collective-permute-start | bytes 196616 | tf_op jit(solution)/shard_map/ppermute | solution.py:405
  9.0 1.4 %collective-permute-start.2 = (bf16[64,512]{1,0:T(8,128)(2,1)S(1)}, bf16[64,512]{1,0:T(8,128)(2,1)S(1)}, u32[]{:S(2)}, u32[]{:S(2)}) collective-permute-start(bf16[64,512]{1,0:T(8,128)(2,1)S(1)} %add_convert_fusion.1), channel_id=1, source_target_pairs={{0,3},{1,0},{2,1},{3,2},{4,7},{5,4},{6,5},{7,6},{8,11},{9,8},{10,9... | collective-permute-start | bytes 196616 | tf_op jit(solution)/shard_map/ppermute | solution.py:405
  10.4 1.6 %collective-permute-start.3 = (bf16[64,512]{1,0:T(8,128)(2,1)S(1)}, bf16[64,512]{1,0:T(8,128)(2,1)S(1)}, u32[]{:S(2)}, u32[]{:S(2)}) collective-permute-start(bf16[64,512]{1,0:T(8,128)(2,1)S(1)} %add_convert_fusion.1), channel_id=1, source_target_pairs={{0,2},{1,3},{2,0},{3,1},{4,6},{5,7},{6,4},{7,5},{8,10},{9,11},{10,... | collective-permute-start | bytes 196616 | tf_op jit(solution)/shard_map/ppermute | solution.py:405
  12.6 2.4 %collective-permute-done.3 = bf16[64,512]{1,0:T(8,128)(2,1)S(1)} collective-permute-done((bf16[64,512]{1,0:T(8,128)(2,1)S(1)}, bf16[64,512]{1,0:T(8,128)(2,1)S(1)}, u32[]{:S(2)}, u32[]{:S(2)}) %collective-permute-start.3) | collective-permute-done | bytes 65568 | tf_op jit(solution)/shard_map/ppermute | solution.py:405
  15.0 1.8 %collective-permute-start.4 = (bf16[64,512]{1,0:T(8,128)(2,1)S(1)}, bf16[64,512]{1,0:T(8,128)(2,1)S(1)}, u32[]{:S(2)}, u32[]{:S(2)}) collective-permute-start(bf16[64,512]{1,0:T(8,128)(2,1)S(1)} %add_convert_fusion.refs_0_), channel_id=1, source_target_pairs={{0,64},{64,0},{1,65},{65,1},{2,66},{66,2},{3,67},{67,3},{4,68},{68... | collective-permute-start | bytes 196616 | tf_op jit(solution)/shard_map/ppermute | solution.py:400
  16.8 0.9 shard_map.77
  19.2 0.7 collective-permute-done.5.got_ref
  19.9 15.6 %all_to_all.20.parts_ref = bf16[16,80,128]{2,1,0:T(8,128)(2,1)S(1)} all-to-all(bf16[16,80,128]{2,1,0:T(8,128)(2,1)S(1)} %shard_map.80), channel_id=1, replica_groups=mesh['dp'=2,'vocab'=16,'mp'=4] {'vocab'}, dimensions={0} | all-to-all | bytes 655360 | tf_op jit(solution)/shard_map/all_to_all | solution.py:448
  35.6 11.5 %all_to_all.21.own_ref = bf16[16,80,128]{2,1,0:T(8,128)(2,1)S(1)} all-to-all(bf16[16,80,128]{2,1,0:T(8,128)(2,1)S(1)} %shard_map.81), channel_id=1, replica_groups=mesh['dp'=2,'vocab'=16,'mp'=4] {'vocab'}, dimensions={0} | all-to-all | bytes 655360 | tf_op jit(solution)/shard_map/all_to_all | solution.py:450
  47.1 2.9 %collective-permute-start.6 = (bf16[16,80,128]{2,1,0:T(8,128)(2,1)S(1)}, bf16[16,80,128]{2,1,0:T(8,128)(2,1)S(1)}, u32[]{:S(2)}, u32[]{:S(2)}) collective-permute-start(bf16[16,80,128]{2,1,0:T(8,128)(2,1)S(1)} %all_to_all.21.own_ref), channel_id=1, source_target_pairs={{0,64},{64,0},{1,65},{65,1},{2,66},{66,2},{3,67},{67,3},{4,68},{68... | collective-permute-start | bytes 983048 | tf_op jit(solution)/shard_map/ppermute | solution.py:400
  50.0 2.6 %shard_map.82 = (bf16[64,192]{1,0:T(8,128)(2,1)S(1)}, f32[64,512]{1,0:T(8,128)S(1)}, f32[64,512]{1,0:T(8,128)S(1)}, f32[64,64]{1,0:T(8,128)S(1)}) custom-call(s32[1]{0:T(128)} %bitcast.me_ref.refs_0_, bf16[16,80,128]{2,1,0:T(8,128)(2,1)S(1)} %all_to_all.21.own_ref, bf16[512,4096]{1,0:T(8,128)(2,1)S(1)} %get-tuple-element.42.slab_ref.refs_3_.theirs_slab_ref, ...), custom_call_target="tpu_custom_call" | custom-call | flops 557842688 | bytes 8716292 | tf_op jit(solution)/shard_map/pallas_call | solution.py:386
  52.6 1.6 %shard_map.84 = bf16[64,512]{1,0:T(8,128)(2,1)S(1)} custom-call(s32[1]{0:T(128)} %bitcast.me_ref.refs_0_, bf16[16,80,128]{2,1,0:T(8,128)(2,1)S(1)} %collective-permute-done.6.other_ref, bf16[64,192]{1,0:T(8,128)(2,1)S(1)} %get-tuple-element.46.factor_ref, f32[64,512]{1,0:T(8,128)S(1)} %get-tuple-element.50.acc_ref, ...), custom_call_target="tpu_custom_call" | custom-call | flops 299368704 | bytes 4677636 | tf_op jit(solution)/shard_map/pallas_call | solution.py:386
  54.3 2.2 %shard_map.83 = (f32[64,512]{1,0:T(8,128)S(1)}, bf16[32,512]{1,0:T(8,128)(2,1)S(1)}) custom-call(s32[1]{0:T(128)} %bitcast.me_ref.refs_0_, bf16[16,80,128]{2,1,0:T(8,128)(2,1)S(1)} %collective-permute-done.6.other_ref, bf16[64,192]{1,0:T(8,128)(2,1)S(1)} %get-tuple-element.46.factor_ref, f32[64,512]{1,0:T(8,128)S(1)} %get-tuple-element.47.acc_ref, ...), custom_call_target="tpu_custom_call" | custom-call | flops 300417280 | bytes 4694020 | tf_op jit(solution)/shard_map/pallas_call | solution.py:386
  56.5 1.6 %collective-permute-start.10 = (bf16[96,512]{1,0:T(8,128)(2,1)S(1)}, bf16[96,512]{1,0:T(8,128)(2,1)S(1)}, u32[]{:S(2)}, u32[]{:S(2)}) collective-permute-start(bf16[96,512]{1,0:T(8,128)(2,1)S(1)} %shard_map.85.a_ref), channel_id=1, source_target_pairs={{0,2},{1,3},{2,0},{3,1},{4,6},{5,7},{6,4},{7,5},{8,10},{9,11},{10,... | collective-permute-start | bytes 294920 | tf_op jit(solution)/shard_map/ppermute | solution.py:405
  58.5 2.4 %collective-permute-start.9 = (bf16[96,512]{1,0:T(8,128)(2,1)S(1)}, bf16[96,512]{1,0:T(8,128)(2,1)S(1)}, u32[]{:S(2)}, u32[]{:S(2)}) collective-permute-start(bf16[96,512]{1,0:T(8,128)(2,1)S(1)} %shard_map.85.a_ref), channel_id=1, source_target_pairs={{0,3},{1,0},{2,1},{3,2},{4,7},{5,4},{6,5},{7,6},{8,11},{9,8},{10,9... | collective-permute-start | bytes 294920 | tf_op jit(solution)/shard_map/ppermute | solution.py:405
  60.8 1.2 %collective-permute-done.10.d_ref = bf16[96,512]{1,0:T(8,128)(2,1)S(1)} collective-permute-done((bf16[96,512]{1,0:T(8,128)(2,1)S(1)}, bf16[96,512]{1,0:T(8,128)(2,1)S(1)}, u32[]{:S(2)}, u32[]{:S(2)}) %collective-permute-start.10) | collective-permute-done | bytes 98336 | tf_op jit(solution)/shard_map/ppermute | solution.py:405
  62.0 2.4 %collective-permute-done.8.b_ref = bf16[96,512]{1,0:T(8,128)(2,1)S(1)} collective-permute-done((bf16[96,512]{1,0:T(8,128)(2,1)S(1)}, bf16[96,512]{1,0:T(8,128)(2,1)S(1)}, u32[]{:S(2)}, u32[]{:S(2)}) %collective-permute-start.8) | collective-permute-done | bytes 98336 | tf_op jit(solution)/shard_map/ppermute | solution.py:405
  64.6 1.2 %collective-permute-start.11 = (bf16[64,512]{1,0:T(8,128)(2,1)S(1)}, bf16[64,512]{1,0:T(8,128)(2,1)S(1)}, u32[]{:S(2)}, u32[]{:S(2)}) collective-permute-start(bf16[64,512]{1,0:T(8,128)(2,1)S(1)} %get-tuple-element.52.refs_0_), channel_id=1, source_target_pairs={{0,64},{64,0},{1,65},{65,1},{2,66},{66,2},{3,67},{67,3},{4,68},{68... | collective-permute-start | bytes 196616 | tf_op jit(solution)/shard_map/ppermute | solution.py:400
  65.8 2.7 %shard_map.87 = (f32[64,4096]{1,0:T(8,128)S(1)}, f32[64,64]{1,0:T(8,128)S(1)}, bf16[64,192]{1,0:T(8,128)(2,1)S(1)}, bf16[64,512]{1,0:T(8,128)(2,1)S(1)}) custom-call(bf16[64,512]{1,0:T(8,128)(2,1)S(1)} %get-tuple-element.52.refs_0_, f32[64,64]{1,0:T(8,128)S(1)} %get-tuple-element.53.refs_1_, ...), custom_call_target="tpu_custom_call" | custom-call | flops 273678336 | bytes 4276224 | tf_op jit(solution)/shard_map/pallas_call | solution.py:386
  69.7 1.0 collective-permute-done.12.got_ref
  70.7 11.4 %all_to_all.22.parts_ref = bf16[16,80,128]{2,1,0:T(8,128)(2,1)S(1)} all-to-all(bf16[16,80,128]{2,1,0:T(8,128)(2,1)S(1)} %shard_map.90), channel_id=1, replica_groups=mesh['dp'=2,'vocab'=16,'mp'=4] {'vocab'}, dimensions={0} | all-to-all | bytes 655360 | tf_op jit(solution)/shard_map/all_to_all | solution.py:448
  82.2 11.6 %all_to_all.23.own_ref = bf16[16,80,128]{2,1,0:T(8,128)(2,1)S(1)} all-to-all(bf16[16,80,128]{2,1,0:T(8,128)(2,1)S(1)} %shard_map.91), channel_id=1, replica_groups=mesh['dp'=2,'vocab'=16,'mp'=4] {'vocab'}, dimensions={0} | all-to-all | bytes 655360 | tf_op jit(solution)/shard_map/all_to_all | solution.py:450
  93.8 2.6 %collective-permute-start.13 = (bf16[16,80,128]{2,1,0:T(8,128)(2,1)S(1)}, bf16[16,80,128]{2,1,0:T(8,128)(2,1)S(1)}, u32[]{:S(2)}, u32[]{:S(2)}) collective-permute-start(bf16[16,80,128]{2,1,0:T(8,128)(2,1)S(1)} %all_to_all.23.own_ref), channel_id=1, source_target_pairs={{0,64},{64,0},{1,65},{65,1},{2,66},{66,2},{3,67},{67,3},{4,68},{68... | collective-permute-start | bytes 983048 | tf_op jit(solution)/shard_map/ppermute | solution.py:400
  96.4 2.6 %shard_map.92 = (bf16[64,192]{1,0:T(8,128)(2,1)S(1)}, f32[64,2048]{1,0:T(8,128)S(1)}, f32[64,64]{1,0:T(8,128)S(1)}, bf16[64,1024]{1,0:T(8,128)(2,1)S(1)}) custom-call(s32[1]{0:T(128)} %bitcast.me_ref.refs_0_, bf16[16,80,128]{2,1,0:T(8,128)(2,1)S(1)} %all_to_all.23.own_ref, bf16[64,512]{1,0:T(8,128)(2,1)S(1)} %get-tuple-element.61.rows_mine_ref, ...), custom_call_target="tpu_custom_call" | custom-call | flops 29360384 | bytes 458756 | tf_op jit(solution)/shard_map/pallas_call | solution.py:386
  99.0 0.9 shard_map.93
  100.1 2.6 %collective-permute-start.15 = (f32[64,64]{1,0:T(8,128)S(1)}, f32[64,64]{1,0:T(8,128)S(1)}, u32[]{:S(2)}, u32[]{:S(2)}) collective-permute-start(f32[64,64]{1,0:T(8,128)S(1)} %get-tuple-element.68.a_ref), channel_id=1, source_target_pairs={{0,3},{1,0},{2,1},{3,2},{4,7},{5,4},{6,5},{7,6},{8,11},{9,8},{10,9... | collective-permute-start | bytes 49160 | tf_op jit(solution)/shard_map/ppermute | solution.py:405
  102.7 0.7 collective-permute-start.16
  103.5 5.3 %shard_map.94 = (bf16[1024,4096]{1,0:T(8,128)(2,1)}, f32[64,4096]{1,0:T(8,128)}, f32[64,4096]{1,0:T(8,128)}, bf16[192,4096]{1,0:T(8,128)(2,1)S(1)}) custom-call(s32[1]{0:T(128)} %bitcast.me_ref.refs_0_, f32[64,2048]{1,0:T(8,128)S(1)} %get-tuple-element.62.own_ref, f32[64,2048]{1,0:T(8,128)S(1)} %get-tuple-element.65.other_ref, ...), custom_call_target="tpu_custom_call" | custom-call | flops 209715456 | bytes 3276804 | tf_op jit(solution)/shard_map/pallas_call | solution.py:386
  108.8 3.1 %shard_map.95 = f32[64,4096]{1,0:T(8,128)} custom-call(f32[64,64]{1,0:T(8,128)S(1)} %get-tuple-element.68.a_ref, f32[64,64]{1,0:T(8,128)S(1)} %collective-permute-done.14.b_ref, f32[64,64]{1,0:T(8,128)S(1)} %collective-permute-done.15.c_ref, f32[64,64]{1,0:T(8,128)S(1)} %collective-permute-done.16.d_ref, bf16[192,4096]{1,0:T(8,128)(2,1)S(1)} %get-tuple-element.69.three_ref), custom_call_target="tpu_custom_call" | custom-call | flops 104857600 | bytes 1638400 | tf_op jit(solution)/shard_map/pallas_call | solution.py:386
  (33 shorter events, 4.3 us)
Async XLA Ops:
  4.7 2.9 %collective-permute-start = (bf16[64,512]{1,0:T(8,128)(2,1)S(1)}, bf16[64,512]{1,0:T(8,128)(2,1)S(1)}, u32[]{:S(2)}, u32[]{:S(2)}) collective-permute-start(bf16[64,512]{1,0:T(8,128)(2,1)S(1)} %get-tuple-element.40), channel_id=1, source_target_pairs={{0,64},{64,0},{1,65},{65,1},{2,66},{66,2},{3,67},{67,3},{4,68},{68... | collective-permute-start | bytes 196616 | tf_op jit(solution)/shard_map/ppermute | solution.py:400
  7.6 5.0 %collective-permute-start.1 = (bf16[64,512]{1,0:T(8,128)(2,1)S(1)}, bf16[64,512]{1,0:T(8,128)(2,1)S(1)}, u32[]{:S(2)}, u32[]{:S(2)}) collective-permute-start(bf16[64,512]{1,0:T(8,128)(2,1)S(1)} %add_convert_fusion.1), channel_id=1, source_target_pairs={{0,1},{1,2},{2,3},{3,0},{4,5},{5,6},{6,7},{7,4},{8,9},{9,10},{10,1... | collective-permute-start | bytes 196616 | tf_op jit(solution)/shard_map/ppermute | solution.py:405
  9.0 3.6 %collective-permute-start.2 = (bf16[64,512]{1,0:T(8,128)(2,1)S(1)}, bf16[64,512]{1,0:T(8,128)(2,1)S(1)}, u32[]{:S(2)}, u32[]{:S(2)}) collective-permute-start(bf16[64,512]{1,0:T(8,128)(2,1)S(1)} %add_convert_fusion.1), channel_id=1, source_target_pairs={{0,3},{1,0},{2,1},{3,2},{4,7},{5,4},{6,5},{7,6},{8,11},{9,8},{10,9... | collective-permute-start | bytes 196616 | tf_op jit(solution)/shard_map/ppermute | solution.py:405
  10.4 4.6 %collective-permute-start.3 = (bf16[64,512]{1,0:T(8,128)(2,1)S(1)}, bf16[64,512]{1,0:T(8,128)(2,1)S(1)}, u32[]{:S(2)}, u32[]{:S(2)}) collective-permute-start(bf16[64,512]{1,0:T(8,128)(2,1)S(1)} %add_convert_fusion.1), channel_id=1, source_target_pairs={{0,2},{1,3},{2,0},{3,1},{4,6},{5,7},{6,4},{7,5},{8,10},{9,11},{10,... | collective-permute-start | bytes 196616 | tf_op jit(solution)/shard_map/ppermute | solution.py:405
  15.0 2.7 %collective-permute-start.4 = (bf16[64,512]{1,0:T(8,128)(2,1)S(1)}, bf16[64,512]{1,0:T(8,128)(2,1)S(1)}, u32[]{:S(2)}, u32[]{:S(2)}) collective-permute-start(bf16[64,512]{1,0:T(8,128)(2,1)S(1)} %add_convert_fusion.refs_0_), channel_id=1, source_target_pairs={{0,64},{64,0},{1,65},{65,1},{2,66},{66,2},{3,67},{67,3},{4,68},{68... | collective-permute-start | bytes 196616 | tf_op jit(solution)/shard_map/ppermute | solution.py:400
  18.2 1.6 %collective-permute-start.5 = (bf16[16,64,128]{2,1,0:T(8,128)(2,1)S(1)}, bf16[16,64,128]{2,1,0:T(8,128)(2,1)S(1)}, u32[]{:S(2)}, u32[]{:S(2)}) collective-permute-start(bf16[16,64,128]{2,1,0:T(8,128)(2,1)S(1)} %shard_map.79), channel_id=1, source_target_pairs={{0,64},{64,0},{1,65},{65,1},{2,66},{66,2},{3,67},{67,3},{4,68},{68... | collective-permute-start | bytes 786440 | tf_op jit(solution)/shard_map/ppermute | solution.py:400
  47.1 5.5 %collective-permute-start.6 = (bf16[16,80,128]{2,1,0:T(8,128)(2,1)S(1)}, bf16[16,80,128]{2,1,0:T(8,128)(2,1)S(1)}, u32[]{:S(2)}, u32[]{:S(2)}) collective-permute-start(bf16[16,80,128]{2,1,0:T(8,128)(2,1)S(1)} %all_to_all.21.own_ref), channel_id=1, source_target_pairs={{0,64},{64,0},{1,65},{65,1},{2,66},{66,2},{3,67},{67,3},{4,68},{68... | collective-permute-start | bytes 983048 | tf_op jit(solution)/shard_map/ppermute | solution.py:400
  54.2 2.3 %collective-permute-start.7 = (bf16[64,512]{1,0:T(8,128)(2,1)S(1)}, bf16[64,512]{1,0:T(8,128)(2,1)S(1)}, u32[]{:S(2)}, u32[]{:S(2)}) collective-permute-start(bf16[64,512]{1,0:T(8,128)(2,1)S(1)} %shard_map.84), channel_id=1, source_target_pairs={{0,64},{64,0},{1,65},{65,1},{2,66},{66,2},{3,67},{67,3},{4,68},{68... | collective-permute-start | bytes 196616 | tf_op jit(solution)/shard_map/ppermute | solution.py:400
  56.5 5.5 %collective-permute-start.10 = (bf16[96,512]{1,0:T(8,128)(2,1)S(1)}, bf16[96,512]{1,0:T(8,128)(2,1)S(1)}, u32[]{:S(2)}, u32[]{:S(2)}) collective-permute-start(bf16[96,512]{1,0:T(8,128)(2,1)S(1)} %shard_map.85.a_ref), channel_id=1, source_target_pairs={{0,2},{1,3},{2,0},{3,1},{4,6},{5,7},{6,4},{7,5},{8,10},{9,11},{10,... | collective-permute-start | bytes 294920 | tf_op jit(solution)/shard_map/ppermute | solution.py:405
  58.2 6.3 %collective-permute-start.8 = (bf16[96,512]{1,0:T(8,128)(2,1)S(1)}, bf16[96,512]{1,0:T(8,128)(2,1)S(1)}, u32[]{:S(2)}, u32[]{:S(2)}) collective-permute-start(bf16[96,512]{1,0:T(8,128)(2,1)S(1)} %shard_map.85.a_ref), channel_id=1, source_target_pairs={{0,1},{1,2},{2,3},{3,0},{4,5},{5,6},{6,7},{7,4},{8,9},{9,10},{10,1... | collective-permute-start | bytes 294920 | tf_op jit(solution)/shard_map/ppermute | solution.py:405
  58.5 6.0 %collective-permute-start.9 = (bf16[96,512]{1,0:T(8,128)(2,1)S(1)}, bf16[96,512]{1,0:T(8,128)(2,1)S(1)}, u32[]{:S(2)}, u32[]{:S(2)}) collective-permute-start(bf16[96,512]{1,0:T(8,128)(2,1)S(1)} %shard_map.85.a_ref), channel_id=1, source_target_pairs={{0,3},{1,0},{2,1},{3,2},{4,7},{5,4},{6,5},{7,6},{8,11},{9,8},{10,9... | collective-permute-start | bytes 294920 | tf_op jit(solution)/shard_map/ppermute | solution.py:405
  64.6 3.9 %collective-permute-start.11 = (bf16[64,512]{1,0:T(8,128)(2,1)S(1)}, bf16[64,512]{1,0:T(8,128)(2,1)S(1)}, u32[]{:S(2)}, u32[]{:S(2)}) collective-permute-start(bf16[64,512]{1,0:T(8,128)(2,1)S(1)} %get-tuple-element.52.refs_0_), channel_id=1, source_target_pairs={{0,64},{64,0},{1,65},{65,1},{2,66},{66,2},{3,67},{67,3},{4,68},{68... | collective-permute-start | bytes 196616 | tf_op jit(solution)/shard_map/ppermute | solution.py:400
  69.1 1.6 %collective-permute-start.12 = (bf16[16,64,128]{2,1,0:T(8,128)(2,1)S(1)}, bf16[16,64,128]{2,1,0:T(8,128)(2,1)S(1)}, u32[]{:S(2)}, u32[]{:S(2)}) collective-permute-start(bf16[16,64,128]{2,1,0:T(8,128)(2,1)S(1)} %get-tuple-element.59), channel_id=1, source_target_pairs={{0,64},{64,0},{1,65},{65,1},{2,66},{66,2},{3,67},{67,3},{4,68},{68... | collective-permute-start | bytes 786440 | tf_op jit(solution)/shard_map/ppermute | solution.py:400
  69.2 34.3 %copy-start = (f32[64,4096]{1,0:T(8,128)S(1)}, f32[64,4096]{1,0:T(8,128)}, u32[]{:S(2)}) copy-start(f32[64,4096]{1,0:T(8,128)} %first_ref.1) | copy-start | bytes 3145732
  69.2 34.3 %copy-start.1 = (f32[64,4096]{1,0:T(8,128)S(1)}, f32[64,4096]{1,0:T(8,128)}, u32[]{:S(2)}) copy-start(f32[64,4096]{1,0:T(8,128)} %second_ref.1) | copy-start | bytes 3145732
  93.8 5.2 %collective-permute-start.13 = (bf16[16,80,128]{2,1,0:T(8,128)(2,1)S(1)}, bf16[16,80,128]{2,1,0:T(8,128)(2,1)S(1)}, u32[]{:S(2)}, u32[]{:S(2)}) collective-permute-start(bf16[16,80,128]{2,1,0:T(8,128)(2,1)S(1)} %all_to_all.23.own_ref), channel_id=1, source_target_pairs={{0,64},{64,0},{1,65},{65,1},{2,66},{66,2},{3,67},{67,3},{4,68},{68... | collective-permute-start | bytes 983048 | tf_op jit(solution)/shard_map/ppermute | solution.py:400
  100.0 8.8 %collective-permute-start.14 = (f32[64,64]{1,0:T(8,128)S(1)}, f32[64,64]{1,0:T(8,128)S(1)}, u32[]{:S(2)}, u32[]{:S(2)}) collective-permute-start(f32[64,64]{1,0:T(8,128)S(1)} %get-tuple-element.68.a_ref), channel_id=1, source_target_pairs={{0,1},{1,2},{2,3},{3,0},{4,5},{5,6},{6,7},{7,4},{8,9},{9,10},{10,1... | collective-permute-start | bytes 49160 | tf_op jit(solution)/shard_map/ppermute | solution.py:405
  100.1 8.7 %collective-permute-start.15 = (f32[64,64]{1,0:T(8,128)S(1)}, f32[64,64]{1,0:T(8,128)S(1)}, u32[]{:S(2)}, u32[]{:S(2)}) collective-permute-start(f32[64,64]{1,0:T(8,128)S(1)} %get-tuple-element.68.a_ref), channel_id=1, source_target_pairs={{0,3},{1,0},{2,1},{3,2},{4,7},{5,4},{6,5},{7,6},{8,11},{9,8},{10,9... | collective-permute-start | bytes 49160 | tf_op jit(solution)/shard_map/ppermute | solution.py:405
  102.7 6.1 %collective-permute-start.16 = (f32[64,64]{1,0:T(8,128)S(1)}, f32[64,64]{1,0:T(8,128)S(1)}, u32[]{:S(2)}, u32[]{:S(2)}) collective-permute-start(f32[64,64]{1,0:T(8,128)S(1)} %get-tuple-element.68.a_ref), channel_id=1, source_target_pairs={{0,2},{1,3},{2,0},{3,1},{4,6},{5,7},{6,4},{7,5},{8,10},{9,11},{10,... | collective-permute-start | bytes 49160 | tf_op jit(solution)/shard_map/ppermute | solution.py:405

commit v6 on v4

--- a/solution.py
+++ b/solution.py
@@ -304,84 +304,86 @@
     for core, ref in ((me, rows_mine_ref), (1 - me, rows_other_ref)):
         left = applied(factor3, ref[...]).astype(BF16)
         left_ref[:, span(core * half, half)] = (left.astype(F32) * scale).astype(BF16)
+    gram_ref[...] = keep_columns(factor3, own_ref, columns_ref)
+
+
+def keep_columns(factor3, chunks_ref, columns_ref):
+    rank = factor3.shape[0]
     total = jnp.zeros((3 * rank, 3 * rank), F32)
-    for at, block in blocks_of(own_ref, rank):
-        columns_ref[:, at] = applied(factor3, block)
-        total = total + gram_of(columns_ref, at)
-    gram_ref[...] = folded(total, rank)
-
-
-def moments_kernel(
-    me_ref, other_ref, factor_ref, own_columns_ref, gram_own_ref, first_ref, second_ref,
-    columns_ref, gram_ref, new_first_ref, new_second_ref, direction_ref,
-):
-    me = me_ref[0]
-    factor3 = factor_ref[...]
-    rank, width = own_columns_ref.shape
+    for at, block in blocks_of(chunks_ref, rank):
+        columns = applied(factor3, block)
+        columns_ref[:, at] = columns
+        three = stacked(columns)
+        total = total + dot(three, three, 1, 1)
+    return folded(total, rank)
+
+
+def final_other_kernel(other_ref, factor_ref, gram_own_ref, columns_ref, gram_ref):
+    gram_ref[...] = gram_own_ref[...] + keep_columns(factor_ref[...], other_ref, columns_ref)
+
+
+def half_update(core, columns_ref, left, first_ref, second_ref, outs, buffers, sems):
     corr_one = 1.0 - 0.9**10
     corr_two = 1.0 - 0.999**10
-
-    def moments(at, columns):
-        columns_ref[:, at] = columns
+    update_ref, new_first_ref, new_second_ref = buffers
+    width = columns_ref.shape[1]
+    for t in range(0, width, TILE):
+        at = span(core * width + t, TILE)
+        columns = columns_ref[:, t : t + TILE]
         new_first = 0.9 * first_ref[:, at] + 0.1 * columns
         new_second = 0.999 * second_ref[:, at] + 0.001 * columns * columns
-        new_first_ref[:, at] = new_first
-        new_second_ref[:, at] = new_second
+        here = slice(t, t + TILE)
+        new_first_ref[:, here] = new_first
+        new_second_ref[:, here] = new_second
         direction = new_first / corr_one / (jnp.sqrt(new_second / corr_two) + 1e-08)
-        direction_ref[:, at] = direction.astype(BF16)
-
-    total = jnp.zeros((3 * rank, 3 * rank), F32)
-    for part, block in blocks_of(other_ref, rank):
-        at = span((1 - me) * width + part.start, TILE)
-        moments(at, applied(factor3, block))
-        total = total + gram_of(columns_ref, at)
-        at = span(me * width + part.start, TILE)
-        moments(at, own_columns_ref[:, part])
-    gram_ref[...] = gram_own_ref[...] + folded(total, rank)
-
-
-def update_kernel(
-    left_ref, direction_ref, first_ref, second_ref, update_hbm, first_hbm, second_hbm, buffer_ref, sems
-):
+        update_ref[:, here] = dot(left, direction.astype(BF16), 1, 0).astype(BF16)
     copies = [
-        pltpu.make_async_copy(first_ref, first_hbm, sems.at[0]),
-        pltpu.make_async_copy(second_ref, second_hbm, sems.at[1]),
+        pltpu.make_async_copy(ref, hbm.at[:, span(core * width, width)], sems.at[i])
+        for i, (ref, hbm) in enumerate(zip(buffers, outs))
     ]
     for copy in copies:
         copy.start()
+    return copies
+
+
+def update_own_kernel(me_ref, columns_ref, left_ref, first_ref, second_ref, *refs):
+    outs, turned_ref, buffers, sems = refs[:3], refs[3], refs[4:7], refs[7]
     left = left_ref[...].T
-    for i in range(left.shape[0] // TILE):
-        rows = slice(i * TILE, (i + 1) * TILE)
-        for t in range(0, direction_ref.shape[1], TILE):
-            product = dot(left[rows, :], direction_ref[:, t : t + TILE], 1, 0)
-            buffer_ref[rows, t : t + TILE] = product.astype(BF16)
-        copy = pltpu.make_async_copy(buffer_ref.at[rows, :], update_hbm.at[rows, :], sems.at[2 + i])
+    turned_ref[...] = left
+    copies = half_update(me_ref[0], columns_ref, left, first_ref, second_ref, outs, buffers, sems)
+    for copy in copies:
+        copy.wait()
+
+
+def update_other_kernel(
+    me_ref, other_ref, turned_ref, first_ref, second_ref, own_ref, a_ref, b_ref, c_ref, d_ref, *refs
+):
+    me = me_ref[0]
+    outs, basis_hbm, buffers, basis_ref, sems = refs[3:6], refs[6], refs[7:10], refs[10], refs[11]
+    copies = half_update(
+        1 - me, other_ref, turned_ref[...], first_ref, second_ref, outs, buffers, sems
+    )
+    factor = inverse_factor((a_ref[...] + b_ref[...]) + (c_ref[...] + d_ref[...]))
+    high, mid, _ = thirds(factor)
+    wide = jnp.concatenate([high, high, mid], axis=1).astype(BF16)
+    width = own_ref.shape[1]
+    for i, (core, ref) in enumerate(((me, own_ref), (1 - me, other_ref))):
+        for t in range(0, width, TILE):
+            high, mid, _ = thirds(ref[:, t : t + TILE])
+            tall = jnp.concatenate([high, mid, high], axis=0).astype(BF16)
+            basis_ref[:, i * width + t : i * width + t + TILE] = dot(wide, tall, 1, 0)
+        copy = pltpu.make_async_copy(
+            basis_ref.at[:, i * width : (i + 1) * width],
+            basis_hbm.at[:, span(core * width, width)],
+            sems.at[3 + i],
+        )
         copy.start()
         copies.append(copy)
     for copy in copies:
         copy.wait()
 
 
-def basis_kernel(a_ref, b_ref, c_ref, d_ref, columns_ref, basis_hbm, basis_ref, sems):
-    factor = inverse_factor((a_ref[...] + b_ref[...]) + (c_ref[...] + d_ref[...]))
-    high, mid, low = thirds(factor)
-    wide = jnp.concatenate([low, mid, high, mid, high, high], axis=1).astype(BF16)
-    copies = []
-    width = columns_ref.shape[1]
-    for part in range(2):
-        for t in range(part * width // 2, (part + 1) * width // 2, TILE):
-            high, mid, low = (x.astype(BF16) for x in thirds(columns_ref[:, t : t + TILE]))
-            tall = jnp.concatenate([high, mid, low, high, mid, high], axis=0)
-            basis_ref[:, t : t + TILE] = dot(wide, tall, 1, 0)
-        at = slice(part * width // 2, (part + 1) * width // 2)
-        copy = pltpu.make_async_copy(basis_ref.at[:, at], basis_hbm.at[:, at], sems.at[part])
-        copy.start()
-        copies.append(copy)
-    for copy in copies:
-        copy.wait()
-
-
-def call(kernel, outs, operands, scratch=(), hbm=(), hbm_out=False):
+def call(kernel, outs, operands, scratch=(), hbm=(), hbm_out=(), aliases=None):
     def spec(i, x):
         if x.dtype == jnp.int32:
             return SMEM
@@ -392,7 +394,10 @@
         kernel,
         out_shape=[jax.ShapeDtypeStruct(s, t) for s, t in outs],
         in_specs=[spec(i, x) for i, x in enumerate(operands)],
-        out_specs=[pl.BlockSpec(memory_space=pl.ANY) if hbm_out else VMEM] * len(outs),
+        out_specs=[
+            pl.BlockSpec(memory_space=pl.ANY) if i in hbm_out else VMEM for i in range(len(outs))
+        ],
+        input_output_aliases=aliases or {},
         scratch_shapes=[pltpu.VMEM(*s) if isinstance(s, tuple) else s for s in scratch],
         compiler_params=pltpu.CompilerParams(vmem_limit_bytes=VMEM_LIMIT),
         cost_estimate=pl.CostEstimate(flops=64 * moved, bytes_accessed=moved, transcendentals=0),
@@ -508,31 +513,33 @@
 
     scale = math.sqrt(vocab * owners)
     assert scale == 2.0 ** round(math.log2(scale))
-    factor, columns, gram, left = call(
+    factor, columns_own, gram, left = call(
         functools.partial(final_own_kernel, scale),
         [factor_out, narrow, square, ((rank, vocab), BF16)],
         [me, own, rows_mine, rows_other],
     )
-    columns, gram, new_first, new_second, direction = call(
-        moments_kernel,
-        [wide, square, wide, wide, ((rank, width), BF16)],
-        [me, other, factor, columns, gram, first_moment, second_moment],
-    )
+    columns_other, gram = call(final_other_kernel, [narrow, square], [other, factor, gram])
     gram_others = others(gram)
-    update, new_first, new_second = call(
-        update_kernel,
-        [((vocab, width), BF16), wide, wide],
-        [left, direction, new_first, new_second],
-        [((vocab, width), BF16), pltpu.SemaphoreType.DMA((2 + vocab // TILE,))],
-        hbm_out=True,
-    )
-    basis = call(
-        basis_kernel,
-        [wide],
-        [gram, *gram_others, columns],
-        [((rank, width), F32), pltpu.SemaphoreType.DMA((2,))],
-        hbm_out=True,
-    )[0]
+    outs = [((vocab, width), BF16), wide, wide]
+    buffers = [((vocab, width // 2), BF16), narrow, narrow]
+    *begun, turned = call(
+        update_own_kernel,
+        outs + [((vocab, rank), BF16)],
+        [me, columns_own, left, first_moment, second_moment],
+        buffers + [pltpu.SemaphoreType.DMA((3,))],
+        hbm_out=(0, 1, 2),
+    )
+    operands = [me, columns_other, turned, first_moment, second_moment, columns_own, gram, *gram_others]
+    n = len(operands)
+    update, new_first, new_second, basis = call(
+        update_other_kernel,
+        outs + [wide],
+        operands + begun,
+        buffers + [wide, pltpu.SemaphoreType.DMA((5,))],
+        hbm=(n, n + 1, n + 2),
+        hbm_out=(0, 1, 2, 3),
+        aliases={n: 0, n + 1: 1, n + 2: 2},
+    )
     return (update, basis, new_first, new_second)
 
 

time: 111 us -> 111 us (level)
  transfers between devices with their start and end apart: 17 -> 17, of which waited for: 8 -> 9; matrix products, arithmetic and copies ran while one was open for 0% -> 0% of each run, Pallas kernels for 16% -> 15%
where the time goes in v6:
time: 111 us; the launch traced here: 110 us
  blocking collectives  50 us (45%)
  Pallas kernels  28.5 us (26%)
  starting transfers between devices  19.2 us (17%)
  waiting for transfers between devices  11.6 us (10%)
    pallas_call x21, Pallas kernels, call(): pl.pallas_call(kernel, out_shape=[jax.ShapeDtypeStruct(s, t) for s, t in...  28.5 us
    all_to_all x2, blocking collectives, columns_of(): parts = lax.all_to_all(chunks, 'vocab', 0, 0)  26.9 us
    all_to_all x2, blocking collectives, columns_of(): own = lax.all_to_all(copies, 'vocab', 0, 0)  23.1 us
    ppermute x8, starting transfers between devices, swapped(): return lax.ppermute(x, 'dp', [(0, 1), (1, 0)])  10.7 us
    ppermute x9, waiting for transfers between devices, others(): lax.ppermute(x, 'mp', [(i, (i + k) % n) for i in range(n)])  9.61 us
    ppermute x9, starting transfers between devices, others(): lax.ppermute(x, 'mp', [(i, (i + k) % n) for i in range(n)])  8.46 us
  transfers between devices with their start and end apart: 17, of which 9 were waited for; matrix products, arithmetic and copies ran while one was open for 0% of the time, Pallas kernels for 15%

profile of v6, /device:TPU:1, one launch (start us, length us, event | category | flops | bytes accessed | tf_op | source)
XLA Modules:
  0.0 110.3 jit_solution(13643898673970416544)
XLA Ops:
  0.6 4.0 %shard_map.75 = (bf16[64,512]{1,0:T(8,128)(2,1)S(1)}, bf16[64,4096]{1,0:T(8,128)(2,1)S(1)}, bf16[512,4096]{1,0:T(8,128)(2,1)S(1)}, bf16[512,4096]{1,0:T(8,128)(2,1)S(1)}) custom-call(s32[1]{0:T(128)} %bitcast.me_ref.refs_0_, f32[64,4096]{1,0:T(8,128)} %basis_hbm.1, bf16[1024,4096]{1,0:T(8,128)(2,1)} %bitcast.2), custom_call_target="tpu_custom_call" | custom-call | flops 603980032 | bytes 9437188 | tf_op jit(solution)/shard_map/pallas_call | solution.py:393
  4.7 1.5 %collective-permute-start = (bf16[64,512]{1,0:T(8,128)(2,1)S(1)}, bf16[64,512]{1,0:T(8,128)(2,1)S(1)}, u32[]{:S(2)}, u32[]{:S(2)}) collective-permute-start(bf16[64,512]{1,0:T(8,128)(2,1)S(1)} %get-tuple-element.47), channel_id=1, source_target_pairs={{0,64},{64,0},{1,65},{65,1},{2,66},{66,2},{3,67},{67,3},{4,68},{68... | collective-permute-start | bytes 196616 | tf_op jit(solution)/shard_map/ppermute | solution.py:408
  6.2 1.4 %shard_map.76 = f32[64,512]{1,0:T(8,128)S(1)} custom-call(bf16[64,4096]{1,0:T(8,128)(2,1)S(1)} %get-tuple-element.45.left_ref, bf16[512,4096]{1,0:T(8,128)(2,1)S(1)} %get-tuple-element.46.slab_ref.refs_1_.mine_slab_ref.refs_2_), custom_call_target="tpu_custom_call" | custom-call | flops 301989888 | bytes 4718592 | tf_op jit(solution)/shard_map/pallas_call | solution.py:393
  7.6 2.9 %collective-permute-start.3 = (bf16[64,512]{1,0:T(8,128)(2,1)S(1)}, bf16[64,512]{1,0:T(8,128)(2,1)S(1)}, u32[]{:S(2)}, u32[]{:S(2)}) collective-permute-start(bf16[64,512]{1,0:T(8,128)(2,1)S(1)} %add_convert_fusion.1), channel_id=1, source_target_pairs={{0,2},{1,3},{2,0},{3,1},{4,6},{5,7},{6,4},{7,5},{8,10},{9,11},{10,... | collective-permute-start | bytes 196616 | tf_op jit(solution)/shard_map/ppermute | solution.py:413
  10.5 0.9 collective-permute-start.2
  11.4 0.6 collective-permute-start.1
  12.0 0.9 collective-permute-done.3
  12.9 1.5 %collective-permute-done.2 = bf16[64,512]{1,0:T(8,128)(2,1)S(1)} collective-permute-done((bf16[64,512]{1,0:T(8,128)(2,1)S(1)}, bf16[64,512]{1,0:T(8,128)(2,1)S(1)}, u32[]{:S(2)}, u32[]{:S(2)}) %collective-permute-start.2) | collective-permute-done | bytes 65568 | tf_op jit(solution)/shard_map/ppermute | solution.py:413
  14.4 1.3 %collective-permute-done.1 = bf16[64,512]{1,0:T(8,128)(2,1)S(1)} collective-permute-done((bf16[64,512]{1,0:T(8,128)(2,1)S(1)}, bf16[64,512]{1,0:T(8,128)(2,1)S(1)}, u32[]{:S(2)}, u32[]{:S(2)}) %collective-permute-start.1) | collective-permute-done | bytes 65568 | tf_op jit(solution)/shard_map/ppermute | solution.py:413
  15.7 1.8 %collective-permute-start.4 = (bf16[64,512]{1,0:T(8,128)(2,1)S(1)}, bf16[64,512]{1,0:T(8,128)(2,1)S(1)}, u32[]{:S(2)}, u32[]{:S(2)}) collective-permute-start(bf16[64,512]{1,0:T(8,128)(2,1)S(1)} %add_convert_fusion.refs_0_), channel_id=1, source_target_pairs={{0,64},{64,0},{1,65},{65,1},{2,66},{66,2},{3,67},{67,3},{4,68},{68... | collective-permute-start | bytes 196616 | tf_op jit(solution)/shard_map/ppermute | solution.py:408
  17.5 0.9 shard_map.77
  19.9 0.7 collective-permute-done.5.got_ref
  20.6 15.5 %all_to_all.20.parts_ref = bf16[16,80,128]{2,1,0:T(8,128)(2,1)S(1)} all-to-all(bf16[16,80,128]{2,1,0:T(8,128)(2,1)S(1)} %shard_map.80), channel_id=1, replica_groups=mesh['dp'=2,'vocab'=16,'mp'=4] {'vocab'}, dimensions={0} | all-to-all | bytes 655360 | tf_op jit(solution)/shard_map/all_to_all | solution.py:456
  36.2 11.5 %all_to_all.21.own_ref = bf16[16,80,128]{2,1,0:T(8,128)(2,1)S(1)} all-to-all(bf16[16,80,128]{2,1,0:T(8,128)(2,1)S(1)} %shard_map.81), channel_id=1, replica_groups=mesh['dp'=2,'vocab'=16,'mp'=4] {'vocab'}, dimensions={0} | all-to-all | bytes 655360 | tf_op jit(solution)/shard_map/all_to_all | solution.py:458
  47.7 2.9 %collective-permute-start.6 = (bf16[16,80,128]{2,1,0:T(8,128)(2,1)S(1)}, bf16[16,80,128]{2,1,0:T(8,128)(2,1)S(1)}, u32[]{:S(2)}, u32[]{:S(2)}) collective-permute-start(bf16[16,80,128]{2,1,0:T(8,128)(2,1)S(1)} %all_to_all.21.own_ref), channel_id=1, source_target_pairs={{0,64},{64,0},{1,65},{65,1},{2,66},{66,2},{3,67},{67,3},{4,68},{68... | collective-permute-start | bytes 983048 | tf_op jit(solution)/shard_map/ppermute | solution.py:408
  50.7 3.4 %shard_map.82 = (bf16[64,192]{1,0:T(8,128)(2,1)S(1)}, f32[64,512]{1,0:T(8,128)S(1)}, f32[64,512]{1,0:T(8,128)S(1)}, f32[64,64]{1,0:T(8,128)S(1)}) custom-call(s32[1]{0:T(128)} %bitcast.me_ref.refs_0_, bf16[16,80,128]{2,1,0:T(8,128)(2,1)S(1)} %all_to_all.21.own_ref, bf16[512,4096]{1,0:T(8,128)(2,1)S(1)} %get-tuple-element.49.slab_ref.refs_3_.theirs_slab_ref, ...), custom_call_target="tpu_custom_call" | custom-call | flops 557842688 | bytes 8716292 | tf_op jit(solution)/shard_map/pallas_call | solution.py:393
  54.0 0.9 shard_map.83
  55.0 0.9 shard_map.84
  56.9 1.3 %collective-permute-start.9 = (bf16[96,512]{1,0:T(8,128)(2,1)S(1)}, bf16[96,512]{1,0:T(8,128)(2,1)S(1)}, u32[]{:S(2)}, u32[]{:S(2)}) collective-permute-start(bf16[96,512]{1,0:T(8,128)(2,1)S(1)} %shard_map.85.a_ref), channel_id=1, source_target_pairs={{0,3},{1,0},{2,1},{3,2},{4,7},{5,4},{6,5},{7,6},{8,11},{9,8},{10,9... | collective-permute-start | bytes 294920 | tf_op jit(solution)/shard_map/ppermute | solution.py:413
  58.3 3.7 %collective-permute-done.10.d_ref = bf16[96,512]{1,0:T(8,128)(2,1)S(1)} collective-permute-done((bf16[96,512]{1,0:T(8,128)(2,1)S(1)}, bf16[96,512]{1,0:T(8,128)(2,1)S(1)}, u32[]{:S(2)}, u32[]{:S(2)}) %collective-permute-start.10) | collective-permute-done | bytes 98336 | tf_op jit(solution)/shard_map/ppermute | solution.py:413
  62.1 2.1 %collective-permute-done.8.b_ref = bf16[96,512]{1,0:T(8,128)(2,1)S(1)} collective-permute-done((bf16[96,512]{1,0:T(8,128)(2,1)S(1)}, bf16[96,512]{1,0:T(8,128)(2,1)S(1)}, u32[]{:S(2)}, u32[]{:S(2)}) %collective-permute-start.8) | collective-permute-done | bytes 98336 | tf_op jit(solution)/shard_map/ppermute | solution.py:413
  64.3 1.2 %collective-permute-start.11 = (bf16[64,512]{1,0:T(8,128)(2,1)S(1)}, bf16[64,512]{1,0:T(8,128)(2,1)S(1)}, u32[]{:S(2)}, u32[]{:S(2)}) collective-permute-start(bf16[64,512]{1,0:T(8,128)(2,1)S(1)} %get-tuple-element.62.refs_0_), channel_id=1, source_target_pairs={{0,64},{64,0},{1,65},{65,1},{2,66},{66,2},{3,67},{67,3},{4,68},{68... | collective-permute-start | bytes 196616 | tf_op jit(solution)/shard_map/ppermute | solution.py:408
  65.5 2.7 %shard_map.87 = (f32[64,4096]{1,0:T(8,128)S(1)}, f32[64,64]{1,0:T(8,128)S(1)}, bf16[64,192]{1,0:T(8,128)(2,1)S(1)}, bf16[64,512]{1,0:T(8,128)(2,1)S(1)}) custom-call(bf16[64,512]{1,0:T(8,128)(2,1)S(1)} %get-tuple-element.62.refs_0_, f32[64,64]{1,0:T(8,128)S(1)} %get-tuple-element.63.refs_1_, ...), custom_call_target="tpu_custom_call" | custom-call | flops 273678336 | bytes 4276224 | tf_op jit(solution)/shard_map/pallas_call | solution.py:393
  69.4 1.0 collective-permute-done.12.got_ref
  70.5 11.4 %all_to_all.22.parts_ref = bf16[16,80,128]{2,1,0:T(8,128)(2,1)S(1)} all-to-all(bf16[16,80,128]{2,1,0:T(8,128)(2,1)S(1)} %shard_map.90), channel_id=1, replica_groups=mesh['dp'=2,'vocab'=16,'mp'=4] {'vocab'}, dimensions={0} | all-to-all | bytes 655360 | tf_op jit(solution)/shard_map/all_to_all | solution.py:456
  81.9 11.6 %all_to_all.23.own_ref = bf16[16,80,128]{2,1,0:T(8,128)(2,1)S(1)} all-to-all(bf16[16,80,128]{2,1,0:T(8,128)(2,1)S(1)} %shard_map.91), channel_id=1, replica_groups=mesh['dp'=2,'vocab'=16,'mp'=4] {'vocab'}, dimensions={0} | all-to-all | bytes 655360 | tf_op jit(solution)/shard_map/all_to_all | solution.py:458
  93.5 2.6 %collective-permute-start.13 = (bf16[16,80,128]{2,1,0:T(8,128)(2,1)S(1)}, bf16[16,80,128]{2,1,0:T(8,128)(2,1)S(1)}, u32[]{:S(2)}, u32[]{:S(2)}) collective-permute-start(bf16[16,80,128]{2,1,0:T(8,128)(2,1)S(1)} %all_to_all.23.own_ref), channel_id=1, source_target_pairs={{0,64},{64,0},{1,65},{65,1},{2,66},{66,2},{3,67},{67,3},{4,68},{68... | collective-permute-start | bytes 983048 | tf_op jit(solution)/shard_map/ppermute | solution.py:408
  96.1 2.6 %shard_map.92 = (bf16[64,192]{1,0:T(8,128)(2,1)S(1)}, f32[64,2048]{1,0:T(8,128)S(1)}, f32[64,64]{1,0:T(8,128)S(1)}, bf16[64,1024]{1,0:T(8,128)(2,1)S(1)}) custom-call(s32[1]{0:T(128)} %bitcast.me_ref.refs_0_, bf16[16,80,128]{2,1,0:T(8,128)(2,1)S(1)} %all_to_all.23.own_ref, bf16[64,512]{1,0:T(8,128)(2,1)S(1)} %get-tuple-element.71.rows_mine_ref, ...), custom_call_target="tpu_custom_call" | custom-call | flops 29360384 | bytes 458756 | tf_op jit(solution)/shard_map/pallas_call | solution.py:393
  98.8 0.9 shard_map.93
  100.3 1.3 %collective-permute-start.15 = (f32[64,64]{1,0:T(8,128)S(1)}, f32[64,64]{1,0:T(8,128)S(1)}, u32[]{:S(2)}, u32[]{:S(2)}) collective-permute-start(f32[64,64]{1,0:T(8,128)S(1)} %get-tuple-element.78.a_ref), channel_id=1, source_target_pairs={{0,3},{1,0},{2,1},{3,2},{4,7},{5,4},{6,5},{7,6},{8,11},{9,8},{10,9... | collective-permute-start | bytes 49160 | tf_op jit(solution)/shard_map/ppermute | solution.py:413
  101.7 3.7 %shard_map.94 = (bf16[1024,4096]{1,0:T(8,128)(2,1)}, f32[64,4096]{1,0:T(8,128)}, f32[64,4096]{1,0:T(8,128)}, bf16[1024,64]{1,0:T(8,128)(2,1)S(1)}) custom-call(s32[1]{0:T(128)} %bitcast.me_ref.refs_0_, f32[64,2048]{1,0:T(8,128)S(1)} %get-tuple-element.75.columns_ref.own_ref, bf16[64,1024]{1,0:T(8,128)(2,1)S(1)} %get-tuple-element.76.left_ref, ...), custom_call_target="tpu_custom_call" | custom-call | flops 176161024 | bytes 2752516 | tf_op jit(solution)/shard_map/pallas_call | solution.py:393
  105.5 4.6 %shard_map.95 = (bf16[1024,4096]{1,0:T(8,128)(2,1)}, f32[64,4096]{1,0:T(8,128)}, f32[64,4096]{1,0:T(8,128)}, f32[64,4096]{1,0:T(8,128)}) custom-call(s32[1]{0:T(128)} %bitcast.me_ref.refs_0_, f32[64,2048]{1,0:T(8,128)S(1)} %get-tuple-element.74.other_ref, ...), custom_call_target="tpu_custom_call", output_to_operand_aliasing={{0}: (10, {}), {1}: (11, {}), {2}: (12, {})} | custom-call | flops 884998400 | bytes 13828100 | tf_op jit(solution)/shard_map/pallas_call | solution.py:393
  (33 shorter events, 5.1 us)
Async XLA Ops:
  4.7 2.9 %collective-permute-start = (bf16[64,512]{1,0:T(8,128)(2,1)S(1)}, bf16[64,512]{1,0:T(8,128)(2,1)S(1)}, u32[]{:S(2)}, u32[]{:S(2)}) collective-permute-start(bf16[64,512]{1,0:T(8,128)(2,1)S(1)} %get-tuple-element.47), channel_id=1, source_target_pairs={{0,64},{64,0},{1,65},{65,1},{2,66},{66,2},{3,67},{67,3},{4,68},{68... | collective-permute-start | bytes 196616 | tf_op jit(solution)/shard_map/ppermute | solution.py:408
  7.6 5.3 %collective-permute-start.3 = (bf16[64,512]{1,0:T(8,128)(2,1)S(1)}, bf16[64,512]{1,0:T(8,128)(2,1)S(1)}, u32[]{:S(2)}, u32[]{:S(2)}) collective-permute-start(bf16[64,512]{1,0:T(8,128)(2,1)S(1)} %add_convert_fusion.1), channel_id=1, source_target_pairs={{0,2},{1,3},{2,0},{3,1},{4,6},{5,7},{6,4},{7,5},{8,10},{9,11},{10,... | collective-permute-start | bytes 196616 | tf_op jit(solution)/shard_map/ppermute | solution.py:413
  10.5 3.9 %collective-permute-start.2 = (bf16[64,512]{1,0:T(8,128)(2,1)S(1)}, bf16[64,512]{1,0:T(8,128)(2,1)S(1)}, u32[]{:S(2)}, u32[]{:S(2)}) collective-permute-start(bf16[64,512]{1,0:T(8,128)(2,1)S(1)} %add_convert_fusion.1), channel_id=1, source_target_pairs={{0,3},{1,0},{2,1},{3,2},{4,7},{5,4},{6,5},{7,6},{8,11},{9,8},{10,9... | collective-permute-start | bytes 196616 | tf_op jit(solution)/shard_map/ppermute | solution.py:413
  11.4 4.3 %collective-permute-start.1 = (bf16[64,512]{1,0:T(8,128)(2,1)S(1)}, bf16[64,512]{1,0:T(8,128)(2,1)S(1)}, u32[]{:S(2)}, u32[]{:S(2)}) collective-permute-start(bf16[64,512]{1,0:T(8,128)(2,1)S(1)} %add_convert_fusion.1), channel_id=1, source_target_pairs={{0,1},{1,2},{2,3},{3,0},{4,5},{5,6},{6,7},{7,4},{8,9},{9,10},{10,1... | collective-permute-start | bytes 196616 | tf_op jit(solution)/shard_map/ppermute | solution.py:413
  15.7 2.7 %collective-permute-start.4 = (bf16[64,512]{1,0:T(8,128)(2,1)S(1)}, bf16[64,512]{1,0:T(8,128)(2,1)S(1)}, u32[]{:S(2)}, u32[]{:S(2)}) collective-permute-start(bf16[64,512]{1,0:T(8,128)(2,1)S(1)} %add_convert_fusion.refs_0_), channel_id=1, source_target_pairs={{0,64},{64,0},{1,65},{65,1},{2,66},{66,2},{3,67},{67,3},{4,68},{68... | collective-permute-start | bytes 196616 | tf_op jit(solution)/shard_map/ppermute | solution.py:408
  19.0 1.6 %collective-permute-start.5 = (bf16[16,64,128]{2,1,0:T(8,128)(2,1)S(1)}, bf16[16,64,128]{2,1,0:T(8,128)(2,1)S(1)}, u32[]{:S(2)}, u32[]{:S(2)}) collective-permute-start(bf16[16,64,128]{2,1,0:T(8,128)(2,1)S(1)} %shard_map.79), channel_id=1, source_target_pairs={{0,64},{64,0},{1,65},{65,1},{2,66},{66,2},{3,67},{67,3},{4,68},{68... | collective-permute-start | bytes 786440 | tf_op jit(solution)/shard_map/ppermute | solution.py:408
  47.7 6.3 %collective-permute-start.6 = (bf16[16,80,128]{2,1,0:T(8,128)(2,1)S(1)}, bf16[16,80,128]{2,1,0:T(8,128)(2,1)S(1)}, u32[]{:S(2)}, u32[]{:S(2)}) collective-permute-start(bf16[16,80,128]{2,1,0:T(8,128)(2,1)S(1)} %all_to_all.21.own_ref), channel_id=1, source_target_pairs={{0,64},{64,0},{1,65},{65,1},{2,66},{66,2},{3,67},{67,3},{4,68},{68... | collective-permute-start | bytes 983048 | tf_op jit(solution)/shard_map/ppermute | solution.py:408
  54.9 1.3 %collective-permute-start.7 = (bf16[64,512]{1,0:T(8,128)(2,1)S(1)}, bf16[64,512]{1,0:T(8,128)(2,1)S(1)}, u32[]{:S(2)}, u32[]{:S(2)}) collective-permute-start(bf16[64,512]{1,0:T(8,128)(2,1)S(1)} %get-tuple-element.60), channel_id=1, source_target_pairs={{0,64},{64,0},{1,65},{65,1},{2,66},{66,2},{3,67},{67,3},{4,68},{68... | collective-permute-start | bytes 196616 | tf_op jit(solution)/shard_map/ppermute | solution.py:408
  56.3 5.8 %collective-permute-start.10 = (bf16[96,512]{1,0:T(8,128)(2,1)S(1)}, bf16[96,512]{1,0:T(8,128)(2,1)S(1)}, u32[]{:S(2)}, u32[]{:S(2)}) collective-permute-start(bf16[96,512]{1,0:T(8,128)(2,1)S(1)} %shard_map.85.a_ref), channel_id=1, source_target_pairs={{0,2},{1,3},{2,0},{3,1},{4,6},{5,7},{6,4},{7,5},{8,10},{9,11},{10,... | collective-permute-start | bytes 294920 | tf_op jit(solution)/shard_map/ppermute | solution.py:413
  56.9 5.2 %collective-permute-start.9 = (bf16[96,512]{1,0:T(8,128)(2,1)S(1)}, bf16[96,512]{1,0:T(8,128)(2,1)S(1)}, u32[]{:S(2)}, u32[]{:S(2)}) collective-permute-start(bf16[96,512]{1,0:T(8,128)(2,1)S(1)} %shard_map.85.a_ref), channel_id=1, source_target_pairs={{0,3},{1,0},{2,1},{3,2},{4,7},{5,4},{6,5},{7,6},{8,11},{9,8},{10,9... | collective-permute-start | bytes 294920 | tf_op jit(solution)/shard_map/ppermute | solution.py:413
  58.2 6.0 %collective-permute-start.8 = (bf16[96,512]{1,0:T(8,128)(2,1)S(1)}, bf16[96,512]{1,0:T(8,128)(2,1)S(1)}, u32[]{:S(2)}, u32[]{:S(2)}) collective-permute-start(bf16[96,512]{1,0:T(8,128)(2,1)S(1)} %shard_map.85.a_ref), channel_id=1, source_target_pairs={{0,1},{1,2},{2,3},{3,0},{4,5},{5,6},{6,7},{7,4},{8,9},{9,10},{10,1... | collective-permute-start | bytes 294920 | tf_op jit(solution)/shard_map/ppermute | solution.py:413
  64.3 3.9 %collective-permute-start.11 = (bf16[64,512]{1,0:T(8,128)(2,1)S(1)}, bf16[64,512]{1,0:T(8,128)(2,1)S(1)}, u32[]{:S(2)}, u32[]{:S(2)}) collective-permute-start(bf16[64,512]{1,0:T(8,128)(2,1)S(1)} %get-tuple-element.62.refs_0_), channel_id=1, source_target_pairs={{0,64},{64,0},{1,65},{65,1},{2,66},{66,2},{3,67},{67,3},{4,68},{68... | collective-permute-start | bytes 196616 | tf_op jit(solution)/shard_map/ppermute | solution.py:408
  68.2 33.6 %copy-start = (f32[64,4096]{1,0:T(8,128)S(1)}, f32[64,4096]{1,0:T(8,128)}, u32[]{:S(2)}) copy-start(f32[64,4096]{1,0:T(8,128)} %first_ref.3) | copy-start | bytes 3145732
  68.2 33.6 %copy-start.1 = (f32[64,4096]{1,0:T(8,128)S(1)}, f32[64,4096]{1,0:T(8,128)}, u32[]{:S(2)}) copy-start(f32[64,4096]{1,0:T(8,128)} %second_ref.3) | copy-start | bytes 3145732
  68.8 1.6 %collective-permute-start.12 = (bf16[16,64,128]{2,1,0:T(8,128)(2,1)S(1)}, bf16[16,64,128]{2,1,0:T(8,128)(2,1)S(1)}, u32[]{:S(2)}, u32[]{:S(2)}) collective-permute-start(bf16[16,64,128]{2,1,0:T(8,128)(2,1)S(1)} %get-tuple-element.69), channel_id=1, source_target_pairs={{0,64},{64,0},{1,65},{65,1},{2,66},{66,2},{3,67},{67,3},{4,68},{68... | collective-permute-start | bytes 786440 | tf_op jit(solution)/shard_map/ppermute | solution.py:408
  93.5 5.2 %collective-permute-start.13 = (bf16[16,80,128]{2,1,0:T(8,128)(2,1)S(1)}, bf16[16,80,128]{2,1,0:T(8,128)(2,1)S(1)}, u32[]{:S(2)}, u32[]{:S(2)}) collective-permute-start(bf16[16,80,128]{2,1,0:T(8,128)(2,1)S(1)} %all_to_all.23.own_ref), channel_id=1, source_target_pairs={{0,64},{64,0},{1,65},{65,1},{2,66},{66,2},{3,67},{67,3},{4,68},{68... | collective-permute-start | bytes 983048 | tf_op jit(solution)/shard_map/ppermute | solution.py:408
  99.7 5.7 %collective-permute-start.16 = (f32[64,64]{1,0:T(8,128)S(1)}, f32[64,64]{1,0:T(8,128)S(1)}, u32[]{:S(2)}, u32[]{:S(2)}) collective-permute-start(f32[64,64]{1,0:T(8,128)S(1)} %get-tuple-element.78.a_ref), channel_id=1, source_target_pairs={{0,2},{1,3},{2,0},{3,1},{4,6},{5,7},{6,4},{7,5},{8,10},{9,11},{10,... | collective-permute-start | bytes 49160 | tf_op jit(solution)/shard_map/ppermute | solution.py:413
  100.3 5.2 %collective-permute-start.15 = (f32[64,64]{1,0:T(8,128)S(1)}, f32[64,64]{1,0:T(8,128)S(1)}, u32[]{:S(2)}, u32[]{:S(2)}) collective-permute-start(f32[64,64]{1,0:T(8,128)S(1)} %get-tuple-element.78.a_ref), channel_id=1, source_target_pairs={{0,3},{1,0},{2,1},{3,2},{4,7},{5,4},{6,5},{7,6},{8,11},{9,8},{10,9... | collective-permute-start | bytes 49160 | tf_op jit(solution)/shard_map/ppermute | solution.py:413
  101.6 4.0 %collective-permute-start.14 = (f32[64,64]{1,0:T(8,128)S(1)}, f32[64,64]{1,0:T(8,128)S(1)}, u32[]{:S(2)}, u32[]{:S(2)}) collective-permute-start(f32[64,64]{1,0:T(8,128)S(1)} %get-tuple-element.78.a_ref), channel_id=1, source_target_pairs={{0,1},{1,2},{2,3},{3,0},{4,5},{5,6},{6,7},{7,4},{8,9},{9,10},{10,1... | collective-permute-start | bytes 49160 | tf_op jit(solution)/shard_map/ppermute | solution.py:413

commit v7 on v6

--- a/solution.py
+++ b/solution.py
@@ -14,6 +14,7 @@
 EXTRA = 16
 TILE = 512
 WIDE = 256
+PIECE = 1024
 VMEM_LIMIT = 28 * 1024 * 1024
 
 VMEM = pl.BlockSpec(memory_space=pltpu.VMEM)
@@ -45,27 +46,28 @@
         eye = jnp.where(lanes == subs[:, :rank] + 8 * b, 1.0, 0.0).astype(F32)
         both.append(jnp.concatenate([gram[8 * b : 8 * b + 8, :], eye], axis=1))
     scale = []
-    for b in range(blocks):
-        diag = jnp.ones((8, LANE), F32)
+    for b0 in range(0, blocks, 2):
+        diags = [jnp.ones((8, LANE), F32)] * 2
         cols = {
-            (j, i): jnp.broadcast_to(both[i][:, 8 * b + j : 8 * b + j + 1], (8, LANE))
-            for j in range(8)
-            for i in range(b, blocks)
+            (j, i): jnp.broadcast_to(both[i][:, 8 * b0 + j : 8 * b0 + j + 1], (8, LANE))
+            for j in range(16)
+            for i in range(b0, blocks)
         }
-        for j in range(8):
-            pivot = cols[j, b][j : j + 1, :]
+        for j in range(16):
+            b, s = b0 + j // 8, j % 8
+            pivot = cols[j, b][s : s + 1, :]
             inverse = 1.0 / pivot
-            diag = jnp.where(subs == j, pivot, diag)
-            row = both[b][j : j + 1, :] * inverse
-            heads = {m: cols[m, b][j : j + 1, :] * inverse for m in range(j + 1, 8)}
+            diags[j // 8] = jnp.where(subs == s, pivot, diags[j // 8])
+            row = both[b][s : s + 1, :] * inverse
+            heads = {m: cols[m, b][s : s + 1, :] * inverse for m in range(j + 1, 16)}
             for i in range(b, blocks):
                 f = cols[j, i]
                 if i == b:
-                    f = jnp.where(subs > j, f, 0.0)
+                    f = jnp.where(subs > s, f, 0.0)
                 both[i] = both[i] - f * row
-                for m in range(j + 1, 8):
+                for m in range(j + 1, 16):
                     cols[m, i] = cols[m, i] - f * heads[m]
-        scale.append(lax.rsqrt(diag))
+        scale.extend(lax.rsqrt(d) for d in diags)
     return jnp.concatenate(
         [both[b][:, rank:] * scale[b][:, :rank] for b in range(blocks)], axis=0
     )
@@ -144,7 +146,7 @@
         copy.wait()
     for t in range(0, half, WIDE):
         at = slice(t, t + WIDE)
-        theirs_ref[:, at] = dot(left, theirs_slab_ref[at, :], 1, 1).astype(BF16)
+        theirs_ref[:, at] = dot(theirs_slab_ref[at, :], left, 1, 1).T.astype(BF16)
     for copy in mine_copies:
         copy.wait()
 
@@ -152,7 +154,7 @@
 def first_mine_kernel(left_ref, slab_ref, mine_ref):
     left = left_ref[...]
     for t in range(0, mine_ref.shape[1], WIDE):
-        mine_ref[:, t : t + WIDE] = dot(left, slab_ref[t : t + WIDE, :], 1, 1)
+        mine_ref[:, t : t + WIDE] = dot(slab_ref[t : t + WIDE, :], left, 1, 1).T
 
 
 def columns_mine_kernel(orthogonal, *refs):
@@ -226,7 +228,7 @@
 def add_rows(columns, core, acc_ref, slab_ref, out_ref):
     at = span(core * columns.shape[1], columns.shape[1])
     for t in range(0, out_ref.shape[1], WIDE):
-        product = dot(columns, slab_ref[t : t + WIDE, at], 1, 1)
+        product = dot(slab_ref[t : t + WIDE, at], columns, 1, 1).T
         if acc_ref is not None:
             product = acc_ref[:, t : t + WIDE] + product
         out_ref[:, t : t + WIDE] = product.astype(out_ref.dtype)
@@ -322,51 +324,57 @@
     gram_ref[...] = gram_own_ref[...] + keep_columns(factor_ref[...], other_ref, columns_ref)
 
 
-def half_update(core, columns_ref, left, first_ref, second_ref, outs, buffers, sems):
+def update_pieces(pieces, left, first_ref, second_ref, outs, buffers, sems):
     corr_one = 1.0 - 0.9**10
     corr_two = 1.0 - 0.999**10
     update_ref, new_first_ref, new_second_ref = buffers
-    width = columns_ref.shape[1]
-    for t in range(0, width, TILE):
-        at = span(core * width + t, TILE)
-        columns = columns_ref[:, t : t + TILE]
-        new_first = 0.9 * first_ref[:, at] + 0.1 * columns
-        new_second = 0.999 * second_ref[:, at] + 0.001 * columns * columns
-        here = slice(t, t + TILE)
-        new_first_ref[:, here] = new_first
-        new_second_ref[:, here] = new_second
-        direction = new_first / corr_one / (jnp.sqrt(new_second / corr_two) + 1e-08)
-        update_ref[:, here] = dot(left, direction.astype(BF16), 1, 0).astype(BF16)
-    copies = [
-        pltpu.make_async_copy(ref, hbm.at[:, span(core * width, width)], sems.at[i])
-        for i, (ref, hbm) in enumerate(zip(buffers, outs))
-    ]
-    for copy in copies:
-        copy.start()
+    copies = []
+    for i, (base, columns_ref, start) in enumerate(pieces):
+        for t in range(0, PIECE, TILE):
+            at = span(base + start + t, TILE)
+            columns = columns_ref[:, start + t : start + t + TILE]
+            new_first = 0.9 * first_ref[:, at] + 0.1 * columns
+            new_second = 0.999 * second_ref[:, at] + 0.001 * columns * columns
+            here = slice(i * PIECE + t, i * PIECE + t + TILE)
+            new_first_ref[:, here] = new_first
+            new_second_ref[:, here] = new_second
+            direction = new_first / corr_one / (jnp.sqrt(new_second / corr_two) + 1e-08)
+            update_ref[:, here] = dot(left, direction.astype(BF16), 1, 0).astype(BF16)
+        here = slice(i * PIECE, (i + 1) * PIECE)
+        for j, (ref, hbm) in enumerate(zip(buffers, outs)):
+            copy = pltpu.make_async_copy(
+                ref.at[:, here], hbm.at[:, span(base + start, PIECE)], sems.at[3 * i + j]
+            )
+            copy.start()
+            copies.append(copy)
     return copies
 
 
-def update_own_kernel(me_ref, columns_ref, left_ref, first_ref, second_ref, *refs):
+def update_most_kernel(me_ref, own_ref, other_ref, left_ref, first_ref, second_ref, *refs):
     outs, turned_ref, buffers, sems = refs[:3], refs[3], refs[4:7], refs[7]
+    me = me_ref[0]
+    width = own_ref.shape[1]
     left = left_ref[...].T
     turned_ref[...] = left
-    copies = half_update(me_ref[0], columns_ref, left, first_ref, second_ref, outs, buffers, sems)
-    for copy in copies:
+    pieces = [(me * width, own_ref, t) for t in range(0, width, PIECE)]
+    pieces += [((1 - me) * width, other_ref, t) for t in range(0, width - PIECE, PIECE)]
+    for copy in update_pieces(pieces, left, first_ref, second_ref, outs, buffers, sems):
         copy.wait()
 
 
-def update_other_kernel(
-    me_ref, other_ref, turned_ref, first_ref, second_ref, own_ref, a_ref, b_ref, c_ref, d_ref, *refs
+def update_last_kernel(
+    me_ref, own_ref, other_ref, turned_ref, first_ref, second_ref, a_ref, b_ref, c_ref, d_ref, *refs
 ):
     me = me_ref[0]
     outs, basis_hbm, buffers, basis_ref, sems = refs[3:6], refs[6], refs[7:10], refs[10], refs[11]
-    copies = half_update(
-        1 - me, other_ref, turned_ref[...], first_ref, second_ref, outs, buffers, sems
+    width = own_ref.shape[1]
+    pieces = [((1 - me) * width, other_ref, width - PIECE)]
+    copies = update_pieces(
+        pieces, turned_ref[...], first_ref, second_ref, outs, buffers, sems
     )
     factor = inverse_factor((a_ref[...] + b_ref[...]) + (c_ref[...] + d_ref[...]))
     high, mid, _ = thirds(factor)
     wide = jnp.concatenate([high, high, mid], axis=1).astype(BF16)
-    width = own_ref.shape[1]
     for i, (core, ref) in enumerate(((me, own_ref), (1 - me, other_ref))):
         for t in range(0, width, TILE):
             high, mid, _ = thirds(ref[:, t : t + TILE])
@@ -521,21 +529,25 @@
     columns_other, gram = call(final_other_kernel, [narrow, square], [other, factor, gram])
     gram_others = others(gram)
     outs = [((vocab, width), BF16), wide, wide]
-    buffers = [((vocab, width // 2), BF16), narrow, narrow]
+
+    def buffers(columns):
+        return [((vocab, columns), BF16), ((rank, columns), F32), ((rank, columns), F32)]
+
     *begun, turned = call(
-        update_own_kernel,
+        update_most_kernel,
         outs + [((vocab, rank), BF16)],
-        [me, columns_own, left, first_moment, second_moment],
-        buffers + [pltpu.SemaphoreType.DMA((3,))],
+        [me, columns_own, columns_other, left, first_moment, second_moment],
+        buffers(width - PIECE) + [pltpu.SemaphoreType.DMA((3 * (width // PIECE - 1),))],
         hbm_out=(0, 1, 2),
     )
-    operands = [me, columns_other, turned, first_moment, second_moment, columns_own, gram, *gram_others]
+    operands = [me, columns_own, columns_other, turned, first_moment, second_moment]
+    operands += [gram, *gram_others]
     n = len(operands)
     update, new_first, new_second, basis = call(
-        update_other_kernel,
+        update_last_kernel,
         outs + [wide],
         operands + begun,
-        buffers + [wide, pltpu.SemaphoreType.DMA((5,))],
+        buffers(PIECE) + [wide, pltpu.SemaphoreType.DMA((5,))],
         hbm=(n, n + 1, n + 2),
         hbm_out=(0, 1, 2, 3),
         aliases={n: 0, n + 1: 1, n + 2: 2},

time: 111 us -> 109 us (0.982)
  Pallas kernels: 28.5 us -> 27.2 us
    pallas_call x21, Pallas kernels: 28.5 us -> 27.2 us  [call(): pl.pallas_call(kernel, out_shape=[jax.ShapeDtypeStruct(s, t) for s, t in...]
  transfers between devices with their start and end apart: 17 -> 17, of which waited for: 9 -> 8; matrix products, arithmetic and copies ran while one was open for 0% -> 0% of each run, Pallas kernels for 15% -> 15%
where the time goes in v7:
time: 109 us
  blocking collectives  50 us (46%)
  Pallas kernels  27.2 us (25%)
  starting transfers between devices  19.2 us (18%)
  waiting for transfers between devices  11.5 us (11%)
    pallas_call x21, Pallas kernels, call(): pl.pallas_call(kernel, out_shape=[jax.ShapeDtypeStruct(s, t) for s, t in...  27.2 us
    all_to_all x2, blocking collectives, columns_of(): parts = lax.all_to_all(chunks, 'vocab', 0, 0)  26.9 us
    all_to_all x2, blocking collectives, columns_of(): own = lax.all_to_all(copies, 'vocab', 0, 0)  23.1 us
    ppermute x8, starting transfers between devices, swapped(): return lax.ppermute(x, 'dp', [(0, 1), (1, 0)])  10.7 us
    ppermute x9, waiting for transfers between devices, others(): lax.ppermute(x, 'mp', [(i, (i + k) % n) for i in range(n)])  9.55 us
    ppermute x9, starting transfers between devices, others(): lax.ppermute(x, 'mp', [(i, (i + k) % n) for i in range(n)])  8.45 us
  transfers between devices with their start and end apart: 17, of which 8 were waited for; matrix products, arithmetic and copies ran while one was open for 0% of the time, Pallas kernels for 15%

profile of v7, /device:TPU:1, one launch (start us, length us, event | category | flops | bytes accessed | tf_op | source)
XLA Modules:
  0.0 108.9 jit_solution(12233449726461670517)
XLA Ops:
  0.6 4.0 %shard_map.75 = (bf16[64,512]{1,0:T(8,128)(2,1)S(1)}, bf16[64,4096]{1,0:T(8,128)(2,1)S(1)}, bf16[512,4096]{1,0:T(8,128)(2,1)S(1)}, bf16[512,4096]{1,0:T(8,128)(2,1)S(1)}) custom-call(s32[1]{0:T(128)} %bitcast.me_ref.refs_0_, f32[64,4096]{1,0:T(8,128)} %basis_hbm.1, bf16[1024,4096]{1,0:T(8,128)(2,1)} %bitcast.2), custom_call_target="tpu_custom_call" | custom-call | flops 603980032 | bytes 9437188 | tf_op jit(solution)/shard_map/pallas_call | solution.py:401
  4.7 1.5 %collective-permute-start = (bf16[64,512]{1,0:T(8,128)(2,1)S(1)}, bf16[64,512]{1,0:T(8,128)(2,1)S(1)}, u32[]{:S(2)}, u32[]{:S(2)}) collective-permute-start(bf16[64,512]{1,0:T(8,128)(2,1)S(1)} %get-tuple-element.47), channel_id=1, source_target_pairs={{0,64},{64,0},{1,65},{65,1},{2,66},{66,2},{3,67},{67,3},{4,68},{68... | collective-permute-start | bytes 196616 | tf_op jit(solution)/shard_map/ppermute | solution.py:416
  6.2 1.3 %shard_map.76 = f32[64,512]{1,0:T(8,128)S(1)} custom-call(bf16[64,4096]{1,0:T(8,128)(2,1)S(1)} %get-tuple-element.45.left_ref, bf16[512,4096]{1,0:T(8,128)(2,1)S(1)} %get-tuple-element.46.slab_ref.refs_1_.mine_slab_ref.refs_2_), custom_call_target="tpu_custom_call" | custom-call | flops 301989888 | bytes 4718592 | tf_op jit(solution)/shard_map/pallas_call | solution.py:401
  7.5 2.9 %collective-permute-start.3 = (bf16[64,512]{1,0:T(8,128)(2,1)S(1)}, bf16[64,512]{1,0:T(8,128)(2,1)S(1)}, u32[]{:S(2)}, u32[]{:S(2)}) collective-permute-start(bf16[64,512]{1,0:T(8,128)(2,1)S(1)} %add_convert_fusion.1), channel_id=1, source_target_pairs={{0,2},{1,3},{2,0},{3,1},{4,6},{5,7},{6,4},{7,5},{8,10},{9,11},{10,... | collective-permute-start | bytes 196616 | tf_op jit(solution)/shard_map/ppermute | solution.py:421
  10.4 0.9 collective-permute-start.2
  11.3 0.6 collective-permute-start.1
  11.9 0.9 collective-permute-done.3
  12.8 1.5 %collective-permute-done.2 = bf16[64,512]{1,0:T(8,128)(2,1)S(1)} collective-permute-done((bf16[64,512]{1,0:T(8,128)(2,1)S(1)}, bf16[64,512]{1,0:T(8,128)(2,1)S(1)}, u32[]{:S(2)}, u32[]{:S(2)}) %collective-permute-start.2) | collective-permute-done | bytes 65568 | tf_op jit(solution)/shard_map/ppermute | solution.py:421
  14.3 1.3 %collective-permute-done.1 = bf16[64,512]{1,0:T(8,128)(2,1)S(1)} collective-permute-done((bf16[64,512]{1,0:T(8,128)(2,1)S(1)}, bf16[64,512]{1,0:T(8,128)(2,1)S(1)}, u32[]{:S(2)}, u32[]{:S(2)}) %collective-permute-start.1) | collective-permute-done | bytes 65568 | tf_op jit(solution)/shard_map/ppermute | solution.py:421
  15.7 1.8 %collective-permute-start.4 = (bf16[64,512]{1,0:T(8,128)(2,1)S(1)}, bf16[64,512]{1,0:T(8,128)(2,1)S(1)}, u32[]{:S(2)}, u32[]{:S(2)}) collective-permute-start(bf16[64,512]{1,0:T(8,128)(2,1)S(1)} %add_convert_fusion.refs_0_), channel_id=1, source_target_pairs={{0,64},{64,0},{1,65},{65,1},{2,66},{66,2},{3,67},{67,3},{4,68},{68... | collective-permute-start | bytes 196616 | tf_op jit(solution)/shard_map/ppermute | solution.py:416
  17.5 0.9 shard_map.77
  19.8 0.7 collective-permute-done.5.got_ref
  20.5 15.5 %all_to_all.20.parts_ref = bf16[16,80,128]{2,1,0:T(8,128)(2,1)S(1)} all-to-all(bf16[16,80,128]{2,1,0:T(8,128)(2,1)S(1)} %shard_map.80), channel_id=1, replica_groups=mesh['dp'=2,'vocab'=16,'mp'=4] {'vocab'}, dimensions={0} | all-to-all | bytes 655360 | tf_op jit(solution)/shard_map/all_to_all | solution.py:464
  36.1 11.5 %all_to_all.21.own_ref = bf16[16,80,128]{2,1,0:T(8,128)(2,1)S(1)} all-to-all(bf16[16,80,128]{2,1,0:T(8,128)(2,1)S(1)} %shard_map.81), channel_id=1, replica_groups=mesh['dp'=2,'vocab'=16,'mp'=4] {'vocab'}, dimensions={0} | all-to-all | bytes 655360 | tf_op jit(solution)/shard_map/all_to_all | solution.py:466
  47.6 2.9 %collective-permute-start.6 = (bf16[16,80,128]{2,1,0:T(8,128)(2,1)S(1)}, bf16[16,80,128]{2,1,0:T(8,128)(2,1)S(1)}, u32[]{:S(2)}, u32[]{:S(2)}) collective-permute-start(bf16[16,80,128]{2,1,0:T(8,128)(2,1)S(1)} %all_to_all.21.own_ref), channel_id=1, source_target_pairs={{0,64},{64,0},{1,65},{65,1},{2,66},{66,2},{3,67},{67,3},{4,68},{68... | collective-permute-start | bytes 983048 | tf_op jit(solution)/shard_map/ppermute | solution.py:416
  50.6 3.2 %shard_map.82 = (bf16[64,192]{1,0:T(8,128)(2,1)S(1)}, f32[64,512]{1,0:T(8,128)S(1)}, f32[64,512]{1,0:T(8,128)S(1)}, f32[64,64]{1,0:T(8,128)S(1)}) custom-call(s32[1]{0:T(128)} %bitcast.me_ref.refs_0_, bf16[16,80,128]{2,1,0:T(8,128)(2,1)S(1)} %all_to_all.21.own_ref, bf16[512,4096]{1,0:T(8,128)(2,1)S(1)} %get-tuple-element.49.slab_ref.refs_3_.theirs_slab_ref, ...), custom_call_target="tpu_custom_call" | custom-call | flops 557842688 | bytes 8716292 | tf_op jit(solution)/shard_map/pallas_call | solution.py:401
  53.7 0.9 shard_map.83
  54.8 0.9 shard_map.84
  56.6 1.3 %collective-permute-start.9 = (bf16[96,512]{1,0:T(8,128)(2,1)S(1)}, bf16[96,512]{1,0:T(8,128)(2,1)S(1)}, u32[]{:S(2)}, u32[]{:S(2)}) collective-permute-start(bf16[96,512]{1,0:T(8,128)(2,1)S(1)} %shard_map.85.a_ref), channel_id=1, source_target_pairs={{0,3},{1,0},{2,1},{3,2},{4,7},{5,4},{6,5},{7,6},{8,11},{9,8},{10,9... | collective-permute-start | bytes 294920 | tf_op jit(solution)/shard_map/ppermute | solution.py:421
  58.1 3.7 %collective-permute-done.10.d_ref = bf16[96,512]{1,0:T(8,128)(2,1)S(1)} collective-permute-done((bf16[96,512]{1,0:T(8,128)(2,1)S(1)}, bf16[96,512]{1,0:T(8,128)(2,1)S(1)}, u32[]{:S(2)}, u32[]{:S(2)}) %collective-permute-start.10) | collective-permute-done | bytes 98336 | tf_op jit(solution)/shard_map/ppermute | solution.py:421
  61.8 2.1 %collective-permute-done.8.b_ref = bf16[96,512]{1,0:T(8,128)(2,1)S(1)} collective-permute-done((bf16[96,512]{1,0:T(8,128)(2,1)S(1)}, bf16[96,512]{1,0:T(8,128)(2,1)S(1)}, u32[]{:S(2)}, u32[]{:S(2)}) %collective-permute-start.8) | collective-permute-done | bytes 98336 | tf_op jit(solution)/shard_map/ppermute | solution.py:421
  64.0 1.3 %collective-permute-start.11 = (bf16[64,512]{1,0:T(8,128)(2,1)S(1)}, bf16[64,512]{1,0:T(8,128)(2,1)S(1)}, u32[]{:S(2)}, u32[]{:S(2)}) collective-permute-start(bf16[64,512]{1,0:T(8,128)(2,1)S(1)} %get-tuple-element.62.refs_0_), channel_id=1, source_target_pairs={{0,64},{64,0},{1,65},{65,1},{2,66},{66,2},{3,67},{67,3},{4,68},{68... | collective-permute-start | bytes 196616 | tf_op jit(solution)/shard_map/ppermute | solution.py:416
  65.3 2.5 %shard_map.87 = (f32[64,4096]{1,0:T(8,128)S(1)}, f32[64,64]{1,0:T(8,128)S(1)}, bf16[64,192]{1,0:T(8,128)(2,1)S(1)}, bf16[64,512]{1,0:T(8,128)(2,1)S(1)}) custom-call(bf16[64,512]{1,0:T(8,128)(2,1)S(1)} %get-tuple-element.62.refs_0_, f32[64,64]{1,0:T(8,128)S(1)} %get-tuple-element.63.refs_1_, ...), custom_call_target="tpu_custom_call" | custom-call | flops 273678336 | bytes 4276224 | tf_op jit(solution)/shard_map/pallas_call | solution.py:401
  69.0 1.0 collective-permute-done.12.got_ref
  70.1 11.4 %all_to_all.22.parts_ref = bf16[16,80,128]{2,1,0:T(8,128)(2,1)S(1)} all-to-all(bf16[16,80,128]{2,1,0:T(8,128)(2,1)S(1)} %shard_map.90), channel_id=1, replica_groups=mesh['dp'=2,'vocab'=16,'mp'=4] {'vocab'}, dimensions={0} | all-to-all | bytes 655360 | tf_op jit(solution)/shard_map/all_to_all | solution.py:464
  81.5 11.6 %all_to_all.23.own_ref = bf16[16,80,128]{2,1,0:T(8,128)(2,1)S(1)} all-to-all(bf16[16,80,128]{2,1,0:T(8,128)(2,1)S(1)} %shard_map.91), channel_id=1, replica_groups=mesh['dp'=2,'vocab'=16,'mp'=4] {'vocab'}, dimensions={0} | all-to-all | bytes 655360 | tf_op jit(solution)/shard_map/all_to_all | solution.py:466
  93.1 2.6 %collective-permute-start.13 = (bf16[16,80,128]{2,1,0:T(8,128)(2,1)S(1)}, bf16[16,80,128]{2,1,0:T(8,128)(2,1)S(1)}, u32[]{:S(2)}, u32[]{:S(2)}) collective-permute-start(bf16[16,80,128]{2,1,0:T(8,128)(2,1)S(1)} %all_to_all.23.own_ref), channel_id=1, source_target_pairs={{0,64},{64,0},{1,65},{65,1},{2,66},{66,2},{3,67},{67,3},{4,68},{68... | collective-permute-start | bytes 983048 | tf_op jit(solution)/shard_map/ppermute | solution.py:416
  95.7 2.4 %shard_map.92 = (bf16[64,192]{1,0:T(8,128)(2,1)S(1)}, f32[64,2048]{1,0:T(8,128)S(1)}, f32[64,64]{1,0:T(8,128)S(1)}, bf16[64,1024]{1,0:T(8,128)(2,1)S(1)}) custom-call(s32[1]{0:T(128)} %bitcast.me_ref.refs_0_, bf16[16,80,128]{2,1,0:T(8,128)(2,1)S(1)} %all_to_all.23.own_ref, bf16[64,512]{1,0:T(8,128)(2,1)S(1)} %get-tuple-element.71.rows_mine_ref, ...), custom_call_target="tpu_custom_call" | custom-call | flops 29360384 | bytes 458756 | tf_op jit(solution)/shard_map/pallas_call | solution.py:401
  98.2 0.9 shard_map.93
  99.7 1.3 %collective-permute-start.15 = (f32[64,64]{1,0:T(8,128)S(1)}, f32[64,64]{1,0:T(8,128)S(1)}, u32[]{:S(2)}, u32[]{:S(2)}) collective-permute-start(f32[64,64]{1,0:T(8,128)S(1)} %get-tuple-element.78.a_ref), channel_id=1, source_target_pairs={{0,3},{1,0},{2,1},{3,2},{4,7},{5,4},{6,5},{7,6},{8,11},{9,8},{10,9... | collective-permute-start | bytes 49160 | tf_op jit(solution)/shard_map/ppermute | solution.py:421
  101.2 4.0 %shard_map.94 = (bf16[1024,4096]{1,0:T(8,128)(2,1)}, f32[64,4096]{1,0:T(8,128)}, f32[64,4096]{1,0:T(8,128)}, bf16[1024,64]{1,0:T(8,128)(2,1)S(1)}) custom-call(s32[1]{0:T(128)} %bitcast.me_ref.refs_0_, f32[64,2048]{1,0:T(8,128)S(1)} %get-tuple-element.72.own_ref, f32[64,2048]{1,0:T(8,128)S(1)} %get-tuple-element.75.other_ref, ...), custom_call_target="tpu_custom_call" | custom-call | flops 209715456 | bytes 3276804 | tf_op jit(solution)/shard_map/pallas_call | solution.py:401
  105.2 3.5 %shard_map.95 = (bf16[1024,4096]{1,0:T(8,128)(2,1)}, f32[64,4096]{1,0:T(8,128)}, f32[64,4096]{1,0:T(8,128)}, f32[64,4096]{1,0:T(8,128)}) custom-call(s32[1]{0:T(128)} %bitcast.me_ref.refs_0_, f32[64,2048]{1,0:T(8,128)S(1)} %get-tuple-element.72.own_ref, ...), custom_call_target="tpu_custom_call", output_to_operand_aliasing={{0}: (10, {}), {1}: (11, {}), {2}: (12, {})} | custom-call | flops 884998400 | bytes 13828100 | tf_op jit(solution)/shard_map/pallas_call | solution.py:401
  (33 shorter events, 5.0 us)
Async XLA Ops:
  4.7 2.8 %collective-permute-start = (bf16[64,512]{1,0:T(8,128)(2,1)S(1)}, bf16[64,512]{1,0:T(8,128)(2,1)S(1)}, u32[]{:S(2)}, u32[]{:S(2)}) collective-permute-start(bf16[64,512]{1,0:T(8,128)(2,1)S(1)} %get-tuple-element.47), channel_id=1, source_target_pairs={{0,64},{64,0},{1,65},{65,1},{2,66},{66,2},{3,67},{67,3},{4,68},{68... | collective-permute-start | bytes 196616 | tf_op jit(solution)/shard_map/ppermute | solution.py:416
  7.5 5.3 %collective-permute-start.3 = (bf16[64,512]{1,0:T(8,128)(2,1)S(1)}, bf16[64,512]{1,0:T(8,128)(2,1)S(1)}, u32[]{:S(2)}, u32[]{:S(2)}) collective-permute-start(bf16[64,512]{1,0:T(8,128)(2,1)S(1)} %add_convert_fusion.1), channel_id=1, source_target_pairs={{0,2},{1,3},{2,0},{3,1},{4,6},{5,7},{6,4},{7,5},{8,10},{9,11},{10,... | collective-permute-start | bytes 196616 | tf_op jit(solution)/shard_map/ppermute | solution.py:421
  10.4 3.9 %collective-permute-start.2 = (bf16[64,512]{1,0:T(8,128)(2,1)S(1)}, bf16[64,512]{1,0:T(8,128)(2,1)S(1)}, u32[]{:S(2)}, u32[]{:S(2)}) collective-permute-start(bf16[64,512]{1,0:T(8,128)(2,1)S(1)} %add_convert_fusion.1), channel_id=1, source_target_pairs={{0,3},{1,0},{2,1},{3,2},{4,7},{5,4},{6,5},{7,6},{8,11},{9,8},{10,9... | collective-permute-start | bytes 196616 | tf_op jit(solution)/shard_map/ppermute | solution.py:421
  11.3 4.3 %collective-permute-start.1 = (bf16[64,512]{1,0:T(8,128)(2,1)S(1)}, bf16[64,512]{1,0:T(8,128)(2,1)S(1)}, u32[]{:S(2)}, u32[]{:S(2)}) collective-permute-start(bf16[64,512]{1,0:T(8,128)(2,1)S(1)} %add_convert_fusion.1), channel_id=1, source_target_pairs={{0,1},{1,2},{2,3},{3,0},{4,5},{5,6},{6,7},{7,4},{8,9},{9,10},{10,1... | collective-permute-start | bytes 196616 | tf_op jit(solution)/shard_map/ppermute | solution.py:421
  15.7 2.7 %collective-permute-start.4 = (bf16[64,512]{1,0:T(8,128)(2,1)S(1)}, bf16[64,512]{1,0:T(8,128)(2,1)S(1)}, u32[]{:S(2)}, u32[]{:S(2)}) collective-permute-start(bf16[64,512]{1,0:T(8,128)(2,1)S(1)} %add_convert_fusion.refs_0_), channel_id=1, source_target_pairs={{0,64},{64,0},{1,65},{65,1},{2,66},{66,2},{3,67},{67,3},{4,68},{68... | collective-permute-start | bytes 196616 | tf_op jit(solution)/shard_map/ppermute | solution.py:416
  18.9 1.6 %collective-permute-start.5 = (bf16[16,64,128]{2,1,0:T(8,128)(2,1)S(1)}, bf16[16,64,128]{2,1,0:T(8,128)(2,1)S(1)}, u32[]{:S(2)}, u32[]{:S(2)}) collective-permute-start(bf16[16,64,128]{2,1,0:T(8,128)(2,1)S(1)} %shard_map.79), channel_id=1, source_target_pairs={{0,64},{64,0},{1,65},{65,1},{2,66},{66,2},{3,67},{67,3},{4,68},{68... | collective-permute-start | bytes 786440 | tf_op jit(solution)/shard_map/ppermute | solution.py:416
  47.6 6.1 %collective-permute-start.6 = (bf16[16,80,128]{2,1,0:T(8,128)(2,1)S(1)}, bf16[16,80,128]{2,1,0:T(8,128)(2,1)S(1)}, u32[]{:S(2)}, u32[]{:S(2)}) collective-permute-start(bf16[16,80,128]{2,1,0:T(8,128)(2,1)S(1)} %all_to_all.21.own_ref), channel_id=1, source_target_pairs={{0,64},{64,0},{1,65},{65,1},{2,66},{66,2},{3,67},{67,3},{4,68},{68... | collective-permute-start | bytes 983048 | tf_op jit(solution)/shard_map/ppermute | solution.py:416
  54.7 1.3 %collective-permute-start.7 = (bf16[64,512]{1,0:T(8,128)(2,1)S(1)}, bf16[64,512]{1,0:T(8,128)(2,1)S(1)}, u32[]{:S(2)}, u32[]{:S(2)}) collective-permute-start(bf16[64,512]{1,0:T(8,128)(2,1)S(1)} %get-tuple-element.60), channel_id=1, source_target_pairs={{0,64},{64,0},{1,65},{65,1},{2,66},{66,2},{3,67},{67,3},{4,68},{68... | collective-permute-start | bytes 196616 | tf_op jit(solution)/shard_map/ppermute | solution.py:416
  56.0 5.8 %collective-permute-start.10 = (bf16[96,512]{1,0:T(8,128)(2,1)S(1)}, bf16[96,512]{1,0:T(8,128)(2,1)S(1)}, u32[]{:S(2)}, u32[]{:S(2)}) collective-permute-start(bf16[96,512]{1,0:T(8,128)(2,1)S(1)} %shard_map.85.a_ref), channel_id=1, source_target_pairs={{0,2},{1,3},{2,0},{3,1},{4,6},{5,7},{6,4},{7,5},{8,10},{9,11},{10,... | collective-permute-start | bytes 294920 | tf_op jit(solution)/shard_map/ppermute | solution.py:421
  56.6 5.2 %collective-permute-start.9 = (bf16[96,512]{1,0:T(8,128)(2,1)S(1)}, bf16[96,512]{1,0:T(8,128)(2,1)S(1)}, u32[]{:S(2)}, u32[]{:S(2)}) collective-permute-start(bf16[96,512]{1,0:T(8,128)(2,1)S(1)} %shard_map.85.a_ref), channel_id=1, source_target_pairs={{0,3},{1,0},{2,1},{3,2},{4,7},{5,4},{6,5},{7,6},{8,11},{9,8},{10,9... | collective-permute-start | bytes 294920 | tf_op jit(solution)/shard_map/ppermute | solution.py:421
  57.9 6.0 %collective-permute-start.8 = (bf16[96,512]{1,0:T(8,128)(2,1)S(1)}, bf16[96,512]{1,0:T(8,128)(2,1)S(1)}, u32[]{:S(2)}, u32[]{:S(2)}) collective-permute-start(bf16[96,512]{1,0:T(8,128)(2,1)S(1)} %shard_map.85.a_ref), channel_id=1, source_target_pairs={{0,1},{1,2},{2,3},{3,0},{4,5},{5,6},{6,7},{7,4},{8,9},{9,10},{10,1... | collective-permute-start | bytes 294920 | tf_op jit(solution)/shard_map/ppermute | solution.py:421
  64.0 3.8 %collective-permute-start.11 = (bf16[64,512]{1,0:T(8,128)(2,1)S(1)}, bf16[64,512]{1,0:T(8,128)(2,1)S(1)}, u32[]{:S(2)}, u32[]{:S(2)}) collective-permute-start(bf16[64,512]{1,0:T(8,128)(2,1)S(1)} %get-tuple-element.62.refs_0_), channel_id=1, source_target_pairs={{0,64},{64,0},{1,65},{65,1},{2,66},{66,2},{3,67},{67,3},{4,68},{68... | collective-permute-start | bytes 196616 | tf_op jit(solution)/shard_map/ppermute | solution.py:416
  67.8 33.4 %copy-start = (f32[64,4096]{1,0:T(8,128)S(1)}, f32[64,4096]{1,0:T(8,128)}, u32[]{:S(2)}) copy-start(f32[64,4096]{1,0:T(8,128)} %first_ref.3) | copy-start | bytes 3145732
  67.8 33.4 %copy-start.1 = (f32[64,4096]{1,0:T(8,128)S(1)}, f32[64,4096]{1,0:T(8,128)}, u32[]{:S(2)}) copy-start(f32[64,4096]{1,0:T(8,128)} %second_ref.3) | copy-start | bytes 3145732
  68.4 1.6 %collective-permute-start.12 = (bf16[16,64,128]{2,1,0:T(8,128)(2,1)S(1)}, bf16[16,64,128]{2,1,0:T(8,128)(2,1)S(1)}, u32[]{:S(2)}, u32[]{:S(2)}) collective-permute-start(bf16[16,64,128]{2,1,0:T(8,128)(2,1)S(1)} %get-tuple-element.69), channel_id=1, source_target_pairs={{0,64},{64,0},{1,65},{65,1},{2,66},{66,2},{3,67},{67,3},{4,68},{68... | collective-permute-start | bytes 786440 | tf_op jit(solution)/shard_map/ppermute | solution.py:416
  93.1 5.1 %collective-permute-start.13 = (bf16[16,80,128]{2,1,0:T(8,128)(2,1)S(1)}, bf16[16,80,128]{2,1,0:T(8,128)(2,1)S(1)}, u32[]{:S(2)}, u32[]{:S(2)}) collective-permute-start(bf16[16,80,128]{2,1,0:T(8,128)(2,1)S(1)} %all_to_all.23.own_ref), channel_id=1, source_target_pairs={{0,64},{64,0},{1,65},{65,1},{2,66},{66,2},{3,67},{67,3},{4,68},{68... | collective-permute-start | bytes 983048 | tf_op jit(solution)/shard_map/ppermute | solution.py:416
  99.1 6.0 %collective-permute-start.16 = (f32[64,64]{1,0:T(8,128)S(1)}, f32[64,64]{1,0:T(8,128)S(1)}, u32[]{:S(2)}, u32[]{:S(2)}) collective-permute-start(f32[64,64]{1,0:T(8,128)S(1)} %get-tuple-element.78.a_ref), channel_id=1, source_target_pairs={{0,2},{1,3},{2,0},{3,1},{4,6},{5,7},{6,4},{7,5},{8,10},{9,11},{10,... | collective-permute-start | bytes 49160 | tf_op jit(solution)/shard_map/ppermute | solution.py:421
  99.7 5.5 %collective-permute-start.15 = (f32[64,64]{1,0:T(8,128)S(1)}, f32[64,64]{1,0:T(8,128)S(1)}, u32[]{:S(2)}, u32[]{:S(2)}) collective-permute-start(f32[64,64]{1,0:T(8,128)S(1)} %get-tuple-element.78.a_ref), channel_id=1, source_target_pairs={{0,3},{1,0},{2,1},{3,2},{4,7},{5,4},{6,5},{7,6},{8,11},{9,8},{10,9... | collective-permute-start | bytes 49160 | tf_op jit(solution)/shard_map/ppermute | solution.py:421
  101.0 4.2 %collective-permute-start.14 = (f32[64,64]{1,0:T(8,128)S(1)}, f32[64,64]{1,0:T(8,128)S(1)}, u32[]{:S(2)}, u32[]{:S(2)}) collective-permute-start(f32[64,64]{1,0:T(8,128)S(1)} %get-tuple-element.78.a_ref), channel_id=1, source_target_pairs={{0,1},{1,2},{2,3},{3,0},{4,5},{5,6},{6,7},{7,4},{8,9},{9,10},{10,1... | collective-permute-start | bytes 49160 | tf_op jit(solution)/shard_map/ppermute | solution.py:421

commit v8 on v7

--- a/solution.py
+++ b/solution.py
@@ -15,6 +15,7 @@
 TILE = 512
 WIDE = 256
 PIECE = 1024
+PANEL = 16
 VMEM_LIMIT = 28 * 1024 * 1024
 
 VMEM = pl.BlockSpec(memory_space=pltpu.VMEM)
@@ -46,26 +47,26 @@
         eye = jnp.where(lanes == subs[:, :rank] + 8 * b, 1.0, 0.0).astype(F32)
         both.append(jnp.concatenate([gram[8 * b : 8 * b + 8, :], eye], axis=1))
     scale = []
-    for b0 in range(0, blocks, 2):
-        diags = [jnp.ones((8, LANE), F32)] * 2
+    for b0 in range(0, blocks, PANEL // 8):
+        diags = [jnp.ones((8, LANE), F32)] * (PANEL // 8)
         cols = {
             (j, i): jnp.broadcast_to(both[i][:, 8 * b0 + j : 8 * b0 + j + 1], (8, LANE))
-            for j in range(16)
+            for j in range(PANEL)
             for i in range(b0, blocks)
         }
-        for j in range(16):
+        for j in range(PANEL):
             b, s = b0 + j // 8, j % 8
             pivot = cols[j, b][s : s + 1, :]
             inverse = 1.0 / pivot
             diags[j // 8] = jnp.where(subs == s, pivot, diags[j // 8])
             row = both[b][s : s + 1, :] * inverse
-            heads = {m: cols[m, b][s : s + 1, :] * inverse for m in range(j + 1, 16)}
+            heads = {m: cols[m, b][s : s + 1, :] * inverse for m in range(j + 1, PANEL)}
             for i in range(b, blocks):
                 f = cols[j, i]
                 if i == b:
                     f = jnp.where(subs > s, f, 0.0)
                 both[i] = both[i] - f * row
-                for m in range(j + 1, 16):
+                for m in range(j + 1, PANEL):
                     cols[m, i] = cols[m, i] - f * heads[m]
         scale.extend(lax.rsqrt(d) for d in diags)
     return jnp.concatenate(
@@ -159,27 +160,26 @@
 
 def columns_mine_kernel(orthogonal, *refs):
     if orthogonal:
-        mine_ref, gram_in_ref, slab_ref, acc_ref, gram_ref, factor_ref, rows_ref = refs
+        me_ref, mine_ref, gram_in_ref, slab_ref, acc_ref, gram_ref, factor_ref, rows_ref = refs
         factor3 = stacked(inverse_factor(gram_in_ref[...]), 1)
         factor_ref[...] = factor3
         mine = applied(factor3, mine_ref[...]).astype(BF16)
         rows_ref[...] = mine
     else:
-        mine_ref, slab_ref, acc_ref, gram_ref = refs
+        me_ref, mine_ref, slab_ref, acc_ref, gram_ref = refs
         mine = mine_ref[...]
     gram_ref[...] = dot(mine, mine, 1, 1)
-    for t in range(0, acc_ref.shape[1], TILE):
-        acc_ref[:, t : t + TILE] = dot(mine, slab_ref[:, t : t + TILE], 1, 0)
-
-
-def add_half(core, rows, acc_ref, slab_ref, out_ref):
-    n = out_ref.shape[0]
+    width = acc_ref.shape[1]
+    for t in range(0, width, TILE):
+        at = span((1 - me_ref[0]) * width + t, TILE)
+        acc_ref[:, t : t + TILE] = dot(mine, slab_ref[:, at], 1, 0)
+
+
+def put_chunks(out_ref, j, product):
     per = TILE // LANE
-    for j in range(n // per):
-        at = span(core * (n * LANE) + j * TILE, TILE)
-        product = (acc_ref[:, at] + dot(rows, slab_ref[:, at], 1, 0)).astype(out_ref.dtype)
-        for q in range(per):
-            out_ref[j * per + q] = product[:, q * LANE : (q + 1) * LANE]
+    product = product.astype(out_ref.dtype)
+    for q in range(per):
+        out_ref[j * per + q] = product[:, q * LANE : (q + 1) * LANE]
 
 
 def columns_theirs_kernel(orthogonal, *refs):
@@ -190,20 +190,29 @@
     else:
         me_ref, other_ref, acc_ref, slab_ref, theirs_ref = refs
         other = other_ref[...]
-    add_half(1 - me_ref[0], other, acc_ref, slab_ref, theirs_ref)
+    width = acc_ref.shape[1]
+    for j in range(width // TILE):
+        at = span((1 - me_ref[0]) * width + j * TILE, TILE)
+        product = acc_ref[:, j * TILE : (j + 1) * TILE] + dot(other, slab_ref[:, at], 1, 0)
+        put_chunks(theirs_ref, j, product)
 
 
 def columns_owned_kernel(
-    me_ref, other_ref, acc_ref, slab_ref, gram_mine_ref, owned_ref, extra_ref, gram_ref
-):
-    other = other_ref[...]
+    me_ref, mine_ref, other_ref, theirs_slab_ref, mine_slab_ref, gram_mine_ref,
+    owned_ref, extra_ref, gram_ref,
+):
+    mine, other = mine_ref[...], other_ref[...]
     rank = other.shape[0]
     gram_ref[...] = jnp.zeros_like(gram_ref)
     gram_ref[:, :rank] = gram_mine_ref[...] + dot(other, other, 1, 1)
     each = rank // extra_ref.shape[0]
     for c in range(extra_ref.shape[0]):
         extra_ref[c] = extra_rows(gram_ref[c * each : (c + 1) * each, :])
-    add_half(me_ref[0], other, acc_ref, slab_ref, owned_ref)
+    width = theirs_slab_ref.shape[1] // 2
+    for j in range(width // TILE):
+        at = span(me_ref[0] * width + j * TILE, TILE)
+        product = dot(mine, mine_slab_ref[:, at], 1, 0) + dot(other, theirs_slab_ref[:, at], 1, 0)
+        put_chunks(owned_ref, j, product)
 
 
 def join_chunks_kernel(owned_ref, got_ref, extra_ref, out_ref):
@@ -427,7 +436,7 @@
     width = mine_slab.shape[1]
     orthogonal = gram is not None
     square = ((rank, rank), F32)
-    acc = ((rank, width), F32)
+    acc = ((rank, width // 2), F32)
     halves = ((rank, half), BF16)
     chunk = (owners, rank, LANE)
     whole = [((owners, rank + EXTRA, LANE), BF16)]
@@ -435,10 +444,10 @@
     other = swapped(mine)
     if orthogonal:
         outs = [acc, square, ((rank, 3 * rank), BF16), halves]
-        operands = [mine, gram, mine_slab]
+        operands = [me, mine, gram, mine_slab]
     else:
         outs = [acc, square]
-        operands = [mine, mine_slab]
+        operands = [me, mine, mine_slab]
     acc, gram_mine, *rest = call(functools.partial(columns_mine_kernel, orthogonal), outs, operands)
     if orthogonal:
         factor, mine = rest
@@ -457,7 +466,7 @@
     owned, extra = call(
         columns_owned_kernel,
         [(chunk, F32), ((owners, EXTRA, LANE), BF16)],
-        [me, other, acc, theirs_slab, gram_mine],
+        [me, mine, other, theirs_slab, mine_slab, gram_mine],
         [((rank, LANE), F32)],
     )
     chunks = call(join_chunks_kernel, whole, [owned, got, extra])[0]

time: 109 us -> 109 us (level)
  transfers between devices with their start and end apart: 17 -> 17, of which waited for: 8 -> 9; matrix products, arithmetic and copies ran while one was open for 0% -> 0% of each run, Pallas kernels for 15% -> 15%
where the time goes in v8:
time: 109 us
  blocking collectives  50 us (46%)
  Pallas kernels  27.1 us (25%)
  starting transfers between devices  19.2 us (18%)
  waiting for transfers between devices  11.2 us (10%)
    pallas_call x21, Pallas kernels, call(): pl.pallas_call(kernel, out_shape=[jax.ShapeDtypeStruct(s, t) for s, t in...  27.1 us
    all_to_all x2, blocking collectives, columns_of(): parts = lax.all_to_all(chunks, 'vocab', 0, 0)  26.9 us
    all_to_all x2, blocking collectives, columns_of(): own = lax.all_to_all(copies, 'vocab', 0, 0)  23.1 us
    ppermute x8, starting transfers between devices, swapped(): return lax.ppermute(x, 'dp', [(0, 1), (1, 0)])  10.7 us
    ppermute x9, waiting for transfers between devices, others(): lax.ppermute(x, 'mp', [(i, (i + k) % n) for i in range(n)])  9.55 us
    ppermute x9, starting transfers between devices, others(): lax.ppermute(x, 'mp', [(i, (i + k) % n) for i in range(n)])  8.46 us
  transfers between devices with their start and end apart: 17, of which 9 were waited for; matrix products, arithmetic and copies ran while one was open for 0% of the time, Pallas kernels for 15%

profile of v8, /device:TPU:1, one launch (start us, length us, event | category | flops | bytes accessed | tf_op | source)
XLA Modules:
  0.0 108.5 jit_solution(9140745226730573083)
XLA Ops:
  0.6 4.0 %shard_map.75 = (bf16[64,512]{1,0:T(8,128)(2,1)S(1)}, bf16[64,4096]{1,0:T(8,128)(2,1)S(1)}, bf16[512,4096]{1,0:T(8,128)(2,1)S(1)}, bf16[512,4096]{1,0:T(8,128)(2,1)S(1)}) custom-call(s32[1]{0:T(128)} %bitcast.me_ref.refs_0_, f32[64,4096]{1,0:T(8,128)} %basis_hbm.1, bf16[1024,4096]{1,0:T(8,128)(2,1)} %bitcast.2), custom_call_target="tpu_custom_call" | custom-call | flops 603980032 | bytes 9437188 | tf_op jit(solution)/shard_map/pallas_call | solution.py:410
  4.7 1.5 %collective-permute-start = (bf16[64,512]{1,0:T(8,128)(2,1)S(1)}, bf16[64,512]{1,0:T(8,128)(2,1)S(1)}, u32[]{:S(2)}, u32[]{:S(2)}) collective-permute-start(bf16[64,512]{1,0:T(8,128)(2,1)S(1)} %get-tuple-element.47), channel_id=1, source_target_pairs={{0,64},{64,0},{1,65},{65,1},{2,66},{66,2},{3,67},{67,3},{4,68},{68... | collective-permute-start | bytes 196616 | tf_op jit(solution)/shard_map/ppermute | solution.py:425
  6.2 1.3 %shard_map.76 = f32[64,512]{1,0:T(8,128)S(1)} custom-call(bf16[64,4096]{1,0:T(8,128)(2,1)S(1)} %get-tuple-element.45.left_ref, bf16[512,4096]{1,0:T(8,128)(2,1)S(1)} %get-tuple-element.46.slab_ref.refs_2_.mine_slab_ref.refs_3_), custom_call_target="tpu_custom_call" | custom-call | flops 301989888 | bytes 4718592 | tf_op jit(solution)/shard_map/pallas_call | solution.py:410
  7.5 2.9 %collective-permute-start.3 = (bf16[64,512]{1,0:T(8,128)(2,1)S(1)}, bf16[64,512]{1,0:T(8,128)(2,1)S(1)}, u32[]{:S(2)}, u32[]{:S(2)}) collective-permute-start(bf16[64,512]{1,0:T(8,128)(2,1)S(1)} %add_convert_fusion.1), channel_id=1, source_target_pairs={{0,2},{1,3},{2,0},{3,1},{4,6},{5,7},{6,4},{7,5},{8,10},{9,11},{10,... | collective-permute-start | bytes 196616 | tf_op jit(solution)/shard_map/ppermute | solution.py:430
  10.4 0.9 collective-permute-start.2
  11.3 0.6 collective-permute-start.1
  11.9 0.9 collective-permute-done.3
  12.8 1.5 %collective-permute-done.2 = bf16[64,512]{1,0:T(8,128)(2,1)S(1)} collective-permute-done((bf16[64,512]{1,0:T(8,128)(2,1)S(1)}, bf16[64,512]{1,0:T(8,128)(2,1)S(1)}, u32[]{:S(2)}, u32[]{:S(2)}) %collective-permute-start.2) | collective-permute-done | bytes 65568 | tf_op jit(solution)/shard_map/ppermute | solution.py:430
  14.3 1.3 %collective-permute-done.1 = bf16[64,512]{1,0:T(8,128)(2,1)S(1)} collective-permute-done((bf16[64,512]{1,0:T(8,128)(2,1)S(1)}, bf16[64,512]{1,0:T(8,128)(2,1)S(1)}, u32[]{:S(2)}, u32[]{:S(2)}) %collective-permute-start.1) | collective-permute-done | bytes 65568 | tf_op jit(solution)/shard_map/ppermute | solution.py:430
  15.7 1.8 %collective-permute-start.4 = (bf16[64,512]{1,0:T(8,128)(2,1)S(1)}, bf16[64,512]{1,0:T(8,128)(2,1)S(1)}, u32[]{:S(2)}, u32[]{:S(2)}) collective-permute-start(bf16[64,512]{1,0:T(8,128)(2,1)S(1)} %add_convert_fusion.refs_1_.mine_ref), channel_id=1, source_target_pairs={{0,64},{64,0},{1,65},{65,1},{2,66},{66,2},{3,67},{67,3},{4,68},{68... | collective-permute-start | bytes 196616 | tf_op jit(solution)/shard_map/ppermute | solution.py:425
  19.3 0.9 shard_map.78
  20.5 15.5 %all_to_all.20.parts_ref = bf16[16,80,128]{2,1,0:T(8,128)(2,1)S(1)} all-to-all(bf16[16,80,128]{2,1,0:T(8,128)(2,1)S(1)} %shard_map.80), channel_id=1, replica_groups=mesh['dp'=2,'vocab'=16,'mp'=4] {'vocab'}, dimensions={0} | all-to-all | bytes 655360 | tf_op jit(solution)/shard_map/all_to_all | solution.py:473
  36.1 11.5 %all_to_all.21.own_ref = bf16[16,80,128]{2,1,0:T(8,128)(2,1)S(1)} all-to-all(bf16[16,80,128]{2,1,0:T(8,128)(2,1)S(1)} %shard_map.81), channel_id=1, replica_groups=mesh['dp'=2,'vocab'=16,'mp'=4] {'vocab'}, dimensions={0} | all-to-all | bytes 655360 | tf_op jit(solution)/shard_map/all_to_all | solution.py:475
  47.6 2.9 %collective-permute-start.6 = (bf16[16,80,128]{2,1,0:T(8,128)(2,1)S(1)}, bf16[16,80,128]{2,1,0:T(8,128)(2,1)S(1)}, u32[]{:S(2)}, u32[]{:S(2)}) collective-permute-start(bf16[16,80,128]{2,1,0:T(8,128)(2,1)S(1)} %all_to_all.21.own_ref), channel_id=1, source_target_pairs={{0,64},{64,0},{1,65},{65,1},{2,66},{66,2},{3,67},{67,3},{4,68},{68... | collective-permute-start | bytes 983048 | tf_op jit(solution)/shard_map/ppermute | solution.py:425
  50.6 3.2 %shard_map.82 = (bf16[64,192]{1,0:T(8,128)(2,1)S(1)}, f32[64,512]{1,0:T(8,128)S(1)}, f32[64,512]{1,0:T(8,128)S(1)}, f32[64,64]{1,0:T(8,128)S(1)}) custom-call(s32[1]{0:T(128)} %bitcast.me_ref.refs_0_, bf16[16,80,128]{2,1,0:T(8,128)(2,1)S(1)} %all_to_all.21.own_ref, bf16[512,4096]{1,0:T(8,128)(2,1)S(1)} %get-tuple-element.48.theirs_slab_ref.refs_3_.slab_ref, ...), custom_call_target="tpu_custom_call" | custom-call | flops 557842688 | bytes 8716292 | tf_op jit(solution)/shard_map/pallas_call | solution.py:410
  53.7 0.9 shard_map.83
  54.8 0.9 shard_map.84
  56.6 1.3 %collective-permute-start.9 = (bf16[96,512]{1,0:T(8,128)(2,1)S(1)}, bf16[96,512]{1,0:T(8,128)(2,1)S(1)}, u32[]{:S(2)}, u32[]{:S(2)}) collective-permute-start(bf16[96,512]{1,0:T(8,128)(2,1)S(1)} %shard_map.85.a_ref), channel_id=1, source_target_pairs={{0,3},{1,0},{2,1},{3,2},{4,7},{5,4},{6,5},{7,6},{8,11},{9,8},{10,9... | collective-permute-start | bytes 294920 | tf_op jit(solution)/shard_map/ppermute | solution.py:430
  58.1 3.7 %collective-permute-done.10.d_ref = bf16[96,512]{1,0:T(8,128)(2,1)S(1)} collective-permute-done((bf16[96,512]{1,0:T(8,128)(2,1)S(1)}, bf16[96,512]{1,0:T(8,128)(2,1)S(1)}, u32[]{:S(2)}, u32[]{:S(2)}) %collective-permute-start.10) | collective-permute-done | bytes 98336 | tf_op jit(solution)/shard_map/ppermute | solution.py:430
  61.8 2.1 %collective-permute-done.8.b_ref = bf16[96,512]{1,0:T(8,128)(2,1)S(1)} collective-permute-done((bf16[96,512]{1,0:T(8,128)(2,1)S(1)}, bf16[96,512]{1,0:T(8,128)(2,1)S(1)}, u32[]{:S(2)}, u32[]{:S(2)}) %collective-permute-start.8) | collective-permute-done | bytes 98336 | tf_op jit(solution)/shard_map/ppermute | solution.py:430
  64.0 1.3 %collective-permute-start.11 = (bf16[64,512]{1,0:T(8,128)(2,1)S(1)}, bf16[64,512]{1,0:T(8,128)(2,1)S(1)}, u32[]{:S(2)}, u32[]{:S(2)}) collective-permute-start(bf16[64,512]{1,0:T(8,128)(2,1)S(1)} %get-tuple-element.62.refs_1_), channel_id=1, source_target_pairs={{0,64},{64,0},{1,65},{65,1},{2,66},{66,2},{3,67},{67,3},{4,68},{68... | collective-permute-start | bytes 196616 | tf_op jit(solution)/shard_map/ppermute | solution.py:425
  65.3 2.1 %shard_map.87 = (f32[64,2048]{1,0:T(8,128)S(1)}, f32[64,64]{1,0:T(8,128)S(1)}, bf16[64,192]{1,0:T(8,128)(2,1)S(1)}, bf16[64,512]{1,0:T(8,128)(2,1)S(1)}) custom-call(s32[1]{0:T(128)} %bitcast.me_ref.refs_0_, bf16[64,512]{1,0:T(8,128)(2,1)S(1)} %get-tuple-element.62.refs_1_, f32[64,64]{1,0:T(8,128)S(1)} %get-tuple-element.63.refs_2_, ...), custom_call_target="tpu_custom_call" | custom-call | flops 273678592 | bytes 4276228 | tf_op jit(solution)/shard_map/pallas_call | solution.py:410
  68.1 0.9 shard_map.89
  69.0 0.6 collective-permute-done.12.got_ref
  69.7 11.4 %all_to_all.22.parts_ref = bf16[16,80,128]{2,1,0:T(8,128)(2,1)S(1)} all-to-all(bf16[16,80,128]{2,1,0:T(8,128)(2,1)S(1)} %shard_map.90), channel_id=1, replica_groups=mesh['dp'=2,'vocab'=16,'mp'=4] {'vocab'}, dimensions={0} | all-to-all | bytes 655360 | tf_op jit(solution)/shard_map/all_to_all | solution.py:473
  81.1 11.6 %all_to_all.23.own_ref = bf16[16,80,128]{2,1,0:T(8,128)(2,1)S(1)} all-to-all(bf16[16,80,128]{2,1,0:T(8,128)(2,1)S(1)} %shard_map.91), channel_id=1, replica_groups=mesh['dp'=2,'vocab'=16,'mp'=4] {'vocab'}, dimensions={0} | all-to-all | bytes 655360 | tf_op jit(solution)/shard_map/all_to_all | solution.py:475
  92.7 2.6 %collective-permute-start.13 = (bf16[16,80,128]{2,1,0:T(8,128)(2,1)S(1)}, bf16[16,80,128]{2,1,0:T(8,128)(2,1)S(1)}, u32[]{:S(2)}, u32[]{:S(2)}) collective-permute-start(bf16[16,80,128]{2,1,0:T(8,128)(2,1)S(1)} %all_to_all.23.own_ref), channel_id=1, source_target_pairs={{0,64},{64,0},{1,65},{65,1},{2,66},{66,2},{3,67},{67,3},{4,68},{68... | collective-permute-start | bytes 983048 | tf_op jit(solution)/shard_map/ppermute | solution.py:425
  95.4 2.4 %shard_map.92 = (bf16[64,192]{1,0:T(8,128)(2,1)S(1)}, f32[64,2048]{1,0:T(8,128)S(1)}, f32[64,64]{1,0:T(8,128)S(1)}, bf16[64,1024]{1,0:T(8,128)(2,1)S(1)}) custom-call(s32[1]{0:T(128)} %bitcast.me_ref.refs_0_, bf16[16,80,128]{2,1,0:T(8,128)(2,1)S(1)} %all_to_all.23.own_ref, bf16[64,512]{1,0:T(8,128)(2,1)S(1)} %get-tuple-element.64.mine_ref.rows_mine_ref, ...), custom_call_target="tpu_custom_call" | custom-call | flops 29360384 | bytes 458756 | tf_op jit(solution)/shard_map/pallas_call | solution.py:410
  97.8 0.9 shard_map.93
  99.3 1.3 %collective-permute-start.15 = (f32[64,64]{1,0:T(8,128)S(1)}, f32[64,64]{1,0:T(8,128)S(1)}, u32[]{:S(2)}, u32[]{:S(2)}) collective-permute-start(f32[64,64]{1,0:T(8,128)S(1)} %get-tuple-element.78.a_ref), channel_id=1, source_target_pairs={{0,3},{1,0},{2,1},{3,2},{4,7},{5,4},{6,5},{7,6},{8,11},{9,8},{10,9... | collective-permute-start | bytes 49160 | tf_op jit(solution)/shard_map/ppermute | solution.py:430
  100.8 4.0 %shard_map.94 = (bf16[1024,4096]{1,0:T(8,128)(2,1)}, f32[64,4096]{1,0:T(8,128)}, f32[64,4096]{1,0:T(8,128)}, bf16[1024,64]{1,0:T(8,128)(2,1)S(1)}) custom-call(s32[1]{0:T(128)} %bitcast.me_ref.refs_0_, f32[64,2048]{1,0:T(8,128)S(1)} %get-tuple-element.72.own_ref, f32[64,2048]{1,0:T(8,128)S(1)} %get-tuple-element.75.other_ref, ...), custom_call_target="tpu_custom_call" | custom-call | flops 209715456 | bytes 3276804 | tf_op jit(solution)/shard_map/pallas_call | solution.py:410
  104.8 3.5 %shard_map.95 = (bf16[1024,4096]{1,0:T(8,128)(2,1)}, f32[64,4096]{1,0:T(8,128)}, f32[64,4096]{1,0:T(8,128)}, f32[64,4096]{1,0:T(8,128)}) custom-call(s32[1]{0:T(128)} %bitcast.me_ref.refs_0_, f32[64,2048]{1,0:T(8,128)S(1)} %get-tuple-element.72.own_ref, ...), custom_call_target="tpu_custom_call", output_to_operand_aliasing={{0}: (10, {}), {1}: (11, {}), {2}: (12, {})} | custom-call | flops 884998400 | bytes 13828100 | tf_op jit(solution)/shard_map/pallas_call | solution.py:410
  (33 shorter events, 5.2 us)
Async XLA Ops:
  4.7 2.8 %collective-permute-start = (bf16[64,512]{1,0:T(8,128)(2,1)S(1)}, bf16[64,512]{1,0:T(8,128)(2,1)S(1)}, u32[]{:S(2)}, u32[]{:S(2)}) collective-permute-start(bf16[64,512]{1,0:T(8,128)(2,1)S(1)} %get-tuple-element.47), channel_id=1, source_target_pairs={{0,64},{64,0},{1,65},{65,1},{2,66},{66,2},{3,67},{67,3},{4,68},{68... | collective-permute-start | bytes 196616 | tf_op jit(solution)/shard_map/ppermute | solution.py:425
  7.5 5.3 %collective-permute-start.3 = (bf16[64,512]{1,0:T(8,128)(2,1)S(1)}, bf16[64,512]{1,0:T(8,128)(2,1)S(1)}, u32[]{:S(2)}, u32[]{:S(2)}) collective-permute-start(bf16[64,512]{1,0:T(8,128)(2,1)S(1)} %add_convert_fusion.1), channel_id=1, source_target_pairs={{0,2},{1,3},{2,0},{3,1},{4,6},{5,7},{6,4},{7,5},{8,10},{9,11},{10,... | collective-permute-start | bytes 196616 | tf_op jit(solution)/shard_map/ppermute | solution.py:430
  10.4 3.9 %collective-permute-start.2 = (bf16[64,512]{1,0:T(8,128)(2,1)S(1)}, bf16[64,512]{1,0:T(8,128)(2,1)S(1)}, u32[]{:S(2)}, u32[]{:S(2)}) collective-permute-start(bf16[64,512]{1,0:T(8,128)(2,1)S(1)} %add_convert_fusion.1), channel_id=1, source_target_pairs={{0,3},{1,0},{2,1},{3,2},{4,7},{5,4},{6,5},{7,6},{8,11},{9,8},{10,9... | collective-permute-start | bytes 196616 | tf_op jit(solution)/shard_map/ppermute | solution.py:430
  11.3 4.3 %collective-permute-start.1 = (bf16[64,512]{1,0:T(8,128)(2,1)S(1)}, bf16[64,512]{1,0:T(8,128)(2,1)S(1)}, u32[]{:S(2)}, u32[]{:S(2)}) collective-permute-start(bf16[64,512]{1,0:T(8,128)(2,1)S(1)} %add_convert_fusion.1), channel_id=1, source_target_pairs={{0,1},{1,2},{2,3},{3,0},{4,5},{5,6},{6,7},{7,4},{8,9},{9,10},{10,1... | collective-permute-start | bytes 196616 | tf_op jit(solution)/shard_map/ppermute | solution.py:430
  15.7 2.7 %collective-permute-start.4 = (bf16[64,512]{1,0:T(8,128)(2,1)S(1)}, bf16[64,512]{1,0:T(8,128)(2,1)S(1)}, u32[]{:S(2)}, u32[]{:S(2)}) collective-permute-start(bf16[64,512]{1,0:T(8,128)(2,1)S(1)} %add_convert_fusion.refs_1_.mine_ref), channel_id=1, source_target_pairs={{0,64},{64,0},{1,65},{65,1},{2,66},{66,2},{3,67},{67,3},{4,68},{68... | collective-permute-start | bytes 196616 | tf_op jit(solution)/shard_map/ppermute | solution.py:425
  18.9 1.6 %collective-permute-start.5 = (bf16[16,64,128]{2,1,0:T(8,128)(2,1)S(1)}, bf16[16,64,128]{2,1,0:T(8,128)(2,1)S(1)}, u32[]{:S(2)}, u32[]{:S(2)}) collective-permute-start(bf16[16,64,128]{2,1,0:T(8,128)(2,1)S(1)} %shard_map.79), channel_id=1, source_target_pairs={{0,64},{64,0},{1,65},{65,1},{2,66},{66,2},{3,67},{67,3},{4,68},{68... | collective-permute-start | bytes 786440 | tf_op jit(solution)/shard_map/ppermute | solution.py:425
  47.6 6.1 %collective-permute-start.6 = (bf16[16,80,128]{2,1,0:T(8,128)(2,1)S(1)}, bf16[16,80,128]{2,1,0:T(8,128)(2,1)S(1)}, u32[]{:S(2)}, u32[]{:S(2)}) collective-permute-start(bf16[16,80,128]{2,1,0:T(8,128)(2,1)S(1)} %all_to_all.21.own_ref), channel_id=1, source_target_pairs={{0,64},{64,0},{1,65},{65,1},{2,66},{66,2},{3,67},{67,3},{4,68},{68... | collective-permute-start | bytes 983048 | tf_op jit(solution)/shard_map/ppermute | solution.py:425
  54.7 1.3 %collective-permute-start.7 = (bf16[64,512]{1,0:T(8,128)(2,1)S(1)}, bf16[64,512]{1,0:T(8,128)(2,1)S(1)}, u32[]{:S(2)}, u32[]{:S(2)}) collective-permute-start(bf16[64,512]{1,0:T(8,128)(2,1)S(1)} %get-tuple-element.60), channel_id=1, source_target_pairs={{0,64},{64,0},{1,65},{65,1},{2,66},{66,2},{3,67},{67,3},{4,68},{68... | collective-permute-start | bytes 196616 | tf_op jit(solution)/shard_map/ppermute | solution.py:425
  56.0 5.8 %collective-permute-start.10 = (bf16[96,512]{1,0:T(8,128)(2,1)S(1)}, bf16[96,512]{1,0:T(8,128)(2,1)S(1)}, u32[]{:S(2)}, u32[]{:S(2)}) collective-permute-start(bf16[96,512]{1,0:T(8,128)(2,1)S(1)} %shard_map.85.a_ref), channel_id=1, source_target_pairs={{0,2},{1,3},{2,0},{3,1},{4,6},{5,7},{6,4},{7,5},{8,10},{9,11},{10,... | collective-permute-start | bytes 294920 | tf_op jit(solution)/shard_map/ppermute | solution.py:430
  56.6 5.2 %collective-permute-start.9 = (bf16[96,512]{1,0:T(8,128)(2,1)S(1)}, bf16[96,512]{1,0:T(8,128)(2,1)S(1)}, u32[]{:S(2)}, u32[]{:S(2)}) collective-permute-start(bf16[96,512]{1,0:T(8,128)(2,1)S(1)} %shard_map.85.a_ref), channel_id=1, source_target_pairs={{0,3},{1,0},{2,1},{3,2},{4,7},{5,4},{6,5},{7,6},{8,11},{9,8},{10,9... | collective-permute-start | bytes 294920 | tf_op jit(solution)/shard_map/ppermute | solution.py:430
  57.9 6.0 %collective-permute-start.8 = (bf16[96,512]{1,0:T(8,128)(2,1)S(1)}, bf16[96,512]{1,0:T(8,128)(2,1)S(1)}, u32[]{:S(2)}, u32[]{:S(2)}) collective-permute-start(bf16[96,512]{1,0:T(8,128)(2,1)S(1)} %shard_map.85.a_ref), channel_id=1, source_target_pairs={{0,1},{1,2},{2,3},{3,0},{4,5},{5,6},{6,7},{7,4},{8,9},{9,10},{10,1... | collective-permute-start | bytes 294920 | tf_op jit(solution)/shard_map/ppermute | solution.py:430
  64.0 3.4 %collective-permute-start.11 = (bf16[64,512]{1,0:T(8,128)(2,1)S(1)}, bf16[64,512]{1,0:T(8,128)(2,1)S(1)}, u32[]{:S(2)}, u32[]{:S(2)}) collective-permute-start(bf16[64,512]{1,0:T(8,128)(2,1)S(1)} %get-tuple-element.62.refs_1_), channel_id=1, source_target_pairs={{0,64},{64,0},{1,65},{65,1},{2,66},{66,2},{3,67},{67,3},{4,68},{68... | collective-permute-start | bytes 196616 | tf_op jit(solution)/shard_map/ppermute | solution.py:425
  67.4 33.4 %copy-start = (f32[64,4096]{1,0:T(8,128)S(1)}, f32[64,4096]{1,0:T(8,128)}, u32[]{:S(2)}) copy-start(f32[64,4096]{1,0:T(8,128)} %first_ref.3) | copy-start | bytes 3145732
  67.4 33.4 %copy-start.1 = (f32[64,4096]{1,0:T(8,128)S(1)}, f32[64,4096]{1,0:T(8,128)}, u32[]{:S(2)}) copy-start(f32[64,4096]{1,0:T(8,128)} %second_ref.3) | copy-start | bytes 3145732
  68.0 1.6 %collective-permute-start.12 = (bf16[16,64,128]{2,1,0:T(8,128)(2,1)S(1)}, bf16[16,64,128]{2,1,0:T(8,128)(2,1)S(1)}, u32[]{:S(2)}, u32[]{:S(2)}) collective-permute-start(bf16[16,64,128]{2,1,0:T(8,128)(2,1)S(1)} %get-tuple-element.70), channel_id=1, source_target_pairs={{0,64},{64,0},{1,65},{65,1},{2,66},{66,2},{3,67},{67,3},{4,68},{68... | collective-permute-start | bytes 786440 | tf_op jit(solution)/shard_map/ppermute | solution.py:425
  92.7 5.1 %collective-permute-start.13 = (bf16[16,80,128]{2,1,0:T(8,128)(2,1)S(1)}, bf16[16,80,128]{2,1,0:T(8,128)(2,1)S(1)}, u32[]{:S(2)}, u32[]{:S(2)}) collective-permute-start(bf16[16,80,128]{2,1,0:T(8,128)(2,1)S(1)} %all_to_all.23.own_ref), channel_id=1, source_target_pairs={{0,64},{64,0},{1,65},{65,1},{2,66},{66,2},{3,67},{67,3},{4,68},{68... | collective-permute-start | bytes 983048 | tf_op jit(solution)/shard_map/ppermute | solution.py:425
  98.8 6.0 %collective-permute-start.16 = (f32[64,64]{1,0:T(8,128)S(1)}, f32[64,64]{1,0:T(8,128)S(1)}, u32[]{:S(2)}, u32[]{:S(2)}) collective-permute-start(f32[64,64]{1,0:T(8,128)S(1)} %get-tuple-element.78.a_ref), channel_id=1, source_target_pairs={{0,2},{1,3},{2,0},{3,1},{4,6},{5,7},{6,4},{7,5},{8,10},{9,11},{10,... | collective-permute-start | bytes 49160 | tf_op jit(solution)/shard_map/ppermute | solution.py:430
  99.3 5.5 %collective-permute-start.15 = (f32[64,64]{1,0:T(8,128)S(1)}, f32[64,64]{1,0:T(8,128)S(1)}, u32[]{:S(2)}, u32[]{:S(2)}) collective-permute-start(f32[64,64]{1,0:T(8,128)S(1)} %get-tuple-element.78.a_ref), channel_id=1, source_target_pairs={{0,3},{1,0},{2,1},{3,2},{4,7},{5,4},{6,5},{7,6},{8,11},{9,8},{10,9... | collective-permute-start | bytes 49160 | tf_op jit(solution)/shard_map/ppermute | solution.py:430
  100.6 4.2 %collective-permute-start.14 = (f32[64,64]{1,0:T(8,128)S(1)}, f32[64,64]{1,0:T(8,128)S(1)}, u32[]{:S(2)}, u32[]{:S(2)}) collective-permute-start(f32[64,64]{1,0:T(8,128)S(1)} %get-tuple-element.78.a_ref), channel_id=1, source_target_pairs={{0,1},{1,2},{2,3},{3,0},{4,5},{5,6},{6,7},{7,4},{8,9},{9,10},{10,1... | collective-permute-start | bytes 49160 | tf_op jit(solution)/shard_map/ppermute | solution.py:430

commit v9 on v8

--- a/solution.py
+++ b/solution.py
@@ -281,10 +281,43 @@
     for t in range(0, width, TILE):
         total = total + gram_of(columns_ref, slice(t, t + TILE))
     gram = gram_own_ref[...] + folded(total, rank)
-    gram = jnp.concatenate([gram[: rank // 2], gram[rank // 2 :]], axis=1)
-    pack_ref[...] = jnp.zeros_like(pack_ref)
-    pack_ref[:, : 3 * LANE] = stacked(gram, 1)
+    pack_ref[...] = packed_gram(gram).astype(BF16)
     add_rows(half_ref[...], 1 - me_ref[0], acc_ref, slab_ref, mine_ref)
+
+
+def square_places(size):
+    return (lax.broadcasted_iota(jnp.int32, (size, size), i) for i in range(2))
+
+
+def packed_gram(gram):
+    size = gram.shape[0] // 2
+    row, column = square_places(size)
+    low, corner = gram[size:, :size], gram[size:, size:]
+    mixed = jnp.where(row >= column, gram[:size, :size], corner)
+    diagonal = jnp.sum(jnp.where(row == column, corner, 0.0), axis=1, keepdims=True)
+    lanes = lax.broadcasted_iota(jnp.int32, (size, 2 * size), 1)
+    tail = jnp.zeros((size, 2 * size), F32)
+    for i, part in enumerate(thirds(diagonal)):
+        tail = jnp.where(lanes == i, part, tail)
+    full = jnp.concatenate([*thirds(jnp.concatenate([low, mixed], axis=1)), tail], axis=1)
+    return jnp.concatenate([full[: size // 2], full[size // 2 :]], axis=1)
+
+
+def unpacked_gram(e, rank):
+    size = rank // 2
+    row, column = square_places(size)
+    full = jnp.concatenate([e[:, : 4 * rank], e[:, 4 * rank :]], axis=0)
+    both = full[:, :rank] + full[:, rank : 2 * rank] + full[:, 2 * rank : 3 * rank]
+    tail = full[:, 3 * rank :]
+    diagonal = tail[:, 0:1] + tail[:, 1:2] + tail[:, 2:3]
+    turned = both.T
+    low, mixed = both[:, :size], both[:, size:]
+    first = jnp.where(row >= column, mixed, turned[size:])
+    corner = jnp.where(row < column, mixed, jnp.where(row > column, turned[size:], diagonal))
+    return jnp.concatenate(
+        [jnp.concatenate([first, turned[:size]], axis=1), jnp.concatenate([low, corner], axis=1)],
+        axis=0,
+    )
 
 
 def join_rows_kernel(mine_ref, got_ref, pack_ref, out_ref):
@@ -299,9 +332,7 @@
     )
     rank = rows_ref.shape[0]
     rows_ref[...] = total[:rank].astype(BF16)
-    e = total[rank:]
-    g = e[:, :LANE] + e[:, LANE : 2 * LANE] + e[:, 2 * LANE : 3 * LANE]
-    gram_ref[...] = jnp.concatenate([g[:, :rank], g[:, rank:]], axis=0)
+    gram_ref[...] = unpacked_gram(total[rank:], rank)
 
 
 def final_own_kernel(
@@ -338,52 +369,59 @@
     corr_two = 1.0 - 0.999**10
     update_ref, new_first_ref, new_second_ref = buffers
     copies = []
-    for i, (base, columns_ref, start) in enumerate(pieces):
-        for t in range(0, PIECE, TILE):
+    put = 0
+    for i, (base, columns_ref, start, size) in enumerate(pieces):
+        for t in range(0, size, TILE):
             at = span(base + start + t, TILE)
             columns = columns_ref[:, start + t : start + t + TILE]
             new_first = 0.9 * first_ref[:, at] + 0.1 * columns
             new_second = 0.999 * second_ref[:, at] + 0.001 * columns * columns
-            here = slice(i * PIECE + t, i * PIECE + t + TILE)
+            here = slice(put + t, put + t + TILE)
             new_first_ref[:, here] = new_first
             new_second_ref[:, here] = new_second
             direction = new_first / corr_one / (jnp.sqrt(new_second / corr_two) + 1e-08)
             update_ref[:, here] = dot(left, direction.astype(BF16), 1, 0).astype(BF16)
-        here = slice(i * PIECE, (i + 1) * PIECE)
+        here = slice(put, put + size)
+        put += size
         for j, (ref, hbm) in enumerate(zip(buffers, outs)):
             copy = pltpu.make_async_copy(
-                ref.at[:, here], hbm.at[:, span(base + start, PIECE)], sems.at[3 * i + j]
+                ref.at[:, here], hbm.at[:, piece_at(base + start, size)], sems.at[3 * i + j]
             )
             copy.start()
             copies.append(copy)
     return copies
 
 
-def update_most_kernel(me_ref, own_ref, other_ref, left_ref, first_ref, second_ref, *refs):
-    outs, turned_ref, buffers, sems = refs[:3], refs[3], refs[4:7], refs[7]
+def piece_at(base, size):
+    return pl.ds(pl.multiple_of(base, TILE), size)
+
+
+def cuts(width):
+    start = 0
+    while start < width:
+        size = PIECE if width - start > PIECE else TILE
+        yield start, size
+        start += size
+
+
+def update_kernel(me_ref, own_ref, other_ref, left_ref, first_ref, second_ref, *refs):
+    outs, buffers, sems = refs[:3], refs[3:6], refs[6]
     me = me_ref[0]
     width = own_ref.shape[1]
     left = left_ref[...].T
-    turned_ref[...] = left
-    pieces = [(me * width, own_ref, t) for t in range(0, width, PIECE)]
-    pieces += [((1 - me) * width, other_ref, t) for t in range(0, width - PIECE, PIECE)]
+    pieces = [(me * width, own_ref, t, PIECE) for t in range(0, width, PIECE)]
+    pieces += [((1 - me) * width, other_ref, t, size) for t, size in cuts(width)]
     for copy in update_pieces(pieces, left, first_ref, second_ref, outs, buffers, sems):
         copy.wait()
 
 
-def update_last_kernel(
-    me_ref, own_ref, other_ref, turned_ref, first_ref, second_ref, a_ref, b_ref, c_ref, d_ref, *refs
-):
+def basis_kernel(me_ref, own_ref, other_ref, a_ref, b_ref, c_ref, d_ref, basis_hbm, basis_ref, sems):
     me = me_ref[0]
-    outs, basis_hbm, buffers, basis_ref, sems = refs[3:6], refs[6], refs[7:10], refs[10], refs[11]
     width = own_ref.shape[1]
-    pieces = [((1 - me) * width, other_ref, width - PIECE)]
-    copies = update_pieces(
-        pieces, turned_ref[...], first_ref, second_ref, outs, buffers, sems
-    )
     factor = inverse_factor((a_ref[...] + b_ref[...]) + (c_ref[...] + d_ref[...]))
     high, mid, _ = thirds(factor)
     wide = jnp.concatenate([high, high, mid], axis=1).astype(BF16)
+    copies = []
     for i, (core, ref) in enumerate(((me, own_ref), (1 - me, other_ref))):
         for t in range(0, width, TILE):
             high, mid, _ = thirds(ref[:, t : t + TILE])
@@ -392,7 +430,7 @@
         copy = pltpu.make_async_copy(
             basis_ref.at[:, i * width : (i + 1) * width],
             basis_hbm.at[:, span(core * width, width)],
-            sems.at[3 + i],
+            sems.at[i],
         )
         copy.start()
         copies.append(copy)
@@ -521,10 +559,10 @@
     got = swapped(theirs)
     mine, pack = call(
         rows_mine_kernel,
-        [mine_out, ((rank // 2, half), BF16)],
+        [mine_out, ((EXTRA, half), BF16)],
         [me, columns_half, columns, gram, mine_acc, mine_slab],
     )
-    mine = call(join_rows_kernel, [((rank + rank // 2, half), BF16)], [mine, got, pack])[0]
+    mine = call(join_rows_kernel, [((rank + EXTRA, half), BF16)], [mine, got, pack])[0]
     mine, gram = call(sum_packed_kernel, [theirs_out, square], [mine, *others(mine)])
     own, other, rows_mine, rows_other = columns_of(me, mine, slabs, owners, gram)
 
@@ -542,25 +580,20 @@
     def buffers(columns):
         return [((vocab, columns), BF16), ((rank, columns), F32), ((rank, columns), F32)]
 
-    *begun, turned = call(
-        update_most_kernel,
-        outs + [((vocab, rank), BF16)],
+    update, new_first, new_second = call(
+        update_kernel,
+        outs,
         [me, columns_own, columns_other, left, first_moment, second_moment],
-        buffers(width - PIECE) + [pltpu.SemaphoreType.DMA((3 * (width // PIECE - 1),))],
+        buffers(width) + [pltpu.SemaphoreType.DMA((3 * (width // TILE),))],
         hbm_out=(0, 1, 2),
     )
-    operands = [me, columns_own, columns_other, turned, first_moment, second_moment]
-    operands += [gram, *gram_others]
-    n = len(operands)
-    update, new_first, new_second, basis = call(
-        update_last_kernel,
-        outs + [wide],
-        operands + begun,
-        buffers(PIECE) + [wide, pltpu.SemaphoreType.DMA((5,))],
-        hbm=(n, n + 1, n + 2),
-        hbm_out=(0, 1, 2, 3),
-        aliases={n: 0, n + 1: 1, n + 2: 2},
-    )
+    basis = call(
+        basis_kernel,
+        [wide],
+        [me, columns_own, columns_other, gram, *gram_others],
+        [wide, pltpu.SemaphoreType.DMA((2,))],
+        hbm_out=(0,),
+    )[0]
     return (update, basis, new_first, new_second)
 
 

time: 109 us -> 108 us (level)
  waiting for transfers between devices: 11.2 us -> 9.95 us
    ppermute x9, waiting for transfers between devices: 9.55 us -> 8.33 us  [others(): lax.ppermute(x, 'mp', [(i, (i + k) % n) for i in range(n)])]
  transfers between devices with their start and end apart: 17 -> 17, of which waited for: 9 -> 9; matrix products, arithmetic and copies ran while one was open for 0% -> 0% of each run, Pallas kernels for 15% -> 16%
where the time goes in v9:
time: 108 us
  blocking collectives  50 us (46%)
  Pallas kernels  27.4 us (25%)
  starting transfers between devices  19.8 us (18%)
  waiting for transfers between devices  9.95 us (9%)
    pallas_call x21, Pallas kernels, call(): pl.pallas_call(kernel, out_shape=[jax.ShapeDtypeStruct(s, t) for s, t in...  27.4 us
    all_to_all x2, blocking collectives, columns_of(): parts = lax.all_to_all(chunks, 'vocab', 0, 0)  26.9 us
    all_to_all x2, blocking collectives, columns_of(): own = lax.all_to_all(copies, 'vocab', 0, 0)  23.1 us
    ppermute x8, starting transfers between devices, swapped(): return lax.ppermute(x, 'dp', [(0, 1), (1, 0)])  11.4 us
    ppermute x9, starting transfers between devices, others(): lax.ppermute(x, 'mp', [(i, (i + k) % n) for i in range(n)])  8.36 us
    ppermute x9, waiting for transfers between devices, others(): lax.ppermute(x, 'mp', [(i, (i + k) % n) for i in range(n)])  8.33 us
  transfers between devices with their start and end apart: 17, of which 9 were waited for; matrix products, arithmetic and copies ran while one was open for 0% of the time, Pallas kernels for 16%

profile of v9, /device:TPU:1, one launch (start us, length us, event | category | flops | bytes accessed | tf_op | source)
XLA Modules:
  0.0 108.1 jit_solution(13313956987747709793)
XLA Ops:
  0.6 4.0 %shard_map.75 = (bf16[64,512]{1,0:T(8,128)(2,1)S(1)}, bf16[64,4096]{1,0:T(8,128)(2,1)S(1)}, bf16[512,4096]{1,0:T(8,128)(2,1)S(1)}, bf16[512,4096]{1,0:T(8,128)(2,1)S(1)}) custom-call(s32[1]{0:T(128)} %bitcast.me_ref.refs_0_, f32[64,4096]{1,0:T(8,128)} %basis_hbm.1, bf16[1024,4096]{1,0:T(8,128)(2,1)} %bitcast.2), custom_call_target="tpu_custom_call" | custom-call | flops 603980032 | bytes 9437188 | tf_op jit(solution)/shard_map/pallas_call | solution.py:448
  4.7 1.5 %collective-permute-start = (bf16[64,512]{1,0:T(8,128)(2,1)S(1)}, bf16[64,512]{1,0:T(8,128)(2,1)S(1)}, u32[]{:S(2)}, u32[]{:S(2)}) collective-permute-start(bf16[64,512]{1,0:T(8,128)(2,1)S(1)} %get-tuple-element.42), channel_id=1, source_target_pairs={{0,64},{64,0},{1,65},{65,1},{2,66},{66,2},{3,67},{67,3},{4,68},{68... | collective-permute-start | bytes 196616 | tf_op jit(solution)/shard_map/ppermute | solution.py:463
  6.2 1.3 %shard_map.76 = f32[64,512]{1,0:T(8,128)S(1)} custom-call(bf16[64,4096]{1,0:T(8,128)(2,1)S(1)} %get-tuple-element.40.left_ref, bf16[512,4096]{1,0:T(8,128)(2,1)S(1)} %get-tuple-element.41.slab_ref.refs_2_.mine_slab_ref.refs_3_), custom_call_target="tpu_custom_call" | custom-call | flops 301989888 | bytes 4718592 | tf_op jit(solution)/shard_map/pallas_call | solution.py:448
  7.5 2.9 %collective-permute-start.3 = (bf16[64,512]{1,0:T(8,128)(2,1)S(1)}, bf16[64,512]{1,0:T(8,128)(2,1)S(1)}, u32[]{:S(2)}, u32[]{:S(2)}) collective-permute-start(bf16[64,512]{1,0:T(8,128)(2,1)S(1)} %add_convert_fusion.1), channel_id=1, source_target_pairs={{0,2},{1,3},{2,0},{3,1},{4,6},{5,7},{6,4},{7,5},{8,10},{9,11},{10,... | collective-permute-start | bytes 196616 | tf_op jit(solution)/shard_map/ppermute | solution.py:468
  10.4 0.9 collective-permute-start.2
  11.3 0.6 collective-permute-start.1
  11.9 0.9 collective-permute-done.3
  12.8 1.5 %collective-permute-done.2 = bf16[64,512]{1,0:T(8,128)(2,1)S(1)} collective-permute-done((bf16[64,512]{1,0:T(8,128)(2,1)S(1)}, bf16[64,512]{1,0:T(8,128)(2,1)S(1)}, u32[]{:S(2)}, u32[]{:S(2)}) %collective-permute-start.2) | collective-permute-done | bytes 65568 | tf_op jit(solution)/shard_map/ppermute | solution.py:468
  14.3 1.3 %collective-permute-done.1 = bf16[64,512]{1,0:T(8,128)(2,1)S(1)} collective-permute-done((bf16[64,512]{1,0:T(8,128)(2,1)S(1)}, bf16[64,512]{1,0:T(8,128)(2,1)S(1)}, u32[]{:S(2)}, u32[]{:S(2)}) %collective-permute-start.1) | collective-permute-done | bytes 65568 | tf_op jit(solution)/shard_map/ppermute | solution.py:468
  15.7 1.8 %collective-permute-start.4 = (bf16[64,512]{1,0:T(8,128)(2,1)S(1)}, bf16[64,512]{1,0:T(8,128)(2,1)S(1)}, u32[]{:S(2)}, u32[]{:S(2)}) collective-permute-start(bf16[64,512]{1,0:T(8,128)(2,1)S(1)} %add_convert_fusion.refs_1_.mine_ref), channel_id=1, source_target_pairs={{0,64},{64,0},{1,65},{65,1},{2,66},{66,2},{3,67},{67,3},{4,68},{68... | collective-permute-start | bytes 196616 | tf_op jit(solution)/shard_map/ppermute | solution.py:463
  19.3 0.9 shard_map.78
  20.5 15.5 %all_to_all.20.parts_ref = bf16[16,80,128]{2,1,0:T(8,128)(2,1)S(1)} all-to-all(bf16[16,80,128]{2,1,0:T(8,128)(2,1)S(1)} %shard_map.80), channel_id=1, replica_groups=mesh['dp'=2,'vocab'=16,'mp'=4] {'vocab'}, dimensions={0} | all-to-all | bytes 655360 | tf_op jit(solution)/shard_map/all_to_all | solution.py:511
  36.1 11.5 %all_to_all.21.own_ref = bf16[16,80,128]{2,1,0:T(8,128)(2,1)S(1)} all-to-all(bf16[16,80,128]{2,1,0:T(8,128)(2,1)S(1)} %shard_map.81), channel_id=1, replica_groups=mesh['dp'=2,'vocab'=16,'mp'=4] {'vocab'}, dimensions={0} | all-to-all | bytes 655360 | tf_op jit(solution)/shard_map/all_to_all | solution.py:513
  47.6 2.9 %collective-permute-start.6 = (bf16[16,80,128]{2,1,0:T(8,128)(2,1)S(1)}, bf16[16,80,128]{2,1,0:T(8,128)(2,1)S(1)}, u32[]{:S(2)}, u32[]{:S(2)}) collective-permute-start(bf16[16,80,128]{2,1,0:T(8,128)(2,1)S(1)} %all_to_all.21.own_ref), channel_id=1, source_target_pairs={{0,64},{64,0},{1,65},{65,1},{2,66},{66,2},{3,67},{67,3},{4,68},{68... | collective-permute-start | bytes 983048 | tf_op jit(solution)/shard_map/ppermute | solution.py:463
  50.6 3.2 %shard_map.82 = (bf16[64,192]{1,0:T(8,128)(2,1)S(1)}, f32[64,512]{1,0:T(8,128)S(1)}, f32[64,512]{1,0:T(8,128)S(1)}, f32[64,64]{1,0:T(8,128)S(1)}) custom-call(s32[1]{0:T(128)} %bitcast.me_ref.refs_0_, bf16[16,80,128]{2,1,0:T(8,128)(2,1)S(1)} %all_to_all.21.own_ref, bf16[512,4096]{1,0:T(8,128)(2,1)S(1)} %get-tuple-element.43.theirs_slab_ref.refs_3_.slab_ref, ...), custom_call_target="tpu_custom_call" | custom-call | flops 557842688 | bytes 8716292 | tf_op jit(solution)/shard_map/pallas_call | solution.py:448
  53.7 0.9 shard_map.83
  54.8 1.0 shard_map.84
  56.6 1.3 %collective-permute-start.9 = (bf16[80,512]{1,0:T(8,128)(2,1)S(1)}, bf16[80,512]{1,0:T(8,128)(2,1)S(1)}, u32[]{:S(2)}, u32[]{:S(2)}) collective-permute-start(bf16[80,512]{1,0:T(8,128)(2,1)S(1)} %shard_map.85.a_ref), channel_id=1, source_target_pairs={{0,3},{1,0},{2,1},{3,2},{4,7},{5,4},{6,5},{7,6},{8,11},{9,8},{10,9... | collective-permute-start | bytes 245768 | tf_op jit(solution)/shard_map/ppermute | solution.py:468
  58.1 3.3 %collective-permute-done.10.d_ref = bf16[80,512]{1,0:T(8,128)(2,1)S(1)} collective-permute-done((bf16[80,512]{1,0:T(8,128)(2,1)S(1)}, bf16[80,512]{1,0:T(8,128)(2,1)S(1)}, u32[]{:S(2)}, u32[]{:S(2)}) %collective-permute-start.10) | collective-permute-done | bytes 81952 | tf_op jit(solution)/shard_map/ppermute | solution.py:468
  61.4 1.3 %collective-permute-done.8.b_ref = bf16[80,512]{1,0:T(8,128)(2,1)S(1)} collective-permute-done((bf16[80,512]{1,0:T(8,128)(2,1)S(1)}, bf16[80,512]{1,0:T(8,128)(2,1)S(1)}, u32[]{:S(2)}, u32[]{:S(2)}) %collective-permute-start.8) | collective-permute-done | bytes 81952 | tf_op jit(solution)/shard_map/ppermute | solution.py:468
  63.0 1.9 %collective-permute-start.11 = (bf16[64,512]{1,0:T(8,128)(2,1)S(1)}, bf16[64,512]{1,0:T(8,128)(2,1)S(1)}, u32[]{:S(2)}, u32[]{:S(2)}) collective-permute-start(bf16[64,512]{1,0:T(8,128)(2,1)S(1)} %get-tuple-element.57.refs_1_), channel_id=1, source_target_pairs={{0,64},{64,0},{1,65},{65,1},{2,66},{66,2},{3,67},{67,3},{4,68},{68... | collective-permute-start | bytes 196616 | tf_op jit(solution)/shard_map/ppermute | solution.py:463
  64.9 2.1 %shard_map.87 = (f32[64,2048]{1,0:T(8,128)S(1)}, f32[64,64]{1,0:T(8,128)S(1)}, bf16[64,192]{1,0:T(8,128)(2,1)S(1)}, bf16[64,512]{1,0:T(8,128)(2,1)S(1)}) custom-call(s32[1]{0:T(128)} %bitcast.me_ref.refs_0_, bf16[64,512]{1,0:T(8,128)(2,1)S(1)} %get-tuple-element.57.refs_1_, f32[64,64]{1,0:T(8,128)S(1)} %get-tuple-element.58.refs_2_, ...), custom_call_target="tpu_custom_call" | custom-call | flops 273678592 | bytes 4276228 | tf_op jit(solution)/shard_map/pallas_call | solution.py:448
  67.8 0.9 shard_map.89
  68.7 0.6 collective-permute-done.12.got_ref
  69.4 11.4 %all_to_all.22.parts_ref = bf16[16,80,128]{2,1,0:T(8,128)(2,1)S(1)} all-to-all(bf16[16,80,128]{2,1,0:T(8,128)(2,1)S(1)} %shard_map.90), channel_id=1, replica_groups=mesh['dp'=2,'vocab'=16,'mp'=4] {'vocab'}, dimensions={0} | all-to-all | bytes 655360 | tf_op jit(solution)/shard_map/all_to_all | solution.py:511
  80.8 11.6 %all_to_all.23.own_ref = bf16[16,80,128]{2,1,0:T(8,128)(2,1)S(1)} all-to-all(bf16[16,80,128]{2,1,0:T(8,128)(2,1)S(1)} %shard_map.91), channel_id=1, replica_groups=mesh['dp'=2,'vocab'=16,'mp'=4] {'vocab'}, dimensions={0} | all-to-all | bytes 655360 | tf_op jit(solution)/shard_map/all_to_all | solution.py:513
  92.4 2.6 %collective-permute-start.13 = (bf16[16,80,128]{2,1,0:T(8,128)(2,1)S(1)}, bf16[16,80,128]{2,1,0:T(8,128)(2,1)S(1)}, u32[]{:S(2)}, u32[]{:S(2)}) collective-permute-start(bf16[16,80,128]{2,1,0:T(8,128)(2,1)S(1)} %all_to_all.23.own_ref), channel_id=1, source_target_pairs={{0,64},{64,0},{1,65},{65,1},{2,66},{66,2},{3,67},{67,3},{4,68},{68... | collective-permute-start | bytes 983048 | tf_op jit(solution)/shard_map/ppermute | solution.py:463
  95.0 2.4 %shard_map.92 = (bf16[64,192]{1,0:T(8,128)(2,1)S(1)}, f32[64,2048]{1,0:T(8,128)S(1)}, f32[64,64]{1,0:T(8,128)S(1)}, bf16[64,1024]{1,0:T(8,128)(2,1)S(1)}) custom-call(s32[1]{0:T(128)} %bitcast.me_ref.refs_0_, bf16[16,80,128]{2,1,0:T(8,128)(2,1)S(1)} %all_to_all.23.own_ref, bf16[64,512]{1,0:T(8,128)(2,1)S(1)} %get-tuple-element.59.mine_ref.rows_mine_ref, ...), custom_call_target="tpu_custom_call" | custom-call | flops 29360384 | bytes 458756 | tf_op jit(solution)/shard_map/pallas_call | solution.py:448
  97.5 0.9 shard_map.93
  98.9 1.3 %collective-permute-start.15 = (f32[64,64]{1,0:T(8,128)S(1)}, f32[64,64]{1,0:T(8,128)S(1)}, u32[]{:S(2)}, u32[]{:S(2)}) collective-permute-start(f32[64,64]{1,0:T(8,128)S(1)} %get-tuple-element.73.a_ref), channel_id=1, source_target_pairs={{0,3},{1,0},{2,1},{3,2},{4,7},{5,4},{6,5},{7,6},{8,11},{9,8},{10,9... | collective-permute-start | bytes 49160 | tf_op jit(solution)/shard_map/ppermute | solution.py:468
  100.3 4.9 %shard_map.94 = (bf16[1024,4096]{1,0:T(8,128)(2,1)}, f32[64,4096]{1,0:T(8,128)}, f32[64,4096]{1,0:T(8,128)}) custom-call(s32[1]{0:T(128)} %bitcast.me_ref.refs_0_, f32[64,2048]{1,0:T(8,128)S(1)} %get-tuple-element.67.own_ref, f32[64,2048]{1,0:T(8,128)S(1)} %get-tuple-element.70.other_ref, bf16[64,1024]{1,0:T(8,128)(2,1)S(1)} %get-tuple-element.71.left_ref, ...), custom_call_target="tpu_custom_call" | custom-call | flops 209715456 | bytes 3276804 | tf_op jit(solution)/shard_map/pallas_call | solution.py:448
  105.3 2.7 %shard_map.95 = f32[64,4096]{1,0:T(8,128)} custom-call(s32[1]{0:T(128)} %bitcast.me_ref.refs_0_, f32[64,2048]{1,0:T(8,128)S(1)} %get-tuple-element.67.own_ref, f32[64,2048]{1,0:T(8,128)S(1)} %get-tuple-element.70.other_ref, f32[64,64]{1,0:T(8,128)S(1)} %get-tuple-element.73.a_ref, f32[64,64]{1,0:T(8,128)S(1)} %collective-permute-done.14.b_ref, ...), custom_call_target="tpu_custom_call" | custom-call | flops 71303424 | bytes 1114116 | tf_op jit(solution)/shard_map/pallas_call | solution.py:448
  (33 shorter events, 5.2 us)
Async XLA Ops:
  4.7 2.8 %collective-permute-start = (bf16[64,512]{1,0:T(8,128)(2,1)S(1)}, bf16[64,512]{1,0:T(8,128)(2,1)S(1)}, u32[]{:S(2)}, u32[]{:S(2)}) collective-permute-start(bf16[64,512]{1,0:T(8,128)(2,1)S(1)} %get-tuple-element.42), channel_id=1, source_target_pairs={{0,64},{64,0},{1,65},{65,1},{2,66},{66,2},{3,67},{67,3},{4,68},{68... | collective-permute-start | bytes 196616 | tf_op jit(solution)/shard_map/ppermute | solution.py:463
  7.5 5.3 %collective-permute-start.3 = (bf16[64,512]{1,0:T(8,128)(2,1)S(1)}, bf16[64,512]{1,0:T(8,128)(2,1)S(1)}, u32[]{:S(2)}, u32[]{:S(2)}) collective-permute-start(bf16[64,512]{1,0:T(8,128)(2,1)S(1)} %add_convert_fusion.1), channel_id=1, source_target_pairs={{0,2},{1,3},{2,0},{3,1},{4,6},{5,7},{6,4},{7,5},{8,10},{9,11},{10,... | collective-permute-start | bytes 196616 | tf_op jit(solution)/shard_map/ppermute | solution.py:468
  10.4 3.9 %collective-permute-start.2 = (bf16[64,512]{1,0:T(8,128)(2,1)S(1)}, bf16[64,512]{1,0:T(8,128)(2,1)S(1)}, u32[]{:S(2)}, u32[]{:S(2)}) collective-permute-start(bf16[64,512]{1,0:T(8,128)(2,1)S(1)} %add_convert_fusion.1), channel_id=1, source_target_pairs={{0,3},{1,0},{2,1},{3,2},{4,7},{5,4},{6,5},{7,6},{8,11},{9,8},{10,9... | collective-permute-start | bytes 196616 | tf_op jit(solution)/shard_map/ppermute | solution.py:468
  11.3 4.3 %collective-permute-start.1 = (bf16[64,512]{1,0:T(8,128)(2,1)S(1)}, bf16[64,512]{1,0:T(8,128)(2,1)S(1)}, u32[]{:S(2)}, u32[]{:S(2)}) collective-permute-start(bf16[64,512]{1,0:T(8,128)(2,1)S(1)} %add_convert_fusion.1), channel_id=1, source_target_pairs={{0,1},{1,2},{2,3},{3,0},{4,5},{5,6},{6,7},{7,4},{8,9},{9,10},{10,1... | collective-permute-start | bytes 196616 | tf_op jit(solution)/shard_map/ppermute | solution.py:468
  15.7 2.7 %collective-permute-start.4 = (bf16[64,512]{1,0:T(8,128)(2,1)S(1)}, bf16[64,512]{1,0:T(8,128)(2,1)S(1)}, u32[]{:S(2)}, u32[]{:S(2)}) collective-permute-start(bf16[64,512]{1,0:T(8,128)(2,1)S(1)} %add_convert_fusion.refs_1_.mine_ref), channel_id=1, source_target_pairs={{0,64},{64,0},{1,65},{65,1},{2,66},{66,2},{3,67},{67,3},{4,68},{68... | collective-permute-start | bytes 196616 | tf_op jit(solution)/shard_map/ppermute | solution.py:463
  18.9 1.6 %collective-permute-start.5 = (bf16[16,64,128]{2,1,0:T(8,128)(2,1)S(1)}, bf16[16,64,128]{2,1,0:T(8,128)(2,1)S(1)}, u32[]{:S(2)}, u32[]{:S(2)}) collective-permute-start(bf16[16,64,128]{2,1,0:T(8,128)(2,1)S(1)} %shard_map.79), channel_id=1, source_target_pairs={{0,64},{64,0},{1,65},{65,1},{2,66},{66,2},{3,67},{67,3},{4,68},{68... | collective-permute-start | bytes 786440 | tf_op jit(solution)/shard_map/ppermute | solution.py:463
  47.6 6.1 %collective-permute-start.6 = (bf16[16,80,128]{2,1,0:T(8,128)(2,1)S(1)}, bf16[16,80,128]{2,1,0:T(8,128)(2,1)S(1)}, u32[]{:S(2)}, u32[]{:S(2)}) collective-permute-start(bf16[16,80,128]{2,1,0:T(8,128)(2,1)S(1)} %all_to_all.21.own_ref), channel_id=1, source_target_pairs={{0,64},{64,0},{1,65},{65,1},{2,66},{66,2},{3,67},{67,3},{4,68},{68... | collective-permute-start | bytes 983048 | tf_op jit(solution)/shard_map/ppermute | solution.py:463
  54.7 1.3 %collective-permute-start.7 = (bf16[64,512]{1,0:T(8,128)(2,1)S(1)}, bf16[64,512]{1,0:T(8,128)(2,1)S(1)}, u32[]{:S(2)}, u32[]{:S(2)}) collective-permute-start(bf16[64,512]{1,0:T(8,128)(2,1)S(1)} %get-tuple-element.55), channel_id=1, source_target_pairs={{0,64},{64,0},{1,65},{65,1},{2,66},{66,2},{3,67},{67,3},{4,68},{68... | collective-permute-start | bytes 196616 | tf_op jit(solution)/shard_map/ppermute | solution.py:463
  56.0 5.4 %collective-permute-start.10 = (bf16[80,512]{1,0:T(8,128)(2,1)S(1)}, bf16[80,512]{1,0:T(8,128)(2,1)S(1)}, u32[]{:S(2)}, u32[]{:S(2)}) collective-permute-start(bf16[80,512]{1,0:T(8,128)(2,1)S(1)} %shard_map.85.a_ref), channel_id=1, source_target_pairs={{0,2},{1,3},{2,0},{3,1},{4,6},{5,7},{6,4},{7,5},{8,10},{9,11},{10,... | collective-permute-start | bytes 245768 | tf_op jit(solution)/shard_map/ppermute | solution.py:468
  56.6 4.8 %collective-permute-start.9 = (bf16[80,512]{1,0:T(8,128)(2,1)S(1)}, bf16[80,512]{1,0:T(8,128)(2,1)S(1)}, u32[]{:S(2)}, u32[]{:S(2)}) collective-permute-start(bf16[80,512]{1,0:T(8,128)(2,1)S(1)} %shard_map.85.a_ref), channel_id=1, source_target_pairs={{0,3},{1,0},{2,1},{3,2},{4,7},{5,4},{6,5},{7,6},{8,11},{9,8},{10,9... | collective-permute-start | bytes 245768 | tf_op jit(solution)/shard_map/ppermute | solution.py:468
  57.9 4.8 %collective-permute-start.8 = (bf16[80,512]{1,0:T(8,128)(2,1)S(1)}, bf16[80,512]{1,0:T(8,128)(2,1)S(1)}, u32[]{:S(2)}, u32[]{:S(2)}) collective-permute-start(bf16[80,512]{1,0:T(8,128)(2,1)S(1)} %shard_map.85.a_ref), channel_id=1, source_target_pairs={{0,1},{1,2},{2,3},{3,0},{4,5},{5,6},{6,7},{7,4},{8,9},{9,10},{10,1... | collective-permute-start | bytes 245768 | tf_op jit(solution)/shard_map/ppermute | solution.py:468
  63.0 4.0 %collective-permute-start.11 = (bf16[64,512]{1,0:T(8,128)(2,1)S(1)}, bf16[64,512]{1,0:T(8,128)(2,1)S(1)}, u32[]{:S(2)}, u32[]{:S(2)}) collective-permute-start(bf16[64,512]{1,0:T(8,128)(2,1)S(1)} %get-tuple-element.57.refs_1_), channel_id=1, source_target_pairs={{0,64},{64,0},{1,65},{65,1},{2,66},{66,2},{3,67},{67,3},{4,68},{68... | collective-permute-start | bytes 196616 | tf_op jit(solution)/shard_map/ppermute | solution.py:463
  67.1 33.3 %copy-start = (f32[64,4096]{1,0:T(8,128)S(1)}, f32[64,4096]{1,0:T(8,128)}, u32[]{:S(2)}) copy-start(f32[64,4096]{1,0:T(8,128)} %first_ref.1) | copy-start | bytes 3145732
  67.1 33.3 %copy-start.1 = (f32[64,4096]{1,0:T(8,128)S(1)}, f32[64,4096]{1,0:T(8,128)}, u32[]{:S(2)}) copy-start(f32[64,4096]{1,0:T(8,128)} %second_ref.1) | copy-start | bytes 3145732
  67.7 1.6 %collective-permute-start.12 = (bf16[16,64,128]{2,1,0:T(8,128)(2,1)S(1)}, bf16[16,64,128]{2,1,0:T(8,128)(2,1)S(1)}, u32[]{:S(2)}, u32[]{:S(2)}) collective-permute-start(bf16[16,64,128]{2,1,0:T(8,128)(2,1)S(1)} %get-tuple-element.65), channel_id=1, source_target_pairs={{0,64},{64,0},{1,65},{65,1},{2,66},{66,2},{3,67},{67,3},{4,68},{68... | collective-permute-start | bytes 786440 | tf_op jit(solution)/shard_map/ppermute | solution.py:463
  92.4 5.1 %collective-permute-start.13 = (bf16[16,80,128]{2,1,0:T(8,128)(2,1)S(1)}, bf16[16,80,128]{2,1,0:T(8,128)(2,1)S(1)}, u32[]{:S(2)}, u32[]{:S(2)}) collective-permute-start(bf16[16,80,128]{2,1,0:T(8,128)(2,1)S(1)} %all_to_all.23.own_ref), channel_id=1, source_target_pairs={{0,64},{64,0},{1,65},{65,1},{2,66},{66,2},{3,67},{67,3},{4,68},{68... | collective-permute-start | bytes 983048 | tf_op jit(solution)/shard_map/ppermute | solution.py:463
  98.4 6.8 %collective-permute-start.16 = (f32[64,64]{1,0:T(8,128)S(1)}, f32[64,64]{1,0:T(8,128)S(1)}, u32[]{:S(2)}, u32[]{:S(2)}) collective-permute-start(f32[64,64]{1,0:T(8,128)S(1)} %get-tuple-element.73.a_ref), channel_id=1, source_target_pairs={{0,2},{1,3},{2,0},{3,1},{4,6},{5,7},{6,4},{7,5},{8,10},{9,11},{10,... | collective-permute-start | bytes 49160 | tf_op jit(solution)/shard_map/ppermute | solution.py:468
  98.9 6.4 %collective-permute-start.15 = (f32[64,64]{1,0:T(8,128)S(1)}, f32[64,64]{1,0:T(8,128)S(1)}, u32[]{:S(2)}, u32[]{:S(2)}) collective-permute-start(f32[64,64]{1,0:T(8,128)S(1)} %get-tuple-element.73.a_ref), channel_id=1, source_target_pairs={{0,3},{1,0},{2,1},{3,2},{4,7},{5,4},{6,5},{7,6},{8,11},{9,8},{10,9... | collective-permute-start | bytes 49160 | tf_op jit(solution)/shard_map/ppermute | solution.py:468
  100.1 5.1 %collective-permute-start.14 = (f32[64,64]{1,0:T(8,128)S(1)}, f32[64,64]{1,0:T(8,128)S(1)}, u32[]{:S(2)}, u32[]{:S(2)}) collective-permute-start(f32[64,64]{1,0:T(8,128)S(1)} %get-tuple-element.73.a_ref), channel_id=1, source_target_pairs={{0,1},{1,2},{2,3},{3,0},{4,5},{5,6},{6,7},{7,4},{8,9},{9,10},{10,1... | collective-permute-start | bytes 49160 | tf_op jit(solution)/shard_map/ppermute | solution.py:468

commit v10 on v9

--- a/solution.py
+++ b/solution.py
@@ -426,14 +426,15 @@
         for t in range(0, width, TILE):
             high, mid, _ = thirds(ref[:, t : t + TILE])
             tall = jnp.concatenate([high, mid, high], axis=0).astype(BF16)
-            basis_ref[:, i * width + t : i * width + t + TILE] = dot(wide, tall, 1, 0)
-        copy = pltpu.make_async_copy(
-            basis_ref.at[:, i * width : (i + 1) * width],
-            basis_hbm.at[:, span(core * width, width)],
-            sems.at[i],
-        )
-        copy.start()
-        copies.append(copy)
+            here = slice(i * width + t, i * width + t + TILE)
+            basis_ref[:, here] = dot(wide, tall, 1, 0)
+            copy = pltpu.make_async_copy(
+                basis_ref.at[:, here],
+                basis_hbm.at[:, span(core * width + t, TILE)],
+                sems.at[len(copies)],
+            )
+            copy.start()
+            copies.append(copy)
     for copy in copies:
         copy.wait()
 
@@ -591,7 +592,7 @@
         basis_kernel,
         [wide],
         [me, columns_own, columns_other, gram, *gram_others],
-        [wide, pltpu.SemaphoreType.DMA((2,))],
+        [wide, pltpu.SemaphoreType.DMA((width // TILE,))],
         hbm_out=(0,),
     )[0]
     return (update, basis, new_first, new_second)

time: 108 us -> 108 us (level)
  no operation moved by 1% of the time
where the time goes in v10:
time: 108 us
  blocking collectives  50 us (46%)
  Pallas kernels  27.3 us (25%)
  starting transfers between devices  19.8 us (18%)
  waiting for transfers between devices  9.95 us (9%)
    pallas_call x21, Pallas kernels, call(): pl.pallas_call(kernel, out_shape=[jax.ShapeDtypeStruct(s, t) for s, t in...  27.3 us
    all_to_all x2, blocking collectives, columns_of(): parts = lax.all_to_all(chunks, 'vocab', 0, 0)  26.9 us
    all_to_all x2, blocking collectives, columns_of(): own = lax.all_to_all(copies, 'vocab', 0, 0)  23.1 us
    ppermute x8, starting transfers between devices, swapped(): return lax.ppermute(x, 'dp', [(0, 1), (1, 0)])  11.4 us
    ppermute x9, starting transfers between devices, others(): lax.ppermute(x, 'mp', [(i, (i + k) % n) for i in range(n)])  8.36 us
    ppermute x9, waiting for transfers between devices, others(): lax.ppermute(x, 'mp', [(i, (i + k) % n) for i in range(n)])  8.33 us
  transfers between devices with their start and end apart: 17, of which 9 were waited for; matrix products, arithmetic and copies ran while one was open for 0% of the time, Pallas kernels for 16%

profile of v10, /device:TPU:1, one launch (start us, length us, event | category | flops | bytes accessed | tf_op | source)
XLA Modules:
  0.0 108.1 jit_solution(15905269873080710362)
XLA Ops:
  0.6 4.0 %shard_map.75 = (bf16[64,512]{1,0:T(8,128)(2,1)S(1)}, bf16[64,4096]{1,0:T(8,128)(2,1)S(1)}, bf16[512,4096]{1,0:T(8,128)(2,1)S(1)}, bf16[512,4096]{1,0:T(8,128)(2,1)S(1)}) custom-call(s32[1]{0:T(128)} %bitcast.me_ref.refs_0_, f32[64,4096]{1,0:T(8,128)} %basis_hbm.1, bf16[1024,4096]{1,0:T(8,128)(2,1)} %bitcast.2), custom_call_target="tpu_custom_call" | custom-call | flops 603980032 | bytes 9437188 | tf_op jit(solution)/shard_map/pallas_call | solution.py:449
  4.7 1.5 %collective-permute-start = (bf16[64,512]{1,0:T(8,128)(2,1)S(1)}, bf16[64,512]{1,0:T(8,128)(2,1)S(1)}, u32[]{:S(2)}, u32[]{:S(2)}) collective-permute-start(bf16[64,512]{1,0:T(8,128)(2,1)S(1)} %get-tuple-element.42), channel_id=1, source_target_pairs={{0,64},{64,0},{1,65},{65,1},{2,66},{66,2},{3,67},{67,3},{4,68},{68... | collective-permute-start | bytes 196616 | tf_op jit(solution)/shard_map/ppermute | solution.py:464
  6.2 1.3 %shard_map.76 = f32[64,512]{1,0:T(8,128)S(1)} custom-call(bf16[64,4096]{1,0:T(8,128)(2,1)S(1)} %get-tuple-element.40.left_ref, bf16[512,4096]{1,0:T(8,128)(2,1)S(1)} %get-tuple-element.41.slab_ref.refs_2_.mine_slab_ref.refs_3_), custom_call_target="tpu_custom_call" | custom-call | flops 301989888 | bytes 4718592 | tf_op jit(solution)/shard_map/pallas_call | solution.py:449
  7.5 2.9 %collective-permute-start.3 = (bf16[64,512]{1,0:T(8,128)(2,1)S(1)}, bf16[64,512]{1,0:T(8,128)(2,1)S(1)}, u32[]{:S(2)}, u32[]{:S(2)}) collective-permute-start(bf16[64,512]{1,0:T(8,128)(2,1)S(1)} %add_convert_fusion.1), channel_id=1, source_target_pairs={{0,2},{1,3},{2,0},{3,1},{4,6},{5,7},{6,4},{7,5},{8,10},{9,11},{10,... | collective-permute-start | bytes 196616 | tf_op jit(solution)/shard_map/ppermute | solution.py:469
  10.4 0.9 collective-permute-start.2
  11.3 0.6 collective-permute-start.1
  11.9 0.9 collective-permute-done.3
  12.8 1.5 %collective-permute-done.2 = bf16[64,512]{1,0:T(8,128)(2,1)S(1)} collective-permute-done((bf16[64,512]{1,0:T(8,128)(2,1)S(1)}, bf16[64,512]{1,0:T(8,128)(2,1)S(1)}, u32[]{:S(2)}, u32[]{:S(2)}) %collective-permute-start.2) | collective-permute-done | bytes 65568 | tf_op jit(solution)/shard_map/ppermute | solution.py:469
  14.3 1.3 %collective-permute-done.1 = bf16[64,512]{1,0:T(8,128)(2,1)S(1)} collective-permute-done((bf16[64,512]{1,0:T(8,128)(2,1)S(1)}, bf16[64,512]{1,0:T(8,128)(2,1)S(1)}, u32[]{:S(2)}, u32[]{:S(2)}) %collective-permute-start.1) | collective-permute-done | bytes 65568 | tf_op jit(solution)/shard_map/ppermute | solution.py:469
  15.7 1.8 %collective-permute-start.4 = (bf16[64,512]{1,0:T(8,128)(2,1)S(1)}, bf16[64,512]{1,0:T(8,128)(2,1)S(1)}, u32[]{:S(2)}, u32[]{:S(2)}) collective-permute-start(bf16[64,512]{1,0:T(8,128)(2,1)S(1)} %add_convert_fusion.refs_1_.mine_ref), channel_id=1, source_target_pairs={{0,64},{64,0},{1,65},{65,1},{2,66},{66,2},{3,67},{67,3},{4,68},{68... | collective-permute-start | bytes 196616 | tf_op jit(solution)/shard_map/ppermute | solution.py:464
  19.3 0.9 shard_map.78
  20.5 15.5 %all_to_all.20.parts_ref = bf16[16,80,128]{2,1,0:T(8,128)(2,1)S(1)} all-to-all(bf16[16,80,128]{2,1,0:T(8,128)(2,1)S(1)} %shard_map.80), channel_id=1, replica_groups=mesh['dp'=2,'vocab'=16,'mp'=4] {'vocab'}, dimensions={0} | all-to-all | bytes 655360 | tf_op jit(solution)/shard_map/all_to_all | solution.py:512
  36.1 11.5 %all_to_all.21.own_ref = bf16[16,80,128]{2,1,0:T(8,128)(2,1)S(1)} all-to-all(bf16[16,80,128]{2,1,0:T(8,128)(2,1)S(1)} %shard_map.81), channel_id=1, replica_groups=mesh['dp'=2,'vocab'=16,'mp'=4] {'vocab'}, dimensions={0} | all-to-all | bytes 655360 | tf_op jit(solution)/shard_map/all_to_all | solution.py:514
  47.6 2.9 %collective-permute-start.6 = (bf16[16,80,128]{2,1,0:T(8,128)(2,1)S(1)}, bf16[16,80,128]{2,1,0:T(8,128)(2,1)S(1)}, u32[]{:S(2)}, u32[]{:S(2)}) collective-permute-start(bf16[16,80,128]{2,1,0:T(8,128)(2,1)S(1)} %all_to_all.21.own_ref), channel_id=1, source_target_pairs={{0,64},{64,0},{1,65},{65,1},{2,66},{66,2},{3,67},{67,3},{4,68},{68... | collective-permute-start | bytes 983048 | tf_op jit(solution)/shard_map/ppermute | solution.py:464
  50.6 3.2 %shard_map.82 = (bf16[64,192]{1,0:T(8,128)(2,1)S(1)}, f32[64,512]{1,0:T(8,128)S(1)}, f32[64,512]{1,0:T(8,128)S(1)}, f32[64,64]{1,0:T(8,128)S(1)}) custom-call(s32[1]{0:T(128)} %bitcast.me_ref.refs_0_, bf16[16,80,128]{2,1,0:T(8,128)(2,1)S(1)} %all_to_all.21.own_ref, bf16[512,4096]{1,0:T(8,128)(2,1)S(1)} %get-tuple-element.43.theirs_slab_ref.refs_3_.slab_ref, ...), custom_call_target="tpu_custom_call" | custom-call | flops 557842688 | bytes 8716292 | tf_op jit(solution)/shard_map/pallas_call | solution.py:449
  53.7 0.9 shard_map.83
  54.8 1.0 shard_map.84
  56.6 1.3 %collective-permute-start.9 = (bf16[80,512]{1,0:T(8,128)(2,1)S(1)}, bf16[80,512]{1,0:T(8,128)(2,1)S(1)}, u32[]{:S(2)}, u32[]{:S(2)}) collective-permute-start(bf16[80,512]{1,0:T(8,128)(2,1)S(1)} %shard_map.85.a_ref), channel_id=1, source_target_pairs={{0,3},{1,0},{2,1},{3,2},{4,7},{5,4},{6,5},{7,6},{8,11},{9,8},{10,9... | collective-permute-start | bytes 245768 | tf_op jit(solution)/shard_map/ppermute | solution.py:469
  58.1 3.3 %collective-permute-done.10.d_ref = bf16[80,512]{1,0:T(8,128)(2,1)S(1)} collective-permute-done((bf16[80,512]{1,0:T(8,128)(2,1)S(1)}, bf16[80,512]{1,0:T(8,128)(2,1)S(1)}, u32[]{:S(2)}, u32[]{:S(2)}) %collective-permute-start.10) | collective-permute-done | bytes 81952 | tf_op jit(solution)/shard_map/ppermute | solution.py:469
  61.4 1.3 %collective-permute-done.8.b_ref = bf16[80,512]{1,0:T(8,128)(2,1)S(1)} collective-permute-done((bf16[80,512]{1,0:T(8,128)(2,1)S(1)}, bf16[80,512]{1,0:T(8,128)(2,1)S(1)}, u32[]{:S(2)}, u32[]{:S(2)}) %collective-permute-start.8) | collective-permute-done | bytes 81952 | tf_op jit(solution)/shard_map/ppermute | solution.py:469
  63.0 1.9 %collective-permute-start.11 = (bf16[64,512]{1,0:T(8,128)(2,1)S(1)}, bf16[64,512]{1,0:T(8,128)(2,1)S(1)}, u32[]{:S(2)}, u32[]{:S(2)}) collective-permute-start(bf16[64,512]{1,0:T(8,128)(2,1)S(1)} %get-tuple-element.57.refs_1_), channel_id=1, source_target_pairs={{0,64},{64,0},{1,65},{65,1},{2,66},{66,2},{3,67},{67,3},{4,68},{68... | collective-permute-start | bytes 196616 | tf_op jit(solution)/shard_map/ppermute | solution.py:464
  64.9 2.1 %shard_map.87 = (f32[64,2048]{1,0:T(8,128)S(1)}, f32[64,64]{1,0:T(8,128)S(1)}, bf16[64,192]{1,0:T(8,128)(2,1)S(1)}, bf16[64,512]{1,0:T(8,128)(2,1)S(1)}) custom-call(s32[1]{0:T(128)} %bitcast.me_ref.refs_0_, bf16[64,512]{1,0:T(8,128)(2,1)S(1)} %get-tuple-element.57.refs_1_, f32[64,64]{1,0:T(8,128)S(1)} %get-tuple-element.58.refs_2_, ...), custom_call_target="tpu_custom_call" | custom-call | flops 273678592 | bytes 4276228 | tf_op jit(solution)/shard_map/pallas_call | solution.py:449
  67.8 0.9 shard_map.89
  68.7 0.6 collective-permute-done.12.got_ref
  69.4 11.4 %all_to_all.22.parts_ref = bf16[16,80,128]{2,1,0:T(8,128)(2,1)S(1)} all-to-all(bf16[16,80,128]{2,1,0:T(8,128)(2,1)S(1)} %shard_map.90), channel_id=1, replica_groups=mesh['dp'=2,'vocab'=16,'mp'=4] {'vocab'}, dimensions={0} | all-to-all | bytes 655360 | tf_op jit(solution)/shard_map/all_to_all | solution.py:512
  80.8 11.6 %all_to_all.23.own_ref = bf16[16,80,128]{2,1,0:T(8,128)(2,1)S(1)} all-to-all(bf16[16,80,128]{2,1,0:T(8,128)(2,1)S(1)} %shard_map.91), channel_id=1, replica_groups=mesh['dp'=2,'vocab'=16,'mp'=4] {'vocab'}, dimensions={0} | all-to-all | bytes 655360 | tf_op jit(solution)/shard_map/all_to_all | solution.py:514
  92.4 2.6 %collective-permute-start.13 = (bf16[16,80,128]{2,1,0:T(8,128)(2,1)S(1)}, bf16[16,80,128]{2,1,0:T(8,128)(2,1)S(1)}, u32[]{:S(2)}, u32[]{:S(2)}) collective-permute-start(bf16[16,80,128]{2,1,0:T(8,128)(2,1)S(1)} %all_to_all.23.own_ref), channel_id=1, source_target_pairs={{0,64},{64,0},{1,65},{65,1},{2,66},{66,2},{3,67},{67,3},{4,68},{68... | collective-permute-start | bytes 983048 | tf_op jit(solution)/shard_map/ppermute | solution.py:464
  95.0 2.4 %shard_map.92 = (bf16[64,192]{1,0:T(8,128)(2,1)S(1)}, f32[64,2048]{1,0:T(8,128)S(1)}, f32[64,64]{1,0:T(8,128)S(1)}, bf16[64,1024]{1,0:T(8,128)(2,1)S(1)}) custom-call(s32[1]{0:T(128)} %bitcast.me_ref.refs_0_, bf16[16,80,128]{2,1,0:T(8,128)(2,1)S(1)} %all_to_all.23.own_ref, bf16[64,512]{1,0:T(8,128)(2,1)S(1)} %get-tuple-element.59.mine_ref.rows_mine_ref, ...), custom_call_target="tpu_custom_call" | custom-call | flops 29360384 | bytes 458756 | tf_op jit(solution)/shard_map/pallas_call | solution.py:449
  97.5 0.9 shard_map.93
  98.9 1.3 %collective-permute-start.15 = (f32[64,64]{1,0:T(8,128)S(1)}, f32[64,64]{1,0:T(8,128)S(1)}, u32[]{:S(2)}, u32[]{:S(2)}) collective-permute-start(f32[64,64]{1,0:T(8,128)S(1)} %get-tuple-element.73.a_ref), channel_id=1, source_target_pairs={{0,3},{1,0},{2,1},{3,2},{4,7},{5,4},{6,5},{7,6},{8,11},{9,8},{10,9... | collective-permute-start | bytes 49160 | tf_op jit(solution)/shard_map/ppermute | solution.py:469
  100.3 4.9 %shard_map.94 = (bf16[1024,4096]{1,0:T(8,128)(2,1)}, f32[64,4096]{1,0:T(8,128)}, f32[64,4096]{1,0:T(8,128)}) custom-call(s32[1]{0:T(128)} %bitcast.me_ref.refs_0_, f32[64,2048]{1,0:T(8,128)S(1)} %get-tuple-element.67.own_ref, f32[64,2048]{1,0:T(8,128)S(1)} %get-tuple-element.70.other_ref, bf16[64,1024]{1,0:T(8,128)(2,1)S(1)} %get-tuple-element.71.left_ref, ...), custom_call_target="tpu_custom_call" | custom-call | flops 209715456 | bytes 3276804 | tf_op jit(solution)/shard_map/pallas_call | solution.py:449
  105.3 2.7 %shard_map.95 = f32[64,4096]{1,0:T(8,128)} custom-call(s32[1]{0:T(128)} %bitcast.me_ref.refs_0_, f32[64,2048]{1,0:T(8,128)S(1)} %get-tuple-element.67.own_ref, f32[64,2048]{1,0:T(8,128)S(1)} %get-tuple-element.70.other_ref, f32[64,64]{1,0:T(8,128)S(1)} %get-tuple-element.73.a_ref, f32[64,64]{1,0:T(8,128)S(1)} %collective-permute-done.14.b_ref, ...), custom_call_target="tpu_custom_call" | custom-call | flops 71303424 | bytes 1114116 | tf_op jit(solution)/shard_map/pallas_call | solution.py:449
  (33 shorter events, 5.2 us)
Async XLA Ops:
  4.7 2.8 %collective-permute-start = (bf16[64,512]{1,0:T(8,128)(2,1)S(1)}, bf16[64,512]{1,0:T(8,128)(2,1)S(1)}, u32[]{:S(2)}, u32[]{:S(2)}) collective-permute-start(bf16[64,512]{1,0:T(8,128)(2,1)S(1)} %get-tuple-element.42), channel_id=1, source_target_pairs={{0,64},{64,0},{1,65},{65,1},{2,66},{66,2},{3,67},{67,3},{4,68},{68... | collective-permute-start | bytes 196616 | tf_op jit(solution)/shard_map/ppermute | solution.py:464
  7.5 5.3 %collective-permute-start.3 = (bf16[64,512]{1,0:T(8,128)(2,1)S(1)}, bf16[64,512]{1,0:T(8,128)(2,1)S(1)}, u32[]{:S(2)}, u32[]{:S(2)}) collective-permute-start(bf16[64,512]{1,0:T(8,128)(2,1)S(1)} %add_convert_fusion.1), channel_id=1, source_target_pairs={{0,2},{1,3},{2,0},{3,1},{4,6},{5,7},{6,4},{7,5},{8,10},{9,11},{10,... | collective-permute-start | bytes 196616 | tf_op jit(solution)/shard_map/ppermute | solution.py:469
  10.4 3.9 %collective-permute-start.2 = (bf16[64,512]{1,0:T(8,128)(2,1)S(1)}, bf16[64,512]{1,0:T(8,128)(2,1)S(1)}, u32[]{:S(2)}, u32[]{:S(2)}) collective-permute-start(bf16[64,512]{1,0:T(8,128)(2,1)S(1)} %add_convert_fusion.1), channel_id=1, source_target_pairs={{0,3},{1,0},{2,1},{3,2},{4,7},{5,4},{6,5},{7,6},{8,11},{9,8},{10,9... | collective-permute-start | bytes 196616 | tf_op jit(solution)/shard_map/ppermute | solution.py:469
  11.3 4.3 %collective-permute-start.1 = (bf16[64,512]{1,0:T(8,128)(2,1)S(1)}, bf16[64,512]{1,0:T(8,128)(2,1)S(1)}, u32[]{:S(2)}, u32[]{:S(2)}) collective-permute-start(bf16[64,512]{1,0:T(8,128)(2,1)S(1)} %add_convert_fusion.1), channel_id=1, source_target_pairs={{0,1},{1,2},{2,3},{3,0},{4,5},{5,6},{6,7},{7,4},{8,9},{9,10},{10,1... | collective-permute-start | bytes 196616 | tf_op jit(solution)/shard_map/ppermute | solution.py:469
  15.7 2.7 %collective-permute-start.4 = (bf16[64,512]{1,0:T(8,128)(2,1)S(1)}, bf16[64,512]{1,0:T(8,128)(2,1)S(1)}, u32[]{:S(2)}, u32[]{:S(2)}) collective-permute-start(bf16[64,512]{1,0:T(8,128)(2,1)S(1)} %add_convert_fusion.refs_1_.mine_ref), channel_id=1, source_target_pairs={{0,64},{64,0},{1,65},{65,1},{2,66},{66,2},{3,67},{67,3},{4,68},{68... | collective-permute-start | bytes 196616 | tf_op jit(solution)/shard_map/ppermute | solution.py:464
  18.9 1.6 %collective-permute-start.5 = (bf16[16,64,128]{2,1,0:T(8,128)(2,1)S(1)}, bf16[16,64,128]{2,1,0:T(8,128)(2,1)S(1)}, u32[]{:S(2)}, u32[]{:S(2)}) collective-permute-start(bf16[16,64,128]{2,1,0:T(8,128)(2,1)S(1)} %shard_map.79), channel_id=1, source_target_pairs={{0,64},{64,0},{1,65},{65,1},{2,66},{66,2},{3,67},{67,3},{4,68},{68... | collective-permute-start | bytes 786440 | tf_op jit(solution)/shard_map/ppermute | solution.py:464
  47.6 6.1 %collective-permute-start.6 = (bf16[16,80,128]{2,1,0:T(8,128)(2,1)S(1)}, bf16[16,80,128]{2,1,0:T(8,128)(2,1)S(1)}, u32[]{:S(2)}, u32[]{:S(2)}) collective-permute-start(bf16[16,80,128]{2,1,0:T(8,128)(2,1)S(1)} %all_to_all.21.own_ref), channel_id=1, source_target_pairs={{0,64},{64,0},{1,65},{65,1},{2,66},{66,2},{3,67},{67,3},{4,68},{68... | collective-permute-start | bytes 983048 | tf_op jit(solution)/shard_map/ppermute | solution.py:464
  54.7 1.3 %collective-permute-start.7 = (bf16[64,512]{1,0:T(8,128)(2,1)S(1)}, bf16[64,512]{1,0:T(8,128)(2,1)S(1)}, u32[]{:S(2)}, u32[]{:S(2)}) collective-permute-start(bf16[64,512]{1,0:T(8,128)(2,1)S(1)} %get-tuple-element.55), channel_id=1, source_target_pairs={{0,64},{64,0},{1,65},{65,1},{2,66},{66,2},{3,67},{67,3},{4,68},{68... | collective-permute-start | bytes 196616 | tf_op jit(solution)/shard_map/ppermute | solution.py:464
  56.0 5.4 %collective-permute-start.10 = (bf16[80,512]{1,0:T(8,128)(2,1)S(1)}, bf16[80,512]{1,0:T(8,128)(2,1)S(1)}, u32[]{:S(2)}, u32[]{:S(2)}) collective-permute-start(bf16[80,512]{1,0:T(8,128)(2,1)S(1)} %shard_map.85.a_ref), channel_id=1, source_target_pairs={{0,2},{1,3},{2,0},{3,1},{4,6},{5,7},{6,4},{7,5},{8,10},{9,11},{10,... | collective-permute-start | bytes 245768 | tf_op jit(solution)/shard_map/ppermute | solution.py:469
  56.6 4.8 %collective-permute-start.9 = (bf16[80,512]{1,0:T(8,128)(2,1)S(1)}, bf16[80,512]{1,0:T(8,128)(2,1)S(1)}, u32[]{:S(2)}, u32[]{:S(2)}) collective-permute-start(bf16[80,512]{1,0:T(8,128)(2,1)S(1)} %shard_map.85.a_ref), channel_id=1, source_target_pairs={{0,3},{1,0},{2,1},{3,2},{4,7},{5,4},{6,5},{7,6},{8,11},{9,8},{10,9... | collective-permute-start | bytes 245768 | tf_op jit(solution)/shard_map/ppermute | solution.py:469
  57.9 4.8 %collective-permute-start.8 = (bf16[80,512]{1,0:T(8,128)(2,1)S(1)}, bf16[80,512]{1,0:T(8,128)(2,1)S(1)}, u32[]{:S(2)}, u32[]{:S(2)}) collective-permute-start(bf16[80,512]{1,0:T(8,128)(2,1)S(1)} %shard_map.85.a_ref), channel_id=1, source_target_pairs={{0,1},{1,2},{2,3},{3,0},{4,5},{5,6},{6,7},{7,4},{8,9},{9,10},{10,1... | collective-permute-start | bytes 245768 | tf_op jit(solution)/shard_map/ppermute | solution.py:469
  63.0 4.0 %collective-permute-start.11 = (bf16[64,512]{1,0:T(8,128)(2,1)S(1)}, bf16[64,512]{1,0:T(8,128)(2,1)S(1)}, u32[]{:S(2)}, u32[]{:S(2)}) collective-permute-start(bf16[64,512]{1,0:T(8,128)(2,1)S(1)} %get-tuple-element.57.refs_1_), channel_id=1, source_target_pairs={{0,64},{64,0},{1,65},{65,1},{2,66},{66,2},{3,67},{67,3},{4,68},{68... | collective-permute-start | bytes 196616 | tf_op jit(solution)/shard_map/ppermute | solution.py:464
  67.1 33.3 %copy-start = (f32[64,4096]{1,0:T(8,128)S(1)}, f32[64,4096]{1,0:T(8,128)}, u32[]{:S(2)}) copy-start(f32[64,4096]{1,0:T(8,128)} %first_ref.1) | copy-start | bytes 3145732
  67.1 33.3 %copy-start.1 = (f32[64,4096]{1,0:T(8,128)S(1)}, f32[64,4096]{1,0:T(8,128)}, u32[]{:S(2)}) copy-start(f32[64,4096]{1,0:T(8,128)} %second_ref.1) | copy-start | bytes 3145732
  67.7 1.6 %collective-permute-start.12 = (bf16[16,64,128]{2,1,0:T(8,128)(2,1)S(1)}, bf16[16,64,128]{2,1,0:T(8,128)(2,1)S(1)}, u32[]{:S(2)}, u32[]{:S(2)}) collective-permute-start(bf16[16,64,128]{2,1,0:T(8,128)(2,1)S(1)} %get-tuple-element.65), channel_id=1, source_target_pairs={{0,64},{64,0},{1,65},{65,1},{2,66},{66,2},{3,67},{67,3},{4,68},{68... | collective-permute-start | bytes 786440 | tf_op jit(solution)/shard_map/ppermute | solution.py:464
  92.4 5.1 %collective-permute-start.13 = (bf16[16,80,128]{2,1,0:T(8,128)(2,1)S(1)}, bf16[16,80,128]{2,1,0:T(8,128)(2,1)S(1)}, u32[]{:S(2)}, u32[]{:S(2)}) collective-permute-start(bf16[16,80,128]{2,1,0:T(8,128)(2,1)S(1)} %all_to_all.23.own_ref), channel_id=1, source_target_pairs={{0,64},{64,0},{1,65},{65,1},{2,66},{66,2},{3,67},{67,3},{4,68},{68... | collective-permute-start | bytes 983048 | tf_op jit(solution)/shard_map/ppermute | solution.py:464
  98.4 6.8 %collective-permute-start.16 = (f32[64,64]{1,0:T(8,128)S(1)}, f32[64,64]{1,0:T(8,128)S(1)}, u32[]{:S(2)}, u32[]{:S(2)}) collective-permute-start(f32[64,64]{1,0:T(8,128)S(1)} %get-tuple-element.73.a_ref), channel_id=1, source_target_pairs={{0,2},{1,3},{2,0},{3,1},{4,6},{5,7},{6,4},{7,5},{8,10},{9,11},{10,... | collective-permute-start | bytes 49160 | tf_op jit(solution)/shard_map/ppermute | solution.py:469
  98.9 6.4 %collective-permute-start.15 = (f32[64,64]{1,0:T(8,128)S(1)}, f32[64,64]{1,0:T(8,128)S(1)}, u32[]{:S(2)}, u32[]{:S(2)}) collective-permute-start(f32[64,64]{1,0:T(8,128)S(1)} %get-tuple-element.73.a_ref), channel_id=1, source_target_pairs={{0,3},{1,0},{2,1},{3,2},{4,7},{5,4},{6,5},{7,6},{8,11},{9,8},{10,9... | collective-permute-start | bytes 49160 | tf_op jit(solution)/shard_map/ppermute | solution.py:469
  100.1 5.1 %collective-permute-start.14 = (f32[64,64]{1,0:T(8,128)S(1)}, f32[64,64]{1,0:T(8,128)S(1)}, u32[]{:S(2)}, u32[]{:S(2)}) collective-permute-start(f32[64,64]{1,0:T(8,128)S(1)} %get-tuple-element.73.a_ref), channel_id=1, source_target_pairs={{0,1},{1,2},{2,3},{3,0},{4,5},{5,6},{6,7},{7,4},{8,9},{9,10},{10,1... | collective-permute-start | bytes 49160 | tf_op jit(solution)/shard_map/ppermute | solution.py:469
